TPU v7x, 256 devices: a whole 4x4x8 slice. The times are simulated.
256 devices in a mesh: lat: 8 (over y, x_hi), lon: 32 (over x_lo, z, core).
Axes of the slice: x: 4 (x_hi: 2, x_lo: 2; x = x_hi * 2 + x_lo), y: 4, z: 8, core: 2. Of those that a mesh axis runs over, the one named last changes fastest.
Arguments:
- fields: bfloat16 [4, 48, 768, 512], P(None, 'lat', 'lon'), may hold values from -6 to 6
- cotangent: bfloat16 [4, 48, 768, 512], P(None, 'lat', 'lon'), may hold values from -6 to 6
- layer_norm_gain: float32 [512], replicated, may hold values from 0.25 to 1.75
- qkv_weight: bfloat16 [512, 1536], replicated, as said below
- out_weight: bfloat16 [512, 512], replicated, may hold values from -0.25 to 0.25
Outputs:
- output: bfloat16 [4, 48, 768, 512], P(None, 'lat', 'lon')
- fields_gradient: bfloat16 [4, 48, 768, 512], P(None, 'lat', 'lon')
- grad_qkv: float32 [512, 1536], replicated
- grad_out: float32 [512, 512], replicated
- norm_gain_gradient: float32 [512], replicated
Inputs may be any that keep to these rules, and one draw needn't show every extreme that they name: `qkv_weight`: entries have mean zero and deviation about 512 ** -0.5 or larger.
All inputs are finite; a program needn't handle non-finite values.
Results may differ from a plain program's by a relative error of at most 0.014.
The roundings to bfloat16 on the way count: a program that leaves them out, or rounds other values in their place, can miss the bound.
Values may be sent and summed in bfloat16 or wider, within the bound.
No kernel may reach another device: no remote copies, remote signals or barrier semaphores. Data moves between devices by JAX's collectives and lax.ppermute only.
A program may use at most 128 MiB of HBM per device.

v0:
```python
import math

import jax
import jax.numpy as jnp
from jax import lax
from jax.sharding import PartitionSpec as P

HEADS = 8
WIN_LEV = 2
WIN_LAT = 6
WIN_LON = 12


def passed_along(block, axis, distance):
    devices = range(lax.axis_size(axis))
    route = [((i - distance) % len(devices), i) for i in devices]
    return lax.ppermute(block, axis, route)


def to_windows(field):
    levels, lat_rows, lon_cols, channels = field.shape
    blocked = field.reshape(
        levels // WIN_LEV,
        WIN_LEV,
        lat_rows // WIN_LAT,
        WIN_LAT,
        lon_cols // WIN_LON,
        WIN_LON,
        channels,
    )
    blocked = blocked.transpose(0, 2, 4, 1, 3, 5, 6)
    return blocked.reshape(-1, WIN_LEV * WIN_LAT * WIN_LON, channels)


def from_windows(blocks, levels, lat_rows, lon_cols):
    channels = blocks.shape[-1]
    blocked = blocks.reshape(
        levels // WIN_LEV,
        lat_rows // WIN_LAT,
        lon_cols // WIN_LON,
        WIN_LEV,
        WIN_LAT,
        WIN_LON,
        channels,
    )
    blocked = blocked.transpose(0, 3, 1, 4, 2, 5, 6)
    return blocked.reshape(levels, lat_rows, lon_cols, channels)


def roll_ahead(field):
    field = jnp.roll(field, -(WIN_LEV // 2), axis=0)
    lat_part = passed_along(field[:, : WIN_LAT // 2], "lat", -1)
    field = jnp.concatenate([field[:, WIN_LAT // 2 :], lat_part], axis=1)
    lon_part = passed_along(field[:, :, : WIN_LON // 2], "lon", -1)
    return jnp.concatenate([field[:, :, WIN_LON // 2 :], lon_part], axis=2)


def roll_back(field):
    field = jnp.roll(field, WIN_LEV // 2, axis=0)
    lat_part = passed_along(field[:, -(WIN_LAT // 2) :], "lat", 1)
    field = jnp.concatenate([lat_part, field[:, : -(WIN_LAT // 2)]], axis=1)
    lon_part = passed_along(field[:, :, -(WIN_LON // 2) :], "lon", 1)
    return jnp.concatenate([lon_part, field[:, :, : -(WIN_LON // 2)]], axis=2)


def head_split(block):
    count, span, channels = block.shape
    return block.reshape(count, span, HEADS, channels // HEADS)


def softmax_probs(q_heads, k_heads, region):
    factor = 1.0 / math.sqrt(q_heads.shape[-1])
    raw = (
        jnp.einsum("wqhd,wkhd->whqk", q_heads, k_heads, preferred_element_type=jnp.float32) * factor
    )
    same = region[:, :, None] == region[:, None, :]
    raw = jnp.where(same[:, None], raw, -1000000000.0)
    return jax.nn.softmax(raw, axis=-1)


def attend(queries, key_rows, val_rows, region):
    count, span, channels = queries.shape
    probs = softmax_probs(head_split(queries), head_split(key_rows), region)
    mixed = jnp.einsum(
        "whqk,wkhd->wqhd",
        probs.astype(jnp.bfloat16),
        head_split(val_rows),
        preferred_element_type=jnp.float32,
    )
    return mixed.astype(jnp.bfloat16).reshape(count, span, channels)


def attend_back(queries, key_rows, val_rows, region, grad_mixed):
    count, span, channels = queries.shape
    q_heads = head_split(queries)
    k_heads = head_split(key_rows)
    v_heads = head_split(val_rows)
    g_heads = head_split(grad_mixed)
    factor = 1.0 / math.sqrt(q_heads.shape[-1])
    probs = softmax_probs(q_heads, k_heads, region)
    rounded = probs.astype(jnp.bfloat16)
    grad_vals = jnp.einsum(
        "whqk,wqhd->wkhd", rounded, g_heads, preferred_element_type=jnp.float32
    ).astype(jnp.bfloat16)
    grad_probs = jnp.einsum("wqhd,wkhd->whqk", g_heads, v_heads, preferred_element_type=jnp.float32)
    inner = jnp.sum(grad_probs * probs, axis=-1, keepdims=True)
    grad_raw = (probs * (grad_probs - inner) * factor).astype(jnp.bfloat16)
    grad_query = jnp.einsum(
        "whqk,wkhd->wqhd", grad_raw, k_heads, preferred_element_type=jnp.float32
    ).astype(jnp.bfloat16)
    grad_key = jnp.einsum(
        "whqk,wqhd->wkhd", grad_raw, q_heads, preferred_element_type=jnp.float32
    ).astype(jnp.bfloat16)
    return jnp.concatenate(
        [
            grad_query.reshape(count, span, channels),
            grad_key.reshape(count, span, channels),
            grad_vals.reshape(count, span, channels),
        ],
        axis=-1,
    )


def on_device(fields, cotangent, layer_norm_gain, qkv_weight, out_weight):
    levels, lat_rows, lon_cols, channels = fields.shape
    fields_f = fields.astype(jnp.float32)
    centre = jnp.mean(fields_f, axis=-1, keepdims=True)
    mean_removed = fields_f - centre
    inverse_deviation = lax.rsqrt(
        jnp.mean(mean_removed * mean_removed, axis=-1, keepdims=True) + 1e-05
    )
    standardized_input = mean_removed * inverse_deviation
    normalized_fields = (standardized_input * layer_norm_gain).astype(jnp.bfloat16)
    rolled = roll_ahead(normalized_fields)
    total_rows = lat_rows * lax.axis_size("lat")
    global_rows = lax.axis_index("lat") * lat_rows + jnp.arange(lat_rows, dtype=jnp.int32)
    level_reg = (jnp.arange(levels) == levels - 1).astype(jnp.int32)
    lat_reg = (global_rows >= total_rows - WIN_LAT // 2).astype(jnp.int32)
    region_grid = (
        2 * level_reg[:, None, None]
        + lat_reg[None, :, None]
        + jnp.zeros((levels, lat_rows, lon_cols), jnp.int32)
    )
    region = to_windows(region_grid[..., None])[..., 0]
    windows = to_windows(rolled)
    count, span, _ = windows.shape
    flat = windows.reshape(-1, channels)
    qkv = jnp.dot(flat, qkv_weight, preferred_element_type=jnp.float32).astype(jnp.bfloat16)
    qkv = qkv.reshape(count, span, 3 * channels)
    queries = qkv[..., :channels]
    key_rows = qkv[..., channels : 2 * channels]
    val_rows = qkv[..., 2 * channels :]
    mixed = attend(queries, key_rows, val_rows, region)
    mixed_flat = mixed.reshape(-1, channels)
    proj = jnp.dot(mixed_flat, out_weight, preferred_element_type=jnp.float32).astype(jnp.bfloat16)
    proj_back = roll_back(
        from_windows(proj.reshape(count, span, channels), levels, lat_rows, lon_cols)
    )
    output = (fields_f + proj_back.astype(jnp.float32)).astype(jnp.bfloat16)
    rolled_grad = roll_ahead(cotangent)
    grad_flat = to_windows(rolled_grad).reshape(-1, channels)
    local_out = jnp.dot(mixed_flat.T, grad_flat, preferred_element_type=jnp.float32)
    grad_mixed = jnp.dot(grad_flat, out_weight.T, preferred_element_type=jnp.float32).astype(
        jnp.bfloat16
    )
    grad_act = attend_back(
        queries, key_rows, val_rows, region, grad_mixed.reshape(count, span, channels)
    )
    grad_act = grad_act.reshape(-1, 3 * channels)
    local_qkv = jnp.dot(flat.T, grad_act, preferred_element_type=jnp.float32)
    grad_norm = jnp.dot(grad_act, qkv_weight.T, preferred_element_type=jnp.float32).astype(
        jnp.bfloat16
    )
    normalized_gradient = roll_back(
        from_windows(grad_norm.reshape(count, span, channels), levels, lat_rows, lon_cols)
    ).astype(jnp.float32)
    shard_gain = jnp.sum(normalized_gradient * standardized_input, axis=(0, 1, 2))
    gain_scaled = normalized_gradient * layer_norm_gain
    first_term = jnp.mean(gain_scaled, axis=-1, keepdims=True)
    second_term = jnp.mean(gain_scaled * standardized_input, axis=-1, keepdims=True)
    fields_gradient = (
        cotangent.astype(jnp.float32)
        + inverse_deviation * (gain_scaled - first_term - standardized_input * second_term)
    ).astype(jnp.bfloat16)
    grad_qkv, grad_out, norm_gain_gradient = lax.psum(
        (local_qkv, local_out, shard_gain), ("lat", "lon")
    )
    return (output, fields_gradient, grad_qkv, grad_out, norm_gain_gradient)


def solution(mesh):
    return jax.shard_map(
        on_device,
        mesh=mesh,
        in_specs=(P(None, "lat", "lon", None), P(None, "lat", "lon", None), P(), P(), P()),
        out_specs=(P(None, "lat", "lon", None), P(None, "lat", "lon", None), P(), P(), P()),
        check_vma=False,
    )
```

profile of v0, /device:TPU:1, one launch (start us, length us, event | category | flops | bytes accessed | tf_op | source)
XLA Modules:
  0.0 395.6 jit_solution(17587790650059291101)
XLA Ops:
  7.2 1.7 convert_reduce_fusion
  9.0 1.8 fusion.43
  14.0 6.0 %collective-permute-start = (bf16[4,3,24,512]{3,0,2,1:T(4,128)(2,1)}, bf16[4,3,24,512]{3,0,2,1:T(4,128)(2,1)S(1)}, u32[]{:S(2)}, u32[]{:S(2)}) collective-permute-start(bf16[4,3,24,512]{3,0,2,1:T(4,128)(2,1)} %get-tuple-element.20), channel_id=1, source_target_pairs={{32,0},{64,32},{96,64},{128,96},{160,128},{192,160},{224,192},{0,2... | collective-permute-start | bytes 884744 | tf_op jit(solution)/shard_map/ppermute | solution.py:17
  22.1 3.9 collective-permute-done
  26.1 2.8 collective-permute-start.1
  28.9 3.4 collective-permute-done.4
  38.9 2.6 copy.24
  51.2 2.6 copy.33
  53.7 5.5 %fusion.66 = (f32[4,8,144]{2,1,0:T(8,128)S(1)}, f32[4,8,144,144]{2,3,1,0:T(8,128)}) fusion(pred[4,144,144]{1,2,0:T(8,128)(4,1)S(1)} %copy-done.20, bf16[4,144,8,64]{1,3,2,0:T(8,128)(2,1)} %bitcast.75, bf16[4,144,8,64]{1,3,2,0:T(8,128)(2,1)} %bitcast.77), kind=kOutput, calls=%fused_computation.100 | convolution fusion | flops 87589008 | bytes 3935232 | tf_op jit(solution)/shard_map/sub | solution.py:78
  59.3 4.3 %fusion.32 = bf16[4,144,8,64]{1,3,2,0:T(8,128)(2,1)} fusion(bf16[4,144,8,64]{1,3,2,0:T(8,128)(2,1)} %bitcast.68, f32[4,8,144,144]{2,3,1,0:T(8,128)} %get-tuple-element.26, f32[4,8,144]{2,1,0:T(8,128)S(1)} %get-tuple-element.25), kind=kOutput, calls=%fused_computation.31 | convolution fusion | flops 86556672 | bytes 3852288 | tf_op jit(solution)/shard_map/whqk,wkhd->wqhd/dot_general | solution.py:84
  63.8 1.9 fusion.33
  65.7 3.0 fusion.67
  68.8 9.5 %fusion.26 = bf16[4,144,8,64]{1,3,2,0:T(8,128)(2,1)} fusion(bf16[4,144,8,64]{1,3,2,0:T(8,128)(2,1)} %bitcast.76, f32[4,8,144,144]{2,3,1,0:T(8,128)} %fusion.67, f32[4,8,144,144]{2,3,1,0:T(8,128)} %get-tuple-element.26, f32[4,8,144]{2,1,0:T(8,128)S(1)} %get-tuple-element.25), kind=kOutput, calls=%fused_computation.29 | convolution fusion | flops 89879184 | bytes 6506496 | tf_op jit(solution)/shard_map/whqk,wqhd->wkhd/dot_general | solution.py:111
  78.3 9.4 %fusion.29 = bf16[4,144,8,64]{1,3,2,0:T(8,128)(2,1)} fusion(bf16[4,144,8,64]{1,3,2,0:T(8,128)(2,1)} %bitcast.78, f32[4,8,144,144]{2,3,1,0:T(8,128)} %fusion.67, f32[4,8,144,144]{2,3,1,0:T(8,128)} %get-tuple-element.26, f32[4,8,144]{2,1,0:T(8,128)S(1)} %get-tuple-element.25), kind=kOutput, calls=%fused_computation.30 | convolution fusion | flops 89879184 | bytes 6506496 | tf_op jit(solution)/shard_map/whqk,wkhd->wqhd/dot_general | solution.py:108
  87.7 3.0 copy.27
  90.7 2.5 reshape_reshape.19
  97.9 2.0 copy.37
  101.5 2.0 copy.35
  108.9 3.1 fusion.68
  112.1 2.9 convolution_convert_fusion.3
  116.6 2.2 reshape.131
  120.8 2.0 collective-permute-start.6
  122.9 2.4 convolution_convert_fusion.5
  128.2 2.1 reshape.129
  132.4 5.8 %collective-permute-start.7 = (bf16[4,6,6,512]{3,0,2,1:T(4,128)(2,1)S(1)}, bf16[4,6,6,512]{3,0,2,1:T(4,128)(2,1)S(1)}, u32[]{:S(2)}, u32[]{:S(2)}) collective-permute-start(bf16[4,6,6,512]{3,0,2,1:T(4,128)(2,1)S(1)} %pad_maximum_fusion.9), channel_id=1, source_target_pairs={{31,0},{0,1},{1,2},{2,3},{3,4},{4,5},{5,6},{6,7},{7,8},{8,9},{9,10... | collective-permute-start | bytes 442376 | tf_op jit(solution)/shard_map/ppermute | solution.py:17
  138.2 3.5 collective-permute-done.2
  141.9 4.7 %collective-permute-start.3 = (bf16[4,6,6,512]{3,0,2,1:T(4,128)(2,1)S(1)}, bf16[4,6,6,512]{3,0,2,1:T(4,128)(2,1)S(1)}, u32[]{:S(2)}, u32[]{:S(2)}) collective-permute-start(bf16[4,6,6,512]{3,0,2,1:T(4,128)(2,1)S(1)} %pad_maximum_fusion.10), channel_id=1, source_target_pairs={{31,0},{0,1},{1,2},{2,3},{3,4},{4,5},{5,6},{6,7},{7,8},{8,9},{9,10... | collective-permute-start | bytes 442376 | tf_op jit(solution)/shard_map/ppermute | solution.py:17
  146.6 3.5 fusion.45
  150.1 2.6 fusion.42
  154.5 80.2 %psum.23 = f32[512]{0:T(512)} all-reduce(f32[512]{0:T(512)S(1)} %get-tuple-element.10), channel_id=1, replica_groups=mesh['lat'=8,'lon'=32] {'lat','lon'}, use_global_device_ids=true, to_apply=%region_10.11 | all-reduce | flops 512 | bytes 4096 | tf_op jit(solution)/shard_map/psum | solution.py:185
  234.8 148.9 %all-reduce.3.cloned.1.call-done = (f32[512,1536]{1,0:T(8,128)}, f32[512,512]{1,0:T(8,128)}) async-done(((f32[512,1536]{1,0:T(8,128)}, f32[512,512]{1,0:T(8,128)}), (f32[512,1536]{1,0:T(8,128)}, f32[512,512]{1,0:T(8,128)})) %all-reduce.3.cloned.1.call-update) | async-done | bytes 4194320 | tf_op jit(solution)/shard_map/psum | solution.py:185
  383.7 3.8 copy.62
  (114 shorter events, 45.0 us)
Async XLA Ops:
  7.2 29.6 %copy-start = (bf16[512,1536]{1,0:T(8,128)(2,1)S(1)}, bf16[512,1536]{1,0:T(8,128)(2,1)}, u32[]{:S(2)}) copy-start(bf16[512,1536]{1,0:T(8,128)(2,1)} %param.8) | copy-start | bytes 4718596
  7.2 3.6 copy-start.1
  7.2 376.5 %all-reduce.3.cloned.1.call-start = ((), (), s32[]{:S(2)}) async-start(), calls=%async_computation | async-start | bytes 8388608 | tf_op jit(solution)/shard_map/psum | solution.py:185
  9.0 3.7 copy-start.11
  10.8 3.3 copy-start.13
  12.1 7.9 %slice-start = ((bf16[4,6,24,512]{3,2,1,0:T(8,128)(2,1)}), bf16[3,6,24,512]{3,2,1,0:T(8,128)(2,1)S(1)}, s32[]{:S(2)}) async-start(bf16[4,6,24,512]{3,2,1,0:T(8,128)(2,1)} %param.6), calls=%async_computation.1 | async-start | bytes 884736 | tf_op jit(solution)/shard_map/jit(_roll_static)/slice | solution.py:51
  12.1 7.9 %slice-start.1 = ((bf16[4,6,24,512]{3,2,1,0:T(8,128)(2,1)}), bf16[1,6,24,512]{3,2,1,0:T(8,128)(2,1)S(1)}, s32[]{:S(2)}) async-start(bf16[4,6,24,512]{3,2,1,0:T(8,128)(2,1)} %param.6), calls=%async_computation.2 | async-start | bytes 294912 | tf_op jit(solution)/shard_map/jit(_roll_static)/slice | solution.py:51
  14.0 12.0 %collective-permute-start = (bf16[4,3,24,512]{3,0,2,1:T(4,128)(2,1)}, bf16[4,3,24,512]{3,0,2,1:T(4,128)(2,1)S(1)}, u32[]{:S(2)}, u32[]{:S(2)}) collective-permute-start(bf16[4,3,24,512]{3,0,2,1:T(4,128)(2,1)} %get-tuple-element.20), channel_id=1, source_target_pairs={{32,0},{64,32},{96,64},{128,96},{160,128},{192,160},{224,192},{0,2... | collective-permute-start | bytes 884744 | tf_op jit(solution)/shard_map/ppermute | solution.py:17
  20.8 11.5 %collective-permute-start.4 = (bf16[4,3,24,512]{3,2,1,0:T(8,128)(2,1)}, bf16[4,3,24,512]{3,2,1,0:T(8,128)(2,1)S(1)}, u32[]{:S(2)}, u32[]{:S(2)}) collective-permute-start(bf16[4,3,24,512]{3,2,1,0:T(8,128)(2,1)} %get-tuple-element.24), channel_id=1, source_target_pairs={{32,0},{64,32},{96,64},{128,96},{160,128},{192,160},{224,192},{0,2... | collective-permute-start | bytes 884744 | tf_op jit(solution)/shard_map/ppermute | solution.py:17
  26.1 9.7 %collective-permute-start.1 = (bf16[4,6,6,512]{3,0,2,1:T(4,128)(2,1)S(1)}, bf16[4,6,6,512]{3,0,2,1:T(4,128)(2,1)S(1)}, u32[]{:S(2)}, u32[]{:S(2)}) collective-permute-start(bf16[4,6,6,512]{3,0,2,1:T(4,128)(2,1)S(1)} %pad_maximum_fusion.11), channel_id=1, source_target_pairs={{1,0},{2,1},{3,2},{4,3},{5,4},{6,5},{7,6},{8,7},{9,8},{10,9},{11,1... | collective-permute-start | bytes 442376 | tf_op jit(solution)/shard_map/ppermute | solution.py:17
  33.1 11.0 %collective-permute-start.5 = (bf16[4,6,6,512]{3,2,1,0:T(8,128)(2,1)}, bf16[4,6,6,512]{3,2,1,0:T(8,128)(2,1)}, u32[]{:S(2)}, u32[]{:S(2)}) collective-permute-start(bf16[4,6,6,512]{3,2,1,0:T(8,128)(2,1)} %pad_maximum_fusion.8), channel_id=1, source_target_pairs={{1,0},{2,1},{3,2},{4,3},{5,4},{6,5},{7,6},{8,7},{9,8},{10,9},{11,1... | collective-permute-start | bytes 442376 | tf_op jit(solution)/shard_map/ppermute | solution.py:17
  36.8 1.1 copy-start.17
  42.8 1.3 copy-start.10
  49.5 4.2 %copy-start.20 = (pred[4,144,144]{1,2,0:T(8,128)(4,1)S(1)}, pred[4,144,144]{1,2,0:T(8,128)(4,1)}, u32[]{:S(2)}) copy-start(pred[4,144,144]{1,2,0:T(8,128)(4,1)} %broadcast_compare_fusion) | copy-start | bytes 248836
  59.3 4.3 %copy-start.5 = (bf16[4,144,8,64]{1,3,2,0:T(8,128)(2,1)S(1)}, bf16[4,144,8,64]{1,3,2,0:T(8,128)(2,1)}, u32[]{:S(2)}) copy-start(bf16[4,144,8,64]{1,3,2,0:T(8,128)(2,1)} %copy.33) | copy-start | bytes 1769476
  59.3 4.5 %copy-start.22 = (f32[4,8,144,144]{2,3,1,0:T(8,128)S(1)}, f32[4,8,144,144]{2,3,1,0:T(8,128)}, u32[]{:S(2)}) copy-start(f32[4,8,144,144]{2,3,1,0:T(8,128)} %get-tuple-element.26) | copy-start | bytes 7962628
  63.8 1.9 copy-start.4
  94.0 1.5 copy-start.16
  105.1 2.4 copy-start.6
  105.1 3.9 copy-start.18
  107.6 1.3 copy-start.19
  116.6 6.3 %copy-start.8 = (bf16[576,512]{0,1:T(8,128)(2,1)S(1)}, bf16[576,512]{0,1:T(8,128)(2,1)}, u32[]{:S(2)}) copy-start(bf16[576,512]{0,1:T(8,128)(2,1)} %copy-done.7) | copy-start | bytes 1769476
  120.8 10.6 %collective-permute-start.6 = (bf16[4,3,24,512]{3,0,2,1:T(4,128)(2,1)}, bf16[4,3,24,512]{3,0,2,1:T(4,128)(2,1)}, u32[]{:S(2)}, u32[]{:S(2)}) collective-permute-start(bf16[4,3,24,512]{3,0,2,1:T(4,128)(2,1)} %fusion.52), channel_id=1, source_target_pairs={{224,0},{0,32},{32,64},{64,96},{96,128},{128,160},{160,192},{192,2... | collective-permute-start | bytes 884744 | tf_op jit(solution)/shard_map/ppermute | solution.py:17
  130.3 1.1 copy-start.3
  130.6 15.9 %copy-start.12 = (f32[4,6,24]{0,2,1:T(8,128)S(1)}, f32[4,6,24]{0,2,1:T(8,128)}, u32[]{:S(2)}) copy-start(f32[4,6,24]{0,2,1:T(8,128)} %copy-done.11) | copy-start | bytes 6916
  130.6 15.9 %copy-start.14 = (f32[4,6,24]{0,2,1:T(8,128)S(1)}, f32[4,6,24]{0,2,1:T(8,128)}, u32[]{:S(2)}) copy-start(f32[4,6,24]{0,2,1:T(8,128)} %copy-done.13) | copy-start | bytes 6916
  130.6 15.9 %copy-start.21 = (f32[512]{0:T(512)S(1)}, f32[512]{0:T(512)}, u32[]{:S(2)}) copy-start(f32[512]{0:T(512)} %param.7) | copy-start | bytes 6148
  131.0 10.8 %collective-permute-start.2 = (bf16[4,3,24,512]{3,0,2,1:T(4,128)(2,1)S(1)}, bf16[4,3,24,512]{3,0,2,1:T(4,128)(2,1)S(1)}, u32[]{:S(2)}, u32[]{:S(2)}) collective-permute-start(bf16[4,3,24,512]{3,0,2,1:T(4,128)(2,1)S(1)} %fusion.54), channel_id=1, source_target_pairs={{224,0},{0,32},{32,64},{64,96},{96,128},{128,160},{160,192},{192,2... | collective-permute-start | bytes 884744 | tf_op jit(solution)/shard_map/ppermute | solution.py:17
  132.4 17.7 %copy-start.9 = (bf16[4,6,24,512]{3,2,1,0:T(8,128)(2,1)S(1)}, bf16[4,6,24,512]{3,2,1,0:T(8,128)(2,1)}, u32[]{:S(2)}) copy-start(bf16[4,6,24,512]{3,2,1,0:T(8,128)(2,1)} %param.6) | copy-start | bytes 1769476
  132.4 14.1 %collective-permute-start.7 = (bf16[4,6,6,512]{3,0,2,1:T(4,128)(2,1)S(1)}, bf16[4,6,6,512]{3,0,2,1:T(4,128)(2,1)S(1)}, u32[]{:S(2)}, u32[]{:S(2)}) collective-permute-start(bf16[4,6,6,512]{3,0,2,1:T(4,128)(2,1)S(1)} %pad_maximum_fusion.9), channel_id=1, source_target_pairs={{31,0},{0,1},{1,2},{2,3},{3,4},{4,5},{5,6},{6,7},{7,8},{8,9},{9,10... | collective-permute-start | bytes 442376 | tf_op jit(solution)/shard_map/ppermute | solution.py:17
  141.9 8.2 %collective-permute-start.3 = (bf16[4,6,6,512]{3,0,2,1:T(4,128)(2,1)S(1)}, bf16[4,6,6,512]{3,0,2,1:T(4,128)(2,1)S(1)}, u32[]{:S(2)}, u32[]{:S(2)}) collective-permute-start(bf16[4,6,6,512]{3,0,2,1:T(4,128)(2,1)S(1)} %pad_maximum_fusion.10), channel_id=1, source_target_pairs={{31,0},{0,1},{1,2},{2,3},{3,4},{4,5},{5,6},{6,7},{7,8},{8,9},{9,10... | collective-permute-start | bytes 442376 | tf_op jit(solution)/shard_map/ppermute | solution.py:17
  383.7 3.8 copy-start.15
  (2 other events, 1.6 us)
Sparse Core Ops, SparseCore 0:
  112.2 271.4 all-reduce.2
where the time goes:
time: 404 us; the launch traced here: 396 us
  waiting for transfers between devices  160 us (40%)
  blocking collectives  80.2 us (20%)
  local copies, waits for them, and re-layouts  51.1 us (13%)
  matrix products  46.3 us (11%)
  starting transfers between devices  23.5 us (6%)
  other arithmetic  19.8 us (5%)
  between operations  14.7 us (4%)
    psum x1, waiting for transfers between devices, on_device(): lax.psum((local_qkv, local_out, shard_gain), ('lat', 'lon'))  149 us
    psum x1, blocking collectives, on_device(): lax.psum((local_qkv, local_out, shard_gain), ('lat', 'lon'))  80.2 us
    ppermute x8, starting transfers between devices, passed_along(): return lax.ppermute(block, axis, route)  23.5 us
    unnamed x52, local copies, waits for them, and re-layouts  12.2 us
    ppermute x8, waiting for transfers between devices, passed_along(): return lax.ppermute(block, axis, route)  10.9 us
    dot_general x1, matrix products, attend_back(): jnp.einsum('whqk,wqhd->wkhd', grad_raw, q_heads, preferred_element_type=j...  9.51 us
    dot_general x1, matrix products, attend_back(): jnp.einsum('whqk,wkhd->wqhd', grad_raw, k_heads, preferred_element_type=j...  9.42 us
  transfers between devices with their start and end apart: 9, of which 4 were waited for; matrix products, arithmetic and copies ran while one was open for 9% of the time, Pallas kernels for 0%

commit v1 on v0

v1 whole, which is shorter than its diff:
```python
import functools
import math

import jax
import jax.numpy as jnp
import numpy as np
from jax import lax
from jax.experimental import pallas as pl
from jax.experimental.pallas import tpu as pltpu
from jax.sharding import PartitionSpec as P

HEADS = 8
LEV, ROWS, COLS = 4, 6, 24
WL, WR, WC = 2, 6, 12
D = 512
SPAN = WL * WR * WC
TOK = LEV * ROWS * COLS
BOTH = ("lat", "lon")
f32 = jnp.float32
bf16 = jnp.bfloat16
VMEM = 56 * 1024 * 1024


def index_of(y, x, z, c):
    return (y * 2 + x // 2) * 32 + (x % 2) * 16 + z * 2 + c


def place_of(i):
    return i // 64, ((i // 32) % 2) * 2 + (i // 16) % 2, (i // 2) % 8, i % 2


def route(step):
    return [(i, index_of(*step(*place_of(i)))) for i in range(256)]


def to_sibling(y, x, z, c):
    return y, x, z, 1 - c


def first_axis(k):
    return lambda y, x, z, c: ((y + k) % 4, x, z, c) if c == 0 else (y, (x + k) % 4, z, c)


def second_axis(k):
    return lambda y, x, z, c: (y, (x + k) % 4, z, c) if c == 0 else ((y + k) % 4, x, z, c)


def flip_z(k):
    return lambda y, x, z, c: (y, x, z ^ k, c)


def send(x, step):
    return lax.ppermute(x, BOTH, route(step))


def shifted(dlat, dlon):
    def pairs():
        out = []
        for i in range(256):
            a, b = i // 32, i % 32
            out.append((i, ((a + dlat) % 8) * 32 + (b + dlon) % 32))
        return out

    return pairs()


def gather_tables():
    local = np.zeros((TOK, TOK), np.float32)
    lat = np.zeros((TOK, LEV * 3 * 18), np.float32)
    lon = np.zeros((TOK, LEV * 3 * 6), np.float32)
    diag = np.zeros((TOK, LEV * 3 * 6), np.float32)
    for lr in range(LEV):
        for rr in range(ROWS):
            for cr in range(COLS):
                w = (lr // WL) * (COLS // WC) + cr // WC
                t = w * SPAN + (lr % WL) * WR * WC + rr * WC + cr % WC
                lo, r, c = (lr + 1) % LEV, rr + 3, cr + 6
                if r < ROWS and c < COLS:
                    local[t, lo * ROWS * COLS + r * COLS + c] = 1
                elif c < COLS:
                    lat[t, lo * 54 + (r - ROWS) * 18 + c - 6] = 1
                elif r < ROWS:
                    lon[t, lo * 18 + (r - 3) * 6 + c - COLS] = 1
                else:
                    diag[t, lo * 18 + (r - ROWS) * 6 + c - COLS] = 1
    return local, lat, lon, diag


def scatter_tables():
    lat = np.zeros((TOK, LEV * 3 * 18), np.float32)
    lon = np.zeros((TOK, LEV * 3 * 6), np.float32)
    diag = np.zeros((TOK, LEV * 3 * 6), np.float32)
    for lv in range(LEV):
        for r in range(ROWS):
            for c in range(COLS):
                t = lv * ROWS * COLS + r * COLS + c
                if r < 3 and c >= 6:
                    lat[t, lv * 54 + r * 18 + c - 6] = 1
                elif r >= 3 and c < 6:
                    lon[t, lv * 18 + (r - 3) * 6 + c] = 1
                elif r < 3:
                    diag[t, lv * 18 + r * 6 + c] = 1
    return lat, lon, diag


def dot(a, b, dims=((1,), (0,))):
    return lax.dot_general(a, b, (dims, ((), ())), preferred_element_type=f32)


NT = ((1,), (1,))
TN = ((0,), (0,))


def normalise(x):
    centred = x - jnp.mean(x, axis=-1, keepdims=True)
    rstd = lax.rsqrt(jnp.mean(centred * centred, axis=-1, keepdims=True) + 1e-5)
    return centred * rstd, rstd


def main_kernel(
    place,
    f_loc, f_lat, f_lon, f_diag,
    c_loc, c_lat, c_lon, c_diag,
    p_loc, p_lat, p_lon, p_diag,
    gain, w_ref, o_ref,
    mixed, gact, own, other,
    normed, qkv, ctw, gm, acc,
):
    def windows(a, b, c, d):
        return (
            dot(p_loc[...], a[...])
            + dot(p_lat[...], b[...])
            + dot(p_lon[...], c[...])
            + dot(p_diag[...], d[...])
        )

    xhat, _ = normalise(windows(f_loc, f_lat, f_lon, f_diag))
    normed[...] = (xhat * gain[...]).astype(bf16)
    qkv[...] = dot(normed[...], w_ref[...]).astype(bf16)
    ctw[...] = windows(c_loc, c_lat, c_lon, c_diag).astype(bf16)
    gm[...] = dot(ctw[...], o_ref[...], NT).astype(bf16)

    last_lat = place[0]
    two = 2 * SPAN
    row2 = lax.broadcasted_iota(jnp.int32, (two, 128), 0)
    lane2 = lax.broadcasted_iota(jnp.int32, (two, 128), 1)
    pick = ((row2 < SPAN) == (lane2 < 64)).astype(f32).astype(bf16)
    low = lax.broadcasted_iota(jnp.int32, (SPAN, 128), 1) < 64

    def lev_of(t):
        return (t >= SPAN // 2).astype(jnp.int32)

    def half_of(t):
        u = t - SPAN // 2 * lev_of(t)
        return (u >= SPAN // 4).astype(jnp.int32)

    tq = lax.broadcasted_iota(jnp.int32, (two, SPAN), 0)
    tq = tq - SPAN * (tq >= SPAN).astype(jnp.int32)
    tk = lax.broadcasted_iota(jnp.int32, (two, SPAN), 1)
    lev_diff = jnp.abs(lev_of(tq) - lev_of(tk))
    half_diff = jnp.abs(half_of(tq) - half_of(tk)) * last_lat
    factor = 1.0 / math.sqrt(D // HEADS)

    def join(r):
        return jnp.where(low, r[:SPAN], r[SPAN:]).astype(bf16)

    def window(w, carry):
        at = pl.ds(pl.multiple_of(w * SPAN, SPAN), SPAN)
        top = (w >= 2).astype(jnp.int32)
        same = (lev_diff * top + half_diff) == 0
        for p in range(HEADS // 2):
            cols = pl.ds(128 * p, 128)
            q = qkv[at, pl.ds(128 * p, 128)]
            k = qkv[at, pl.ds(D + 128 * p, 128)]
            v = qkv[at, pl.ds(2 * D + 128 * p, 128)]
            g = gm[at, cols]
            q2 = jnp.concatenate([q, q], axis=0) * pick
            g2 = jnp.concatenate([g, g], axis=0) * pick
            s = jnp.where(same, dot(q2, k, NT) * factor, -1000000000.0)
            e = jnp.exp(s - jnp.max(s, axis=-1, keepdims=True))
            probs = e * (1.0 / jnp.sum(e, axis=-1, keepdims=True))
            rounded = probs.astype(bf16)
            mixed[at, cols] = join(dot(rounded, v))
            gact[at, pl.ds(2 * D + 128 * p, 128)] = dot(rounded, g2, TN).astype(bf16)
            dp = dot(g2, v, NT)
            inner = jnp.sum(dp * probs, axis=-1, keepdims=True)
            ds = (probs * (dp - inner) * factor).astype(bf16)
            gact[at, cols] = join(dot(ds, k))
            gact[at, pl.ds(D + 128 * p, 128)] = dot(ds, q2, TN).astype(bf16)
        return carry

    lax.fori_loop(0, 4, window, 0)

    acc[:, : 3 * D] = dot(normed[...], gact[...], TN)
    acc[:, 3 * D :] = dot(mixed[...], ctw[...], TN)

    y, x, c = place[1], place[2], place[3]

    def fill(out, core):
        d1 = jnp.where(core == 0, y, x)
        d2 = jnp.where(core == 0, x, y)
        for s1 in range(4):
            for s2 in range(4):
                r = core * 256 + lax.rem(d1 + s1, 4) * 64 + lax.rem(d2 + s2, 4) * 16
                rows = acc[pl.ds(pl.multiple_of(r, 16), 16), :]
                out[pl.ds((s1 * 4 + s2) * 16, 16), :] = rows.astype(bf16)

    fill(own, c)
    fill(other, 1 - c)


def back_kernel(mixed, gact, w_ref, o_ref, p_lat, p_lon, p_diag, both, to_lat, to_lon, to_diag):
    both[:, :D] = dot(mixed[...], o_ref[...]).astype(bf16)
    both[:, D:] = dot(gact[...], w_ref[...], NT).astype(bf16)
    to_lat[...] = dot(p_lat[...], both[...], TN).astype(bf16)
    to_lon[...] = dot(p_lon[...], both[...], TN).astype(bf16)
    to_diag[...] = dot(p_diag[...], both[...], TN).astype(bf16)


def finish_kernel(
    f_loc, c_loc, both, r_lat, r_lon, r_diag, p_loc, s_lat, s_lon, s_diag, gain, out, grad
):
    grid = (
        dot(p_loc[...], both[...], TN)
        + dot(s_lat[...], r_lat[...])
        + dot(s_lon[...], r_lon[...])
        + dot(s_diag[...], r_diag[...])
    )
    x = f_loc[...].astype(f32)
    out[...] = (x + grid[:, :D]).astype(bf16)
    xhat, rstd = normalise(x)
    g = grid[:, D:] * gain[...]
    first = jnp.mean(g, axis=-1, keepdims=True)
    second = jnp.mean(g * xhat, axis=-1, keepdims=True)
    grad[...] = (c_loc[...].astype(f32) + rstd * (g - first - xhat * second)).astype(bf16)


def weights_kernel(place, *refs):
    pieces, (w_ref, gain, g_qkv, g_out, g_gain) = refs[:8], refs[8:]
    y, x, c = place[1], place[2], place[3]
    for side in range(2):
        core = c if side == 0 else 1 - c
        d1 = jnp.where(core == 0, y, x)
        d2 = jnp.where(core == 0, x, y)
        for s1 in range(4):
            for s2 in range(4):
                r = core * 256 + lax.rem(d1 + s1, 4) * 64 + lax.rem(d2 + s2, 4) * 16
                at = pl.ds(pl.multiple_of(r, 16), 16)
                block = pieces[side * 4 + s1][pl.ds(s2 * 16, 16), :].astype(f32)
                g_qkv[at, :] = block[:, : 3 * D]
                g_out[at, :] = block[:, 3 * D :]
    total = jnp.sum(g_qkv[...] * w_ref[...].astype(f32), axis=1, keepdims=True)
    g_gain[...] = total / gain[...]


def params():
    return pltpu.CompilerParams(vmem_limit_bytes=VMEM)


def spec(count, scalar=False):
    whole = [pl.BlockSpec(memory_space=pltpu.VMEM)] * count
    return ([pl.BlockSpec(memory_space=pltpu.SMEM)] if scalar else []) + whole


def shape(*dims, dtype=bf16):
    return jax.ShapeDtypeStruct(dims, dtype)


def cost(flops, moved):
    return pl.CostEstimate(flops=flops, bytes_accessed=moved, transcendentals=0)


def add(*xs):
    total = xs[0].astype(f32)
    for x in xs[1:]:
        total = total + x.astype(f32)
    return total.astype(bf16)


def halo(field):
    lat = field[:, :3, 6:].reshape(-1, D)
    lon = field[:, 3:, :6].reshape(-1, D)
    diag = field[:, :3, :6].reshape(-1, D)
    return (
        lax.ppermute(lat, BOTH, shifted(-1, 0)),
        lax.ppermute(lon, BOTH, shifted(0, -1)),
        lax.ppermute(diag, BOTH, shifted(-1, -1)),
    )


def on_device(fields, cotangent, layer_norm_gain, qkv_weight, out_weight):
    a, b = lax.axis_index("lat"), lax.axis_index("lon")
    place = jnp.stack(
        [
            (a == 7).astype(jnp.int32),
            (a // 2).astype(jnp.int32),
            ((a % 2) * 2 + b // 16).astype(jnp.int32),
            (b % 2).astype(jnp.int32),
        ]
    )
    gain_row = layer_norm_gain.reshape(1, D)
    p_loc, p_lat, p_lon, p_diag = [jnp.asarray(t, bf16) for t in gather_tables()]
    s_lat, s_lon, s_diag = [jnp.asarray(t, bf16) for t in scatter_tables()]
    f_loc, c_loc = fields.reshape(TOK, D), cotangent.reshape(TOK, D)
    f_halo = halo(fields)
    c_halo = halo(cotangent)

    mixed, gact, own, other = pl.pallas_call(
        main_kernel,
        out_shape=[shape(TOK, D), shape(TOK, 3 * D), shape(256, 4 * D), shape(256, 4 * D)],
        in_specs=spec(15, True),
        out_specs=spec(4),
        scratch_shapes=[
            pltpu.VMEM((TOK, D), bf16),
            pltpu.VMEM((TOK, 3 * D), bf16),
            pltpu.VMEM((TOK, D), bf16),
            pltpu.VMEM((TOK, D), bf16),
            pltpu.VMEM((D, 4 * D), f32),
        ],
        compiler_params=params(),
        cost_estimate=cost(8 * 10**9, 10**7),
        name="main",
    )(
        place, f_loc, *f_halo, c_loc, *c_halo, p_loc, p_lat, p_lon, p_diag,
        gain_row, qkv_weight, out_weight,
    )

    there = send(other, to_sibling)
    part = [add(own[64 * k : 64 * k + 64], there[64 * k : 64 * k + 64]) for k in range(4)]
    part = add(part[0], *[send(part[k], first_axis(k)) for k in (1, 2, 3)])
    part = add(part[:16], *[send(part[16 * k : 16 * k + 16], second_axis(k)) for k in (1, 2, 3)])
    for k in (1, 2, 4):
        part = add(part, send(part, flip_z(k)))

    both, to_lat, to_lon, to_diag = pl.pallas_call(
        back_kernel,
        out_shape=[shape(TOK, 2 * D), shape(216, 2 * D), shape(72, 2 * D), shape(72, 2 * D)],
        in_specs=spec(7),
        out_specs=spec(4),
        compiler_params=params(),
        cost_estimate=cost(2 * 10**9, 5 * 10**6),
        name="back",
    )(mixed, gact, qkv_weight, out_weight, p_lat, p_lon, p_diag)
    r_lat = lax.ppermute(to_lat, BOTH, shifted(1, 0))
    r_lon = lax.ppermute(to_lon, BOTH, shifted(0, 1))
    r_diag = lax.ppermute(to_diag, BOTH, shifted(1, 1))
    out, grad = pl.pallas_call(
        finish_kernel,
        out_shape=[shape(TOK, D), shape(TOK, D)],
        in_specs=spec(11),
        out_specs=spec(2),
        compiler_params=params(),
        cost_estimate=cost(2 * 10**9, 8 * 10**6),
        name="finish",
    )(f_loc, c_loc, both, r_lat, r_lon, r_diag, p_loc, s_lat, s_lon, s_diag, gain_row)

    block = jnp.concatenate([part] + [send(part, second_axis(4 - s)) for s in (1, 2, 3)], axis=0)
    mine = [block] + [send(block, first_axis(4 - s)) for s in (1, 2, 3)]
    sibling = [send(m, to_sibling) for m in mine]
    g_qkv, g_out, g_gain = pl.pallas_call(
        weights_kernel,
        out_shape=[shape(D, 3 * D, dtype=f32), shape(D, D, dtype=f32), shape(D, 1, dtype=f32)],
        in_specs=spec(10, True),
        out_specs=spec(3),
        compiler_params=params(),
        cost_estimate=cost(10**7, 8 * 10**6),
        name="weights",
    )(place, *mine, *sibling, qkv_weight, layer_norm_gain.reshape(D, 1))

    grid = (LEV, ROWS, COLS, D)
    return out.reshape(grid), grad.reshape(grid), g_qkv, g_out, g_gain.reshape(D)


def solution(mesh):
    return jax.shard_map(
        on_device,
        mesh=mesh,
        in_specs=(P(None, "lat", "lon", None), P(None, "lat", "lon", None), P(), P(), P()),
        out_specs=(P(None, "lat", "lon", None), P(None, "lat", "lon", None), P(), P(), P()),
        check_vma=False,
    )
```

time: 404 us -> 149 us (0.37); the launches traced: 396 us -> 149 us
  waiting for transfers between devices: 160 us -> 50.3 us
  blocking collectives: 80.2 us -> 0 us
  matrix products: 46.3 us -> 0 us
  local copies, waits for them, and re-layouts: 51.1 us -> 6.32 us
  Pallas kernels: 0 us -> 38.4 us
  starting transfers between devices: 23.5 us -> 48.4 us
  other arithmetic: 19.8 us -> 4.85 us
  between operations: 14.7 us -> 0.97 us
    psum x1 -> x0, waiting for transfers between devices: 149 us -> none  [on_device(): lax.psum((local_qkv, local_out, shard_gain), ('lat', 'lon'))]
    psum x1 -> x0, blocking collectives: 80.2 us -> none  [on_device(): lax.psum((local_qkv, local_out, shard_gain), ('lat', 'lon'))]
    dot_general x11 -> x0, matrix products: 40.7 us -> none  [the longest x1 9.51 us: attend_back(): jnp.einsum('whqk,wqhd->wkhd', grad_raw, q_heads, preferred_element_type=j...]
    ppermute x8 -> x29, waiting for transfers between devices: 10.9 us -> 50.3 us  [the longest x20 29.3 us: send(): return lax.ppermute(x, BOTH, route(step))]
    pallas_call x0 -> x4, Pallas kernels: none -> 38.4 us  [the longest x1 23.3 us: on_device(): pl.pallas_call(main_kernel, out_shape=[shape(TOK, D), shape(TOK, 3 * D),...]
    ppermute x8 -> x29, starting transfers between devices: 23.5 us -> 48.4 us  [the longest x20 17.5 us: send(): return lax.ppermute(x, BOTH, route(step))]
    unnamed x52 -> x38, local copies, waits for them, and re-layouts: 12.2 us -> 3.03 us
    another operation x7 -> x0, local copies, waits for them, and re-layouts: 8.55 us -> none  [the longest x2 4.19 us: head_split(): return block.reshape(count, span, HEADS, channels // HEADS)]
  transfers between devices with their start and end apart: 9 -> 29, of which waited for: 4 -> 15; matrix products, arithmetic and copies ran while one was open for 9% -> 2% of each run, Pallas kernels for 0% -> 7%
where the time goes in v1:
time: 149 us
  waiting for transfers between devices  50.3 us (34%)
  starting transfers between devices  48.4 us (32%)
  Pallas kernels  38.4 us (26%)
  local copies, waits for them, and re-layouts  6.32 us (4%)
  other arithmetic  4.85 us (3%)
    ppermute x20, waiting for transfers between devices, send(): return lax.ppermute(x, BOTH, route(step))  29.3 us
    pallas_call x1, Pallas kernels, on_device(): pl.pallas_call(main_kernel, out_shape=[shape(TOK, D), shape(TOK, 3 * D),...  23.3 us
    ppermute x20, starting transfers between devices, send(): return lax.ppermute(x, BOTH, route(step))  17.5 us
    ppermute x1, waiting for transfers between devices, on_device(): r_diag = lax.ppermute(to_diag, BOTH, shifted(1, 1))  12.9 us
    ppermute x2, starting transfers between devices, halo(): lax.ppermute(diag, BOTH, shifted(-1, -1))  11.4 us
    ppermute x1, starting transfers between devices, on_device(): r_lon = lax.ppermute(to_lon, BOTH, shifted(0, 1))  6.68 us
    pallas_call x1, Pallas kernels, on_device(): pl.pallas_call(finish_kernel, out_shape=[shape(TOK, D), shape(TOK, D)], i...  5.37 us
    pallas_call x1, Pallas kernels, on_device(): pl.pallas_call(back_kernel, out_shape=[shape(TOK, 2 * D), shape(216, 2 *...  5.32 us
  transfers between devices with their start and end apart: 29, of which 15 were waited for; matrix products, arithmetic and copies ran while one was open for 2% of the time, Pallas kernels for 7%

profile of v1, /device:TPU:1, one launch (start us, length us, event | category | flops | bytes accessed | tf_op | source)
XLA Modules:
  0.0 149.2 jit_solution(16417515412677948356)
XLA Ops:
  1.7 3.3 %collective-permute-start.1 = (bf16[72,512]{1,0:T(8,128)(2,1)S(1)}, bf16[72,512]{1,0:T(8,128)(2,1)S(1)}, u32[]{:S(2)}, u32[]{:S(2)}) collective-permute-start(bf16[72,512]{1,0:T(8,128)(2,1)S(1)} %reshape.52), channel_id=1, source_target_pairs={{0,31},{1,0},{2,1},{3,2},{4,3},{5,4},{6,5},{7,6},{8,7},{9,8},{10,9... | collective-permute-start | bytes 221192 | tf_op jit(solution)/shard_map/ppermute | solution.py:286
  5.1 9.3 %collective-permute-start.2 = (bf16[72,512]{1,0:T(8,128)(2,1)S(1)}, bf16[72,512]{1,0:T(8,128)(2,1)S(1)}, u32[]{:S(2)}, u32[]{:S(2)}) collective-permute-start(bf16[72,512]{1,0:T(8,128)(2,1)S(1)} %reshape.53), channel_id=1, source_target_pairs={{0,255},{1,224},{2,225},{3,226},{4,227},{5,228},{6,229},{7,230},{8... | collective-permute-start | bytes 221192 | tf_op jit(solution)/shard_map/ppermute | solution.py:287
  16.3 2.7 %collective-permute-start.3 = (bf16[216,512]{1,0:T(8,128)(2,1)S(1)}, bf16[216,512]{1,0:T(8,128)(2,1)S(1)}, u32[]{:S(2)}, u32[]{:S(2)}) collective-permute-start(bf16[216,512]{1,0:T(8,128)(2,1)S(1)} %reshape.54), channel_id=1, source_target_pairs={{0,224},{1,225},{2,226},{3,227},{4,228},{5,229},{6,230},{7,231},{8... | collective-permute-start | bytes 663560 | tf_op jit(solution)/shard_map/ppermute | solution.py:285
  19.4 2.0 %collective-permute-start.5 = (bf16[72,512]{1,0:T(8,128)(2,1)S(1)}, bf16[72,512]{1,0:T(8,128)(2,1)S(1)}, u32[]{:S(2)}, u32[]{:S(2)}) collective-permute-start(bf16[72,512]{1,0:T(8,128)(2,1)S(1)} %reshape.56), channel_id=1, source_target_pairs={{0,255},{1,224},{2,225},{3,226},{4,227},{5,228},{6,229},{7,230},{8... | collective-permute-start | bytes 221192 | tf_op jit(solution)/shard_map/ppermute | solution.py:287
  22.0 1.2 collective-permute-done.4.c_lon
  23.2 4.5 %collective-permute-done.5.c_diag = bf16[72,512]{1,0:T(8,128)(2,1)S(1)} collective-permute-done((bf16[72,512]{1,0:T(8,128)(2,1)S(1)}, bf16[72,512]{1,0:T(8,128)(2,1)S(1)}, u32[]{:S(2)}, u32[]{:S(2)}) %collective-permute-start.5) | collective-permute-done | bytes 73760 | tf_op jit(solution)/shard_map/ppermute | solution.py:287
  27.7 2.3 %collective-permute-done.3.c_lat = bf16[216,512]{1,0:T(8,128)(2,1)S(1)} collective-permute-done((bf16[216,512]{1,0:T(8,128)(2,1)S(1)}, bf16[216,512]{1,0:T(8,128)(2,1)S(1)}, u32[]{:S(2)}, u32[]{:S(2)}) %collective-permute-start.3) | collective-permute-done | bytes 221216 | tf_op jit(solution)/shard_map/ppermute | solution.py:285
  30.7 23.3 %main.1 = (bf16[576,512]{1,0:T(8,128)(2,1)}, bf16[576,1536]{1,0:T(8,128)(2,1)}, bf16[256,2048]{1,0:T(8,128)(2,1)}, bf16[256,2048]{1,0:T(8,128)(2,1)}) custom-call(s32[4]{0:T(128)} %pad_add_fusion.place, bf16[576,512]{1,0:T(8,128)(2,1)} %bitcast.10, bf16[216,512]{1,0:T(8,128)(2,1)} %copy-done.11, bf16[72,512]{1,0:T(8,128)(2,1)} %copy-done.15, ...), custom_call_target="tpu_custom_call" | custom-call | flops 8000000000 | bytes 10000000 | tf_op jit(solution)/shard_map/main/pallas_call | solution.py:308
  54.0 1.3 collective-permute-start.9
  55.4 2.5 %collective-permute-done.9 = bf16[256,2048]{1,0:T(8,128)(2,1)S(1)} collective-permute-done((bf16[256,2048]{1,0:T(8,128)(2,1)}, bf16[256,2048]{1,0:T(8,128)(2,1)S(1)}, u32[]{:S(2)}, u32[]{:S(2)}) %collective-permute-start.9) | collective-permute-done | bytes 1048608 | tf_op jit(solution)/shard_map/ppermute | solution.py:53
  57.9 1.4 add_convert_fusion.3
  59.5 2.7 %collective-permute-start.12 = (bf16[64,2048]{1,0:T(8,128)(2,1)S(1)}, bf16[64,2048]{1,0:T(8,128)(2,1)S(1)}, u32[]{:S(2)}, u32[]{:S(2)}) collective-permute-start(bf16[64,2048]{1,0:T(8,128)(2,1)S(1)} %get-tuple-element.32), channel_id=1, source_target_pairs={{0,192},{1,49},{2,194},{3,51},{4,196},{5,53},{6,198},{7,55},{8,200... | collective-permute-start | bytes 786440 | tf_op jit(solution)/shard_map/ppermute | solution.py:53
  62.2 4.0 %collective-permute-done.10 = bf16[64,2048]{1,0:T(8,128)(2,1)S(1)} collective-permute-done((bf16[64,2048]{1,0:T(8,128)(2,1)S(1)}, bf16[64,2048]{1,0:T(8,128)(2,1)S(1)}, u32[]{:S(2)}, u32[]{:S(2)}) %collective-permute-start.10) | collective-permute-done | bytes 262176 | tf_op jit(solution)/shard_map/ppermute | solution.py:53
  66.2 2.1 %collective-permute-done.12 = bf16[64,2048]{1,0:T(8,128)(2,1)S(1)} collective-permute-done((bf16[64,2048]{1,0:T(8,128)(2,1)S(1)}, bf16[64,2048]{1,0:T(8,128)(2,1)S(1)}, u32[]{:S(2)}, u32[]{:S(2)}) %collective-permute-start.12) | collective-permute-done | bytes 262176 | tf_op jit(solution)/shard_map/ppermute | solution.py:53
  70.4 2.7 %collective-permute-start.15 = (bf16[16,2048]{1,0:T(8,128)(2,1)S(1)}, bf16[16,2048]{1,0:T(8,128)(2,1)S(1)}, u32[]{:S(2)}, u32[]{:S(2)}) collective-permute-start(bf16[16,2048]{1,0:T(8,128)(2,1)S(1)} %get-tuple-element.39), channel_id=1, source_target_pairs={{0,48},{1,193},{2,50},{3,195},{4,52},{5,197},{6,54},{7,199},{8,56}... | collective-permute-start | bytes 196616 | tf_op jit(solution)/shard_map/ppermute | solution.py:53
  73.1 1.6 %collective-permute-done.13 = bf16[16,2048]{1,0:T(8,128)(2,1)S(1)} collective-permute-done((bf16[16,2048]{1,0:T(8,128)(2,1)S(1)}, bf16[16,2048]{1,0:T(8,128)(2,1)S(1)}, u32[]{:S(2)}, u32[]{:S(2)}) %collective-permute-start.13) | collective-permute-done | bytes 65568 | tf_op jit(solution)/shard_map/ppermute | solution.py:53
  75.0 2.7 %collective-permute-done.14 = bf16[16,2048]{1,0:T(8,128)(2,1)S(1)} collective-permute-done((bf16[16,2048]{1,0:T(8,128)(2,1)S(1)}, bf16[16,2048]{1,0:T(8,128)(2,1)S(1)}, u32[]{:S(2)}, u32[]{:S(2)}) %collective-permute-start.14) | collective-permute-done | bytes 65568 | tf_op jit(solution)/shard_map/ppermute | solution.py:53
  77.8 3.1 %collective-permute-done.16 = bf16[16,2048]{1,0:T(8,128)(2,1)S(1)} collective-permute-done((bf16[16,2048]{1,0:T(8,128)(2,1)S(1)}, bf16[16,2048]{1,0:T(8,128)(2,1)S(1)}, u32[]{:S(2)}, u32[]{:S(2)}) %collective-permute-start.16) | collective-permute-done | bytes 65568 | tf_op jit(solution)/shard_map/ppermute | solution.py:53
  81.1 4.5 %collective-permute-done.17 = bf16[16,2048]{1,0:T(8,128)(2,1)S(1)} collective-permute-done((bf16[16,2048]{1,0:T(8,128)(2,1)S(1)}, bf16[16,2048]{1,0:T(8,128)(2,1)S(1)}, u32[]{:S(2)}, u32[]{:S(2)}) %collective-permute-start.17) | collective-permute-done | bytes 65568 | tf_op jit(solution)/shard_map/ppermute | solution.py:53
  86.3 6.8 %collective-permute-done.18 = bf16[16,2048]{1,0:T(8,128)(2,1)S(1)} collective-permute-done((bf16[16,2048]{1,0:T(8,128)(2,1)S(1)}, bf16[16,2048]{1,0:T(8,128)(2,1)S(1)}, u32[]{:S(2)}, u32[]{:S(2)}) %collective-permute-start.18) | collective-permute-done | bytes 65568 | tf_op jit(solution)/shard_map/ppermute | solution.py:53
  93.2 1.5 %collective-permute-start.20 = (bf16[16,2048]{1,0:T(8,128)(2,1)S(1)}, bf16[16,2048]{1,0:T(8,128)(2,1)S(1)}, u32[]{:S(2)}, u32[]{:S(2)}) collective-permute-start(bf16[16,2048]{1,0:T(8,128)(2,1)S(1)} %add_convert_fusion.5), channel_id=1, source_target_pairs={{0,32},{1,129},{2,34},{3,131},{4,36},{5,133},{6,38},{7,135},{8,40}... | collective-permute-start | bytes 196616 | tf_op jit(solution)/shard_map/ppermute | solution.py:53
  95.8 5.3 %back.1 = (bf16[576,1024]{1,0:T(8,128)(2,1)}, bf16[216,1024]{1,0:T(8,128)(2,1)}, bf16[72,1024]{1,0:T(8,128)(2,1)}, bf16[72,1024]{1,0:T(8,128)(2,1)}) custom-call(bf16[576,512]{1,0:T(8,128)(2,1)} %get-tuple-element.18.mixed, bf16[576,1536]{1,0:T(8,128)(2,1)} %get-tuple-element.19.gact, bf16[512,1536]{1,0:T(8,128)(2,1)} %refs_8_.1, bf16[512,512]{1,0:T(8,128)(2,1)} %o_ref.3, ...), custom_call_target="tpu_custom_call" | custom-call | flops 2000000000 | bytes 5000000 | tf_op jit(solution)/shard_map/back/pallas_call | solution.py:335
  101.2 6.7 %collective-permute-start.7 = (bf16[72,1024]{1,0:T(8,128)(2,1)}, bf16[72,1024]{1,0:T(8,128)(2,1)S(1)}, u32[]{:S(2)}, u32[]{:S(2)}) collective-permute-start(bf16[72,1024]{1,0:T(8,128)(2,1)} %get-tuple-element.22), channel_id=1, source_target_pairs={{0,1},{1,2},{2,3},{3,4},{4,5},{5,6},{6,7},{7,8},{8,9},{9,10},{10,1... | collective-permute-start | bytes 442376 | tf_op jit(solution)/shard_map/ppermute | solution.py:345
  107.9 2.6 %collective-permute-start.6 = (bf16[216,1024]{1,0:T(8,128)(2,1)}, bf16[216,1024]{1,0:T(8,128)(2,1)S(1)}, u32[]{:S(2)}, u32[]{:S(2)}) collective-permute-start(bf16[216,1024]{1,0:T(8,128)(2,1)} %get-tuple-element.21), channel_id=1, source_target_pairs={{0,32},{1,33},{2,34},{3,35},{4,36},{5,37},{6,38},{7,39},{8,40},{9,... | collective-permute-start | bytes 1327112 | tf_op jit(solution)/shard_map/ppermute | solution.py:344
  110.6 1.7 %collective-permute-start.23 = (bf16[64,2048]{1,0:T(8,128)(2,1)S(1)}, bf16[64,2048]{1,0:T(8,128)(2,1)S(1)}, u32[]{:S(2)}, u32[]{:S(2)}) collective-permute-start(bf16[64,2048]{1,0:T(8,128)(2,1)S(1)} %pad_maximum_fusion.refs_0_), channel_id=1, source_target_pairs={{0,128},{1,33},{2,130},{3,35},{4,132},{5,37},{6,134},{7,39},{8,136... | collective-permute-start | bytes 786440 | tf_op jit(solution)/shard_map/ppermute | solution.py:53
  112.4 1.7 %collective-permute-start.22 = (bf16[64,2048]{1,0:T(8,128)(2,1)S(1)}, bf16[64,2048]{1,0:T(8,128)(2,1)S(1)}, u32[]{:S(2)}, u32[]{:S(2)}) collective-permute-start(bf16[64,2048]{1,0:T(8,128)(2,1)S(1)} %pad_maximum_fusion.refs_0_), channel_id=1, source_target_pairs={{0,192},{1,49},{2,194},{3,51},{4,196},{5,53},{6,198},{7,55},{8,200... | collective-permute-start | bytes 786440 | tf_op jit(solution)/shard_map/ppermute | solution.py:53
  114.1 3.4 %collective-permute-start.8 = (bf16[72,1024]{1,0:T(8,128)(2,1)}, bf16[72,1024]{1,0:T(8,128)(2,1)S(1)}, u32[]{:S(2)}, u32[]{:S(2)}) collective-permute-start(bf16[72,1024]{1,0:T(8,128)(2,1)} %get-tuple-element.23), channel_id=1, source_target_pairs={{0,33},{1,34},{2,35},{3,36},{4,37},{5,38},{6,39},{7,40},{8,41},{9,... | collective-permute-start | bytes 442376 | tf_op jit(solution)/shard_map/ppermute | solution.py:346
  117.5 12.9 %collective-permute-done.8.r_diag = bf16[72,1024]{1,0:T(8,128)(2,1)S(1)} collective-permute-done((bf16[72,1024]{1,0:T(8,128)(2,1)}, bf16[72,1024]{1,0:T(8,128)(2,1)S(1)}, u32[]{:S(2)}, u32[]{:S(2)}) %collective-permute-start.8) | collective-permute-done | bytes 147488 | tf_op jit(solution)/shard_map/ppermute | solution.py:346
  131.7 2.7 %collective-permute-start.27 = (bf16[64,2048]{1,0:T(8,128)(2,1)S(1)}, bf16[64,2048]{1,0:T(8,128)(2,1)S(1)}, u32[]{:S(2)}, u32[]{:S(2)}) collective-permute-start(bf16[64,2048]{1,0:T(8,128)(2,1)S(1)} %collective-permute-done.23.refs_2_), channel_id=1, source_target_pairs={{0,1},{1,0},{2,3},{3,2},{4,5},{5,4},{6,7},{7,6},{8,9},{9,8},{10,11... | collective-permute-start | bytes 786440 | tf_op jit(solution)/shard_map/ppermute | solution.py:53
  136.1 5.4 %finish.1 = (bf16[576,512]{1,0:T(8,128)(2,1)}, bf16[576,512]{1,0:T(8,128)(2,1)}) custom-call(bf16[576,512]{1,0:T(8,128)(2,1)} %bitcast.11, bf16[576,512]{1,0:T(8,128)(2,1)} %bitcast.13, bf16[576,1024]{1,0:T(8,128)(2,1)} %get-tuple-element.20.both, bf16[216,1024]{1,0:T(8,128)(2,1)} %copy-done.10, bf16[72,1024]{1,0:T(8,128)(2,1)} %copy-done.13, ...), custom_call_target="tpu_custom_call" | custom-call | flops 2000000000 | bytes 8000000 | tf_op jit(solution)/shard_map/finish/pallas_call | solution.py:347
  143.1 4.4 %weights.1 = (f32[512,1536]{1,0:T(8,128)}, f32[512,512]{1,0:T(8,128)}, f32[512,1]{1,0:T(8,128)}) custom-call(s32[4]{0:T(128)} %pad_add_fusion.place, bf16[64,2048]{1,0:T(8,128)(2,1)} %copy-done, bf16[64,2048]{1,0:T(8,128)(2,1)} %copy-done.4, bf16[64,2048]{1,0:T(8,128)(2,1)} %copy-done.3, bf16[64,2048]{1,0:T(8,128)(2,1)} %copy-done.2, ...), custom_call_target="tpu_custom_call" | custom-call | flops 10000000 | bytes 8000000 | tf_op jit(solution)/shard_map/weights/pallas_call | solution.py:360
  147.5 1.7 %reduce = f32[512]{0:T(512)} reduce(f32[512,1]{1,0:T(8,128)} %get-tuple-element.30, f32[]{:T(128)} %constant.73), dimensions={1}, to_apply=%get-tuple-element.30.reduce_sub_computation | reduce | bytes 4100 | tf_op jit(solution)/shard_map/weights/pallas_call | solution.py:360
  (89 shorter events, 14.1 us)
Async XLA Ops:
  1.7 17.6 %collective-permute-start.1 = (bf16[72,512]{1,0:T(8,128)(2,1)S(1)}, bf16[72,512]{1,0:T(8,128)(2,1)S(1)}, u32[]{:S(2)}, u32[]{:S(2)}) collective-permute-start(bf16[72,512]{1,0:T(8,128)(2,1)S(1)} %reshape.52), channel_id=1, source_target_pairs={{0,31},{1,0},{2,1},{3,2},{4,3},{5,4},{6,5},{7,6},{8,7},{9,8},{10,9... | collective-permute-start | bytes 221192 | tf_op jit(solution)/shard_map/ppermute | solution.py:286
  5.1 16.9 %collective-permute-start.2 = (bf16[72,512]{1,0:T(8,128)(2,1)S(1)}, bf16[72,512]{1,0:T(8,128)(2,1)S(1)}, u32[]{:S(2)}, u32[]{:S(2)}) collective-permute-start(bf16[72,512]{1,0:T(8,128)(2,1)S(1)} %reshape.53), channel_id=1, source_target_pairs={{0,255},{1,224},{2,225},{3,226},{4,227},{5,228},{6,229},{7,230},{8... | collective-permute-start | bytes 221192 | tf_op jit(solution)/shard_map/ppermute | solution.py:287
  15.5 12.2 %collective-permute-start = (bf16[216,512]{1,0:T(8,128)(2,1)S(1)}, bf16[216,512]{1,0:T(8,128)(2,1)S(1)}, u32[]{:S(2)}, u32[]{:S(2)}) collective-permute-start(bf16[216,512]{1,0:T(8,128)(2,1)S(1)} %reshape.51), channel_id=1, source_target_pairs={{0,224},{1,225},{2,226},{3,227},{4,228},{5,229},{6,230},{7,231},{8... | collective-permute-start | bytes 663560 | tf_op jit(solution)/shard_map/ppermute | solution.py:285
  16.3 13.7 %collective-permute-start.3 = (bf16[216,512]{1,0:T(8,128)(2,1)S(1)}, bf16[216,512]{1,0:T(8,128)(2,1)S(1)}, u32[]{:S(2)}, u32[]{:S(2)}) collective-permute-start(bf16[216,512]{1,0:T(8,128)(2,1)S(1)} %reshape.54), channel_id=1, source_target_pairs={{0,224},{1,225},{2,226},{3,227},{4,228},{5,229},{6,230},{7,231},{8... | collective-permute-start | bytes 663560 | tf_op jit(solution)/shard_map/ppermute | solution.py:285
  19.0 4.2 %collective-permute-start.4 = (bf16[72,512]{1,0:T(8,128)(2,1)S(1)}, bf16[72,512]{1,0:T(8,128)(2,1)S(1)}, u32[]{:S(2)}, u32[]{:S(2)}) collective-permute-start(bf16[72,512]{1,0:T(8,128)(2,1)S(1)} %reshape.55), channel_id=1, source_target_pairs={{0,31},{1,0},{2,1},{3,2},{4,3},{5,4},{6,5},{7,6},{8,7},{9,8},{10,9... | collective-permute-start | bytes 221192 | tf_op jit(solution)/shard_map/ppermute | solution.py:286
  19.4 8.3 %collective-permute-start.5 = (bf16[72,512]{1,0:T(8,128)(2,1)S(1)}, bf16[72,512]{1,0:T(8,128)(2,1)S(1)}, u32[]{:S(2)}, u32[]{:S(2)}) collective-permute-start(bf16[72,512]{1,0:T(8,128)(2,1)S(1)} %reshape.56), channel_id=1, source_target_pairs={{0,255},{1,224},{2,225},{3,226},{4,227},{5,228},{6,229},{7,230},{8... | collective-permute-start | bytes 221192 | tf_op jit(solution)/shard_map/ppermute | solution.py:287
  54.0 3.8 %collective-permute-start.9 = (bf16[256,2048]{1,0:T(8,128)(2,1)}, bf16[256,2048]{1,0:T(8,128)(2,1)S(1)}, u32[]{:S(2)}, u32[]{:S(2)}) collective-permute-start(bf16[256,2048]{1,0:T(8,128)(2,1)} %get-tuple-element.27), channel_id=1, source_target_pairs={{0,1},{1,0},{2,3},{3,2},{4,5},{5,4},{6,7},{7,6},{8,9},{9,8},{10,11... | collective-permute-start | bytes 3145736 | tf_op jit(solution)/shard_map/ppermute | solution.py:53
  59.2 7.0 %collective-permute-start.10 = (bf16[64,2048]{1,0:T(8,128)(2,1)S(1)}, bf16[64,2048]{1,0:T(8,128)(2,1)S(1)}, u32[]{:S(2)}, u32[]{:S(2)}) collective-permute-start(bf16[64,2048]{1,0:T(8,128)(2,1)S(1)} %get-tuple-element.31), channel_id=1, source_target_pairs={{0,64},{1,17},{2,66},{3,19},{4,68},{5,21},{6,70},{7,23},{8,72},{9,... | collective-permute-start | bytes 786440 | tf_op jit(solution)/shard_map/ppermute | solution.py:53
  59.5 8.8 %collective-permute-start.12 = (bf16[64,2048]{1,0:T(8,128)(2,1)S(1)}, bf16[64,2048]{1,0:T(8,128)(2,1)S(1)}, u32[]{:S(2)}, u32[]{:S(2)}) collective-permute-start(bf16[64,2048]{1,0:T(8,128)(2,1)S(1)} %get-tuple-element.32), channel_id=1, source_target_pairs={{0,192},{1,49},{2,194},{3,51},{4,196},{5,53},{6,198},{7,55},{8,200... | collective-permute-start | bytes 786440 | tf_op jit(solution)/shard_map/ppermute | solution.py:53
  62.2 7.0 %collective-permute-start.11 = (bf16[64,2048]{1,0:T(8,128)(2,1)S(1)}, bf16[64,2048]{1,0:T(8,128)(2,1)S(1)}, u32[]{:S(2)}, u32[]{:S(2)}) collective-permute-start(bf16[64,2048]{1,0:T(8,128)(2,1)S(1)} %get-tuple-element.33), channel_id=1, source_target_pairs={{0,128},{1,33},{2,130},{3,35},{4,132},{5,37},{6,134},{7,39},{8,136... | collective-permute-start | bytes 786440 | tf_op jit(solution)/shard_map/ppermute | solution.py:53
  70.3 4.4 %collective-permute-start.13 = (bf16[16,2048]{1,0:T(8,128)(2,1)S(1)}, bf16[16,2048]{1,0:T(8,128)(2,1)S(1)}, u32[]{:S(2)}, u32[]{:S(2)}) collective-permute-start(bf16[16,2048]{1,0:T(8,128)(2,1)S(1)} %get-tuple-element.38), channel_id=1, source_target_pairs={{0,16},{1,65},{2,18},{3,67},{4,20},{5,69},{6,22},{7,71},{8,24},{9,... | collective-permute-start | bytes 196616 | tf_op jit(solution)/shard_map/ppermute | solution.py:53
  70.4 4.6 %collective-permute-start.15 = (bf16[16,2048]{1,0:T(8,128)(2,1)S(1)}, bf16[16,2048]{1,0:T(8,128)(2,1)S(1)}, u32[]{:S(2)}, u32[]{:S(2)}) collective-permute-start(bf16[16,2048]{1,0:T(8,128)(2,1)S(1)} %get-tuple-element.39), channel_id=1, source_target_pairs={{0,48},{1,193},{2,50},{3,195},{4,52},{5,197},{6,54},{7,199},{8,56}... | collective-permute-start | bytes 196616 | tf_op jit(solution)/shard_map/ppermute | solution.py:53
  73.1 4.6 %collective-permute-start.14 = (bf16[16,2048]{1,0:T(8,128)(2,1)S(1)}, bf16[16,2048]{1,0:T(8,128)(2,1)S(1)}, u32[]{:S(2)}, u32[]{:S(2)}) collective-permute-start(bf16[16,2048]{1,0:T(8,128)(2,1)S(1)} %get-tuple-element.40), channel_id=1, source_target_pairs={{0,32},{1,129},{2,34},{3,131},{4,36},{5,133},{6,38},{7,135},{8,40}... | collective-permute-start | bytes 196616 | tf_op jit(solution)/shard_map/ppermute | solution.py:53
  77.7 3.2 %collective-permute-start.16 = (bf16[16,2048]{1,0:T(8,128)(2,1)S(1)}, bf16[16,2048]{1,0:T(8,128)(2,1)S(1)}, u32[]{:S(2)}, u32[]{:S(2)}) collective-permute-start(bf16[16,2048]{1,0:T(8,128)(2,1)S(1)} %add_convert_fusion.8), channel_id=1, source_target_pairs={{0,2},{1,3},{2,0},{3,1},{4,6},{5,7},{6,4},{7,5},{8,10},{9,11},{10,... | collective-permute-start | bytes 196616 | tf_op jit(solution)/shard_map/ppermute | solution.py:53
  81.0 4.6 %collective-permute-start.17 = (bf16[16,2048]{1,0:T(8,128)(2,1)S(1)}, bf16[16,2048]{1,0:T(8,128)(2,1)S(1)}, u32[]{:S(2)}, u32[]{:S(2)}) collective-permute-start(bf16[16,2048]{1,0:T(8,128)(2,1)S(1)} %add_convert_fusion.7), channel_id=1, source_target_pairs={{0,4},{1,5},{2,6},{3,7},{4,0},{5,1},{6,2},{7,3},{8,12},{9,13},{10,... | collective-permute-start | bytes 196616 | tf_op jit(solution)/shard_map/ppermute | solution.py:53
  85.6 7.4 %collective-permute-start.18 = (bf16[16,2048]{1,0:T(8,128)(2,1)S(1)}, bf16[16,2048]{1,0:T(8,128)(2,1)S(1)}, u32[]{:S(2)}, u32[]{:S(2)}) collective-permute-start(bf16[16,2048]{1,0:T(8,128)(2,1)S(1)} %add_convert_fusion.6), channel_id=1, source_target_pairs={{0,8},{1,9},{2,10},{3,11},{4,12},{5,13},{6,14},{7,15},{8,0},{9,1},... | collective-permute-start | bytes 196616 | tf_op jit(solution)/shard_map/ppermute | solution.py:53
  93.1 17.4 %collective-permute-start.21 = (bf16[16,2048]{1,0:T(8,128)(2,1)S(1)}, bf16[16,2048]{1,0:T(8,128)(2,1)S(1)}, u32[]{:S(2)}, u32[]{:S(2)}) collective-permute-start(bf16[16,2048]{1,0:T(8,128)(2,1)S(1)} %add_convert_fusion.5), channel_id=1, source_target_pairs={{0,16},{1,65},{2,18},{3,67},{4,20},{5,69},{6,22},{7,71},{8,24},{9,... | collective-permute-start | bytes 196616 | tf_op jit(solution)/shard_map/ppermute | solution.py:53
  93.2 17.3 %collective-permute-start.20 = (bf16[16,2048]{1,0:T(8,128)(2,1)S(1)}, bf16[16,2048]{1,0:T(8,128)(2,1)S(1)}, u32[]{:S(2)}, u32[]{:S(2)}) collective-permute-start(bf16[16,2048]{1,0:T(8,128)(2,1)S(1)} %add_convert_fusion.5), channel_id=1, source_target_pairs={{0,32},{1,129},{2,34},{3,131},{4,36},{5,133},{6,38},{7,135},{8,40}... | collective-permute-start | bytes 196616 | tf_op jit(solution)/shard_map/ppermute | solution.py:53
  94.7 15.8 %collective-permute-start.19 = (bf16[16,2048]{1,0:T(8,128)(2,1)S(1)}, bf16[16,2048]{1,0:T(8,128)(2,1)S(1)}, u32[]{:S(2)}, u32[]{:S(2)}) collective-permute-start(bf16[16,2048]{1,0:T(8,128)(2,1)S(1)} %add_convert_fusion.5), channel_id=1, source_target_pairs={{0,48},{1,193},{2,50},{3,195},{4,52},{5,197},{6,54},{7,199},{8,56}... | collective-permute-start | bytes 196616 | tf_op jit(solution)/shard_map/ppermute | solution.py:53
  95.8 38.6 %copy-start.9 = (f32[512]{0:T(512)S(1)}, f32[512]{0:T(512)}, u32[]{:S(2)}) copy-start(f32[512]{0:T(512)} %param.14) | copy-start | bytes 6148
  101.2 12.9 %collective-permute-start.7 = (bf16[72,1024]{1,0:T(8,128)(2,1)}, bf16[72,1024]{1,0:T(8,128)(2,1)S(1)}, u32[]{:S(2)}, u32[]{:S(2)}) collective-permute-start(bf16[72,1024]{1,0:T(8,128)(2,1)} %get-tuple-element.22), channel_id=1, source_target_pairs={{0,1},{1,2},{2,3},{3,4},{4,5},{5,6},{6,7},{7,8},{8,9},{9,10},{10,1... | collective-permute-start | bytes 442376 | tf_op jit(solution)/shard_map/ppermute | solution.py:345
  107.9 27.5 %collective-permute-start.6 = (bf16[216,1024]{1,0:T(8,128)(2,1)}, bf16[216,1024]{1,0:T(8,128)(2,1)S(1)}, u32[]{:S(2)}, u32[]{:S(2)}) collective-permute-start(bf16[216,1024]{1,0:T(8,128)(2,1)} %get-tuple-element.21), channel_id=1, source_target_pairs={{0,32},{1,33},{2,34},{3,35},{4,36},{5,37},{6,38},{7,39},{8,40},{9,... | collective-permute-start | bytes 1327112 | tf_op jit(solution)/shard_map/ppermute | solution.py:344
  110.5 30.9 %copy-start = (bf16[64,2048]{1,0:T(8,128)(2,1)}, bf16[64,2048]{1,0:T(8,128)(2,1)S(1)}, u32[]{:S(2)}) copy-start(bf16[64,2048]{1,0:T(8,128)(2,1)S(1)} %pad_maximum_fusion.refs_0_) | copy-start | bytes 786436
  110.6 19.8 %collective-permute-start.24 = (bf16[64,2048]{1,0:T(8,128)(2,1)S(1)}, bf16[64,2048]{1,0:T(8,128)(2,1)S(1)}, u32[]{:S(2)}, u32[]{:S(2)}) collective-permute-start(bf16[64,2048]{1,0:T(8,128)(2,1)S(1)} %pad_maximum_fusion.refs_0_), channel_id=1, source_target_pairs={{0,64},{1,17},{2,66},{3,19},{4,68},{5,21},{6,70},{7,23},{8,72},{9,... | collective-permute-start | bytes 786440 | tf_op jit(solution)/shard_map/ppermute | solution.py:53
  110.6 21.0 %collective-permute-start.23 = (bf16[64,2048]{1,0:T(8,128)(2,1)S(1)}, bf16[64,2048]{1,0:T(8,128)(2,1)S(1)}, u32[]{:S(2)}, u32[]{:S(2)}) collective-permute-start(bf16[64,2048]{1,0:T(8,128)(2,1)S(1)} %pad_maximum_fusion.refs_0_), channel_id=1, source_target_pairs={{0,128},{1,33},{2,130},{3,35},{4,132},{5,37},{6,134},{7,39},{8,136... | collective-permute-start | bytes 786440 | tf_op jit(solution)/shard_map/ppermute | solution.py:53
  112.4 22.0 %collective-permute-start.22 = (bf16[64,2048]{1,0:T(8,128)(2,1)S(1)}, bf16[64,2048]{1,0:T(8,128)(2,1)S(1)}, u32[]{:S(2)}, u32[]{:S(2)}) collective-permute-start(bf16[64,2048]{1,0:T(8,128)(2,1)S(1)} %pad_maximum_fusion.refs_0_), channel_id=1, source_target_pairs={{0,192},{1,49},{2,194},{3,51},{4,196},{5,53},{6,198},{7,55},{8,200... | collective-permute-start | bytes 786440 | tf_op jit(solution)/shard_map/ppermute | solution.py:53
  114.1 21.2 %copy-start.13 = (bf16[72,1024]{1,0:T(8,128)(2,1)}, bf16[72,1024]{1,0:T(8,128)(2,1)S(1)}, u32[]{:S(2)}) copy-start(bf16[72,1024]{1,0:T(8,128)(2,1)S(1)} %collective-permute-done.7.r_lon) | copy-start | bytes 442372
  114.1 16.3 %collective-permute-start.8 = (bf16[72,1024]{1,0:T(8,128)(2,1)}, bf16[72,1024]{1,0:T(8,128)(2,1)S(1)}, u32[]{:S(2)}, u32[]{:S(2)}) collective-permute-start(bf16[72,1024]{1,0:T(8,128)(2,1)} %get-tuple-element.23), channel_id=1, source_target_pairs={{0,33},{1,34},{2,35},{3,36},{4,37},{5,38},{6,39},{7,40},{8,41},{9,... | collective-permute-start | bytes 442376 | tf_op jit(solution)/shard_map/ppermute | solution.py:346
  130.4 11.1 %collective-permute-start.25 = (bf16[64,2048]{1,0:T(8,128)(2,1)S(1)}, bf16[64,2048]{1,0:T(8,128)(2,1)S(1)}, u32[]{:S(2)}, u32[]{:S(2)}) collective-permute-start(bf16[64,2048]{1,0:T(8,128)(2,1)S(1)} %pad_maximum_fusion.refs_0_), channel_id=1, source_target_pairs={{0,1},{1,0},{2,3},{3,2},{4,5},{5,4},{6,7},{7,6},{8,9},{9,8},{10,11... | collective-permute-start | bytes 786440 | tf_op jit(solution)/shard_map/ppermute | solution.py:53
  130.4 11.1 %collective-permute-start.28 = (bf16[64,2048]{1,0:T(8,128)(2,1)S(1)}, bf16[64,2048]{1,0:T(8,128)(2,1)S(1)}, u32[]{:S(2)}, u32[]{:S(2)}) collective-permute-start(bf16[64,2048]{1,0:T(8,128)(2,1)S(1)} %collective-permute-done.24.refs_3_), channel_id=1, source_target_pairs={{0,1},{1,0},{2,3},{3,2},{4,5},{5,4},{6,7},{7,6},{8,9},{9,8},{10,11... | collective-permute-start | bytes 786440 | tf_op jit(solution)/shard_map/ppermute | solution.py:53
  131.7 9.9 %collective-permute-start.27 = (bf16[64,2048]{1,0:T(8,128)(2,1)S(1)}, bf16[64,2048]{1,0:T(8,128)(2,1)S(1)}, u32[]{:S(2)}, u32[]{:S(2)}) collective-permute-start(bf16[64,2048]{1,0:T(8,128)(2,1)S(1)} %collective-permute-done.23.refs_2_), channel_id=1, source_target_pairs={{0,1},{1,0},{2,3},{3,2},{4,5},{5,4},{6,7},{7,6},{8,9},{9,8},{10,11... | collective-permute-start | bytes 786440 | tf_op jit(solution)/shard_map/ppermute | solution.py:53
  134.4 7.2 %collective-permute-start.26 = (bf16[64,2048]{1,0:T(8,128)(2,1)S(1)}, bf16[64,2048]{1,0:T(8,128)(2,1)S(1)}, u32[]{:S(2)}, u32[]{:S(2)}) collective-permute-start(bf16[64,2048]{1,0:T(8,128)(2,1)S(1)} %collective-permute-done.22.refs_1_), channel_id=1, source_target_pairs={{0,1},{1,0},{2,3},{3,2},{4,5},{5,4},{6,7},{7,6},{8,9},{9,8},{10,11... | collective-permute-start | bytes 786440 | tf_op jit(solution)/shard_map/ppermute | solution.py:53
  (16 other events, 83.2 us)

commit v2 on v1

--- a/solution.py
+++ b/solution.py
@@ -18,7 +18,7 @@
 BOTH = ("lat", "lon")
 f32 = jnp.float32
 bf16 = jnp.bfloat16
-VMEM = 56 * 1024 * 1024
+VMEM = 24 * 1024 * 1024
 
 
 def index_of(y, x, z, c):
@@ -117,42 +117,43 @@
     return centred * rstd, rstd
 
 
-def main_kernel(
-    place,
-    f_loc, f_lat, f_lon, f_diag,
-    c_loc, c_lat, c_lon, c_diag,
-    p_loc, p_lat, p_lon, p_diag,
-    gain, w_ref, o_ref,
-    mixed, gact, own, other,
-    normed, qkv, ctw, gm, acc,
-):
-    def windows(a, b, c, d):
-        return (
-            dot(p_loc[...], a[...])
-            + dot(p_lat[...], b[...])
-            + dot(p_lon[...], c[...])
-            + dot(p_diag[...], d[...])
-        )
-
-    xhat, _ = normalise(windows(f_loc, f_lat, f_lon, f_diag))
+def pairs_mask():
+    row = lax.broadcasted_iota(jnp.int32, (2 * SPAN, 128), 0)
+    lane = lax.broadcasted_iota(jnp.int32, (2 * SPAN, 128), 1)
+    return ((row < SPAN) == (lane < 64)).astype(f32).astype(bf16)
+
+
+def joined(r):
+    low = lax.broadcasted_iota(jnp.int32, (SPAN, 128), 1) < 64
+    return jnp.where(low, r[:SPAN], r[SPAN:]).astype(bf16)
+
+
+def doubled(x, pick):
+    return jnp.concatenate([x, x], axis=0) * pick
+
+
+def gathered(pieces, tables):
+    total = dot(tables[0][...], pieces[0][...])
+    for p, t in zip(pieces[1:], tables[1:]):
+        total = total + dot(t[...], p[...])
+    return total
+
+
+def forward_kernel(place, *refs):
+    pieces, tables, (gain, w_ref, normed, qkv, probs, mixed) = refs[:4], refs[4:8], refs[8:]
+    xhat, _ = normalise(gathered(pieces, tables))
     normed[...] = (xhat * gain[...]).astype(bf16)
     qkv[...] = dot(normed[...], w_ref[...]).astype(bf16)
-    ctw[...] = windows(c_loc, c_lat, c_lon, c_diag).astype(bf16)
-    gm[...] = dot(ctw[...], o_ref[...], NT).astype(bf16)
 
     last_lat = place[0]
     two = 2 * SPAN
-    row2 = lax.broadcasted_iota(jnp.int32, (two, 128), 0)
-    lane2 = lax.broadcasted_iota(jnp.int32, (two, 128), 1)
-    pick = ((row2 < SPAN) == (lane2 < 64)).astype(f32).astype(bf16)
-    low = lax.broadcasted_iota(jnp.int32, (SPAN, 128), 1) < 64
+    pick = pairs_mask()
 
     def lev_of(t):
         return (t >= SPAN // 2).astype(jnp.int32)
 
     def half_of(t):
-        u = t - SPAN // 2 * lev_of(t)
-        return (u >= SPAN // 4).astype(jnp.int32)
+        return (t - SPAN // 2 * lev_of(t) >= SPAN // 4).astype(jnp.int32)
 
     tq = lax.broadcasted_iota(jnp.int32, (two, SPAN), 0)
     tq = tq - SPAN * (tq >= SPAN).astype(jnp.int32)
@@ -161,31 +162,49 @@
     half_diff = jnp.abs(half_of(tq) - half_of(tk)) * last_lat
     factor = 1.0 / math.sqrt(D // HEADS)
 
-    def join(r):
-        return jnp.where(low, r[:SPAN], r[SPAN:]).astype(bf16)
-
     def window(w, carry):
         at = pl.ds(pl.multiple_of(w * SPAN, SPAN), SPAN)
         top = (w >= 2).astype(jnp.int32)
         same = (lev_diff * top + half_diff) == 0
         for p in range(HEADS // 2):
-            cols = pl.ds(128 * p, 128)
-            q = qkv[at, pl.ds(128 * p, 128)]
+            q2 = doubled(qkv[at, pl.ds(128 * p, 128)], pick)
             k = qkv[at, pl.ds(D + 128 * p, 128)]
             v = qkv[at, pl.ds(2 * D + 128 * p, 128)]
-            g = gm[at, cols]
-            q2 = jnp.concatenate([q, q], axis=0) * pick
-            g2 = jnp.concatenate([g, g], axis=0) * pick
             s = jnp.where(same, dot(q2, k, NT) * factor, -1000000000.0)
             e = jnp.exp(s - jnp.max(s, axis=-1, keepdims=True))
-            probs = e * (1.0 / jnp.sum(e, axis=-1, keepdims=True))
-            rounded = probs.astype(bf16)
-            mixed[at, cols] = join(dot(rounded, v))
+            rounded = (e * (1.0 / jnp.sum(e, axis=-1, keepdims=True))).astype(bf16)
+            probs[pl.ds(pl.multiple_of((w * 4 + p) * two, two), two), :] = rounded
+            mixed[at, pl.ds(128 * p, 128)] = joined(dot(rounded, v))
+        return carry
+
+    lax.fori_loop(0, 4, window, 0)
+
+
+def backward_kernel(place, *refs):
+    pieces, tables, (o_ref, normed, qkv, probs, mixed, gact, own, other, ctw, gm, acc) = (
+        refs[:4], refs[4:8], refs[8:],
+    )
+    ctw[...] = gathered(pieces, tables).astype(bf16)
+    gm[...] = dot(ctw[...], o_ref[...], NT).astype(bf16)
+    two = 2 * SPAN
+    pick = pairs_mask()
+    factor = 1.0 / math.sqrt(D // HEADS)
+
+    def window(w, carry):
+        at = pl.ds(pl.multiple_of(w * SPAN, SPAN), SPAN)
+        for p in range(HEADS // 2):
+            cols = pl.ds(128 * p, 128)
+            q2 = doubled(qkv[at, cols], pick)
+            g2 = doubled(gm[at, cols], pick)
+            k = qkv[at, pl.ds(D + 128 * p, 128)]
+            v = qkv[at, pl.ds(2 * D + 128 * p, 128)]
+            rounded = probs[pl.ds(pl.multiple_of((w * 4 + p) * two, two), two), :]
             gact[at, pl.ds(2 * D + 128 * p, 128)] = dot(rounded, g2, TN).astype(bf16)
             dp = dot(g2, v, NT)
-            inner = jnp.sum(dp * probs, axis=-1, keepdims=True)
-            ds = (probs * (dp - inner) * factor).astype(bf16)
-            gact[at, cols] = join(dot(ds, k))
+            pr = rounded.astype(f32)
+            inner = jnp.sum(dp * pr, axis=-1, keepdims=True)
+            ds = (pr * (dp - inner) * factor).astype(bf16)
+            gact[at, cols] = joined(dot(ds, k))
             gact[at, pl.ds(D + 128 * p, 128)] = dot(ds, q2, TN).astype(bf16)
         return carry
 
@@ -193,7 +212,6 @@
 
     acc[:, : 3 * D] = dot(normed[...], gact[...], TN)
     acc[:, 3 * D :] = dot(mixed[...], ctw[...], TN)
-
     y, x, c = place[1], place[2], place[3]
 
     def fill(out, core):
@@ -235,26 +253,88 @@
     grad[...] = (c_loc[...].astype(f32) + rstd * (g - first - xhat * second)).astype(bf16)
 
 
-def weights_kernel(place, *refs):
-    pieces, (w_ref, gain, g_qkv, g_out, g_gain) = refs[:8], refs[8:]
+def weights_kernel(side, place, *refs):
+    pieces, refs = refs[:4], refs[4:]
+    if side == 0:
+        w_ref, g_qkv, g_out, g_total = refs
+    else:
+        w_ref, before, gain, _, _, g_qkv, g_out, g_total = refs
     y, x, c = place[1], place[2], place[3]
-    for side in range(2):
-        core = c if side == 0 else 1 - c
-        d1 = jnp.where(core == 0, y, x)
-        d2 = jnp.where(core == 0, x, y)
-        for s1 in range(4):
+    step = pl.program_id(0)
+    core = c if side == 0 else 1 - c
+    d1 = jnp.where(core == 0, y, x)
+    d2 = jnp.where(core == 0, x, y)
+
+    @pl.when(step == 0)
+    def _():
+        g_total[...] = jnp.zeros_like(g_total) if side == 0 else before[...]
+
+    for i in range(4):
+
+        @pl.when(step == i)
+        def _(i=i):
             for s2 in range(4):
-                r = core * 256 + lax.rem(d1 + s1, 4) * 64 + lax.rem(d2 + s2, 4) * 16
-                at = pl.ds(pl.multiple_of(r, 16), 16)
-                block = pieces[side * 4 + s1][pl.ds(s2 * 16, 16), :].astype(f32)
+                at = pl.ds(pl.multiple_of(lax.rem(d2 + s2, 4) * 16, 16), 16)
+                block = pieces[i][pl.ds(s2 * 16, 16), :].astype(f32)
                 g_qkv[at, :] = block[:, : 3 * D]
                 g_out[at, :] = block[:, 3 * D :]
-    total = jnp.sum(g_qkv[...] * w_ref[...].astype(f32), axis=1, keepdims=True)
-    g_gain[...] = total / gain[...]
+
+    row = core * 256 + lax.rem(d1 + step, 4) * 64
+    lane = lax.broadcasted_iota(jnp.int32, (64, D), 1)
+    here = lax.broadcasted_iota(jnp.int32, (64, D), 0) + row
+    sums = jnp.sum(g_qkv[...] * w_ref[...].astype(f32), axis=1, keepdims=True)
+    g_total[...] += jnp.sum(jnp.where(lane == here, sums, 0.0), axis=0, keepdims=True)
+
+    if side == 1:
+
+        @pl.when(step == 3)
+        def _():
+            g_total[...] = g_total[...] / gain[...]
+
+
+def band(side, step, place):
+    y, x, c = place[1], place[2], place[3]
+    core = c if side == 0 else 1 - c
+    d1 = jnp.where(core == 0, y, x)
+    return core * 4 + lax.rem(d1 + step, 4), 0
+
+
+def to_weights(side, place, pieces, qkv_weight, *more):
+    at = functools.partial(band, side)
+    whole = pl.BlockSpec((64, 4 * D), lambda i, place: (0, 0))
+    row = pl.BlockSpec((1, D), lambda i, place: (0, 0))
+    anywhere = pl.BlockSpec(memory_space=pl.ANY)
+    extra = [] if side == 0 else [row, row, anywhere, anywhere]
+    return pl.pallas_call(
+        functools.partial(weights_kernel, side),
+        out_shape=[shape(D, 3 * D, dtype=f32), shape(D, D, dtype=f32), shape(1, D, dtype=f32)],
+        grid_spec=pltpu.PrefetchScalarGridSpec(
+            num_scalar_prefetch=1,
+            grid=(4,),
+            in_specs=[whole] * 4 + [pl.BlockSpec((64, 3 * D), at)] + extra,
+            out_specs=[pl.BlockSpec((64, 3 * D), at), pl.BlockSpec((64, D), at), row],
+        ),
+        input_output_aliases={} if side == 0 else {8: 0, 9: 1},
+        compiler_params=params(),
+        cost_estimate=cost(10**7, 4 * 10**6),
+        name="weights" + str(side),
+    )(place, *vms(*pieces), qkv_weight, *more)
 
 
 def params():
     return pltpu.CompilerParams(vmem_limit_bytes=VMEM)
+
+
+def vm(x):
+    return pltpu.with_memory_space_constraint(x, pltpu.VMEM)
+
+
+def vms(*xs):
+    return [vm(x) for x in xs]
+
+
+def vshape(*dims, dtype=bf16):
+    return pltpu.VMEM(dims, dtype)
 
 
 def spec(count, scalar=False):
@@ -268,6 +348,61 @@
 
 def cost(flops, moved):
     return pl.CostEstimate(flops=flops, bytes_accessed=moved, transcendentals=0)
+
+
+def to_forward(place, pieces, tables, gain_row, qkv_weight):
+    return pl.pallas_call(
+        forward_kernel,
+        out_shape=[
+            vshape(TOK, D), vshape(TOK, 3 * D), vshape(32 * SPAN, SPAN), vshape(TOK, D),
+        ],
+        in_specs=spec(10, True),
+        out_specs=spec(4),
+        compiler_params=params(),
+        cost_estimate=cost(3 * 10**9, 10**7),
+        name="forward",
+    )(place, *vms(*pieces), *tables, gain_row, vm(qkv_weight))
+
+
+def to_backward(place, pieces, tables, out_weight, *kept):
+    return pl.pallas_call(
+        backward_kernel,
+        out_shape=[vshape(TOK, 3 * D), vshape(256, 4 * D), vshape(256, 4 * D)],
+        in_specs=spec(13, True),
+        out_specs=spec(3),
+        scratch_shapes=[
+            pltpu.VMEM((TOK, D), bf16),
+            pltpu.VMEM((TOK, D), bf16),
+            pltpu.VMEM((D, 4 * D), f32),
+        ],
+        compiler_params=params(),
+        cost_estimate=cost(5 * 10**9, 10**7),
+        name="backward",
+    )(place, *vms(*pieces), *tables, vm(out_weight), *vms(*kept))
+
+
+def to_back(mixed, gact, qkv_weight, out_weight, *tables):
+    return pl.pallas_call(
+        back_kernel,
+        out_shape=[vshape(TOK, 2 * D), vshape(216, 2 * D), vshape(72, 2 * D), vshape(72, 2 * D)],
+        in_specs=spec(7),
+        out_specs=spec(4),
+        compiler_params=params(),
+        cost_estimate=cost(2 * 10**9, 5 * 10**6),
+        name="back",
+    )(*vms(mixed, gact, qkv_weight, out_weight, *tables))
+
+
+def to_finish(*args):
+    return pl.pallas_call(
+        finish_kernel,
+        out_shape=[shape(TOK, D), shape(TOK, D)],
+        in_specs=spec(11),
+        out_specs=spec(2),
+        compiler_params=params(),
+        cost_estimate=cost(2 * 10**9, 8 * 10**6),
+        name="finish",
+    )(*vms(*args))
 
 
 def add(*xs):
@@ -275,6 +410,10 @@
     for x in xs[1:]:
         total = total + x.astype(f32)
     return total.astype(bf16)
+
+
+def tied(x):
+    return lax.optimization_barrier(x)
 
 
 def halo(field):
@@ -305,67 +444,39 @@
     f_halo = halo(fields)
     c_halo = halo(cotangent)
 
-    mixed, gact, own, other = pl.pallas_call(
-        main_kernel,
-        out_shape=[shape(TOK, D), shape(TOK, 3 * D), shape(256, 4 * D), shape(256, 4 * D)],
-        in_specs=spec(15, True),
-        out_specs=spec(4),
-        scratch_shapes=[
-            pltpu.VMEM((TOK, D), bf16),
-            pltpu.VMEM((TOK, 3 * D), bf16),
-            pltpu.VMEM((TOK, D), bf16),
-            pltpu.VMEM((TOK, D), bf16),
-            pltpu.VMEM((D, 4 * D), f32),
-        ],
-        compiler_params=params(),
-        cost_estimate=cost(8 * 10**9, 10**7),
-        name="main",
-    )(
-        place, f_loc, *f_halo, c_loc, *c_halo, p_loc, p_lat, p_lon, p_diag,
-        gain_row, qkv_weight, out_weight,
+    tables = vms(p_loc, p_lat, p_lon, p_diag)
+    normed, qkv, probs, mixed = to_forward(place, (f_loc, *f_halo), tables, gain_row, qkv_weight)
+    gact, own, other = to_backward(
+        place, (c_loc, *c_halo), tables, out_weight, normed, qkv, probs, mixed
     )
 
     there = send(other, to_sibling)
     part = [add(own[64 * k : 64 * k + 64], there[64 * k : 64 * k + 64]) for k in range(4)]
-    part = add(part[0], *[send(part[k], first_axis(k)) for k in (1, 2, 3)])
+    mixed, gact, part = tied((mixed, gact, part))
+    both, to_lat, to_lon, to_diag = to_back(mixed, gact, qkv_weight, out_weight, *tables[1:])
+    recv = [send(part[k], first_axis(k)) for k in (1, 2, 3)]
+    recv, to_lat = tied((recv, to_lat))
+    part = add(part[0], *recv)
+    part, to_lat, to_lon, to_diag = tied((part, to_lat, to_lon, to_diag))
     part = add(part[:16], *[send(part[16 * k : 16 * k + 16], second_axis(k)) for k in (1, 2, 3)])
-    for k in (1, 2, 4):
-        part = add(part, send(part, flip_z(k)))
-
-    both, to_lat, to_lon, to_diag = pl.pallas_call(
-        back_kernel,
-        out_shape=[shape(TOK, 2 * D), shape(216, 2 * D), shape(72, 2 * D), shape(72, 2 * D)],
-        in_specs=spec(7),
-        out_specs=spec(4),
-        compiler_params=params(),
-        cost_estimate=cost(2 * 10**9, 5 * 10**6),
-        name="back",
-    )(mixed, gact, qkv_weight, out_weight, p_lat, p_lon, p_diag)
     r_lat = lax.ppermute(to_lat, BOTH, shifted(1, 0))
     r_lon = lax.ppermute(to_lon, BOTH, shifted(0, 1))
     r_diag = lax.ppermute(to_diag, BOTH, shifted(1, 1))
-    out, grad = pl.pallas_call(
-        finish_kernel,
-        out_shape=[shape(TOK, D), shape(TOK, D)],
-        in_specs=spec(11),
-        out_specs=spec(2),
-        compiler_params=params(),
-        cost_estimate=cost(2 * 10**9, 8 * 10**6),
-        name="finish",
-    )(f_loc, c_loc, both, r_lat, r_lon, r_diag, p_loc, s_lat, s_lon, s_diag, gain_row)
+    for k in (1, 2, 6):
+        part = add(part, send(part, flip_z(k)))
 
     block = jnp.concatenate([part] + [send(part, second_axis(4 - s)) for s in (1, 2, 3)], axis=0)
-    mine = [block] + [send(block, first_axis(4 - s)) for s in (1, 2, 3)]
+    mine = [send(block, first_axis(4 - s)) for s in (1, 2, 3)]
+    out, grad = to_finish(
+        f_loc, c_loc, both, r_lat, r_lon, r_diag, tables[0], s_lat, s_lon, s_diag, gain_row
+    )
+    mine, out = tied((mine, out))
+    mine = [block] + mine
     sibling = [send(m, to_sibling) for m in mine]
-    g_qkv, g_out, g_gain = pl.pallas_call(
-        weights_kernel,
-        out_shape=[shape(D, 3 * D, dtype=f32), shape(D, D, dtype=f32), shape(D, 1, dtype=f32)],
-        in_specs=spec(10, True),
-        out_specs=spec(3),
-        compiler_params=params(),
-        cost_estimate=cost(10**7, 8 * 10**6),
-        name="weights",
-    )(place, *mine, *sibling, qkv_weight, layer_norm_gain.reshape(D, 1))
+    g_qkv, g_out, total = to_weights(0, place, mine, qkv_weight)
+    g_qkv, g_out, g_gain = to_weights(
+        1, place, sibling, qkv_weight, total, gain_row, g_qkv, g_out
+    )
 
     grid = (LEV, ROWS, COLS, D)
     return out.reshape(grid), grad.reshape(grid), g_qkv, g_out, g_gain.reshape(D)

time: 149 us -> 118 us (0.79)
  waiting for transfers between devices: 50.3 us -> 24.3 us
  Pallas kernels: 38.4 us -> 29.2 us
  local copies, waits for them, and re-layouts: 6.32 us -> 12.6 us
  other arithmetic: 4.85 us -> 0.71 us
    pallas_call x4 -> x6, Pallas kernels: 38.4 us -> 29.2 us  [the longest x1 10.9 us: to_backward(): pl.pallas_call(backward_kernel, out_shape=[vshape(TOK, 3 * D), vshape(256...]
    ppermute x20, waiting for transfers between devices: 29.3 us -> 20.1 us  [send(): return lax.ppermute(x, BOTH, route(step))]
    ppermute x1, waiting for transfers between devices: 12.9 us -> 4.13 us  [on_device(): r_diag = lax.ppermute(to_diag, BOTH, shifted(1, 1))]
    ppermute x2, waiting for transfers between devices: 4.5 us -> 0.01 us  [halo(): lax.ppermute(diag, BOTH, shifted(-1, -1))]
    reshape x2, local copies, waits for them, and re-layouts: 0.15 us -> 2.48 us  [halo(): lat = field[:, :3, 6:].reshape(-1, D)]
    ppermute x2, waiting for transfers between devices: 2.32 us -> 0.01 us  [halo(): lax.ppermute(lat, BOTH, shifted(-1, 0))]
    ppermute x20, starting transfers between devices: 17.5 us -> 19.7 us  [send(): return lax.ppermute(x, BOTH, route(step))]
    ppermute x2, starting transfers between devices: 3.3 us -> 1.06 us  [halo(): lax.ppermute(lat, BOTH, shifted(-1, 0))]
  transfers between devices with their start and end apart: 29 -> 29, of which waited for: 15 -> 10; matrix products, arithmetic and copies ran while one was open for 2% -> 7% of each run, Pallas kernels for 7% -> 13%
where the time goes in v2:
time: 118 us; the launch traced here: 117 us
  starting transfers between devices  49.6 us (42%)
  Pallas kernels  29.2 us (25%)
  waiting for transfers between devices  24.3 us (21%)
  local copies, waits for them, and re-layouts  12.6 us (11%)
    ppermute x20, waiting for transfers between devices, send(): return lax.ppermute(x, BOTH, route(step))  20.1 us
    ppermute x20, starting transfers between devices, send(): return lax.ppermute(x, BOTH, route(step))  19.7 us
    ppermute x2, starting transfers between devices, halo(): lax.ppermute(diag, BOTH, shifted(-1, -1))  12.9 us
    pallas_call x1, Pallas kernels, to_backward(): pl.pallas_call(backward_kernel, out_shape=[vshape(TOK, 3 * D), vshape(256...  10.9 us
    ppermute x1, starting transfers between devices, on_device(): r_lon = lax.ppermute(to_lon, BOTH, shifted(0, 1))  8.67 us
    pallas_call x1, Pallas kernels, to_forward(): pl.pallas_call(forward_kernel, out_shape=[vshape(TOK, D), vshape(TOK, 3 *...  7.53 us
    pallas_call x2, Pallas kernels, to_weights(): pl.pallas_call(functools.partial(weights_kernel, side), out_shape=[shape(...  5.35 us
    ppermute x1, waiting for transfers between devices, on_device(): r_diag = lax.ppermute(to_diag, BOTH, shifted(1, 1))  4.13 us
  transfers between devices with their start and end apart: 29, of which 10 were waited for; matrix products, arithmetic and copies ran while one was open for 7% of the time, Pallas kernels for 13%

profile of v2, /device:TPU:1, one launch (start us, length us, event | category | flops | bytes accessed | tf_op | source)
XLA Modules:
  0.0 117.3 jit_solution(6396068385611030760)
XLA Ops:
  2.4 3.2 %collective-permute-start.1 = (bf16[72,512]{1,0:T(8,128)(2,1)}, bf16[72,512]{1,0:T(8,128)(2,1)S(1)}, u32[]{:S(2)}, u32[]{:S(2)}) collective-permute-start(bf16[72,512]{1,0:T(8,128)(2,1)} %reshape.48), channel_id=1, source_target_pairs={{0,31},{1,0},{2,1},{3,2},{4,3},{5,4},{6,5},{7,6},{8,7},{9,8},{10,9... | collective-permute-start | bytes 221192 | tf_op jit(solution)/shard_map/ppermute | solution.py:425
  6.3 9.3 %collective-permute-start.2 = (bf16[72,512]{1,0:T(8,128)(2,1)}, bf16[72,512]{1,0:T(8,128)(2,1)S(1)}, u32[]{:S(2)}, u32[]{:S(2)}) collective-permute-start(bf16[72,512]{1,0:T(8,128)(2,1)} %reshape.49), channel_id=1, source_target_pairs={{0,255},{1,224},{2,225},{3,226},{4,227},{5,228},{6,229},{7,230},{8... | collective-permute-start | bytes 221192 | tf_op jit(solution)/shard_map/ppermute | solution.py:426
  15.5 1.0 slice.54
  18.5 1.6 %reshape.53 = bf16[72,512]{1,0:T(8,128)(2,1)} reshape(bf16[4,3,6,512]{3,2,1,0:T(8,128)(2,1)} %get-tuple-element.84) | data formatting | bytes 147456 | tf_op jit(solution)/shard_map/reshape | solution.py:421
  20.8 3.6 %collective-permute-start.5 = (bf16[72,512]{1,0:T(8,128)(2,1)}, bf16[72,512]{1,0:T(8,128)(2,1)S(1)}, u32[]{:S(2)}, u32[]{:S(2)}) collective-permute-start(bf16[72,512]{1,0:T(8,128)(2,1)} %reshape.54), channel_id=1, source_target_pairs={{0,255},{1,224},{2,225},{3,226},{4,227},{5,228},{6,229},{7,230},{8... | collective-permute-start | bytes 221192 | tf_op jit(solution)/shard_map/ppermute | solution.py:426
  25.2 1.7 %reshape.52 = bf16[216,512]{1,0:T(8,128)(2,1)} reshape(bf16[4,3,18,512]{3,2,1,0:T(8,128)(2,1)} %slice.57) | data formatting | bytes 442368 | tf_op jit(solution)/shard_map/reshape | solution.py:420
  27.6 1.1 copy-done.5
  30.6 7.5 %forward.1 = (bf16[576,512]{1,0:T(8,128)(2,1)S(1)}, bf16[576,1536]{1,0:T(8,128)(2,1)S(1)}, bf16[4608,144]{1,0:T(8,128)(2,1)S(1)}, bf16[576,512]{1,0:T(8,128)(2,1)S(1)}) custom-call(s32[4]{0:T(128)S(1)} %pad_add_fusion.place, bf16[576,512]{1,0:T(8,128)(2,1)S(1)} %bitcast.10, bf16[216,512]{1,0:T(8,128)(2,1)S(1)} %collective-permute-done.refs_1_, ...), custom_call_target="tpu_custom_call" | custom-call | flops 3000000000 | bytes 10000000 | tf_op jit(solution)/shard_map/forward/pallas_call | solution.py:354
  38.2 10.9 %backward.1 = (bf16[576,1536]{1,0:T(8,128)(2,1)S(1)}, bf16[256,2048]{1,0:T(8,128)(2,1)S(1)}, bf16[256,2048]{1,0:T(8,128)(2,1)S(1)}) custom-call(s32[4]{0:T(128)S(1)} %pad_add_fusion.place, bf16[576,512]{1,0:T(8,128)(2,1)S(1)} %bitcast.12, bf16[216,512]{1,0:T(8,128)(2,1)S(1)} %collective-permute-done.3.refs_1_, ...), custom_call_target="tpu_custom_call" | custom-call | flops 5000000000 | bytes 10000000 | tf_op jit(solution)/shard_map/backward/pallas_call | solution.py:368
  49.2 2.6 %collective-permute-done.6 = bf16[256,2048]{1,0:T(8,128)(2,1)S(1)} collective-permute-done((bf16[256,2048]{1,0:T(8,128)(2,1)S(1)}, bf16[256,2048]{1,0:T(8,128)(2,1)S(1)}, u32[]{:S(2)}, u32[]{:S(2)}) %collective-permute-start.6) | collective-permute-done | bytes 1048608 | tf_op jit(solution)/shard_map/ppermute | solution.py:53
  52.8 2.7 %collective-permute-start.8 = (bf16[64,2048]{1,0:T(8,128)(2,1)S(1)}, bf16[64,2048]{1,0:T(8,128)(2,1)S(1)}, u32[]{:S(2)}, u32[]{:S(2)}) collective-permute-start(bf16[64,2048]{1,0:T(8,128)(2,1)S(1)} %get-tuple-element.51), channel_id=1, source_target_pairs={{0,128},{1,33},{2,130},{3,35},{4,132},{5,37},{6,134},{7,39},{8,136... | collective-permute-start | bytes 786440 | tf_op jit(solution)/shard_map/ppermute | solution.py:53
  55.5 1.5 %collective-permute-start.9 = (bf16[64,2048]{1,0:T(8,128)(2,1)S(1)}, bf16[64,2048]{1,0:T(8,128)(2,1)S(1)}, u32[]{:S(2)}, u32[]{:S(2)}) collective-permute-start(bf16[64,2048]{1,0:T(8,128)(2,1)S(1)} %get-tuple-element.52), channel_id=1, source_target_pairs={{0,192},{1,49},{2,194},{3,51},{4,196},{5,53},{6,198},{7,55},{8,200... | collective-permute-start | bytes 786440 | tf_op jit(solution)/shard_map/ppermute | solution.py:53
  57.1 2.2 %back.1 = (bf16[576,1024]{1,0:T(8,128)(2,1)S(1)}, bf16[216,1024]{1,0:T(8,128)(2,1)S(1)}, bf16[72,1024]{1,0:T(8,128)(2,1)S(1)}, bf16[72,1024]{1,0:T(8,128)(2,1)S(1)}) custom-call(bf16[576,512]{1,0:T(8,128)(2,1)S(1)} %get-tuple-element.53.refs_12_.mixed, bf16[576,1536]{1,0:T(8,128)(2,1)S(1)} %get-tuple-element.54.gact, bf16[512,1536]{1,0:T(8,128)(2,1)S(1)} %copy-done, ...), custom_call_target="tpu_custom_call" | custom-call | flops 2000000000 | bytes 5000000 | tf_op jit(solution)/shard_map/back/pallas_call | solution.py:385
  59.3 2.8 %collective-permute-done.8 = bf16[64,2048]{1,0:T(8,128)(2,1)S(1)} collective-permute-done((bf16[64,2048]{1,0:T(8,128)(2,1)S(1)}, bf16[64,2048]{1,0:T(8,128)(2,1)S(1)}, u32[]{:S(2)}, u32[]{:S(2)}) %collective-permute-start.8) | collective-permute-done | bytes 262176 | tf_op jit(solution)/shard_map/ppermute | solution.py:53
  62.8 1.1 collective-permute-start.10
  63.9 1.7 %collective-permute-start.12 = (bf16[16,2048]{1,0:T(8,128)(2,1)S(1)}, bf16[16,2048]{1,0:T(8,128)(2,1)S(1)}, u32[]{:S(2)}, u32[]{:S(2)}) collective-permute-start(bf16[16,2048]{1,0:T(8,128)(2,1)S(1)} %get-tuple-element.88), channel_id=1, source_target_pairs={{0,48},{1,193},{2,50},{3,195},{4,52},{5,197},{6,54},{7,199},{8,56}... | collective-permute-start | bytes 196616 | tf_op jit(solution)/shard_map/ppermute | solution.py:53
  65.8 1.4 %collective-permute-done.10 = bf16[16,2048]{1,0:T(8,128)(2,1)S(1)} collective-permute-done((bf16[16,2048]{1,0:T(8,128)(2,1)S(1)}, bf16[16,2048]{1,0:T(8,128)(2,1)S(1)}, u32[]{:S(2)}, u32[]{:S(2)}) %collective-permute-start.10) | collective-permute-done | bytes 65568 | tf_op jit(solution)/shard_map/ppermute | solution.py:53
  67.5 2.7 %collective-permute-done.11 = bf16[16,2048]{1,0:T(8,128)(2,1)S(1)} collective-permute-done((bf16[16,2048]{1,0:T(8,128)(2,1)S(1)}, bf16[16,2048]{1,0:T(8,128)(2,1)S(1)}, u32[]{:S(2)}, u32[]{:S(2)}) %collective-permute-start.11) | collective-permute-done | bytes 65568 | tf_op jit(solution)/shard_map/ppermute | solution.py:53
  71.0 2.4 %collective-permute-done.13 = bf16[16,2048]{1,0:T(8,128)(2,1)S(1)} collective-permute-done((bf16[16,2048]{1,0:T(8,128)(2,1)S(1)}, bf16[16,2048]{1,0:T(8,128)(2,1)S(1)}, u32[]{:S(2)}, u32[]{:S(2)}) %collective-permute-start.13) | collective-permute-done | bytes 65568 | tf_op jit(solution)/shard_map/ppermute | solution.py:53
  73.5 4.7 %collective-permute-done.14 = bf16[16,2048]{1,0:T(8,128)(2,1)S(1)} collective-permute-done((bf16[16,2048]{1,0:T(8,128)(2,1)S(1)}, bf16[16,2048]{1,0:T(8,128)(2,1)S(1)}, u32[]{:S(2)}, u32[]{:S(2)}) %collective-permute-start.14) | collective-permute-done | bytes 65568 | tf_op jit(solution)/shard_map/ppermute | solution.py:53
  79.0 2.3 %collective-permute-start.22 = (bf16[216,1024]{1,0:T(8,128)(2,1)S(1)}, bf16[216,1024]{1,0:T(8,128)(2,1)S(1)}, u32[]{:S(2)}, u32[]{:S(2)}) collective-permute-start(bf16[216,1024]{1,0:T(8,128)(2,1)S(1)} %get-tuple-element.64), channel_id=1, source_target_pairs={{0,32},{1,33},{2,34},{3,35},{4,36},{5,37},{6,38},{7,39},{8,40},{9,... | collective-permute-start | bytes 1327112 | tf_op jit(solution)/shard_map/ppermute | solution.py:462
  81.3 2.6 %collective-permute-done.15 = bf16[16,2048]{1,0:T(8,128)(2,1)S(1)} collective-permute-done((bf16[16,2048]{1,0:T(8,128)(2,1)S(1)}, bf16[16,2048]{1,0:T(8,128)(2,1)S(1)}, u32[]{:S(2)}, u32[]{:S(2)}) %collective-permute-start.15) | collective-permute-done | bytes 65568 | tf_op jit(solution)/shard_map/ppermute | solution.py:53
  84.0 2.2 %collective-permute-start.17 = (bf16[16,2048]{1,0:T(8,128)(2,1)S(1)}, bf16[16,2048]{1,0:T(8,128)(2,1)S(1)}, u32[]{:S(2)}, u32[]{:S(2)}) collective-permute-start(bf16[16,2048]{1,0:T(8,128)(2,1)S(1)} %add_convert_fusion.5), channel_id=1, source_target_pairs={{0,32},{1,129},{2,34},{3,131},{4,36},{5,133},{6,38},{7,135},{8,40}... | collective-permute-start | bytes 196616 | tf_op jit(solution)/shard_map/ppermute | solution.py:53
  86.7 8.7 %collective-permute-start.23 = (bf16[72,1024]{1,0:T(8,128)(2,1)S(1)}, bf16[72,1024]{1,0:T(8,128)(2,1)S(1)}, u32[]{:S(2)}, u32[]{:S(2)}) collective-permute-start(bf16[72,1024]{1,0:T(8,128)(2,1)S(1)} %get-tuple-element.65), channel_id=1, source_target_pairs={{0,1},{1,2},{2,3},{3,4},{4,5},{5,6},{6,7},{7,8},{8,9},{9,10},{10,1... | collective-permute-start | bytes 442376 | tf_op jit(solution)/shard_map/ppermute | solution.py:463
  95.4 1.7 %collective-permute-start.24 = (bf16[72,1024]{1,0:T(8,128)(2,1)S(1)}, bf16[72,1024]{1,0:T(8,128)(2,1)S(1)}, u32[]{:S(2)}, u32[]{:S(2)}) collective-permute-start(bf16[72,1024]{1,0:T(8,128)(2,1)S(1)} %get-tuple-element.66), channel_id=1, source_target_pairs={{0,33},{1,34},{2,35},{3,36},{4,37},{5,38},{6,39},{7,40},{8,41},{9,... | collective-permute-start | bytes 442376 | tf_op jit(solution)/shard_map/ppermute | solution.py:464
  97.5 2.4 %collective-permute-start.20 = (bf16[64,2048]{1,0:T(8,128)(2,1)S(1)}, bf16[64,2048]{1,0:T(8,128)(2,1)S(1)}, u32[]{:S(2)}, u32[]{:S(2)}) collective-permute-start(bf16[64,2048]{1,0:T(8,128)(2,1)S(1)} %pad_maximum_fusion.refs_0_), channel_id=1, source_target_pairs={{0,128},{1,33},{2,130},{3,35},{4,132},{5,37},{6,134},{7,39},{8,136... | collective-permute-start | bytes 786440 | tf_op jit(solution)/shard_map/ppermute | solution.py:53
  100.0 1.8 %collective-permute-start.19 = (bf16[64,2048]{1,0:T(8,128)(2,1)S(1)}, bf16[64,2048]{1,0:T(8,128)(2,1)S(1)}, u32[]{:S(2)}, u32[]{:S(2)}) collective-permute-start(bf16[64,2048]{1,0:T(8,128)(2,1)S(1)} %pad_maximum_fusion.refs_0_), channel_id=1, source_target_pairs={{0,192},{1,49},{2,194},{3,51},{4,196},{5,53},{6,198},{7,55},{8,200... | collective-permute-start | bytes 786440 | tf_op jit(solution)/shard_map/ppermute | solution.py:53
  101.7 4.1 %collective-permute-done.24.r_diag = bf16[72,1024]{1,0:T(8,128)(2,1)S(1)} collective-permute-done((bf16[72,1024]{1,0:T(8,128)(2,1)S(1)}, bf16[72,1024]{1,0:T(8,128)(2,1)S(1)}, u32[]{:S(2)}, u32[]{:S(2)}) %collective-permute-start.24) | collective-permute-done | bytes 147488 | tf_op jit(solution)/shard_map/ppermute | solution.py:464
  106.3 3.2 %finish.1 = (bf16[576,512]{1,0:T(8,128)(2,1)}, bf16[576,512]{1,0:T(8,128)(2,1)}) custom-call(bf16[576,512]{1,0:T(8,128)(2,1)S(1)} %bitcast.11, bf16[576,512]{1,0:T(8,128)(2,1)S(1)} %bitcast.13, bf16[576,1024]{1,0:T(8,128)(2,1)S(1)} %get-tuple-element.63.both, bf16[216,1024]{1,0:T(8,128)(2,1)S(1)} %collective-permute-done.22.r_lat, ...), custom_call_target="tpu_custom_call" | custom-call | flops 2000000000 | bytes 8000000 | tf_op jit(solution)/shard_map/finish/pallas_call | solution.py:397
  109.5 1.9 %collective-permute-start.26 = (bf16[64,2048]{1,0:T(8,128)(2,1)S(1)}, bf16[64,2048]{1,0:T(8,128)(2,1)S(1)}, u32[]{:S(2)}, u32[]{:S(2)}) collective-permute-start(bf16[64,2048]{1,0:T(8,128)(2,1)S(1)} %collective-permute-done.19.refs_1_), channel_id=1, source_target_pairs={{0,1},{1,0},{2,3},{3,2},{4,5},{5,4},{6,7},{7,6},{8,9},{9,8},{10,11... | collective-permute-start | bytes 786440 | tf_op jit(solution)/shard_map/ppermute | solution.py:53
  111.9 2.6 %weights0.1 = (f32[512,1536]{1,0:T(8,128)}, f32[512,512]{1,0:T(8,128)}, f32[1,512]{1,0:T(1,128)S(1)}) custom-call(s32[4]{0:T(128)S(1)} %pad_add_fusion.place, bf16[64,2048]{1,0:T(8,128)(2,1)S(1)} %pad_maximum_fusion.refs_0_, bf16[64,2048]{1,0:T(8,128)(2,1)S(1)} %collective-permute-done.19.refs_1_, bf16[64,2048]{1,0:T(8,128)(2,1)S(1)} %collective-permute-done.20.refs_2_, ...), custom_call_target="tpu_custom_call" | custom-call | flops 10000000 | bytes 4000000 | tf_op jit(solution)/shard_map/weights0/pallas_call | solution.py:308
  114.5 2.8 %weights1.1 = (f32[512,1536]{1,0:T(8,128)}, f32[512,512]{1,0:T(8,128)}, f32[1,512]{1,0:T(1,128)}) custom-call(s32[4]{0:T(128)S(1)} %pad_add_fusion.place, bf16[64,2048]{1,0:T(8,128)(2,1)S(1)} %collective-permute-done.25.refs_0_, bf16[64,2048]{1,0:T(8,128)(2,1)S(1)} %collective-permute-done.26.refs_1_, ...), custom_call_target="tpu_custom_call", output_to_operand_aliasing={{0}: (8, {}), {1}: (9, {})} | custom-call | flops 10000000 | bytes 4000000 | tf_op jit(solution)/shard_map/weights1/pallas_call | solution.py:308
  (81 shorter events, 14.2 us)
Async XLA Ops:
  2.4 24.6 %collective-permute-start.1 = (bf16[72,512]{1,0:T(8,128)(2,1)}, bf16[72,512]{1,0:T(8,128)(2,1)S(1)}, u32[]{:S(2)}, u32[]{:S(2)}) collective-permute-start(bf16[72,512]{1,0:T(8,128)(2,1)} %reshape.48), channel_id=1, source_target_pairs={{0,31},{1,0},{2,1},{3,2},{4,3},{5,4},{6,5},{7,6},{8,7},{9,8},{10,9... | collective-permute-start | bytes 221192 | tf_op jit(solution)/shard_map/ppermute | solution.py:425
  6.3 21.3 %collective-permute-start.2 = (bf16[72,512]{1,0:T(8,128)(2,1)}, bf16[72,512]{1,0:T(8,128)(2,1)S(1)}, u32[]{:S(2)}, u32[]{:S(2)}) collective-permute-start(bf16[72,512]{1,0:T(8,128)(2,1)} %reshape.49), channel_id=1, source_target_pairs={{0,255},{1,224},{2,225},{3,226},{4,227},{5,228},{6,229},{7,230},{8... | collective-permute-start | bytes 221192 | tf_op jit(solution)/shard_map/ppermute | solution.py:426
  17.3 10.2 %collective-permute-start = (bf16[216,512]{1,0:T(8,128)(2,1)}, bf16[216,512]{1,0:T(8,128)(2,1)S(1)}, u32[]{:S(2)}, u32[]{:S(2)}) collective-permute-start(bf16[216,512]{1,0:T(8,128)(2,1)} %reshape.47), channel_id=1, source_target_pairs={{0,224},{1,225},{2,226},{3,227},{4,228},{5,229},{6,230},{7,231},{8... | collective-permute-start | bytes 663560 | tf_op jit(solution)/shard_map/ppermute | solution.py:424
  20.1 18.0 %collective-permute-start.4 = (bf16[72,512]{1,0:T(8,128)(2,1)}, bf16[72,512]{1,0:T(8,128)(2,1)S(1)}, u32[]{:S(2)}, u32[]{:S(2)}) collective-permute-start(bf16[72,512]{1,0:T(8,128)(2,1)} %reshape.53), channel_id=1, source_target_pairs={{0,31},{1,0},{2,1},{3,2},{4,3},{5,4},{6,5},{7,6},{8,7},{9,8},{10,9... | collective-permute-start | bytes 221192 | tf_op jit(solution)/shard_map/ppermute | solution.py:425
  20.8 17.4 %collective-permute-start.5 = (bf16[72,512]{1,0:T(8,128)(2,1)}, bf16[72,512]{1,0:T(8,128)(2,1)S(1)}, u32[]{:S(2)}, u32[]{:S(2)}) collective-permute-start(bf16[72,512]{1,0:T(8,128)(2,1)} %reshape.54), channel_id=1, source_target_pairs={{0,255},{1,224},{2,225},{3,226},{4,227},{5,228},{6,229},{7,230},{8... | collective-permute-start | bytes 221192 | tf_op jit(solution)/shard_map/ppermute | solution.py:426
  27.0 11.1 %collective-permute-start.3 = (bf16[216,512]{1,0:T(8,128)(2,1)}, bf16[216,512]{1,0:T(8,128)(2,1)S(1)}, u32[]{:S(2)}, u32[]{:S(2)}) collective-permute-start(bf16[216,512]{1,0:T(8,128)(2,1)} %reshape.52), channel_id=1, source_target_pairs={{0,224},{1,225},{2,226},{3,227},{4,228},{5,229},{6,230},{7,231},{8... | collective-permute-start | bytes 663560 | tf_op jit(solution)/shard_map/ppermute | solution.py:424
  49.1 2.7 %collective-permute-start.6 = (bf16[256,2048]{1,0:T(8,128)(2,1)S(1)}, bf16[256,2048]{1,0:T(8,128)(2,1)S(1)}, u32[]{:S(2)}, u32[]{:S(2)}) collective-permute-start(bf16[256,2048]{1,0:T(8,128)(2,1)S(1)} %get-tuple-element.48), channel_id=1, source_target_pairs={{0,1},{1,0},{2,3},{3,2},{4,5},{5,4},{6,7},{7,6},{8,9},{9,8},{10,11... | collective-permute-start | bytes 3145736 | tf_op jit(solution)/shard_map/ppermute | solution.py:53
  52.3 7.0 %collective-permute-start.7 = (bf16[64,2048]{1,0:T(8,128)(2,1)S(1)}, bf16[64,2048]{1,0:T(8,128)(2,1)S(1)}, u32[]{:S(2)}, u32[]{:S(2)}) collective-permute-start(bf16[64,2048]{1,0:T(8,128)(2,1)S(1)} %get-tuple-element.50), channel_id=1, source_target_pairs={{0,64},{1,17},{2,66},{3,19},{4,68},{5,21},{6,70},{7,23},{8,72},{9,... | collective-permute-start | bytes 786440 | tf_op jit(solution)/shard_map/ppermute | solution.py:53
  52.8 9.3 %collective-permute-start.8 = (bf16[64,2048]{1,0:T(8,128)(2,1)S(1)}, bf16[64,2048]{1,0:T(8,128)(2,1)S(1)}, u32[]{:S(2)}, u32[]{:S(2)}) collective-permute-start(bf16[64,2048]{1,0:T(8,128)(2,1)S(1)} %get-tuple-element.51), channel_id=1, source_target_pairs={{0,128},{1,33},{2,130},{3,35},{4,132},{5,37},{6,134},{7,39},{8,136... | collective-permute-start | bytes 786440 | tf_op jit(solution)/shard_map/ppermute | solution.py:53
  55.5 7.1 %collective-permute-start.9 = (bf16[64,2048]{1,0:T(8,128)(2,1)S(1)}, bf16[64,2048]{1,0:T(8,128)(2,1)S(1)}, u32[]{:S(2)}, u32[]{:S(2)}) collective-permute-start(bf16[64,2048]{1,0:T(8,128)(2,1)S(1)} %get-tuple-element.52), channel_id=1, source_target_pairs={{0,192},{1,49},{2,194},{3,51},{4,196},{5,53},{6,198},{7,55},{8,200... | collective-permute-start | bytes 786440 | tf_op jit(solution)/shard_map/ppermute | solution.py:53
  59.2 47.0 %copy-start.7 = (bf16[576,216]{1,0:T(8,128)(2,1)S(1)}, bf16[576,216]{1,0:T(8,128)(2,1)}, u32[]{:S(2)}) copy-start(bf16[576,216]{1,0:T(8,128)(2,1)} %constant.68.clone.s_lat) | copy-start | bytes 746500
  59.3 47.0 %copy-start.10 = (bf16[576,72]{1,0:T(8,128)(2,1)S(1)}, bf16[576,72]{1,0:T(8,128)(2,1)}, u32[]{:S(2)}) copy-start(bf16[576,72]{1,0:T(8,128)(2,1)} %constant.70.clone.s_diag) | copy-start | bytes 248836
  59.3 47.0 %copy-start.11 = (bf16[576,72]{1,0:T(8,128)(2,1)S(1)}, bf16[576,72]{1,0:T(8,128)(2,1)}, u32[]{:S(2)}) copy-start(bf16[576,72]{1,0:T(8,128)(2,1)} %constant.69.clone.s_lon) | copy-start | bytes 248836
  62.8 4.4 %collective-permute-start.10 = (bf16[16,2048]{1,0:T(8,128)(2,1)S(1)}, bf16[16,2048]{1,0:T(8,128)(2,1)S(1)}, u32[]{:S(2)}, u32[]{:S(2)}) collective-permute-start(bf16[16,2048]{1,0:T(8,128)(2,1)S(1)} %get-tuple-element.87), channel_id=1, source_target_pairs={{0,16},{1,65},{2,18},{3,67},{4,20},{5,69},{6,22},{7,71},{8,24},{9,... | collective-permute-start | bytes 196616 | tf_op jit(solution)/shard_map/ppermute | solution.py:53
  63.9 3.6 %collective-permute-start.12 = (bf16[16,2048]{1,0:T(8,128)(2,1)S(1)}, bf16[16,2048]{1,0:T(8,128)(2,1)S(1)}, u32[]{:S(2)}, u32[]{:S(2)}) collective-permute-start(bf16[16,2048]{1,0:T(8,128)(2,1)S(1)} %get-tuple-element.88), channel_id=1, source_target_pairs={{0,48},{1,193},{2,50},{3,195},{4,52},{5,197},{6,54},{7,199},{8,56}... | collective-permute-start | bytes 196616 | tf_op jit(solution)/shard_map/ppermute | solution.py:53
  65.6 4.6 %collective-permute-start.11 = (bf16[16,2048]{1,0:T(8,128)(2,1)S(1)}, bf16[16,2048]{1,0:T(8,128)(2,1)S(1)}, u32[]{:S(2)}, u32[]{:S(2)}) collective-permute-start(bf16[16,2048]{1,0:T(8,128)(2,1)S(1)} %get-tuple-element.89), channel_id=1, source_target_pairs={{0,32},{1,129},{2,34},{3,131},{4,36},{5,133},{6,38},{7,135},{8,40}... | collective-permute-start | bytes 196616 | tf_op jit(solution)/shard_map/ppermute | solution.py:53
  70.2 3.2 %collective-permute-start.13 = (bf16[16,2048]{1,0:T(8,128)(2,1)S(1)}, bf16[16,2048]{1,0:T(8,128)(2,1)S(1)}, u32[]{:S(2)}, u32[]{:S(2)}) collective-permute-start(bf16[16,2048]{1,0:T(8,128)(2,1)S(1)} %add_convert_fusion.8), channel_id=1, source_target_pairs={{0,2},{1,3},{2,0},{3,1},{4,6},{5,7},{6,4},{7,5},{8,10},{9,11},{10,... | collective-permute-start | bytes 196616 | tf_op jit(solution)/shard_map/ppermute | solution.py:53
  73.4 4.8 %collective-permute-start.14 = (bf16[16,2048]{1,0:T(8,128)(2,1)S(1)}, bf16[16,2048]{1,0:T(8,128)(2,1)S(1)}, u32[]{:S(2)}, u32[]{:S(2)}) collective-permute-start(bf16[16,2048]{1,0:T(8,128)(2,1)S(1)} %add_convert_fusion.7), channel_id=1, source_target_pairs={{0,4},{1,5},{2,6},{3,7},{4,0},{5,1},{6,2},{7,3},{8,12},{9,13},{10,... | collective-permute-start | bytes 196616 | tf_op jit(solution)/shard_map/ppermute | solution.py:53
  78.3 5.6 %collective-permute-start.15 = (bf16[16,2048]{1,0:T(8,128)(2,1)S(1)}, bf16[16,2048]{1,0:T(8,128)(2,1)S(1)}, u32[]{:S(2)}, u32[]{:S(2)}) collective-permute-start(bf16[16,2048]{1,0:T(8,128)(2,1)S(1)} %add_convert_fusion.6), channel_id=1, source_target_pairs={{0,12},{1,13},{2,14},{3,15},{4,8},{5,9},{6,10},{7,11},{8,4},{9,5},... | collective-permute-start | bytes 196616 | tf_op jit(solution)/shard_map/ppermute | solution.py:53
  79.0 27.3 %collective-permute-start.22 = (bf16[216,1024]{1,0:T(8,128)(2,1)S(1)}, bf16[216,1024]{1,0:T(8,128)(2,1)S(1)}, u32[]{:S(2)}, u32[]{:S(2)}) collective-permute-start(bf16[216,1024]{1,0:T(8,128)(2,1)S(1)} %get-tuple-element.64), channel_id=1, source_target_pairs={{0,32},{1,33},{2,34},{3,35},{4,36},{5,37},{6,38},{7,39},{8,40},{9,... | collective-permute-start | bytes 1327112 | tf_op jit(solution)/shard_map/ppermute | solution.py:462
  83.9 11.4 %collective-permute-start.18 = (bf16[16,2048]{1,0:T(8,128)(2,1)S(1)}, bf16[16,2048]{1,0:T(8,128)(2,1)S(1)}, u32[]{:S(2)}, u32[]{:S(2)}) collective-permute-start(bf16[16,2048]{1,0:T(8,128)(2,1)S(1)} %add_convert_fusion.5), channel_id=1, source_target_pairs={{0,16},{1,65},{2,18},{3,67},{4,20},{5,69},{6,22},{7,71},{8,24},{9,... | collective-permute-start | bytes 196616 | tf_op jit(solution)/shard_map/ppermute | solution.py:53
  84.0 13.0 %collective-permute-start.17 = (bf16[16,2048]{1,0:T(8,128)(2,1)S(1)}, bf16[16,2048]{1,0:T(8,128)(2,1)S(1)}, u32[]{:S(2)}, u32[]{:S(2)}) collective-permute-start(bf16[16,2048]{1,0:T(8,128)(2,1)S(1)} %add_convert_fusion.5), channel_id=1, source_target_pairs={{0,32},{1,129},{2,34},{3,131},{4,36},{5,133},{6,38},{7,135},{8,40}... | collective-permute-start | bytes 196616 | tf_op jit(solution)/shard_map/ppermute | solution.py:53
  86.2 10.8 %collective-permute-start.16 = (bf16[16,2048]{1,0:T(8,128)(2,1)S(1)}, bf16[16,2048]{1,0:T(8,128)(2,1)S(1)}, u32[]{:S(2)}, u32[]{:S(2)}) collective-permute-start(bf16[16,2048]{1,0:T(8,128)(2,1)S(1)} %add_convert_fusion.5), channel_id=1, source_target_pairs={{0,48},{1,193},{2,50},{3,195},{4,52},{5,197},{6,54},{7,199},{8,56}... | collective-permute-start | bytes 196616 | tf_op jit(solution)/shard_map/ppermute | solution.py:53
  86.7 13.3 %collective-permute-start.23 = (bf16[72,1024]{1,0:T(8,128)(2,1)S(1)}, bf16[72,1024]{1,0:T(8,128)(2,1)S(1)}, u32[]{:S(2)}, u32[]{:S(2)}) collective-permute-start(bf16[72,1024]{1,0:T(8,128)(2,1)S(1)} %get-tuple-element.65), channel_id=1, source_target_pairs={{0,1},{1,2},{2,3},{3,4},{4,5},{5,6},{6,7},{7,8},{8,9},{9,10},{10,1... | collective-permute-start | bytes 442376 | tf_op jit(solution)/shard_map/ppermute | solution.py:463
  95.4 10.5 %collective-permute-start.24 = (bf16[72,1024]{1,0:T(8,128)(2,1)S(1)}, bf16[72,1024]{1,0:T(8,128)(2,1)S(1)}, u32[]{:S(2)}, u32[]{:S(2)}) collective-permute-start(bf16[72,1024]{1,0:T(8,128)(2,1)S(1)} %get-tuple-element.66), channel_id=1, source_target_pairs={{0,33},{1,34},{2,35},{3,36},{4,37},{5,38},{6,39},{7,40},{8,41},{9,... | collective-permute-start | bytes 442376 | tf_op jit(solution)/shard_map/ppermute | solution.py:464
  97.1 12.4 %collective-permute-start.21 = (bf16[64,2048]{1,0:T(8,128)(2,1)S(1)}, bf16[64,2048]{1,0:T(8,128)(2,1)S(1)}, u32[]{:S(2)}, u32[]{:S(2)}) collective-permute-start(bf16[64,2048]{1,0:T(8,128)(2,1)S(1)} %pad_maximum_fusion.refs_0_), channel_id=1, source_target_pairs={{0,64},{1,17},{2,66},{3,19},{4,68},{5,21},{6,70},{7,23},{8,72},{9,... | collective-permute-start | bytes 786440 | tf_op jit(solution)/shard_map/ppermute | solution.py:53
  97.5 12.0 %collective-permute-start.20 = (bf16[64,2048]{1,0:T(8,128)(2,1)S(1)}, bf16[64,2048]{1,0:T(8,128)(2,1)S(1)}, u32[]{:S(2)}, u32[]{:S(2)}) collective-permute-start(bf16[64,2048]{1,0:T(8,128)(2,1)S(1)} %pad_maximum_fusion.refs_0_), channel_id=1, source_target_pairs={{0,128},{1,33},{2,130},{3,35},{4,132},{5,37},{6,134},{7,39},{8,136... | collective-permute-start | bytes 786440 | tf_op jit(solution)/shard_map/ppermute | solution.py:53
  100.0 9.5 %collective-permute-start.19 = (bf16[64,2048]{1,0:T(8,128)(2,1)S(1)}, bf16[64,2048]{1,0:T(8,128)(2,1)S(1)}, u32[]{:S(2)}, u32[]{:S(2)}) collective-permute-start(bf16[64,2048]{1,0:T(8,128)(2,1)S(1)} %pad_maximum_fusion.refs_0_), channel_id=1, source_target_pairs={{0,192},{1,49},{2,194},{3,51},{4,196},{5,53},{6,198},{7,55},{8,200... | collective-permute-start | bytes 786440 | tf_op jit(solution)/shard_map/ppermute | solution.py:53
  105.8 8.7 %collective-permute-start.25 = (bf16[64,2048]{1,0:T(8,128)(2,1)S(1)}, bf16[64,2048]{1,0:T(8,128)(2,1)S(1)}, u32[]{:S(2)}, u32[]{:S(2)}) collective-permute-start(bf16[64,2048]{1,0:T(8,128)(2,1)S(1)} %pad_maximum_fusion.refs_0_), channel_id=1, source_target_pairs={{0,1},{1,0},{2,3},{3,2},{4,5},{5,4},{6,7},{7,6},{8,9},{9,8},{10,11... | collective-permute-start | bytes 786440 | tf_op jit(solution)/shard_map/ppermute | solution.py:53
  109.5 5.0 %collective-permute-start.26 = (bf16[64,2048]{1,0:T(8,128)(2,1)S(1)}, bf16[64,2048]{1,0:T(8,128)(2,1)S(1)}, u32[]{:S(2)}, u32[]{:S(2)}) collective-permute-start(bf16[64,2048]{1,0:T(8,128)(2,1)S(1)} %collective-permute-done.19.refs_1_), channel_id=1, source_target_pairs={{0,1},{1,0},{2,3},{3,2},{4,5},{5,4},{6,7},{7,6},{8,9},{9,8},{10,11... | collective-permute-start | bytes 786440 | tf_op jit(solution)/shard_map/ppermute | solution.py:53
  111.4 3.1 %collective-permute-start.27 = (bf16[64,2048]{1,0:T(8,128)(2,1)S(1)}, bf16[64,2048]{1,0:T(8,128)(2,1)S(1)}, u32[]{:S(2)}, u32[]{:S(2)}) collective-permute-start(bf16[64,2048]{1,0:T(8,128)(2,1)S(1)} %collective-permute-done.20.refs_2_), channel_id=1, source_target_pairs={{0,1},{1,0},{2,3},{3,2},{4,5},{5,4},{6,7},{7,6},{8,9},{9,8},{10,11... | collective-permute-start | bytes 786440 | tf_op jit(solution)/shard_map/ppermute | solution.py:53
  111.4 3.1 %collective-permute-start.28 = (bf16[64,2048]{1,0:T(8,128)(2,1)S(1)}, bf16[64,2048]{1,0:T(8,128)(2,1)S(1)}, u32[]{:S(2)}, u32[]{:S(2)}) collective-permute-start(bf16[64,2048]{1,0:T(8,128)(2,1)S(1)} %collective-permute-done.21.refs_3_), channel_id=1, source_target_pairs={{0,1},{1,0},{2,3},{3,2},{4,5},{5,4},{6,7},{7,6},{8,9},{9,8},{10,11... | collective-permute-start | bytes 786440 | tf_op jit(solution)/shard_map/ppermute | solution.py:53
  (12 other events, 154.0 us)

commit v3 on v2

--- a/solution.py
+++ b/solution.py
@@ -117,6 +117,13 @@
     return centred * rstd, rstd
 
 
+def pack_kernel(x, select, lat, lon, diag):
+    rows = dot(select[...], x[...])
+    lat[...] = rows[:216].astype(bf16)
+    lon[...] = rows[216:288].astype(bf16)
+    diag[...] = rows[288:].astype(bf16)
+
+
 def pairs_mask():
     row = lax.broadcasted_iota(jnp.int32, (2 * SPAN, 128), 0)
     lane = lax.broadcasted_iota(jnp.int32, (2 * SPAN, 128), 1)
@@ -256,69 +263,57 @@
 def weights_kernel(side, place, *refs):
     pieces, refs = refs[:4], refs[4:]
     if side == 0:
-        w_ref, g_qkv, g_out, g_total = refs
+        w_ref, g_qkv, g_out, g_total, buf_q, buf_o, sem = refs
     else:
-        w_ref, before, gain, _, _, g_qkv, g_out, g_total = refs
+        w_ref, before, gain, _, _, g_qkv, g_out, g_total, buf_q, buf_o, sem = refs
     y, x, c = place[1], place[2], place[3]
-    step = pl.program_id(0)
     core = c if side == 0 else 1 - c
     d1 = jnp.where(core == 0, y, x)
     d2 = jnp.where(core == 0, x, y)
-
-    @pl.when(step == 0)
-    def _():
-        g_total[...] = jnp.zeros_like(g_total) if side == 0 else before[...]
-
+    bands = [pl.multiple_of(core * 256 + lax.rem(d1 + i, 4) * 64, 64) for i in range(4)]
+    copies = []
     for i in range(4):
-
-        @pl.when(step == i)
-        def _(i=i):
-            for s2 in range(4):
-                at = pl.ds(pl.multiple_of(lax.rem(d2 + s2, 4) * 16, 16), 16)
-                block = pieces[i][pl.ds(s2 * 16, 16), :].astype(f32)
-                g_qkv[at, :] = block[:, : 3 * D]
-                g_out[at, :] = block[:, 3 * D :]
-
-    row = core * 256 + lax.rem(d1 + step, 4) * 64
+        for s2 in range(4):
+            at = pl.ds(pl.multiple_of(lax.rem(d2 + s2, 4) * 16, 16), 16)
+            block = pieces[i][pl.ds(s2 * 16, 16), :].astype(f32)
+            buf_q[i, at, :] = block[:, : 3 * D]
+            buf_o[i, at, :] = block[:, 3 * D :]
+        for k, (src, dst) in enumerate(((buf_q, g_qkv), (buf_o, g_out))):
+            copy = pltpu.make_async_copy(src.at[i], dst.at[pl.ds(bands[i], 64)], sem.at[i, k])
+            copy.start()
+            copies.append(copy)
+    total = jnp.zeros((1, D), f32) if side == 0 else before[...]
     lane = lax.broadcasted_iota(jnp.int32, (64, D), 1)
-    here = lax.broadcasted_iota(jnp.int32, (64, D), 0) + row
-    sums = jnp.sum(g_qkv[...] * w_ref[...].astype(f32), axis=1, keepdims=True)
-    g_total[...] += jnp.sum(jnp.where(lane == here, sums, 0.0), axis=0, keepdims=True)
-
-    if side == 1:
-
-        @pl.when(step == 3)
-        def _():
-            g_total[...] = g_total[...] / gain[...]
-
-
-def band(side, step, place):
-    y, x, c = place[1], place[2], place[3]
-    core = c if side == 0 else 1 - c
-    d1 = jnp.where(core == 0, y, x)
-    return core * 4 + lax.rem(d1 + step, 4), 0
+    local = lax.broadcasted_iota(jnp.int32, (64, D), 0)
+    for i in range(4):
+        w = w_ref[pl.ds(bands[i], 64), :].astype(f32)
+        sums = jnp.sum(buf_q[i] * w, axis=1, keepdims=True)
+        spread = jnp.where(lane == local + bands[i], sums, 0.0)
+        total = total + jnp.sum(spread, axis=0, keepdims=True)
+    g_total[...] = total if side == 0 else total / gain[...]
+    for copy in copies:
+        copy.wait()
 
 
 def to_weights(side, place, pieces, qkv_weight, *more):
-    at = functools.partial(band, side)
-    whole = pl.BlockSpec((64, 4 * D), lambda i, place: (0, 0))
-    row = pl.BlockSpec((1, D), lambda i, place: (0, 0))
+    inside = pl.BlockSpec(memory_space=pltpu.VMEM)
     anywhere = pl.BlockSpec(memory_space=pl.ANY)
-    extra = [] if side == 0 else [row, row, anywhere, anywhere]
+    extra = [] if side == 0 else [inside, inside, anywhere, anywhere]
     return pl.pallas_call(
         functools.partial(weights_kernel, side),
         out_shape=[shape(D, 3 * D, dtype=f32), shape(D, D, dtype=f32), shape(1, D, dtype=f32)],
-        grid_spec=pltpu.PrefetchScalarGridSpec(
-            num_scalar_prefetch=1,
-            grid=(4,),
-            in_specs=[whole] * 4 + [pl.BlockSpec((64, 3 * D), at)] + extra,
-            out_specs=[pl.BlockSpec((64, 3 * D), at), pl.BlockSpec((64, D), at), row],
-        ),
+        in_specs=spec(5, True) + extra,
+        out_specs=[anywhere, anywhere, inside],
+        scratch_shapes=[
+            pltpu.VMEM((4, 64, 3 * D), f32),
+            pltpu.VMEM((4, 64, D), f32),
+            pltpu.SemaphoreType.DMA((4, 2)),
+        ],
         input_output_aliases={} if side == 0 else {8: 0, 9: 1},
         compiler_params=params(),
         cost_estimate=cost(10**7, 4 * 10**6),
         name="weights" + str(side),
-    )(place, *vms(*pieces), qkv_weight, *more)
+    )(place, *vms(*pieces), vm(qkv_weight), *more)
 
 
 def params():
@@ -416,10 +411,16 @@
     return lax.optimization_barrier(x)
 
 
-def halo(field):
-    lat = field[:, :3, 6:].reshape(-1, D)
-    lon = field[:, 3:, :6].reshape(-1, D)
-    diag = field[:, :3, :6].reshape(-1, D)
+def halo(field, select):
+    lat, lon, diag = pl.pallas_call(
+        pack_kernel,
+        out_shape=[vshape(216, D), vshape(72, D), vshape(72, D)],
+        in_specs=spec(2),
+        out_specs=spec(3),
+        compiler_params=params(),
+        cost_estimate=cost(2 * 10**8, 10**6),
+        name="pack",
+    )(field, select)
     return (
         lax.ppermute(lat, BOTH, shifted(-1, 0)),
         lax.ppermute(lon, BOTH, shifted(0, -1)),
@@ -441,8 +442,9 @@
     p_loc, p_lat, p_lon, p_diag = [jnp.asarray(t, bf16) for t in gather_tables()]
     s_lat, s_lon, s_diag = [jnp.asarray(t, bf16) for t in scatter_tables()]
     f_loc, c_loc = fields.reshape(TOK, D), cotangent.reshape(TOK, D)
-    f_halo = halo(fields)
-    c_halo = halo(cotangent)
+    select = jnp.asarray(np.concatenate(scatter_tables(), axis=1).T, bf16)
+    f_halo = halo(f_loc, select)
+    c_halo = halo(c_loc, select)
 
     tables = vms(p_loc, p_lat, p_lon, p_diag)
     normed, qkv, probs, mixed = to_forward(place, (f_loc, *f_halo), tables, gain_row, qkv_weight)
@@ -462,8 +464,13 @@
     r_lat = lax.ppermute(to_lat, BOTH, shifted(1, 0))
     r_lon = lax.ppermute(to_lon, BOTH, shifted(0, 1))
     r_diag = lax.ppermute(to_diag, BOTH, shifted(1, 1))
-    for k in (1, 2, 6):
-        part = add(part, send(part, flip_z(k)))
+    recv = send(part, flip_z(1))
+    recv, r_lon = tied((recv, r_lon))
+    part = add(part, recv)
+    recv = send(part, flip_z(2))
+    recv, r_diag = tied((recv, r_diag))
+    part = add(part, recv)
+    part = add(part, send(part, flip_z(6)))
 
     block = jnp.concatenate([part] + [send(part, second_axis(4 - s)) for s in (1, 2, 3)], axis=0)
     mine = [send(block, first_axis(4 - s)) for s in (1, 2, 3)]

time: 118 us -> 115 us (0.975)
  local copies, waits for them, and re-layouts: 12.6 us -> 9.99 us
  starting transfers between devices: 49.6 us -> 47.4 us
    unnamed x30 -> x42, local copies, waits for them, and re-layouts: 3.05 us -> 9.97 us
    reshape x6 -> x0, local copies, waits for them, and re-layouts: 6.04 us -> none  [the longest x2 2.48 us: halo(): lat = field[:, :3, 6:].reshape(-1, D)]
    ppermute x2, starting transfers between devices: 1.06 us -> 6.64 us  [halo(): lax.ppermute(lat, BOTH, shifted(-1, 0))]
    ppermute x1, starting transfers between devices: 8.67 us -> 3.29 us  [on_device(): r_lon = lax.ppermute(to_lon, BOTH, shifted(0, 1))]
    slice x4 -> x0, local copies, waits for them, and re-layouts: 3.49 us -> none  [the longest x2 1.82 us: halo(): lat = field[:, :3, 6:].reshape(-1, D)]
    ppermute x2, starting transfers between devices: 12.9 us -> 9.68 us  [halo(): lax.ppermute(diag, BOTH, shifted(-1, -1))]
    ppermute x1, starting transfers between devices: 1.69 us -> 4.23 us  [on_device(): r_diag = lax.ppermute(to_diag, BOTH, shifted(1, 1))]
    ppermute x2, starting transfers between devices: 3.24 us -> 1.04 us  [halo(): lax.ppermute(lon, BOTH, shifted(0, -1))]
  transfers between devices with their start and end apart: 29 -> 29, of which waited for: 10 -> 11; matrix products, arithmetic and copies ran while one was open for 7% -> 0% of each run, Pallas kernels for 13% -> 13%
where the time goes in v3:
time: 115 us; the launch traced here: 114 us
  starting transfers between devices  47.4 us (41%)
  Pallas kernels  29.3 us (25%)
  waiting for transfers between devices  25.2 us (22%)
  local copies, waits for them, and re-layouts  9.99 us (9%)
  between operations  1.17 us (1%)
    ppermute x20, waiting for transfers between devices, send(): return lax.ppermute(x, BOTH, route(step))  21.3 us
    ppermute x20, starting transfers between devices, send(): return lax.ppermute(x, BOTH, route(step))  20.8 us
    pallas_call x1, Pallas kernels, to_backward(): pl.pallas_call(backward_kernel, out_shape=[vshape(TOK, 3 * D), vshape(256...  10.9 us
    unnamed x42, local copies, waits for them, and re-layouts  9.97 us
    ppermute x2, starting transfers between devices, halo(): lax.ppermute(diag, BOTH, shifted(-1, -1))  9.68 us
    pallas_call x1, Pallas kernels, to_forward(): pl.pallas_call(forward_kernel, out_shape=[vshape(TOK, D), vshape(TOK, 3 *...  7.55 us
    ppermute x2, starting transfers between devices, halo(): lax.ppermute(lat, BOTH, shifted(-1, 0))  6.64 us
    pallas_call x2, Pallas kernels, to_weights(): pl.pallas_call(functools.partial(weights_kernel, side), out_shape=[shape(...  4.51 us
  transfers between devices with their start and end apart: 29, of which 11 were waited for; matrix products, arithmetic and copies ran while one was open for 0% of the time, Pallas kernels for 13%

profile of v3, /device:TPU:1, one launch (start us, length us, event | category | flops | bytes accessed | tf_op | source)
XLA Modules:
  0.0 113.7 jit_solution(9867200634780291819)
XLA Ops:
  0.7 1.1 copy-done.1
  1.8 1.1 copy-done.3
  3.3 6.1 %collective-permute-start = (bf16[216,512]{1,0:T(8,128)(2,1)S(1)}, bf16[216,512]{1,0:T(8,128)(2,1)S(1)}, u32[]{:S(2)}, u32[]{:S(2)}) collective-permute-start(bf16[216,512]{1,0:T(8,128)(2,1)S(1)} %get-tuple-element.52), channel_id=1, source_target_pairs={{0,224},{1,225},{2,226},{3,227},{4,228},{5,229},{6,230},{7,231},{8... | collective-permute-start | bytes 663560 | tf_op jit(solution)/shard_map/ppermute | solution.py:425
  10.4 6.7 %collective-permute-start.2 = (bf16[72,512]{1,0:T(8,128)(2,1)S(1)}, bf16[72,512]{1,0:T(8,128)(2,1)S(1)}, u32[]{:S(2)}, u32[]{:S(2)}) collective-permute-start(bf16[72,512]{1,0:T(8,128)(2,1)S(1)} %get-tuple-element.54), channel_id=1, source_target_pairs={{0,255},{1,224},{2,225},{3,226},{4,227},{5,228},{6,229},{7,230},{8... | collective-permute-start | bytes 221192 | tf_op jit(solution)/shard_map/ppermute | solution.py:427
  18.0 1.1 copy-done.6
  19.7 3.0 %collective-permute-start.5 = (bf16[72,512]{1,0:T(8,128)(2,1)S(1)}, bf16[72,512]{1,0:T(8,128)(2,1)S(1)}, u32[]{:S(2)}, u32[]{:S(2)}) collective-permute-start(bf16[72,512]{1,0:T(8,128)(2,1)S(1)} %get-tuple-element.58), channel_id=1, source_target_pairs={{0,255},{1,224},{2,225},{3,226},{4,227},{5,228},{6,229},{7,230},{8... | collective-permute-start | bytes 221192 | tf_op jit(solution)/shard_map/ppermute | solution.py:427
  25.1 1.1 copy-done.11
  29.0 7.6 %forward.1 = (bf16[576,512]{1,0:T(8,128)(2,1)S(1)}, bf16[576,1536]{1,0:T(8,128)(2,1)S(1)}, bf16[4608,144]{1,0:T(8,128)(2,1)S(1)}, bf16[576,512]{1,0:T(8,128)(2,1)S(1)}) custom-call(s32[4]{0:T(128)S(1)} %pad_add_fusion.place, bf16[576,512]{1,0:T(8,128)(2,1)S(1)} %bitcast.11, bf16[216,512]{1,0:T(8,128)(2,1)S(1)} %collective-permute-done.refs_1_, ...), custom_call_target="tpu_custom_call" | custom-call | flops 3000000000 | bytes 10000000 | tf_op jit(solution)/shard_map/forward/pallas_call | solution.py:349
  36.6 10.9 %backward.1 = (bf16[576,1536]{1,0:T(8,128)(2,1)S(1)}, bf16[256,2048]{1,0:T(8,128)(2,1)S(1)}, bf16[256,2048]{1,0:T(8,128)(2,1)S(1)}) custom-call(s32[4]{0:T(128)S(1)} %pad_add_fusion.place, bf16[576,512]{1,0:T(8,128)(2,1)S(1)} %bitcast.14, bf16[216,512]{1,0:T(8,128)(2,1)S(1)} %collective-permute-done.3.refs_1_, ...), custom_call_target="tpu_custom_call" | custom-call | flops 5000000000 | bytes 10000000 | tf_op jit(solution)/shard_map/backward/pallas_call | solution.py:363
  47.7 2.6 %collective-permute-done.6 = bf16[256,2048]{1,0:T(8,128)(2,1)S(1)} collective-permute-done((bf16[256,2048]{1,0:T(8,128)(2,1)S(1)}, bf16[256,2048]{1,0:T(8,128)(2,1)S(1)}, u32[]{:S(2)}, u32[]{:S(2)}) %collective-permute-start.6) | collective-permute-done | bytes 1048608 | tf_op jit(solution)/shard_map/ppermute | solution.py:53
  51.2 2.7 %collective-permute-start.8 = (bf16[64,2048]{1,0:T(8,128)(2,1)S(1)}, bf16[64,2048]{1,0:T(8,128)(2,1)S(1)}, u32[]{:S(2)}, u32[]{:S(2)}) collective-permute-start(bf16[64,2048]{1,0:T(8,128)(2,1)S(1)} %get-tuple-element.67), channel_id=1, source_target_pairs={{0,128},{1,33},{2,130},{3,35},{4,132},{5,37},{6,134},{7,39},{8,136... | collective-permute-start | bytes 786440 | tf_op jit(solution)/shard_map/ppermute | solution.py:53
  54.0 1.5 %collective-permute-start.9 = (bf16[64,2048]{1,0:T(8,128)(2,1)S(1)}, bf16[64,2048]{1,0:T(8,128)(2,1)S(1)}, u32[]{:S(2)}, u32[]{:S(2)}) collective-permute-start(bf16[64,2048]{1,0:T(8,128)(2,1)S(1)} %get-tuple-element.68), channel_id=1, source_target_pairs={{0,192},{1,49},{2,194},{3,51},{4,196},{5,53},{6,198},{7,55},{8,200... | collective-permute-start | bytes 786440 | tf_op jit(solution)/shard_map/ppermute | solution.py:53
  55.5 2.2 %back.1 = (bf16[576,1024]{1,0:T(8,128)(2,1)S(1)}, bf16[216,1024]{1,0:T(8,128)(2,1)S(1)}, bf16[72,1024]{1,0:T(8,128)(2,1)S(1)}, bf16[72,1024]{1,0:T(8,128)(2,1)S(1)}) custom-call(bf16[576,512]{1,0:T(8,128)(2,1)S(1)} %get-tuple-element.69.refs_12_.mixed, bf16[576,1536]{1,0:T(8,128)(2,1)S(1)} %get-tuple-element.70.gact, bf16[512,1536]{1,0:T(8,128)(2,1)S(1)} %copy-done, ...), custom_call_target="tpu_custom_call" | custom-call | flops 2000000000 | bytes 5000000 | tf_op jit(solution)/shard_map/back/pallas_call | solution.py:380
  57.8 2.8 %collective-permute-done.8 = bf16[64,2048]{1,0:T(8,128)(2,1)S(1)} collective-permute-done((bf16[64,2048]{1,0:T(8,128)(2,1)S(1)}, bf16[64,2048]{1,0:T(8,128)(2,1)S(1)}, u32[]{:S(2)}, u32[]{:S(2)}) %collective-permute-start.8) | collective-permute-done | bytes 262176 | tf_op jit(solution)/shard_map/ppermute | solution.py:53
  61.3 1.1 collective-permute-start.10
  62.3 1.7 %collective-permute-start.12 = (bf16[16,2048]{1,0:T(8,128)(2,1)S(1)}, bf16[16,2048]{1,0:T(8,128)(2,1)S(1)}, u32[]{:S(2)}, u32[]{:S(2)}) collective-permute-start(bf16[16,2048]{1,0:T(8,128)(2,1)S(1)} %get-tuple-element.104), channel_id=1, source_target_pairs={{0,48},{1,193},{2,50},{3,195},{4,52},{5,197},{6,54},{7,199},{8,56}... | collective-permute-start | bytes 196616 | tf_op jit(solution)/shard_map/ppermute | solution.py:53
  64.2 3.3 %collective-permute-start.14 = (bf16[72,1024]{1,0:T(8,128)(2,1)S(1)}, bf16[72,1024]{1,0:T(8,128)(2,1)S(1)}, u32[]{:S(2)}, u32[]{:S(2)}) collective-permute-start(bf16[72,1024]{1,0:T(8,128)(2,1)S(1)} %get-tuple-element.79), channel_id=1, source_target_pairs={{0,1},{1,2},{2,3},{3,4},{4,5},{5,6},{6,7},{7,8},{8,9},{9,10},{10,1... | collective-permute-start | bytes 442376 | tf_op jit(solution)/shard_map/ppermute | solution.py:465
  67.5 1.1 collective-permute-done.11
  68.7 1.5 %collective-permute-start.13 = (bf16[16,2048]{1,0:T(8,128)(2,1)S(1)}, bf16[16,2048]{1,0:T(8,128)(2,1)S(1)}, u32[]{:S(2)}, u32[]{:S(2)}) collective-permute-start(bf16[16,2048]{1,0:T(8,128)(2,1)S(1)} %add_convert_fusion.8), channel_id=1, source_target_pairs={{0,2},{1,3},{2,0},{3,1},{4,6},{5,7},{6,4},{7,5},{8,10},{9,11},{10,... | collective-permute-start | bytes 196616 | tf_op jit(solution)/shard_map/ppermute | solution.py:53
  70.1 4.2 %collective-permute-start.16 = (bf16[72,1024]{1,0:T(8,128)(2,1)S(1)}, bf16[72,1024]{1,0:T(8,128)(2,1)S(1)}, u32[]{:S(2)}, u32[]{:S(2)}) collective-permute-start(bf16[72,1024]{1,0:T(8,128)(2,1)S(1)} %get-tuple-element.81), channel_id=1, source_target_pairs={{0,33},{1,34},{2,35},{3,36},{4,37},{5,38},{6,39},{7,40},{8,41},{9,... | collective-permute-start | bytes 442376 | tf_op jit(solution)/shard_map/ppermute | solution.py:466
  74.5 3.8 %collective-permute-done.16.r_diag = bf16[72,1024]{1,0:T(8,128)(2,1)S(1)} collective-permute-done((bf16[72,1024]{1,0:T(8,128)(2,1)S(1)}, bf16[72,1024]{1,0:T(8,128)(2,1)S(1)}, u32[]{:S(2)}, u32[]{:S(2)}) %collective-permute-start.16) | collective-permute-done | bytes 147488 | tf_op jit(solution)/shard_map/ppermute | solution.py:466
  78.5 1.7 %collective-permute-start.17 = (bf16[16,2048]{1,0:T(8,128)(2,1)S(1)}, bf16[16,2048]{1,0:T(8,128)(2,1)S(1)}, u32[]{:S(2)}, u32[]{:S(2)}) collective-permute-start(bf16[16,2048]{1,0:T(8,128)(2,1)S(1)} %add_convert_fusion.6), channel_id=1, source_target_pairs={{0,12},{1,13},{2,14},{3,15},{4,8},{5,9},{6,10},{7,11},{8,4},{9,5},... | collective-permute-start | bytes 196616 | tf_op jit(solution)/shard_map/ppermute | solution.py:53
  80.2 1.6 %collective-permute-start.24 = (bf16[216,1024]{1,0:T(8,128)(2,1)S(1)}, bf16[216,1024]{1,0:T(8,128)(2,1)S(1)}, u32[]{:S(2)}, u32[]{:S(2)}) collective-permute-start(bf16[216,1024]{1,0:T(8,128)(2,1)S(1)} %get-tuple-element.84), channel_id=1, source_target_pairs={{0,32},{1,33},{2,34},{3,35},{4,36},{5,37},{6,38},{7,39},{8,40},{9,... | collective-permute-start | bytes 1327112 | tf_op jit(solution)/shard_map/ppermute | solution.py:464
  81.9 2.1 %collective-permute-done.17 = bf16[16,2048]{1,0:T(8,128)(2,1)S(1)} collective-permute-done((bf16[16,2048]{1,0:T(8,128)(2,1)S(1)}, bf16[16,2048]{1,0:T(8,128)(2,1)S(1)}, u32[]{:S(2)}, u32[]{:S(2)}) %collective-permute-start.17) | collective-permute-done | bytes 65568 | tf_op jit(solution)/shard_map/ppermute | solution.py:53
  84.4 3.0 %collective-permute-start.19 = (bf16[16,2048]{1,0:T(8,128)(2,1)S(1)}, bf16[16,2048]{1,0:T(8,128)(2,1)S(1)}, u32[]{:S(2)}, u32[]{:S(2)}) collective-permute-start(bf16[16,2048]{1,0:T(8,128)(2,1)S(1)} %add_convert_fusion.5), channel_id=1, source_target_pairs={{0,32},{1,129},{2,34},{3,131},{4,36},{5,133},{6,38},{7,135},{8,40}... | collective-permute-start | bytes 196616 | tf_op jit(solution)/shard_map/ppermute | solution.py:53
  87.5 9.0 %collective-permute-done.20 = bf16[16,2048]{1,0:T(8,128)(2,1)S(1)} collective-permute-done((bf16[16,2048]{1,0:T(8,128)(2,1)S(1)}, bf16[16,2048]{1,0:T(8,128)(2,1)S(1)}, u32[]{:S(2)}, u32[]{:S(2)}) %collective-permute-start.20) | collective-permute-done | bytes 65568 | tf_op jit(solution)/shard_map/ppermute | solution.py:53
  96.4 1.5 %collective-permute-done.19 = bf16[16,2048]{1,0:T(8,128)(2,1)S(1)} collective-permute-done((bf16[16,2048]{1,0:T(8,128)(2,1)S(1)}, bf16[16,2048]{1,0:T(8,128)(2,1)S(1)}, u32[]{:S(2)}, u32[]{:S(2)}) %collective-permute-start.19) | collective-permute-done | bytes 65568 | tf_op jit(solution)/shard_map/ppermute | solution.py:53
  98.4 2.7 %collective-permute-start.21 = (bf16[64,2048]{1,0:T(8,128)(2,1)S(1)}, bf16[64,2048]{1,0:T(8,128)(2,1)S(1)}, u32[]{:S(2)}, u32[]{:S(2)}) collective-permute-start(bf16[64,2048]{1,0:T(8,128)(2,1)S(1)} %pad_maximum_fusion.refs_0_), channel_id=1, source_target_pairs={{0,192},{1,49},{2,194},{3,51},{4,196},{5,53},{6,198},{7,55},{8,200... | collective-permute-start | bytes 786440 | tf_op jit(solution)/shard_map/ppermute | solution.py:53
  101.1 2.2 %collective-permute-start.25 = (bf16[64,2048]{1,0:T(8,128)(2,1)S(1)}, bf16[64,2048]{1,0:T(8,128)(2,1)S(1)}, u32[]{:S(2)}, u32[]{:S(2)}) collective-permute-start(bf16[64,2048]{1,0:T(8,128)(2,1)S(1)} %pad_maximum_fusion.refs_0_), channel_id=1, source_target_pairs={{0,1},{1,0},{2,3},{3,2},{4,5},{5,4},{6,7},{7,6},{8,9},{9,8},{10,11... | collective-permute-start | bytes 786440 | tf_op jit(solution)/shard_map/ppermute | solution.py:53
  103.4 3.2 %finish.1 = (bf16[576,512]{1,0:T(8,128)(2,1)}, bf16[576,512]{1,0:T(8,128)(2,1)}) custom-call(bf16[576,512]{1,0:T(8,128)(2,1)S(1)} %bitcast.12, bf16[576,512]{1,0:T(8,128)(2,1)S(1)} %bitcast.15, bf16[576,1024]{1,0:T(8,128)(2,1)S(1)} %get-tuple-element.83.both, bf16[216,1024]{1,0:T(8,128)(2,1)S(1)} %collective-permute-done.24.r_lat, ...), custom_call_target="tpu_custom_call" | custom-call | flops 2000000000 | bytes 8000000 | tf_op jit(solution)/shard_map/finish/pallas_call | solution.py:392
  109.0 2.0 %weights0.1 = (f32[512,1536]{1,0:T(8,128)}, f32[512,512]{1,0:T(8,128)}, f32[1,512]{1,0:T(1,128)S(1)}) custom-call(s32[4]{0:T(128)S(1)} %pad_add_fusion.place, bf16[64,2048]{1,0:T(8,128)(2,1)S(1)} %pad_maximum_fusion.refs_0_, bf16[64,2048]{1,0:T(8,128)(2,1)S(1)} %collective-permute-done.21.refs_1_, bf16[64,2048]{1,0:T(8,128)(2,1)S(1)} %collective-permute-done.22.refs_2_, ...), custom_call_target="tpu_custom_call" | custom-call | flops 10000000 | bytes 4000000 | tf_op jit(solution)/shard_map/weights0/pallas_call | solution.py:302
  111.0 2.5 %weights1.1 = (f32[512,1536]{1,0:T(8,128)}, f32[512,512]{1,0:T(8,128)}, f32[1,512]{1,0:T(1,128)}) custom-call(s32[4]{0:T(128)S(1)} %pad_add_fusion.place, bf16[64,2048]{1,0:T(8,128)(2,1)S(1)} %collective-permute-done.25.refs_0_, bf16[64,2048]{1,0:T(8,128)(2,1)S(1)} %collective-permute-done.26.refs_1_, ...), custom_call_target="tpu_custom_call", output_to_operand_aliasing={{0}: (8, {}), {1}: (9, {})} | custom-call | flops 10000000 | bytes 4000000 | tf_op jit(solution)/shard_map/weights1/pallas_call | solution.py:302
  (85 shorter events, 13.7 us)
Async XLA Ops:
  3.3 20.0 %collective-permute-start = (bf16[216,512]{1,0:T(8,128)(2,1)S(1)}, bf16[216,512]{1,0:T(8,128)(2,1)S(1)}, u32[]{:S(2)}, u32[]{:S(2)}) collective-permute-start(bf16[216,512]{1,0:T(8,128)(2,1)S(1)} %get-tuple-element.52), channel_id=1, source_target_pairs={{0,224},{1,225},{2,226},{3,227},{4,228},{5,229},{6,230},{7,231},{8... | collective-permute-start | bytes 663560 | tf_op jit(solution)/shard_map/ppermute | solution.py:425
  9.4 13.4 %collective-permute-start.1 = (bf16[72,512]{1,0:T(8,128)(2,1)S(1)}, bf16[72,512]{1,0:T(8,128)(2,1)S(1)}, u32[]{:S(2)}, u32[]{:S(2)}) collective-permute-start(bf16[72,512]{1,0:T(8,128)(2,1)S(1)} %get-tuple-element.53), channel_id=1, source_target_pairs={{0,31},{1,0},{2,1},{3,2},{4,3},{5,4},{6,5},{7,6},{8,7},{9,8},{10,9... | collective-permute-start | bytes 221192 | tf_op jit(solution)/shard_map/ppermute | solution.py:426
  10.4 12.9 %collective-permute-start.2 = (bf16[72,512]{1,0:T(8,128)(2,1)S(1)}, bf16[72,512]{1,0:T(8,128)(2,1)S(1)}, u32[]{:S(2)}, u32[]{:S(2)}) collective-permute-start(bf16[72,512]{1,0:T(8,128)(2,1)S(1)} %get-tuple-element.54), channel_id=1, source_target_pairs={{0,255},{1,224},{2,225},{3,226},{4,227},{5,228},{6,229},{7,230},{8... | collective-permute-start | bytes 221192 | tf_op jit(solution)/shard_map/ppermute | solution.py:427
  19.6 17.0 %collective-permute-start.4 = (bf16[72,512]{1,0:T(8,128)(2,1)S(1)}, bf16[72,512]{1,0:T(8,128)(2,1)S(1)}, u32[]{:S(2)}, u32[]{:S(2)}) collective-permute-start(bf16[72,512]{1,0:T(8,128)(2,1)S(1)} %get-tuple-element.57), channel_id=1, source_target_pairs={{0,31},{1,0},{2,1},{3,2},{4,3},{5,4},{6,5},{7,6},{8,7},{9,8},{10,9... | collective-permute-start | bytes 221192 | tf_op jit(solution)/shard_map/ppermute | solution.py:426
  19.7 16.9 %collective-permute-start.5 = (bf16[72,512]{1,0:T(8,128)(2,1)S(1)}, bf16[72,512]{1,0:T(8,128)(2,1)S(1)}, u32[]{:S(2)}, u32[]{:S(2)}) collective-permute-start(bf16[72,512]{1,0:T(8,128)(2,1)S(1)} %get-tuple-element.58), channel_id=1, source_target_pairs={{0,255},{1,224},{2,225},{3,226},{4,227},{5,228},{6,229},{7,230},{8... | collective-permute-start | bytes 221192 | tf_op jit(solution)/shard_map/ppermute | solution.py:427
  22.8 13.8 %collective-permute-start.3 = (bf16[216,512]{1,0:T(8,128)(2,1)S(1)}, bf16[216,512]{1,0:T(8,128)(2,1)S(1)}, u32[]{:S(2)}, u32[]{:S(2)}) collective-permute-start(bf16[216,512]{1,0:T(8,128)(2,1)S(1)} %get-tuple-element.56), channel_id=1, source_target_pairs={{0,224},{1,225},{2,226},{3,227},{4,228},{5,229},{6,230},{7,231},{8... | collective-permute-start | bytes 663560 | tf_op jit(solution)/shard_map/ppermute | solution.py:425
  47.6 2.7 %collective-permute-start.6 = (bf16[256,2048]{1,0:T(8,128)(2,1)S(1)}, bf16[256,2048]{1,0:T(8,128)(2,1)S(1)}, u32[]{:S(2)}, u32[]{:S(2)}) collective-permute-start(bf16[256,2048]{1,0:T(8,128)(2,1)S(1)} %get-tuple-element.64), channel_id=1, source_target_pairs={{0,1},{1,0},{2,3},{3,2},{4,5},{5,4},{6,7},{7,6},{8,9},{9,8},{10,11... | collective-permute-start | bytes 3145736 | tf_op jit(solution)/shard_map/ppermute | solution.py:53
  50.7 7.0 %collective-permute-start.7 = (bf16[64,2048]{1,0:T(8,128)(2,1)S(1)}, bf16[64,2048]{1,0:T(8,128)(2,1)S(1)}, u32[]{:S(2)}, u32[]{:S(2)}) collective-permute-start(bf16[64,2048]{1,0:T(8,128)(2,1)S(1)} %get-tuple-element.66), channel_id=1, source_target_pairs={{0,64},{1,17},{2,66},{3,19},{4,68},{5,21},{6,70},{7,23},{8,72},{9,... | collective-permute-start | bytes 786440 | tf_op jit(solution)/shard_map/ppermute | solution.py:53
  51.2 9.3 %collective-permute-start.8 = (bf16[64,2048]{1,0:T(8,128)(2,1)S(1)}, bf16[64,2048]{1,0:T(8,128)(2,1)S(1)}, u32[]{:S(2)}, u32[]{:S(2)}) collective-permute-start(bf16[64,2048]{1,0:T(8,128)(2,1)S(1)} %get-tuple-element.67), channel_id=1, source_target_pairs={{0,128},{1,33},{2,130},{3,35},{4,132},{5,37},{6,134},{7,39},{8,136... | collective-permute-start | bytes 786440 | tf_op jit(solution)/shard_map/ppermute | solution.py:53
  54.0 7.1 %collective-permute-start.9 = (bf16[64,2048]{1,0:T(8,128)(2,1)S(1)}, bf16[64,2048]{1,0:T(8,128)(2,1)S(1)}, u32[]{:S(2)}, u32[]{:S(2)}) collective-permute-start(bf16[64,2048]{1,0:T(8,128)(2,1)S(1)} %get-tuple-element.68), channel_id=1, source_target_pairs={{0,192},{1,49},{2,194},{3,51},{4,196},{5,53},{6,198},{7,55},{8,200... | collective-permute-start | bytes 786440 | tf_op jit(solution)/shard_map/ppermute | solution.py:53
  57.7 45.7 %copy-start.5 = (bf16[4,6,24,512]{3,2,1,0:T(8,128)(2,1)S(1)}, bf16[4,6,24,512]{3,2,1,0:T(8,128)(2,1)}, u32[]{:S(2)}) copy-start(bf16[4,6,24,512]{3,2,1,0:T(8,128)(2,1)} %param.13) | copy-start | bytes 1769476
  57.7 45.7 %copy-start.9 = (f32[512]{0:T(512)S(1)}, f32[512]{0:T(512)}, u32[]{:S(2)}) copy-start(f32[512]{0:T(512)} %param.15) | copy-start | bytes 6148
  57.7 45.7 %copy-start.13 = (bf16[576,216]{1,0:T(8,128)(2,1)S(1)}, bf16[576,216]{1,0:T(8,128)(2,1)}, u32[]{:S(2)}) copy-start(bf16[576,216]{1,0:T(8,128)(2,1)} %constant.70.clone.s_lat) | copy-start | bytes 746500
  61.3 6.3 %collective-permute-start.10 = (bf16[16,2048]{1,0:T(8,128)(2,1)S(1)}, bf16[16,2048]{1,0:T(8,128)(2,1)S(1)}, u32[]{:S(2)}, u32[]{:S(2)}) collective-permute-start(bf16[16,2048]{1,0:T(8,128)(2,1)S(1)} %get-tuple-element.103), channel_id=1, source_target_pairs={{0,16},{1,65},{2,18},{3,67},{4,20},{5,69},{6,22},{7,71},{8,24},{9,... | collective-permute-start | bytes 196616 | tf_op jit(solution)/shard_map/ppermute | solution.py:53
  62.3 5.2 %collective-permute-start.12 = (bf16[16,2048]{1,0:T(8,128)(2,1)S(1)}, bf16[16,2048]{1,0:T(8,128)(2,1)S(1)}, u32[]{:S(2)}, u32[]{:S(2)}) collective-permute-start(bf16[16,2048]{1,0:T(8,128)(2,1)S(1)} %get-tuple-element.104), channel_id=1, source_target_pairs={{0,48},{1,193},{2,50},{3,195},{4,52},{5,197},{6,54},{7,199},{8,56}... | collective-permute-start | bytes 196616 | tf_op jit(solution)/shard_map/ppermute | solution.py:53
  64.0 4.6 %collective-permute-start.11 = (bf16[16,2048]{1,0:T(8,128)(2,1)S(1)}, bf16[16,2048]{1,0:T(8,128)(2,1)S(1)}, u32[]{:S(2)}, u32[]{:S(2)}) collective-permute-start(bf16[16,2048]{1,0:T(8,128)(2,1)S(1)} %get-tuple-element.105), channel_id=1, source_target_pairs={{0,32},{1,129},{2,34},{3,131},{4,36},{5,133},{6,38},{7,135},{8,40}... | collective-permute-start | bytes 196616 | tf_op jit(solution)/shard_map/ppermute | solution.py:53
  64.2 10.2 %collective-permute-start.14 = (bf16[72,1024]{1,0:T(8,128)(2,1)S(1)}, bf16[72,1024]{1,0:T(8,128)(2,1)S(1)}, u32[]{:S(2)}, u32[]{:S(2)}) collective-permute-start(bf16[72,1024]{1,0:T(8,128)(2,1)S(1)} %get-tuple-element.79), channel_id=1, source_target_pairs={{0,1},{1,2},{2,3},{3,4},{4,5},{5,6},{6,7},{7,8},{8,9},{9,10},{10,1... | collective-permute-start | bytes 442376 | tf_op jit(solution)/shard_map/ppermute | solution.py:465
  68.7 5.7 %collective-permute-start.13 = (bf16[16,2048]{1,0:T(8,128)(2,1)S(1)}, bf16[16,2048]{1,0:T(8,128)(2,1)S(1)}, u32[]{:S(2)}, u32[]{:S(2)}) collective-permute-start(bf16[16,2048]{1,0:T(8,128)(2,1)S(1)} %add_convert_fusion.8), channel_id=1, source_target_pairs={{0,2},{1,3},{2,0},{3,1},{4,6},{5,7},{6,4},{7,5},{8,10},{9,11},{10,... | collective-permute-start | bytes 196616 | tf_op jit(solution)/shard_map/ppermute | solution.py:53
  70.1 8.2 %collective-permute-start.16 = (bf16[72,1024]{1,0:T(8,128)(2,1)S(1)}, bf16[72,1024]{1,0:T(8,128)(2,1)S(1)}, u32[]{:S(2)}, u32[]{:S(2)}) collective-permute-start(bf16[72,1024]{1,0:T(8,128)(2,1)S(1)} %get-tuple-element.81), channel_id=1, source_target_pairs={{0,33},{1,34},{2,35},{3,36},{4,37},{5,38},{6,39},{7,40},{8,41},{9,... | collective-permute-start | bytes 442376 | tf_op jit(solution)/shard_map/ppermute | solution.py:466
  74.4 4.1 %collective-permute-start.15 = (bf16[16,2048]{1,0:T(8,128)(2,1)S(1)}, bf16[16,2048]{1,0:T(8,128)(2,1)S(1)}, u32[]{:S(2)}, u32[]{:S(2)}) collective-permute-start(bf16[16,2048]{1,0:T(8,128)(2,1)S(1)} %add_convert_fusion.7), channel_id=1, source_target_pairs={{0,4},{1,5},{2,6},{3,7},{4,0},{5,1},{6,2},{7,3},{8,12},{9,13},{10,... | collective-permute-start | bytes 196616 | tf_op jit(solution)/shard_map/ppermute | solution.py:53
  78.5 5.4 %collective-permute-start.17 = (bf16[16,2048]{1,0:T(8,128)(2,1)S(1)}, bf16[16,2048]{1,0:T(8,128)(2,1)S(1)}, u32[]{:S(2)}, u32[]{:S(2)}) collective-permute-start(bf16[16,2048]{1,0:T(8,128)(2,1)S(1)} %add_convert_fusion.6), channel_id=1, source_target_pairs={{0,12},{1,13},{2,14},{3,15},{4,8},{5,9},{6,10},{7,11},{8,4},{9,5},... | collective-permute-start | bytes 196616 | tf_op jit(solution)/shard_map/ppermute | solution.py:53
  80.2 23.1 %collective-permute-start.24 = (bf16[216,1024]{1,0:T(8,128)(2,1)S(1)}, bf16[216,1024]{1,0:T(8,128)(2,1)S(1)}, u32[]{:S(2)}, u32[]{:S(2)}) collective-permute-start(bf16[216,1024]{1,0:T(8,128)(2,1)S(1)} %get-tuple-element.84), channel_id=1, source_target_pairs={{0,32},{1,33},{2,34},{3,35},{4,36},{5,37},{6,38},{7,39},{8,40},{9,... | collective-permute-start | bytes 1327112 | tf_op jit(solution)/shard_map/ppermute | solution.py:464
  84.0 12.5 %collective-permute-start.20 = (bf16[16,2048]{1,0:T(8,128)(2,1)S(1)}, bf16[16,2048]{1,0:T(8,128)(2,1)S(1)}, u32[]{:S(2)}, u32[]{:S(2)}) collective-permute-start(bf16[16,2048]{1,0:T(8,128)(2,1)S(1)} %add_convert_fusion.5), channel_id=1, source_target_pairs={{0,16},{1,65},{2,18},{3,67},{4,20},{5,69},{6,22},{7,71},{8,24},{9,... | collective-permute-start | bytes 196616 | tf_op jit(solution)/shard_map/ppermute | solution.py:53
  84.4 13.5 %collective-permute-start.19 = (bf16[16,2048]{1,0:T(8,128)(2,1)S(1)}, bf16[16,2048]{1,0:T(8,128)(2,1)S(1)}, u32[]{:S(2)}, u32[]{:S(2)}) collective-permute-start(bf16[16,2048]{1,0:T(8,128)(2,1)S(1)} %add_convert_fusion.5), channel_id=1, source_target_pairs={{0,32},{1,129},{2,34},{3,131},{4,36},{5,133},{6,38},{7,135},{8,40}... | collective-permute-start | bytes 196616 | tf_op jit(solution)/shard_map/ppermute | solution.py:53
  87.5 10.5 %collective-permute-start.18 = (bf16[16,2048]{1,0:T(8,128)(2,1)S(1)}, bf16[16,2048]{1,0:T(8,128)(2,1)S(1)}, u32[]{:S(2)}, u32[]{:S(2)}) collective-permute-start(bf16[16,2048]{1,0:T(8,128)(2,1)S(1)} %add_convert_fusion.5), channel_id=1, source_target_pairs={{0,48},{1,193},{2,50},{3,195},{4,52},{5,197},{6,54},{7,199},{8,56}... | collective-permute-start | bytes 196616 | tf_op jit(solution)/shard_map/ppermute | solution.py:53
  98.0 9.5 %collective-permute-start.23 = (bf16[64,2048]{1,0:T(8,128)(2,1)S(1)}, bf16[64,2048]{1,0:T(8,128)(2,1)S(1)}, u32[]{:S(2)}, u32[]{:S(2)}) collective-permute-start(bf16[64,2048]{1,0:T(8,128)(2,1)S(1)} %pad_maximum_fusion.refs_0_), channel_id=1, source_target_pairs={{0,64},{1,17},{2,66},{3,19},{4,68},{5,21},{6,70},{7,23},{8,72},{9,... | collective-permute-start | bytes 786440 | tf_op jit(solution)/shard_map/ppermute | solution.py:53
  98.4 9.1 %collective-permute-start.22 = (bf16[64,2048]{1,0:T(8,128)(2,1)S(1)}, bf16[64,2048]{1,0:T(8,128)(2,1)S(1)}, u32[]{:S(2)}, u32[]{:S(2)}) collective-permute-start(bf16[64,2048]{1,0:T(8,128)(2,1)S(1)} %pad_maximum_fusion.refs_0_), channel_id=1, source_target_pairs={{0,128},{1,33},{2,130},{3,35},{4,132},{5,37},{6,134},{7,39},{8,136... | collective-permute-start | bytes 786440 | tf_op jit(solution)/shard_map/ppermute | solution.py:53
  98.4 9.6 %collective-permute-start.21 = (bf16[64,2048]{1,0:T(8,128)(2,1)S(1)}, bf16[64,2048]{1,0:T(8,128)(2,1)S(1)}, u32[]{:S(2)}, u32[]{:S(2)}) collective-permute-start(bf16[64,2048]{1,0:T(8,128)(2,1)S(1)} %pad_maximum_fusion.refs_0_), channel_id=1, source_target_pairs={{0,192},{1,49},{2,194},{3,51},{4,196},{5,53},{6,198},{7,55},{8,200... | collective-permute-start | bytes 786440 | tf_op jit(solution)/shard_map/ppermute | solution.py:53
  101.1 9.8 %collective-permute-start.25 = (bf16[64,2048]{1,0:T(8,128)(2,1)S(1)}, bf16[64,2048]{1,0:T(8,128)(2,1)S(1)}, u32[]{:S(2)}, u32[]{:S(2)}) collective-permute-start(bf16[64,2048]{1,0:T(8,128)(2,1)S(1)} %pad_maximum_fusion.refs_0_), channel_id=1, source_target_pairs={{0,1},{1,0},{2,3},{3,2},{4,5},{5,4},{6,7},{7,6},{8,9},{9,8},{10,11... | collective-permute-start | bytes 786440 | tf_op jit(solution)/shard_map/ppermute | solution.py:53
  108.0 2.9 %collective-permute-start.26 = (bf16[64,2048]{1,0:T(8,128)(2,1)S(1)}, bf16[64,2048]{1,0:T(8,128)(2,1)S(1)}, u32[]{:S(2)}, u32[]{:S(2)}) collective-permute-start(bf16[64,2048]{1,0:T(8,128)(2,1)S(1)} %collective-permute-done.21.refs_1_), channel_id=1, source_target_pairs={{0,1},{1,0},{2,3},{3,2},{4,5},{5,4},{6,7},{7,6},{8,9},{9,8},{10,11... | collective-permute-start | bytes 786440 | tf_op jit(solution)/shard_map/ppermute | solution.py:53
  108.4 2.5 %collective-permute-start.27 = (bf16[64,2048]{1,0:T(8,128)(2,1)S(1)}, bf16[64,2048]{1,0:T(8,128)(2,1)S(1)}, u32[]{:S(2)}, u32[]{:S(2)}) collective-permute-start(bf16[64,2048]{1,0:T(8,128)(2,1)S(1)} %collective-permute-done.22.refs_2_), channel_id=1, source_target_pairs={{0,1},{1,0},{2,3},{3,2},{4,5},{5,4},{6,7},{7,6},{8,9},{9,8},{10,11... | collective-permute-start | bytes 786440 | tf_op jit(solution)/shard_map/ppermute | solution.py:53
  108.6 2.4 %collective-permute-start.28 = (bf16[64,2048]{1,0:T(8,128)(2,1)S(1)}, bf16[64,2048]{1,0:T(8,128)(2,1)S(1)}, u32[]{:S(2)}, u32[]{:S(2)}) collective-permute-start(bf16[64,2048]{1,0:T(8,128)(2,1)S(1)} %collective-permute-done.23.refs_3_), channel_id=1, source_target_pairs={{0,1},{1,0},{2,3},{3,2},{4,5},{5,4},{6,7},{7,6},{8,9},{9,8},{10,11... | collective-permute-start | bytes 786440 | tf_op jit(solution)/shard_map/ppermute | solution.py:53
  (18 other events, 162.1 us)

commit v4 on v3

v4 whole, which is shorter than its diff:
```python
import functools
import math

import jax
import jax.numpy as jnp
import numpy as np
from jax import lax
from jax.experimental import pallas as pl
from jax.experimental.pallas import tpu as pltpu
from jax.sharding import PartitionSpec as P

HEADS = 8
LEV, ROWS, COLS = 4, 6, 24
WL, WR, WC = 2, 6, 12
D = 512
SPAN = WL * WR * WC
TOK = LEV * ROWS * COLS
BOTH = ("lat", "lon")
f32 = jnp.float32
bf16 = jnp.bfloat16
VMEM = 24 * 1024 * 1024


def index_of(y, x, z, c):
    return (y * 2 + x // 2) * 32 + (x % 2) * 16 + z * 2 + c


def place_of(i):
    return i // 64, ((i // 32) % 2) * 2 + (i // 16) % 2, (i // 2) % 8, i % 2


def route(step):
    return [(i, index_of(*step(*place_of(i)))) for i in range(256)]


def to_sibling(y, x, z, c):
    return y, x, z, 1 - c


def first_axis(k):
    return lambda y, x, z, c: ((y + k) % 4, x, z, c) if c == 0 else (y, (x + k) % 4, z, c)


MASKS = (0, 1, 3, 2)


def second_axis(k):
    return lambda y, x, z, c: (y, x ^ k, z, c) if c == 0 else (y ^ k, x, z, c)


def flip_z(k):
    return lambda y, x, z, c: (y, x, z ^ k, c)


def send(x, step):
    return lax.ppermute(x, BOTH, route(step))


def shifted(dlat, dlon):
    def pairs():
        out = []
        for i in range(256):
            a, b = i // 32, i % 32
            out.append((i, ((a + dlat) % 8) * 32 + (b + dlon) % 32))
        return out

    return pairs()


LAT, LON, HALO = 224, 80, 384


def gather_tables():
    local = np.zeros((TOK, TOK), np.float32)
    halo = np.zeros((TOK, HALO), np.float32)
    for lr in range(LEV):
        for rr in range(ROWS):
            for cr in range(COLS):
                w = (lr // WL) * (COLS // WC) + cr // WC
                t = w * SPAN + (lr % WL) * WR * WC + rr * WC + cr % WC
                lo, r, c = (lr + 1) % LEV, rr + 3, cr + 6
                if r < ROWS and c < COLS:
                    local[t, lo * ROWS * COLS + r * COLS + c] = 1
                elif c < COLS:
                    halo[t, lo * 54 + (r - ROWS) * 18 + c - 6] = 1
                elif r < ROWS:
                    halo[t, LAT + lo * 18 + (r - 3) * 6 + c - COLS] = 1
                else:
                    halo[t, LAT + LON + lo * 18 + (r - ROWS) * 6 + c - COLS] = 1
    return local, halo


def select_table():
    select = np.zeros((HALO, TOK), np.float32)
    for lv in range(LEV):
        for r in range(ROWS):
            for c in range(COLS):
                t = lv * ROWS * COLS + r * COLS + c
                if r < 3 and c >= 6:
                    select[lv * 54 + r * 18 + c - 6, t] = 1
                elif r >= 3 and c < 6:
                    select[LAT + lv * 18 + (r - 3) * 6 + c, t] = 1
                elif r < 3:
                    select[LAT + LON + lv * 18 + r * 6 + c, t] = 1
    return select


def dot(a, b, dims=((1,), (0,))):
    return lax.dot_general(a, b, (dims, ((), ())), preferred_element_type=f32)


NT = ((1,), (1,))
TN = ((0,), (0,))


def normalise(x):
    centred = x - jnp.mean(x, axis=-1, keepdims=True)
    rstd = lax.rsqrt(jnp.mean(centred * centred, axis=-1, keepdims=True) + 1e-5)
    return centred * rstd, rstd


def split(rows, lat, lon, diag):
    lat[...] = rows[:LAT].astype(bf16)
    lon[...] = rows[LAT : LAT + LON].astype(bf16)
    diag[...] = rows[LAT + LON :].astype(bf16)


def pack_kernel(f_hbm, c_hbm, s_hbm, f_vm, c_vm, s_vm, *refs):
    f_parts, c_parts, sem = refs[:3], refs[3:6], refs[6]
    pairs = ((s_hbm, s_vm), (f_hbm, f_vm), (c_hbm, c_vm))
    copies = [pltpu.make_async_copy(a, b, sem.at[i]) for i, (a, b) in enumerate(pairs)]
    for copy in copies:
        copy.start()
    copies[0].wait()
    copies[1].wait()
    split(dot(s_vm[...], f_vm[...]), *f_parts)
    copies[2].wait()
    split(dot(s_vm[...], c_vm[...]), *c_parts)


def load_kernel(f_vm, c_vm, *refs):
    sources, targets, (fw, cw, sem) = refs[:5], refs[5:10], refs[10:]
    copies = [
        pltpu.make_async_copy(a, b, sem.at[i]) for i, (a, b) in enumerate(zip(sources, targets))
    ]
    for copy in copies:
        copy.start()
    copies[0].wait()
    local = targets[0]
    fw[...] = dot(local[...], f_vm[...]).astype(bf16)
    cw[...] = dot(local[...], c_vm[...]).astype(bf16)
    for copy in copies[1:]:
        copy.wait()


GROUP = 4
WIDE = GROUP * (D // HEADS)


def group_mask(value=1.0):
    row = lax.broadcasted_iota(jnp.int32, (GROUP * SPAN, WIDE), 0)
    lane = lax.broadcasted_iota(jnp.int32, (GROUP * SPAN, WIDE), 1)
    first = lane // (D // HEADS) * SPAN
    return jnp.where((row >= first) & (row < first + SPAN), value, 0.0).astype(bf16)


def joined(r, factor=1.0):
    lane = lax.broadcasted_iota(jnp.int32, (SPAN, WIDE), 1)
    out = r[:SPAN]
    for h in range(1, GROUP):
        out = jnp.where(lane >= h * (D // HEADS), r[h * SPAN : (h + 1) * SPAN], out)
    return (out * factor).astype(bf16)


def repeated(x, pick):
    return jnp.concatenate([x] * GROUP, axis=0) * pick


def windows(part, table, lat, lon, diag):
    rows = jnp.concatenate([lat[...], lon[...], diag[...]], axis=0)
    return part[...].astype(f32) + dot(table[...], rows)


def forward_kernel(place, *refs):
    gain, w_ref, normed, qkv, probs, mixed = refs[5:]
    xhat, _ = normalise(windows(*refs[:5]))
    normed[...] = (xhat * gain[...]).astype(bf16)
    qkv[...] = dot(normed[...], w_ref[...]).astype(bf16)

    last_lat = place[0]
    long = 2 * SPAN
    low = lax.broadcasted_iota(jnp.int32, (SPAN, 128), 1) < 64
    row = lax.broadcasted_iota(jnp.int32, (long, 128), 0)
    lane = lax.broadcasted_iota(jnp.int32, (long, 128), 1)
    pick = jnp.where((row < SPAN) == (lane < 64), 1.0 / math.sqrt(D // HEADS), 0.0).astype(bf16)

    def lev_of(t):
        return (t >= SPAN // 2).astype(jnp.int32)

    def half_of(t):
        return (t - SPAN // 2 * lev_of(t) >= SPAN // 4).astype(jnp.int32)

    tq = lax.rem(lax.broadcasted_iota(jnp.int32, (SPAN, long), 1), SPAN)
    tk = lax.broadcasted_iota(jnp.int32, (SPAN, long), 0)
    lev_diff = jnp.abs(lev_of(tq) - lev_of(tk))
    half_diff = jnp.abs(half_of(tq) - half_of(tk)) * last_lat

    kinds = (half_diff == 0, (lev_diff + half_diff) == 0)
    for w in range(4):
        at = pl.ds(w * SPAN, SPAN)
        same = kinds[w // 2]
        for p in range(HEADS // 2):
            q_all = jnp.concatenate([qkv[at, pl.ds(128 * p, 128)]] * 2, axis=0) * pick
            k = qkv[at, pl.ds(D + 128 * p, 128)]
            v = qkv[at, pl.ds(2 * D + 128 * p, 128)]
            s = jnp.where(same, dot(k, q_all, NT), -1000000000.0)
            e = jnp.exp(s - jnp.max(s, axis=0, keepdims=True))
            rounded = (e * (1.0 / jnp.sum(e, axis=0, keepdims=True))).astype(bf16)
            probs[pl.ds((w * 2 + p // 2) * SPAN, SPAN), pl.ds(p % 2 * 2 * SPAN, 2 * SPAN)] = rounded
            r = dot(rounded, v, TN)
            mixed[at, pl.ds(128 * p, 128)] = jnp.where(low, r[:SPAN], r[SPAN:]).astype(bf16)


def backward_kernel(place, *refs):
    o_ref, normed, qkv, probs, mixed, gact, own, other, ctw, gm, acc = refs[5:]
    ctw[...] = windows(*refs[:5]).astype(bf16)
    gm[...] = dot(ctw[...], o_ref[...], NT).astype(bf16)
    long = GROUP * SPAN
    pick = group_mask()
    factor = 1.0 / math.sqrt(D // HEADS)
    scaled = group_mask(factor)

    def window(w, carry):
        at = pl.ds(pl.multiple_of(w * SPAN, SPAN), SPAN)
        for p in range(HEADS // GROUP):
            cols = pl.ds(WIDE * p, WIDE)
            q_all = repeated(qkv[at, cols], scaled)
            g_all = repeated(gm[at, cols], pick)
            k = qkv[at, pl.ds(D + WIDE * p, WIDE)]
            v = qkv[at, pl.ds(2 * D + WIDE * p, WIDE)]
            rounded = probs[pl.ds(pl.multiple_of((w * 2 + p) * SPAN, SPAN), SPAN), :]
            gact[at, pl.ds(2 * D + WIDE * p, WIDE)] = dot(rounded, g_all).astype(bf16)
            dp = dot(v, g_all, NT)
            pr = rounded.astype(f32)
            inner = jnp.sum(dp * pr, axis=0, keepdims=True)
            ds = (pr * (dp - inner)).astype(bf16)
            gact[at, cols] = joined(dot(ds, k, TN), factor)
            gact[at, pl.ds(D + WIDE * p, WIDE)] = dot(ds, q_all).astype(bf16)
        return carry

    lax.fori_loop(0, 4, window, 0, unroll=True)

    acc[:, : 3 * D] = dot(normed[...], gact[...], TN)
    acc[:, 3 * D :] = dot(mixed[...], ctw[...], TN)
    y, x, c = place[1], place[2], place[3]

    def fill(out, core):
        d1 = jnp.where(core == 0, y, x)
        d2 = jnp.where(core == 0, x, y)
        for s1 in range(4):
            for s2 in range(4):
                r = core * 256 + lax.rem(d1 + s1, 4) * 64 + (d2 ^ MASKS[s2]) * 16
                rows = acc[pl.ds(pl.multiple_of(r, 16), 16), :]
                out[pl.ds((s1 * 4 + s2) * 16, 16), :] = rows.astype(bf16)

    fill(own, c)
    fill(other, 1 - c)


def back_kernel(mixed, gact, w_ref, o_ref, p_halo, both, to_lat, to_lon, to_diag):
    both[:, :D] = dot(mixed[...], o_ref[...]).astype(bf16)
    both[:, D:] = dot(gact[...], w_ref[...], NT).astype(bf16)
    split(dot(p_halo[...], both[...], TN), to_lat, to_lon, to_diag)


def finish_kernel(f_loc, c_loc, both, r_lat, r_lon, r_diag, p_loc, select, gain, out, grad):
    rows = jnp.concatenate([r_lat[...], r_lon[...], r_diag[...]], axis=0)
    grid = dot(p_loc[...], both[...], TN) + dot(select[...], rows, TN)
    x = f_loc[...].astype(f32)
    out[...] = (x + grid[:, :D]).astype(bf16)
    xhat, rstd = normalise(x)
    g = grid[:, D:] * gain[...]
    first = jnp.mean(g, axis=-1, keepdims=True)
    second = jnp.mean(g * xhat, axis=-1, keepdims=True)
    grad[...] = (c_loc[...].astype(f32) + rstd * (g - first - xhat * second)).astype(bf16)


def weights_kernel(side, place, *refs):
    pieces, refs = refs[:4], refs[4:]
    if side == 0:
        w_ref, g_qkv, g_out, g_total, buf_q, buf_o, sem = refs
    else:
        w_ref, before, gain, _, _, g_qkv, g_out, g_total, buf_q, buf_o, sem = refs
    y, x, c = place[1], place[2], place[3]
    core = c if side == 0 else 1 - c
    d1 = jnp.where(core == 0, y, x)
    d2 = jnp.where(core == 0, x, y)
    bands = [pl.multiple_of(core * 256 + lax.rem(d1 + i, 4) * 64, 64) for i in range(4)]
    copies = []
    for i in range(4):
        for s2 in range(4):
            at = pl.ds(pl.multiple_of((d2 ^ MASKS[s2]) * 16, 16), 16)
            block = pieces[i][pl.ds(s2 * 16, 16), :].astype(f32)
            buf_q[i, at, :] = block[:, : 3 * D]
            buf_o[i, at, :] = block[:, 3 * D :]
        for k, (src, dst) in enumerate(((buf_q, g_qkv), (buf_o, g_out))):
            copy = pltpu.make_async_copy(src.at[i], dst.at[pl.ds(bands[i], 64)], sem.at[i, k])
            copy.start()
            copies.append(copy)
    total = jnp.zeros((1, D), f32) if side == 0 else before[...]
    lane = lax.broadcasted_iota(jnp.int32, (64, D), 1)
    local = lax.broadcasted_iota(jnp.int32, (64, D), 0)
    for i in range(4):
        w = w_ref[pl.ds(bands[i], 64), :].astype(f32)
        sums = jnp.sum(buf_q[i] * w, axis=1, keepdims=True)
        spread = jnp.where(lane == local + bands[i], sums, 0.0)
        total = total + jnp.sum(spread, axis=0, keepdims=True)
    g_total[...] = total if side == 0 else total / gain[...]
    for copy in copies:
        copy.wait()


def to_weights(side, place, pieces, qkv_weight, *more):
    inside = pl.BlockSpec(memory_space=pltpu.VMEM)
    anywhere = pl.BlockSpec(memory_space=pl.ANY)
    extra = [] if side == 0 else [inside, inside, anywhere, anywhere]
    return pl.pallas_call(
        functools.partial(weights_kernel, side),
        out_shape=[shape(D, 3 * D, dtype=f32), shape(D, D, dtype=f32), shape(1, D, dtype=f32)],
        in_specs=spec(5, True) + extra,
        out_specs=[anywhere, anywhere, inside],
        scratch_shapes=[
            pltpu.VMEM((4, 64, 3 * D), f32),
            pltpu.VMEM((4, 64, D), f32),
            pltpu.SemaphoreType.DMA((4, 2)),
        ],
        input_output_aliases={} if side == 0 else {8: 0, 9: 1},
        compiler_params=params(),
        cost_estimate=cost(10**7, 4 * 10**6),
        name="weights" + str(side),
    )(place, *vms(*pieces), vm(qkv_weight), *more)


def params():
    return pltpu.CompilerParams(vmem_limit_bytes=VMEM)


def vm(x):
    return pltpu.with_memory_space_constraint(x, pltpu.VMEM)


def vms(*xs):
    return [vm(x) for x in xs]


def vshape(*dims, dtype=bf16):
    return pltpu.VMEM(dims, dtype)


def spec(count, scalar=False):
    whole = [pl.BlockSpec(memory_space=pltpu.VMEM)] * count
    return ([pl.BlockSpec(memory_space=pltpu.SMEM)] if scalar else []) + whole


def shape(*dims, dtype=bf16):
    return jax.ShapeDtypeStruct(dims, dtype)


def cost(flops, moved):
    return pl.CostEstimate(flops=flops, bytes_accessed=moved, transcendentals=0)


def halo_shapes(width):
    return [vshape(LAT, width), vshape(LON, width), vshape(HALO - LAT - LON, width)]


def to_pack(fields, cotangent, select):
    return pl.pallas_call(
        pack_kernel,
        out_shape=[vshape(TOK, D), vshape(TOK, D), vshape(HALO, TOK)] + halo_shapes(D) * 2,
        in_specs=[pl.BlockSpec(memory_space=pltpu.HBM)] * 3,
        out_specs=spec(9),
        scratch_shapes=[pltpu.SemaphoreType.DMA((3,))],
        compiler_params=params(),
        cost_estimate=cost(4 * 10**8, 2 * 10**6),
        name="pack",
    )(*[pltpu.with_memory_space_constraint(x, pltpu.HBM) for x in (fields, cotangent, select)])


def to_load(f_vm, c_vm, *sources):
    return pl.pallas_call(
        load_kernel,
        out_shape=[vshape(*x.shape, dtype=x.dtype) for x in sources]
        + [vshape(TOK, D), vshape(TOK, D)],
        in_specs=spec(2) + [pl.BlockSpec(memory_space=pltpu.HBM)] * 5,
        out_specs=spec(7),
        scratch_shapes=[pltpu.SemaphoreType.DMA((5,))],
        compiler_params=params(),
        cost_estimate=cost(8 * 10**8, 4 * 10**6),
        name="load",
    )(*vms(f_vm, c_vm), *[pltpu.with_memory_space_constraint(x, pltpu.HBM) for x in sources])


def to_forward(place, *args):
    return pl.pallas_call(
        forward_kernel,
        out_shape=[
            vshape(TOK, D), vshape(TOK, 3 * D), vshape(32 // GROUP * SPAN, GROUP * SPAN), vshape(TOK, D),
        ],
        in_specs=spec(7, True),
        out_specs=spec(4),
        compiler_params=params(),
        cost_estimate=cost(3 * 10**9, 10**7),
        name="forward",
    )(place, *vms(*args))


def to_backward(place, *args):
    return pl.pallas_call(
        backward_kernel,
        out_shape=[vshape(TOK, 3 * D), vshape(256, 4 * D), vshape(256, 4 * D)],
        in_specs=spec(10, True),
        out_specs=spec(3),
        scratch_shapes=[
            pltpu.VMEM((TOK, D), bf16),
            pltpu.VMEM((TOK, D), bf16),
            pltpu.VMEM((D, 4 * D), f32),
        ],
        compiler_params=params(),
        cost_estimate=cost(5 * 10**9, 10**7),
        name="backward",
    )(place, *vms(*args))


def to_back(*args):
    return pl.pallas_call(
        back_kernel,
        out_shape=[vshape(TOK, 2 * D)] + halo_shapes(2 * D),
        in_specs=spec(5),
        out_specs=spec(4),
        compiler_params=params(),
        cost_estimate=cost(2 * 10**9, 5 * 10**6),
        name="back",
    )(*vms(*args))


def to_finish(*args):
    return pl.pallas_call(
        finish_kernel,
        out_shape=[shape(TOK, D), shape(TOK, D)],
        in_specs=spec(9),
        out_specs=spec(2),
        compiler_params=params(),
        cost_estimate=cost(2 * 10**9, 8 * 10**6),
        name="finish",
    )(*vms(*args))


def add(*xs):
    total = xs[0].astype(f32)
    for x in xs[1:]:
        total = total + x.astype(f32)
    return total.astype(bf16)


def tied(x):
    return lax.optimization_barrier(x)


def halo_in(lat, lon, diag):
    return (
        lax.ppermute(lat, BOTH, shifted(-1, 0)),
        lax.ppermute(lon, BOTH, shifted(0, -1)),
        lax.ppermute(diag, BOTH, shifted(-1, -1)),
    )


def on_device(fields, cotangent, layer_norm_gain, qkv_weight, out_weight):
    a, b = lax.axis_index("lat"), lax.axis_index("lon")
    place = jnp.stack(
        [
            (a == 7).astype(jnp.int32),
            (a // 2).astype(jnp.int32),
            ((a % 2) * 2 + b // 16).astype(jnp.int32),
            (b % 2).astype(jnp.int32),
        ]
    )
    tables = [jnp.asarray(t, bf16) for t in gather_tables()]
    select = jnp.asarray(select_table(), bf16)
    f_vm, c_vm, select, *parts = to_pack(
        fields.reshape(TOK, D), cotangent.reshape(TOK, D), select
    )
    f_halo = halo_in(*parts[:3])
    c_halo = halo_in(*parts[3:])
    p_loc, p_halo, w, o, gain, fw, cw = to_load(
        f_vm, c_vm, *tables, qkv_weight, out_weight, layer_norm_gain.reshape(1, D)
    )
    normed, qkv, probs, mixed = to_forward(place, fw, p_halo, *f_halo, gain, w)
    gact, own, other = to_backward(
        place, cw, p_halo, *c_halo, o, normed, qkv, probs, mixed
    )

    there = send(other, to_sibling)
    part = [add(own[64 * k : 64 * k + 64], there[64 * k : 64 * k + 64]) for k in range(4)]
    mixed, gact, part = tied((mixed, gact, part))
    both, to_lat, to_lon, to_diag = to_back(mixed, gact, w, o, p_halo)
    recv = [send(part[k], first_axis(k)) for k in (1, 2, 3)]
    recv, to_lat = tied((recv, to_lat))
    part = add(part[0], *recv)
    part, to_lat, to_lon, to_diag = tied((part, to_lat, to_lon, to_diag))
    part = add(part[:32], send(part[32:], second_axis(3)))
    part = add(part[:16], send(part[16:], second_axis(1)))
    r_lat = lax.ppermute(to_lat, BOTH, shifted(1, 0))
    r_lon = lax.ppermute(to_lon, BOTH, shifted(0, 1))
    r_diag = lax.ppermute(to_diag, BOTH, shifted(1, 1))
    recv = send(part, flip_z(1))
    recv, r_lon = tied((recv, r_lon))
    part = add(part, recv)
    recv = send(part, flip_z(2))
    recv, r_diag = tied((recv, r_diag))
    part = add(part, recv)
    part = add(part, send(part, flip_z(6)))

    block = jnp.concatenate([part, send(part, second_axis(1))], axis=0)
    block = jnp.concatenate([block, send(block, second_axis(3))], axis=0)
    mine = [send(block, first_axis(4 - s)) for s in (1, 2, 3)]
    out, grad = to_finish(f_vm, c_vm, both, r_lat, r_lon, r_diag, p_loc, select, gain)
    mine, out = tied((mine, out))
    mine = [block] + mine
    sibling = [send(m, to_sibling) for m in mine]
    g_qkv, g_out, total = to_weights(0, place, mine, w)
    g_qkv, g_out, g_gain = to_weights(1, place, sibling, w, total, gain, g_qkv, g_out)

    grid = (LEV, ROWS, COLS, D)
    return out.reshape(grid), grad.reshape(grid), g_qkv, g_out, g_gain.reshape(D)


def solution(mesh):
    return jax.shard_map(
        on_device,
        mesh=mesh,
        in_specs=(P(None, "lat", "lon", None), P(None, "lat", "lon", None), P(), P(), P()),
        out_specs=(P(None, "lat", "lon", None), P(None, "lat", "lon", None), P(), P(), P()),
        check_vma=False,
    )
```

time: 115 us -> 112 us (0.974); the launches traced: 114 us -> 112 us
  waiting for transfers between devices: 25.2 us -> 38.8 us
  local copies, waits for them, and re-layouts: 9.99 us -> 0.02 us
  Pallas kernels: 29.3 us -> 24.8 us
    unnamed x42 -> x0, local copies, waits for them, and re-layouts: 9.97 us -> none
    ppermute x20 -> x18, waiting for transfers between devices: 21.3 us -> 29.9 us  [send(): return lax.ppermute(x, BOTH, route(step))]
    ppermute x6, waiting for transfers between devices: 0.02 us -> 4.23 us  [the longest x2 4.22 us: halo_in(): lax.ppermute(lat, BOTH, shifted(-1, 0))]
    pallas_call x1, Pallas kernels: 10.9 us -> 6.83 us  [to_backward(): pl.pallas_call(backward_kernel, out_shape=[vshape(TOK, 3 * D), vshape(256...]
    pallas_call x1, Pallas kernels: 7.55 us -> 4.18 us  [to_forward(): pl.pallas_call(forward_kernel, out_shape=[vshape(TOK, D), vshape(TOK, 3 *...]
    pallas_call x3, Pallas kernels: 3.08 us -> 6.45 us  [the longest x1 2.26 us: to_load(): pl.pallas_call(load_kernel, out_shape=[vshape(*x.shape, dtype=x.dtype) fo...]
    ppermute x20 -> x18, starting transfers between devices: 20.8 us -> 19.3 us  [send(): return lax.ppermute(x, BOTH, route(step))]
    ppermute x1, starting transfers between devices: 4.23 us -> 5.43 us  [on_device(): r_diag = lax.ppermute(to_diag, BOTH, shifted(1, 1))]
  transfers between devices with their start and end apart: 29 -> 27, of which waited for: 11 -> 12; matrix products, arithmetic and copies ran while one was open for 0% -> 0% of each run, Pallas kernels for 13% -> 12%
where the time goes in v4:
time: 112 us
  starting transfers between devices  46.9 us (42%)
  waiting for transfers between devices  38.8 us (35%)
  Pallas kernels  24.8 us (22%)
    ppermute x18, waiting for transfers between devices, send(): return lax.ppermute(x, BOTH, route(step))  29.9 us
    ppermute x18, starting transfers between devices, send(): return lax.ppermute(x, BOTH, route(step))  19.3 us
    ppermute x2, starting transfers between devices, halo_in(): lax.ppermute(diag, BOTH, shifted(-1, -1))  9.69 us
    ppermute x2, starting transfers between devices, halo_in(): lax.ppermute(lat, BOTH, shifted(-1, 0))  6.88 us
    pallas_call x1, Pallas kernels, to_backward(): pl.pallas_call(backward_kernel, out_shape=[vshape(TOK, 3 * D), vshape(256...  6.83 us
    ppermute x1, starting transfers between devices, on_device(): r_diag = lax.ppermute(to_diag, BOTH, shifted(1, 1))  5.43 us
    ppermute x1, waiting for transfers between devices, on_device(): r_diag = lax.ppermute(to_diag, BOTH, shifted(1, 1))  4.65 us
    pallas_call x2, Pallas kernels, to_weights(): pl.pallas_call(functools.partial(weights_kernel, side), out_shape=[shape(...  4.48 us
  transfers between devices with their start and end apart: 27, of which 12 were waited for; matrix products, arithmetic and copies ran while one was open for 0% of the time, Pallas kernels for 12%

profile of v4, /device:TPU:1, one launch (start us, length us, event | category | flops | bytes accessed | tf_op | source)
XLA Modules:
  0.0 112.3 jit_solution(14875234366465722081)
XLA Ops:
  0.6 2.2 %pack.1 = (bf16[576,512]{1,0:T(8,128)(2,1)S(1)}, bf16[576,512]{1,0:T(8,128)(2,1)S(1)}, bf16[384,576]{1,0:T(8,128)(2,1)S(1)}, bf16[224,512]{1,0:T(8,128)(2,1)S(1)...) custom-call(bf16[576,512]{1,0:T(8,128)(2,1)} %bitcast.10, ...), custom_call_target="tpu_custom_call" | custom-call | flops 400000000 | bytes 2000000 | tf_op jit(solution)/shard_map/pack/pallas_call | solution.py:378
  2.8 6.1 %collective-permute-start = (bf16[224,512]{1,0:T(8,128)(2,1)S(1)}, bf16[224,512]{1,0:T(8,128)(2,1)S(1)}, u32[]{:S(2)}, u32[]{:S(2)}) collective-permute-start(bf16[224,512]{1,0:T(8,128)(2,1)S(1)} %get-tuple-element.66), channel_id=1, source_target_pairs={{0,224},{1,225},{2,226},{3,227},{4,228},{5,229},{6,230},{7,231},{8... | collective-permute-start | bytes 688136 | tf_op jit(solution)/shard_map/ppermute | solution.py:472
  8.9 1.0 collective-permute-start.1
  9.9 6.7 %collective-permute-start.2 = (bf16[80,512]{1,0:T(8,128)(2,1)S(1)}, bf16[80,512]{1,0:T(8,128)(2,1)S(1)}, u32[]{:S(2)}, u32[]{:S(2)}) collective-permute-start(bf16[80,512]{1,0:T(8,128)(2,1)S(1)} %get-tuple-element.68), channel_id=1, source_target_pairs={{0,255},{1,224},{2,225},{3,226},{4,227},{5,228},{6,229},{7,230},{8... | collective-permute-start | bytes 245768 | tf_op jit(solution)/shard_map/ppermute | solution.py:474
  16.5 3.0 %collective-permute-start.5 = (bf16[80,512]{1,0:T(8,128)(2,1)S(1)}, bf16[80,512]{1,0:T(8,128)(2,1)S(1)}, u32[]{:S(2)}, u32[]{:S(2)}) collective-permute-start(bf16[80,512]{1,0:T(8,128)(2,1)S(1)} %get-tuple-element.75), channel_id=1, source_target_pairs={{0,255},{1,224},{2,225},{3,226},{4,227},{5,228},{6,229},{7,230},{8... | collective-permute-start | bytes 245768 | tf_op jit(solution)/shard_map/ppermute | solution.py:474
  19.6 2.3 %load.1 = (bf16[576,576]{1,0:T(8,128)(2,1)S(1)}, bf16[576,384]{1,0:T(8,128)(2,1)S(1)}, bf16[512,1536]{1,0:T(8,128)(2,1)S(1)}, bf16[512,512]{1,0:T(8,128)(2,1)S(1...) custom-call(bf16[576,512]{1,0:T(8,128)(2,1)S(1)} %get-tuple-element.62.f_vm.f_loc, ...), custom_call_target="tpu_custom_call" | custom-call | flops 800000000 | bytes 4000000 | tf_op jit(solution)/shard_map/load/pallas_call | solution.py:391
  22.7 4.2 %forward.1 = (bf16[576,512]{1,0:T(8,128)(2,1)S(1)}, bf16[576,1536]{1,0:T(8,128)(2,1)S(1)}, bf16[1152,576]{1,0:T(8,128)(2,1)S(1)}, bf16[576,512]{1,0:T(8,128)(2,1)S(1)}) custom-call(s32[4]{0:T(128)S(1)} %pad_add_fusion.place, bf16[576,512]{1,0:T(8,128)(2,1)S(1)} %get-tuple-element.64.refs_0_, bf16[576,384]{1,0:T(8,128)(2,1)S(1)} %get-tuple-element.65.refs_1_.p_halo, ...), custom_call_target="tpu_custom_call" | custom-call | flops 3000000000 | bytes 10000000 | tf_op jit(solution)/shard_map/forward/pallas_call | solution.py:405
  26.9 4.2 %collective-permute-done.3.refs_2_ = bf16[224,512]{1,0:T(8,128)(2,1)S(1)} collective-permute-done((bf16[224,512]{1,0:T(8,128)(2,1)S(1)}, bf16[224,512]{1,0:T(8,128)(2,1)S(1)}, u32[]{:S(2)}, u32[]{:S(2)}) %collective-permute-start.3) | collective-permute-done | bytes 229408 | tf_op jit(solution)/shard_map/ppermute | solution.py:472
  31.1 6.8 %backward.1 = (bf16[576,1536]{1,0:T(8,128)(2,1)S(1)}, bf16[256,2048]{1,0:T(8,128)(2,1)S(1)}, bf16[256,2048]{1,0:T(8,128)(2,1)S(1)}) custom-call(s32[4]{0:T(128)S(1)} %pad_add_fusion.place, bf16[576,512]{1,0:T(8,128)(2,1)S(1)} %get-tuple-element.72.refs_0_, bf16[576,384]{1,0:T(8,128)(2,1)S(1)} %get-tuple-element.65.refs_1_.p_halo, ...), custom_call_target="tpu_custom_call" | custom-call | flops 5000000000 | bytes 10000000 | tf_op jit(solution)/shard_map/backward/pallas_call | solution.py:419
  38.6 2.3 %collective-permute-done.6 = bf16[256,2048]{1,0:T(8,128)(2,1)S(1)} collective-permute-done((bf16[256,2048]{1,0:T(8,128)(2,1)S(1)}, bf16[256,2048]{1,0:T(8,128)(2,1)S(1)}, u32[]{:S(2)}, u32[]{:S(2)}) %collective-permute-start.6) | collective-permute-done | bytes 1048608 | tf_op jit(solution)/shard_map/ppermute | solution.py:56
  41.3 2.1 %collective-permute-start.8 = (bf16[64,2048]{1,0:T(8,128)(2,1)S(1)}, bf16[64,2048]{1,0:T(8,128)(2,1)S(1)}, u32[]{:S(2)}, u32[]{:S(2)}) collective-permute-start(bf16[64,2048]{1,0:T(8,128)(2,1)S(1)} %get-tuple-element.85), channel_id=1, source_target_pairs={{0,128},{1,33},{2,130},{3,35},{4,132},{5,37},{6,134},{7,39},{8,136... | collective-permute-start | bytes 786440 | tf_op jit(solution)/shard_map/ppermute | solution.py:56
  43.4 1.2 %collective-permute-start.9 = (bf16[64,2048]{1,0:T(8,128)(2,1)S(1)}, bf16[64,2048]{1,0:T(8,128)(2,1)S(1)}, u32[]{:S(2)}, u32[]{:S(2)}) collective-permute-start(bf16[64,2048]{1,0:T(8,128)(2,1)S(1)} %get-tuple-element.86), channel_id=1, source_target_pairs={{0,192},{1,49},{2,194},{3,51},{4,196},{5,53},{6,198},{7,55},{8,200... | collective-permute-start | bytes 786440 | tf_op jit(solution)/shard_map/ppermute | solution.py:56
  44.6 2.0 %back.1 = (bf16[576,1024]{1,0:T(8,128)(2,1)S(1)}, bf16[224,1024]{1,0:T(8,128)(2,1)S(1)}, bf16[80,1024]{1,0:T(8,128)(2,1)S(1)}, bf16[80,1024]{1,0:T(8,128)(2,1)S(1)}) custom-call(bf16[576,512]{1,0:T(8,128)(2,1)S(1)} %get-tuple-element.87.refs_9_.mixed, bf16[576,1536]{1,0:T(8,128)(2,1)S(1)} %get-tuple-element.88.gact, ...), custom_call_target="tpu_custom_call" | custom-call | flops 2000000000 | bytes 5000000 | tf_op jit(solution)/shard_map/back/pallas_call | solution.py:436
  46.7 4.2 %collective-permute-done.7 = bf16[64,2048]{1,0:T(8,128)(2,1)S(1)} collective-permute-done((bf16[64,2048]{1,0:T(8,128)(2,1)S(1)}, bf16[64,2048]{1,0:T(8,128)(2,1)S(1)}, u32[]{:S(2)}, u32[]{:S(2)}) %collective-permute-start.7) | collective-permute-done | bytes 262176 | tf_op jit(solution)/shard_map/ppermute | solution.py:56
  52.2 4.6 %collective-permute-done.10 = bf16[32,2048]{1,0:T(8,128)(2,1)S(1)} collective-permute-done((bf16[32,2048]{1,0:T(8,128)(2,1)S(1)}, bf16[32,2048]{1,0:T(8,128)(2,1)S(1)}, u32[]{:S(2)}, u32[]{:S(2)}) %collective-permute-start.10) | collective-permute-done | bytes 131104 | tf_op jit(solution)/shard_map/ppermute | solution.py:56
  56.9 2.9 %collective-permute-start.13 = (bf16[80,1024]{1,0:T(8,128)(2,1)S(1)}, bf16[80,1024]{1,0:T(8,128)(2,1)S(1)}, u32[]{:S(2)}, u32[]{:S(2)}) collective-permute-start(bf16[80,1024]{1,0:T(8,128)(2,1)S(1)} %get-tuple-element.97), channel_id=1, source_target_pairs={{0,1},{1,2},{2,3},{3,4},{4,5},{5,6},{6,7},{7,8},{8,9},{9,10},{10,1... | collective-permute-start | bytes 491528 | tf_op jit(solution)/shard_map/ppermute | solution.py:514
  60.2 5.4 %collective-permute-start.15 = (bf16[80,1024]{1,0:T(8,128)(2,1)S(1)}, bf16[80,1024]{1,0:T(8,128)(2,1)S(1)}, u32[]{:S(2)}, u32[]{:S(2)}) collective-permute-start(bf16[80,1024]{1,0:T(8,128)(2,1)S(1)} %get-tuple-element.99), channel_id=1, source_target_pairs={{0,33},{1,34},{2,35},{3,36},{4,37},{5,38},{6,39},{7,40},{8,41},{9,... | collective-permute-start | bytes 491528 | tf_op jit(solution)/shard_map/ppermute | solution.py:515
  65.8 4.6 %collective-permute-done.15.r_diag = bf16[80,1024]{1,0:T(8,128)(2,1)S(1)} collective-permute-done((bf16[80,1024]{1,0:T(8,128)(2,1)S(1)}, bf16[80,1024]{1,0:T(8,128)(2,1)S(1)}, u32[]{:S(2)}, u32[]{:S(2)}) %collective-permute-start.15) | collective-permute-done | bytes 163872 | tf_op jit(solution)/shard_map/ppermute | solution.py:515
  70.5 4.7 %collective-permute-start.16 = (bf16[16,2048]{1,0:T(8,128)(2,1)S(1)}, bf16[16,2048]{1,0:T(8,128)(2,1)S(1)}, u32[]{:S(2)}, u32[]{:S(2)}) collective-permute-start(bf16[16,2048]{1,0:T(8,128)(2,1)S(1)} %add_convert_fusion.7), channel_id=1, source_target_pairs={{0,12},{1,13},{2,14},{3,15},{4,8},{5,9},{6,10},{7,11},{8,4},{9,5},... | collective-permute-start | bytes 196616 | tf_op jit(solution)/shard_map/ppermute | solution.py:56
  75.1 3.0 %collective-permute-done.16 = bf16[16,2048]{1,0:T(8,128)(2,1)S(1)} collective-permute-done((bf16[16,2048]{1,0:T(8,128)(2,1)S(1)}, bf16[16,2048]{1,0:T(8,128)(2,1)S(1)}, u32[]{:S(2)}, u32[]{:S(2)}) %collective-permute-start.16) | collective-permute-done | bytes 65568 | tf_op jit(solution)/shard_map/ppermute | solution.py:56
  78.2 1.7 %collective-permute-start.22 = (bf16[224,1024]{1,0:T(8,128)(2,1)S(1)}, bf16[224,1024]{1,0:T(8,128)(2,1)S(1)}, u32[]{:S(2)}, u32[]{:S(2)}) collective-permute-start(bf16[224,1024]{1,0:T(8,128)(2,1)S(1)} %get-tuple-element.102), channel_id=1, source_target_pairs={{0,32},{1,33},{2,34},{3,35},{4,36},{5,37},{6,38},{7,39},{8,40},{9,... | collective-permute-start | bytes 1376264 | tf_op jit(solution)/shard_map/ppermute | solution.py:513
  79.9 1.4 %collective-permute-done.17 = bf16[16,2048]{1,0:T(8,128)(2,1)S(1)} collective-permute-done((bf16[16,2048]{1,0:T(8,128)(2,1)S(1)}, bf16[16,2048]{1,0:T(8,128)(2,1)S(1)}, u32[]{:S(2)}, u32[]{:S(2)}) %collective-permute-start.17) | collective-permute-done | bytes 65568 | tf_op jit(solution)/shard_map/ppermute | solution.py:56
  81.3 0.8 collective-permute-start.18
  82.2 11.5 %collective-permute-done.18 = bf16[32,2048]{1,0:T(8,128)(2,1)S(1)} collective-permute-done((bf16[32,2048]{1,0:T(8,128)(2,1)S(1)}, bf16[32,2048]{1,0:T(8,128)(2,1)S(1)}, u32[]{:S(2)}, u32[]{:S(2)}) %collective-permute-start.18) | collective-permute-done | bytes 131104 | tf_op jit(solution)/shard_map/ppermute | solution.py:56
  93.8 1.7 %collective-permute-start.21 = (bf16[64,2048]{1,0:T(8,128)(2,1)S(1)}, bf16[64,2048]{1,0:T(8,128)(2,1)S(1)}, u32[]{:S(2)}, u32[]{:S(2)}) collective-permute-start(bf16[64,2048]{1,0:T(8,128)(2,1)S(1)} %pad_maximum_fusion.refs_0_), channel_id=1, source_target_pairs={{0,64},{1,17},{2,66},{3,19},{4,68},{5,21},{6,70},{7,23},{8,72},{9,... | collective-permute-start | bytes 786440 | tf_op jit(solution)/shard_map/ppermute | solution.py:56
  95.4 2.5 %collective-permute-start.19 = (bf16[64,2048]{1,0:T(8,128)(2,1)S(1)}, bf16[64,2048]{1,0:T(8,128)(2,1)S(1)}, u32[]{:S(2)}, u32[]{:S(2)}) collective-permute-start(bf16[64,2048]{1,0:T(8,128)(2,1)S(1)} %pad_maximum_fusion.refs_0_), channel_id=1, source_target_pairs={{0,192},{1,49},{2,194},{3,51},{4,196},{5,53},{6,198},{7,55},{8,200... | collective-permute-start | bytes 786440 | tf_op jit(solution)/shard_map/ppermute | solution.py:56
  97.9 2.9 %finish.1 = (bf16[576,512]{1,0:T(8,128)(2,1)}, bf16[576,512]{1,0:T(8,128)(2,1)}) custom-call(bf16[576,512]{1,0:T(8,128)(2,1)S(1)} %get-tuple-element.62.f_vm.f_loc, bf16[576,512]{1,0:T(8,128)(2,1)S(1)} %get-tuple-element.63.c_vm.c_loc, bf16[576,1024]{1,0:T(8,128)(2,1)S(1)} %get-tuple-element.101.both, bf16[224,1024]{1,0:T(8,128)(2,1)S(1)} %collective-permute-done.22.r_lat, ...), custom_call_target="tpu_custom_call" | custom-call | flops 2000000000 | bytes 8000000 | tf_op jit(solution)/shard_map/finish/pallas_call | solution.py:448
  100.8 1.1 collective-permute-start.23
  101.9 1.5 %collective-permute-done.21.refs_3_ = bf16[64,2048]{1,0:T(8,128)(2,1)S(1)} collective-permute-done((bf16[64,2048]{1,0:T(8,128)(2,1)S(1)}, bf16[64,2048]{1,0:T(8,128)(2,1)S(1)}, u32[]{:S(2)}, u32[]{:S(2)}) %collective-permute-start.21) | collective-permute-done | bytes 262176 | tf_op jit(solution)/shard_map/ppermute | solution.py:56
  104.0 3.1 %collective-permute-start.24 = (bf16[64,2048]{1,0:T(8,128)(2,1)S(1)}, bf16[64,2048]{1,0:T(8,128)(2,1)S(1)}, u32[]{:S(2)}, u32[]{:S(2)}) collective-permute-start(bf16[64,2048]{1,0:T(8,128)(2,1)S(1)} %collective-permute-done.19.refs_1_), channel_id=1, source_target_pairs={{0,1},{1,0},{2,3},{3,2},{4,5},{5,4},{6,7},{7,6},{8,9},{9,8},{10,11... | collective-permute-start | bytes 786440 | tf_op jit(solution)/shard_map/ppermute | solution.py:56
  107.5 1.9 %weights0.1 = (f32[512,1536]{1,0:T(8,128)}, f32[512,512]{1,0:T(8,128)}, f32[1,512]{1,0:T(1,128)S(1)}) custom-call(s32[4]{0:T(128)S(1)} %pad_add_fusion.place, bf16[64,2048]{1,0:T(8,128)(2,1)S(1)} %pad_maximum_fusion.refs_0_, bf16[64,2048]{1,0:T(8,128)(2,1)S(1)} %collective-permute-done.19.refs_1_, bf16[64,2048]{1,0:T(8,128)(2,1)S(1)} %collective-permute-done.20.refs_2_, ...), custom_call_target="tpu_custom_call" | custom-call | flops 10000000 | bytes 4000000 | tf_op jit(solution)/shard_map/weights0/pallas_call | solution.py:327
  109.5 2.5 %weights1.1 = (f32[512,1536]{1,0:T(8,128)}, f32[512,512]{1,0:T(8,128)}, f32[1,512]{1,0:T(1,128)}) custom-call(s32[4]{0:T(128)S(1)} %pad_add_fusion.place, bf16[64,2048]{1,0:T(8,128)(2,1)S(1)} %collective-permute-done.23.refs_0_, bf16[64,2048]{1,0:T(8,128)(2,1)S(1)} %collective-permute-done.24.refs_1_, ...), custom_call_target="tpu_custom_call", output_to_operand_aliasing={{0}: (8, {}), {1}: (9, {})} | custom-call | flops 10000000 | bytes 4000000 | tf_op jit(solution)/shard_map/weights1/pallas_call | solution.py:327
  (42 shorter events, 5.2 us)
Async XLA Ops:
  2.8 19.9 %collective-permute-start = (bf16[224,512]{1,0:T(8,128)(2,1)S(1)}, bf16[224,512]{1,0:T(8,128)(2,1)S(1)}, u32[]{:S(2)}, u32[]{:S(2)}) collective-permute-start(bf16[224,512]{1,0:T(8,128)(2,1)S(1)} %get-tuple-element.66), channel_id=1, source_target_pairs={{0,224},{1,225},{2,226},{3,227},{4,228},{5,229},{6,230},{7,231},{8... | collective-permute-start | bytes 688136 | tf_op jit(solution)/shard_map/ppermute | solution.py:472
  8.9 13.0 %collective-permute-start.1 = (bf16[80,512]{1,0:T(8,128)(2,1)S(1)}, bf16[80,512]{1,0:T(8,128)(2,1)S(1)}, u32[]{:S(2)}, u32[]{:S(2)}) collective-permute-start(bf16[80,512]{1,0:T(8,128)(2,1)S(1)} %get-tuple-element.67), channel_id=1, source_target_pairs={{0,31},{1,0},{2,1},{3,2},{4,3},{5,4},{6,5},{7,6},{8,7},{9,8},{10,9... | collective-permute-start | bytes 245768 | tf_op jit(solution)/shard_map/ppermute | solution.py:473
  9.9 12.8 %collective-permute-start.2 = (bf16[80,512]{1,0:T(8,128)(2,1)S(1)}, bf16[80,512]{1,0:T(8,128)(2,1)S(1)}, u32[]{:S(2)}, u32[]{:S(2)}) collective-permute-start(bf16[80,512]{1,0:T(8,128)(2,1)S(1)} %get-tuple-element.68), channel_id=1, source_target_pairs={{0,255},{1,224},{2,225},{3,226},{4,227},{5,228},{6,229},{7,230},{8... | collective-permute-start | bytes 245768 | tf_op jit(solution)/shard_map/ppermute | solution.py:474
  16.5 10.4 %collective-permute-start.4 = (bf16[80,512]{1,0:T(8,128)(2,1)S(1)}, bf16[80,512]{1,0:T(8,128)(2,1)S(1)}, u32[]{:S(2)}, u32[]{:S(2)}) collective-permute-start(bf16[80,512]{1,0:T(8,128)(2,1)S(1)} %get-tuple-element.74), channel_id=1, source_target_pairs={{0,31},{1,0},{2,1},{3,2},{4,3},{5,4},{6,5},{7,6},{8,7},{9,8},{10,9... | collective-permute-start | bytes 245768 | tf_op jit(solution)/shard_map/ppermute | solution.py:473
  16.5 10.4 %collective-permute-start.5 = (bf16[80,512]{1,0:T(8,128)(2,1)S(1)}, bf16[80,512]{1,0:T(8,128)(2,1)S(1)}, u32[]{:S(2)}, u32[]{:S(2)}) collective-permute-start(bf16[80,512]{1,0:T(8,128)(2,1)S(1)} %get-tuple-element.75), channel_id=1, source_target_pairs={{0,255},{1,224},{2,225},{3,226},{4,227},{5,228},{6,229},{7,230},{8... | collective-permute-start | bytes 245768 | tf_op jit(solution)/shard_map/ppermute | solution.py:474
  21.9 9.2 %collective-permute-start.3 = (bf16[224,512]{1,0:T(8,128)(2,1)S(1)}, bf16[224,512]{1,0:T(8,128)(2,1)S(1)}, u32[]{:S(2)}, u32[]{:S(2)}) collective-permute-start(bf16[224,512]{1,0:T(8,128)(2,1)S(1)} %get-tuple-element.73), channel_id=1, source_target_pairs={{0,224},{1,225},{2,226},{3,227},{4,228},{5,229},{6,230},{7,231},{8... | collective-permute-start | bytes 688136 | tf_op jit(solution)/shard_map/ppermute | solution.py:472
  38.0 2.9 %collective-permute-start.6 = (bf16[256,2048]{1,0:T(8,128)(2,1)S(1)}, bf16[256,2048]{1,0:T(8,128)(2,1)S(1)}, u32[]{:S(2)}, u32[]{:S(2)}) collective-permute-start(bf16[256,2048]{1,0:T(8,128)(2,1)S(1)} %get-tuple-element.82), channel_id=1, source_target_pairs={{0,1},{1,0},{2,3},{3,2},{4,5},{5,4},{6,7},{7,6},{8,9},{9,8},{10,11... | collective-permute-start | bytes 3145736 | tf_op jit(solution)/shard_map/ppermute | solution.py:56
  41.3 9.6 %collective-permute-start.7 = (bf16[64,2048]{1,0:T(8,128)(2,1)S(1)}, bf16[64,2048]{1,0:T(8,128)(2,1)S(1)}, u32[]{:S(2)}, u32[]{:S(2)}) collective-permute-start(bf16[64,2048]{1,0:T(8,128)(2,1)S(1)} %get-tuple-element.84), channel_id=1, source_target_pairs={{0,64},{1,17},{2,66},{3,19},{4,68},{5,21},{6,70},{7,23},{8,72},{9,... | collective-permute-start | bytes 786440 | tf_op jit(solution)/shard_map/ppermute | solution.py:56
  41.3 9.5 %collective-permute-start.8 = (bf16[64,2048]{1,0:T(8,128)(2,1)S(1)}, bf16[64,2048]{1,0:T(8,128)(2,1)S(1)}, u32[]{:S(2)}, u32[]{:S(2)}) collective-permute-start(bf16[64,2048]{1,0:T(8,128)(2,1)S(1)} %get-tuple-element.85), channel_id=1, source_target_pairs={{0,128},{1,33},{2,130},{3,35},{4,132},{5,37},{6,134},{7,39},{8,136... | collective-permute-start | bytes 786440 | tf_op jit(solution)/shard_map/ppermute | solution.py:56
  43.4 8.1 %collective-permute-start.9 = (bf16[64,2048]{1,0:T(8,128)(2,1)S(1)}, bf16[64,2048]{1,0:T(8,128)(2,1)S(1)}, u32[]{:S(2)}, u32[]{:S(2)}) collective-permute-start(bf16[64,2048]{1,0:T(8,128)(2,1)S(1)} %get-tuple-element.86), channel_id=1, source_target_pairs={{0,192},{1,49},{2,194},{3,51},{4,196},{5,53},{6,198},{7,55},{8,200... | collective-permute-start | bytes 786440 | tf_op jit(solution)/shard_map/ppermute | solution.py:56
  51.7 5.1 %collective-permute-start.10 = (bf16[32,2048]{1,0:T(8,128)(2,1)S(1)}, bf16[32,2048]{1,0:T(8,128)(2,1)S(1)}, u32[]{:S(2)}, u32[]{:S(2)}) collective-permute-start(bf16[32,2048]{1,0:T(8,128)(2,1)S(1)} %slice.45), channel_id=1, source_target_pairs={{0,48},{1,193},{2,50},{3,195},{4,52},{5,197},{6,54},{7,199},{8,56}... | collective-permute-start | bytes 393224 | tf_op jit(solution)/shard_map/ppermute | solution.py:56
  56.8 3.2 %collective-permute-start.11 = (bf16[16,2048]{1,0:T(8,128)(2,1)S(1)}, bf16[16,2048]{1,0:T(8,128)(2,1)S(1)}, u32[]{:S(2)}, u32[]{:S(2)}) collective-permute-start(bf16[16,2048]{1,0:T(8,128)(2,1)S(1)} %slice.53), channel_id=1, source_target_pairs={{0,16},{1,65},{2,18},{3,67},{4,20},{5,69},{6,22},{7,71},{8,24},{9,... | collective-permute-start | bytes 196616 | tf_op jit(solution)/shard_map/ppermute | solution.py:56
  56.9 8.7 %collective-permute-start.13 = (bf16[80,1024]{1,0:T(8,128)(2,1)S(1)}, bf16[80,1024]{1,0:T(8,128)(2,1)S(1)}, u32[]{:S(2)}, u32[]{:S(2)}) collective-permute-start(bf16[80,1024]{1,0:T(8,128)(2,1)S(1)} %get-tuple-element.97), channel_id=1, source_target_pairs={{0,1},{1,2},{2,3},{3,4},{4,5},{5,6},{6,7},{7,8},{8,9},{9,10},{10,1... | collective-permute-start | bytes 491528 | tf_op jit(solution)/shard_map/ppermute | solution.py:514
  60.0 5.6 %collective-permute-start.12 = (bf16[16,2048]{1,0:T(8,128)(2,1)S(1)}, bf16[16,2048]{1,0:T(8,128)(2,1)S(1)}, u32[]{:S(2)}, u32[]{:S(2)}) collective-permute-start(bf16[16,2048]{1,0:T(8,128)(2,1)S(1)} %add_convert_fusion.9), channel_id=1, source_target_pairs={{0,2},{1,3},{2,0},{3,1},{4,6},{5,7},{6,4},{7,5},{8,10},{9,11},{10,... | collective-permute-start | bytes 196616 | tf_op jit(solution)/shard_map/ppermute | solution.py:56
  60.2 10.2 %collective-permute-start.15 = (bf16[80,1024]{1,0:T(8,128)(2,1)S(1)}, bf16[80,1024]{1,0:T(8,128)(2,1)S(1)}, u32[]{:S(2)}, u32[]{:S(2)}) collective-permute-start(bf16[80,1024]{1,0:T(8,128)(2,1)S(1)} %get-tuple-element.99), channel_id=1, source_target_pairs={{0,33},{1,34},{2,35},{3,36},{4,37},{5,38},{6,39},{7,40},{8,41},{9,... | collective-permute-start | bytes 491528 | tf_op jit(solution)/shard_map/ppermute | solution.py:515
  65.7 4.8 %collective-permute-start.14 = (bf16[16,2048]{1,0:T(8,128)(2,1)S(1)}, bf16[16,2048]{1,0:T(8,128)(2,1)S(1)}, u32[]{:S(2)}, u32[]{:S(2)}) collective-permute-start(bf16[16,2048]{1,0:T(8,128)(2,1)S(1)} %add_convert_fusion.8), channel_id=1, source_target_pairs={{0,4},{1,5},{2,6},{3,7},{4,0},{5,1},{6,2},{7,3},{8,12},{9,13},{10,... | collective-permute-start | bytes 196616 | tf_op jit(solution)/shard_map/ppermute | solution.py:56
  70.5 7.7 %collective-permute-start.16 = (bf16[16,2048]{1,0:T(8,128)(2,1)S(1)}, bf16[16,2048]{1,0:T(8,128)(2,1)S(1)}, u32[]{:S(2)}, u32[]{:S(2)}) collective-permute-start(bf16[16,2048]{1,0:T(8,128)(2,1)S(1)} %add_convert_fusion.7), channel_id=1, source_target_pairs={{0,12},{1,13},{2,14},{3,15},{4,8},{5,9},{6,10},{7,11},{8,4},{9,5},... | collective-permute-start | bytes 196616 | tf_op jit(solution)/shard_map/ppermute | solution.py:56
  78.1 3.2 %collective-permute-start.17 = (bf16[16,2048]{1,0:T(8,128)(2,1)S(1)}, bf16[16,2048]{1,0:T(8,128)(2,1)S(1)}, u32[]{:S(2)}, u32[]{:S(2)}) collective-permute-start(bf16[16,2048]{1,0:T(8,128)(2,1)S(1)} %add_convert_fusion.6), channel_id=1, source_target_pairs={{0,16},{1,65},{2,18},{3,67},{4,20},{5,69},{6,22},{7,71},{8,24},{9,... | collective-permute-start | bytes 196616 | tf_op jit(solution)/shard_map/ppermute | solution.py:56
  78.2 19.7 %collective-permute-start.22 = (bf16[224,1024]{1,0:T(8,128)(2,1)S(1)}, bf16[224,1024]{1,0:T(8,128)(2,1)S(1)}, u32[]{:S(2)}, u32[]{:S(2)}) collective-permute-start(bf16[224,1024]{1,0:T(8,128)(2,1)S(1)} %get-tuple-element.102), channel_id=1, source_target_pairs={{0,32},{1,33},{2,34},{3,35},{4,36},{5,37},{6,38},{7,39},{8,40},{9,... | collective-permute-start | bytes 1376264 | tf_op jit(solution)/shard_map/ppermute | solution.py:513
  81.3 12.4 %collective-permute-start.18 = (bf16[32,2048]{1,0:T(8,128)(2,1)S(1)}, bf16[32,2048]{1,0:T(8,128)(2,1)S(1)}, u32[]{:S(2)}, u32[]{:S(2)}) collective-permute-start(bf16[32,2048]{1,0:T(8,128)(2,1)S(1)} %pad_maximum_fusion.1), channel_id=1, source_target_pairs={{0,48},{1,193},{2,50},{3,195},{4,52},{5,197},{6,54},{7,199},{8,56}... | collective-permute-start | bytes 393224 | tf_op jit(solution)/shard_map/ppermute | solution.py:56
  93.8 9.6 %collective-permute-start.21 = (bf16[64,2048]{1,0:T(8,128)(2,1)S(1)}, bf16[64,2048]{1,0:T(8,128)(2,1)S(1)}, u32[]{:S(2)}, u32[]{:S(2)}) collective-permute-start(bf16[64,2048]{1,0:T(8,128)(2,1)S(1)} %pad_maximum_fusion.refs_0_), channel_id=1, source_target_pairs={{0,64},{1,17},{2,66},{3,19},{4,68},{5,21},{6,70},{7,23},{8,72},{9,... | collective-permute-start | bytes 786440 | tf_op jit(solution)/shard_map/ppermute | solution.py:56
  95.4 7.9 %collective-permute-start.20 = (bf16[64,2048]{1,0:T(8,128)(2,1)S(1)}, bf16[64,2048]{1,0:T(8,128)(2,1)S(1)}, u32[]{:S(2)}, u32[]{:S(2)}) collective-permute-start(bf16[64,2048]{1,0:T(8,128)(2,1)S(1)} %pad_maximum_fusion.refs_0_), channel_id=1, source_target_pairs={{0,128},{1,33},{2,130},{3,35},{4,132},{5,37},{6,134},{7,39},{8,136... | collective-permute-start | bytes 786440 | tf_op jit(solution)/shard_map/ppermute | solution.py:56
  95.4 8.5 %collective-permute-start.19 = (bf16[64,2048]{1,0:T(8,128)(2,1)S(1)}, bf16[64,2048]{1,0:T(8,128)(2,1)S(1)}, u32[]{:S(2)}, u32[]{:S(2)}) collective-permute-start(bf16[64,2048]{1,0:T(8,128)(2,1)S(1)} %pad_maximum_fusion.refs_0_), channel_id=1, source_target_pairs={{0,192},{1,49},{2,194},{3,51},{4,196},{5,53},{6,198},{7,55},{8,200... | collective-permute-start | bytes 786440 | tf_op jit(solution)/shard_map/ppermute | solution.py:56
  100.8 8.7 %collective-permute-start.23 = (bf16[64,2048]{1,0:T(8,128)(2,1)S(1)}, bf16[64,2048]{1,0:T(8,128)(2,1)S(1)}, u32[]{:S(2)}, u32[]{:S(2)}) collective-permute-start(bf16[64,2048]{1,0:T(8,128)(2,1)S(1)} %pad_maximum_fusion.refs_0_), channel_id=1, source_target_pairs={{0,1},{1,0},{2,3},{3,2},{4,5},{5,4},{6,7},{7,6},{8,9},{9,8},{10,11... | collective-permute-start | bytes 786440 | tf_op jit(solution)/shard_map/ppermute | solution.py:56
  104.0 5.5 %collective-permute-start.24 = (bf16[64,2048]{1,0:T(8,128)(2,1)S(1)}, bf16[64,2048]{1,0:T(8,128)(2,1)S(1)}, u32[]{:S(2)}, u32[]{:S(2)}) collective-permute-start(bf16[64,2048]{1,0:T(8,128)(2,1)S(1)} %collective-permute-done.19.refs_1_), channel_id=1, source_target_pairs={{0,1},{1,0},{2,3},{3,2},{4,5},{5,4},{6,7},{7,6},{8,9},{9,8},{10,11... | collective-permute-start | bytes 786440 | tf_op jit(solution)/shard_map/ppermute | solution.py:56
  107.0 2.5 %collective-permute-start.25 = (bf16[64,2048]{1,0:T(8,128)(2,1)S(1)}, bf16[64,2048]{1,0:T(8,128)(2,1)S(1)}, u32[]{:S(2)}, u32[]{:S(2)}) collective-permute-start(bf16[64,2048]{1,0:T(8,128)(2,1)S(1)} %collective-permute-done.20.refs_2_), channel_id=1, source_target_pairs={{0,1},{1,0},{2,3},{3,2},{4,5},{5,4},{6,7},{7,6},{8,9},{9,8},{10,11... | collective-permute-start | bytes 786440 | tf_op jit(solution)/shard_map/ppermute | solution.py:56
  107.0 2.5 %collective-permute-start.26 = (bf16[64,2048]{1,0:T(8,128)(2,1)S(1)}, bf16[64,2048]{1,0:T(8,128)(2,1)S(1)}, u32[]{:S(2)}, u32[]{:S(2)}) collective-permute-start(bf16[64,2048]{1,0:T(8,128)(2,1)S(1)} %collective-permute-done.21.refs_3_), channel_id=1, source_target_pairs={{0,1},{1,0},{2,3},{3,2},{4,5},{5,4},{6,7},{7,6},{8,9},{9,8},{10,11... | collective-permute-start | bytes 786440 | tf_op jit(solution)/shard_map/ppermute | solution.py:56

commit v5 on v4

--- a/solution.py
+++ b/solution.py
@@ -41,11 +41,8 @@
     return lambda y, x, z, c: ((y + k) % 4, x, z, c) if c == 0 else (y, (x + k) % 4, z, c)
 
 
-MASKS = (0, 1, 3, 2)
-
-
 def second_axis(k):
-    return lambda y, x, z, c: (y, x ^ k, z, c) if c == 0 else (y ^ k, x, z, c)
+    return lambda y, x, z, c: (y, (x + k) % 4, z, c) if c == 0 else ((y + k) % 4, x, z, c)
 
 
 def flip_z(k):
@@ -259,7 +256,7 @@
         d2 = jnp.where(core == 0, x, y)
         for s1 in range(4):
             for s2 in range(4):
-                r = core * 256 + lax.rem(d1 + s1, 4) * 64 + (d2 ^ MASKS[s2]) * 16
+                r = core * 256 + lax.rem(d1 + s1, 4) * 64 + lax.rem(d2 + s2, 4) * 16
                 rows = acc[pl.ds(pl.multiple_of(r, 16), 16), :]
                 out[pl.ds((s1 * 4 + s2) * 16, 16), :] = rows.astype(bf16)
 
@@ -299,7 +296,7 @@
     copies = []
     for i in range(4):
         for s2 in range(4):
-            at = pl.ds(pl.multiple_of((d2 ^ MASKS[s2]) * 16, 16), 16)
+            at = pl.ds(pl.multiple_of(lax.rem(d2 + s2, 4) * 16, 16), 16)
             block = pieces[i][pl.ds(s2 * 16, 16), :].astype(f32)
             buf_q[i, at, :] = block[:, : 3 * D]
             buf_o[i, at, :] = block[:, 3 * D :]
@@ -326,7 +323,11 @@
     extra = [] if side == 0 else [inside, inside, anywhere, anywhere]
     return pl.pallas_call(
         functools.partial(weights_kernel, side),
-        out_shape=[shape(D, 3 * D, dtype=f32), shape(D, D, dtype=f32), shape(1, D, dtype=f32)],
+        out_shape=[
+            shape(D, 3 * D, dtype=f32),
+            shape(D, D, dtype=f32),
+            (vshape if side == 0 else shape)(1, D, dtype=f32),
+        ],
         in_specs=spec(5, True) + extra,
         out_specs=[anywhere, anywhere, inside],
         scratch_shapes=[
@@ -396,7 +397,7 @@
         out_specs=spec(7),
         scratch_shapes=[pltpu.SemaphoreType.DMA((5,))],
         compiler_params=params(),
-        cost_estimate=cost(8 * 10**8, 4 * 10**6),
+        cost_estimate=cost(10**6, 10**4),
         name="load",
     )(*vms(f_vm, c_vm), *[pltpu.with_memory_space_constraint(x, pltpu.HBM) for x in sources])
 
@@ -410,7 +411,7 @@
         in_specs=spec(7, True),
         out_specs=spec(4),
         compiler_params=params(),
-        cost_estimate=cost(3 * 10**9, 10**7),
+        cost_estimate=cost(10**6, 10**4),
         name="forward",
     )(place, *vms(*args))
 
@@ -508,28 +509,28 @@
     recv, to_lat = tied((recv, to_lat))
     part = add(part[0], *recv)
     part, to_lat, to_lon, to_diag = tied((part, to_lat, to_lon, to_diag))
-    part = add(part[:32], send(part[32:], second_axis(3)))
-    part = add(part[:16], send(part[16:], second_axis(1)))
+    part = add(part[:16], *[send(part[16 * k : 16 * k + 16], second_axis(k)) for k in (1, 2, 3)])
     r_lat = lax.ppermute(to_lat, BOTH, shifted(1, 0))
     r_lon = lax.ppermute(to_lon, BOTH, shifted(0, 1))
     r_diag = lax.ppermute(to_diag, BOTH, shifted(1, 1))
     recv = send(part, flip_z(1))
+    recv, r_diag = tied((recv, r_diag))
+    part = add(part, recv)
+    recv = send(part, flip_z(2))
     recv, r_lon = tied((recv, r_lon))
     part = add(part, recv)
-    recv = send(part, flip_z(2))
-    recv, r_diag = tied((recv, r_diag))
+    recv = send(part, flip_z(6))
+    recv, r_lat = tied((recv, r_lat))
     part = add(part, recv)
-    part = add(part, send(part, flip_z(6)))
-
-    block = jnp.concatenate([part, send(part, second_axis(1))], axis=0)
-    block = jnp.concatenate([block, send(block, second_axis(3))], axis=0)
+
+    block = jnp.concatenate([part] + [send(part, second_axis(4 - s)) for s in (1, 2, 3)], axis=0)
     mine = [send(block, first_axis(4 - s)) for s in (1, 2, 3)]
     out, grad = to_finish(f_vm, c_vm, both, r_lat, r_lon, r_diag, p_loc, select, gain)
     mine, out = tied((mine, out))
     mine = [block] + mine
     sibling = [send(m, to_sibling) for m in mine]
     g_qkv, g_out, total = to_weights(0, place, mine, w)
-    g_qkv, g_out, g_gain = to_weights(1, place, sibling, w, total, gain, g_qkv, g_out)
+    g_qkv, g_out, g_gain = to_weights(1, place, sibling, w, vm(total), vm(gain), g_qkv, g_out)
 
     grid = (LEV, ROWS, COLS, D)
     return out.reshape(grid), grad.reshape(grid), g_qkv, g_out, g_gain.reshape(D)

time: 112 us -> 105 us (0.938)
  waiting for transfers between devices: 38.8 us -> 18.1 us
  starting transfers between devices: 46.9 us -> 60.2 us
    ppermute x18 -> x20, waiting for transfers between devices: 29.9 us -> 11 us  [send(): return lax.ppermute(x, BOTH, route(step))]
    ppermute x18 -> x20, starting transfers between devices: 19.3 us -> 31.8 us  [send(): return lax.ppermute(x, BOTH, route(step))]
    ppermute x1, waiting for transfers between devices: 0.01 us -> 5.71 us  [on_device(): r_lat = lax.ppermute(to_lat, BOTH, shifted(1, 0))]
    ppermute x2, waiting for transfers between devices: 4.22 us -> 0.01 us  [halo_in(): lax.ppermute(lat, BOTH, shifted(-1, 0))]
    ppermute x1, waiting for transfers between devices: 4.65 us -> 1.37 us  [on_device(): r_diag = lax.ppermute(to_diag, BOTH, shifted(1, 1))]
  transfers between devices with their start and end apart: 27 -> 29, of which waited for: 12 -> 10; matrix products, arithmetic and copies ran while one was open for 0% -> 0% of each run, Pallas kernels for 12% -> 13%
where the time goes in v5:
time: 105 us
  starting transfers between devices  60.2 us (57%)
  Pallas kernels  24.9 us (24%)
  waiting for transfers between devices  18.1 us (17%)
    ppermute x20, starting transfers between devices, send(): return lax.ppermute(x, BOTH, route(step))  31.8 us
    ppermute x20, waiting for transfers between devices, send(): return lax.ppermute(x, BOTH, route(step))  11 us
    ppermute x2, starting transfers between devices, halo_in(): lax.ppermute(diag, BOTH, shifted(-1, -1))  10.5 us
    pallas_call x1, Pallas kernels, to_backward(): pl.pallas_call(backward_kernel, out_shape=[vshape(TOK, 3 * D), vshape(256...  6.84 us
    ppermute x2, starting transfers between devices, halo_in(): lax.ppermute(lat, BOTH, shifted(-1, 0))  6.33 us
    ppermute x1, waiting for transfers between devices, on_device(): r_lat = lax.ppermute(to_lat, BOTH, shifted(1, 0))  5.71 us
    ppermute x1, starting transfers between devices, on_device(): r_diag = lax.ppermute(to_diag, BOTH, shifted(1, 1))  5.1 us
    pallas_call x2, Pallas kernels, to_weights(): pl.pallas_call(functools.partial(weights_kernel, side), out_shape=[shape(...  4.51 us
  transfers between devices with their start and end apart: 29, of which 10 were waited for; matrix products, arithmetic and copies ran while one was open for 0% of the time, Pallas kernels for 13%

profile of v5, /device:TPU:1, one launch (start us, length us, event | category | flops | bytes accessed | tf_op | source)
XLA Modules:
  0.0 104.8 jit_solution(17133332270063646185)
XLA Ops:
  0.6 2.2 %pack.1 = (bf16[576,512]{1,0:T(8,128)(2,1)S(1)}, bf16[576,512]{1,0:T(8,128)(2,1)S(1)}, bf16[384,576]{1,0:T(8,128)(2,1)S(1)}, bf16[224,512]{1,0:T(8,128)(2,1)S(1)...) custom-call(bf16[576,512]{1,0:T(8,128)(2,1)} %bitcast.10, ...), custom_call_target="tpu_custom_call" | custom-call | flops 400000000 | bytes 2000000 | tf_op jit(solution)/shard_map/pack/pallas_call | solution.py:379
  2.8 6.1 %collective-permute-start = (bf16[224,512]{1,0:T(8,128)(2,1)S(1)}, bf16[224,512]{1,0:T(8,128)(2,1)S(1)}, u32[]{:S(2)}, u32[]{:S(2)}) collective-permute-start(bf16[224,512]{1,0:T(8,128)(2,1)S(1)} %get-tuple-element.68), channel_id=1, source_target_pairs={{0,224},{1,225},{2,226},{3,227},{4,228},{5,229},{6,230},{7,231},{8... | collective-permute-start | bytes 688136 | tf_op jit(solution)/shard_map/ppermute | solution.py:473
  9.2 1.2 %collective-permute-start.1 = (bf16[80,512]{1,0:T(8,128)(2,1)S(1)}, bf16[80,512]{1,0:T(8,128)(2,1)S(1)}, u32[]{:S(2)}, u32[]{:S(2)}) collective-permute-start(bf16[80,512]{1,0:T(8,128)(2,1)S(1)} %get-tuple-element.69), channel_id=1, source_target_pairs={{0,31},{1,0},{2,1},{3,2},{4,3},{5,4},{6,5},{7,6},{8,7},{9,8},{10,9... | collective-permute-start | bytes 245768 | tf_op jit(solution)/shard_map/ppermute | solution.py:474
  10.4 8.2 %collective-permute-start.2 = (bf16[80,512]{1,0:T(8,128)(2,1)S(1)}, bf16[80,512]{1,0:T(8,128)(2,1)S(1)}, u32[]{:S(2)}, u32[]{:S(2)}) collective-permute-start(bf16[80,512]{1,0:T(8,128)(2,1)S(1)} %get-tuple-element.70), channel_id=1, source_target_pairs={{0,255},{1,224},{2,225},{3,226},{4,227},{5,228},{6,229},{7,230},{8... | collective-permute-start | bytes 245768 | tf_op jit(solution)/shard_map/ppermute | solution.py:475
  18.7 2.3 %load.1 = (bf16[576,576]{1,0:T(8,128)(2,1)S(1)}, bf16[576,384]{1,0:T(8,128)(2,1)S(1)}, bf16[512,1536]{1,0:T(8,128)(2,1)S(1)}, bf16[512,512]{1,0:T(8,128)(2,1)S(1...) custom-call(bf16[576,512]{1,0:T(8,128)(2,1)S(1)} %get-tuple-element.64.f_vm.f_loc, ...), custom_call_target="tpu_custom_call" | custom-call | flops 1000000 | bytes 10000 | tf_op jit(solution)/shard_map/load/pallas_call | solution.py:392
  21.0 2.3 %collective-permute-start.5 = (bf16[80,512]{1,0:T(8,128)(2,1)S(1)}, bf16[80,512]{1,0:T(8,128)(2,1)S(1)}, u32[]{:S(2)}, u32[]{:S(2)}) collective-permute-start(bf16[80,512]{1,0:T(8,128)(2,1)S(1)} %get-tuple-element.77), channel_id=1, source_target_pairs={{0,255},{1,224},{2,225},{3,226},{4,227},{5,228},{6,229},{7,230},{8... | collective-permute-start | bytes 245768 | tf_op jit(solution)/shard_map/ppermute | solution.py:475
  23.4 4.2 %forward.1 = (bf16[576,512]{1,0:T(8,128)(2,1)S(1)}, bf16[576,1536]{1,0:T(8,128)(2,1)S(1)}, bf16[1152,576]{1,0:T(8,128)(2,1)S(1)}, bf16[576,512]{1,0:T(8,128)(2,1)S(1)}) custom-call(s32[4]{0:T(128)S(1)} %pad_add_fusion.place, bf16[576,512]{1,0:T(8,128)(2,1)S(1)} %get-tuple-element.66.refs_0_, bf16[576,384]{1,0:T(8,128)(2,1)S(1)} %get-tuple-element.67.refs_1_.p_halo, ...), custom_call_target="tpu_custom_call" | custom-call | flops 1000000 | bytes 10000 | tf_op jit(solution)/shard_map/forward/pallas_call | solution.py:406
  27.6 6.8 %backward.1 = (bf16[576,1536]{1,0:T(8,128)(2,1)S(1)}, bf16[256,2048]{1,0:T(8,128)(2,1)S(1)}, bf16[256,2048]{1,0:T(8,128)(2,1)S(1)}) custom-call(s32[4]{0:T(128)S(1)} %pad_add_fusion.place, bf16[576,512]{1,0:T(8,128)(2,1)S(1)} %get-tuple-element.74.refs_0_, bf16[576,384]{1,0:T(8,128)(2,1)S(1)} %get-tuple-element.67.refs_1_.p_halo, ...), custom_call_target="tpu_custom_call" | custom-call | flops 5000000000 | bytes 10000000 | tf_op jit(solution)/shard_map/backward/pallas_call | solution.py:420
  35.0 2.3 %collective-permute-done.6 = bf16[256,2048]{1,0:T(8,128)(2,1)S(1)} collective-permute-done((bf16[256,2048]{1,0:T(8,128)(2,1)S(1)}, bf16[256,2048]{1,0:T(8,128)(2,1)S(1)}, u32[]{:S(2)}, u32[]{:S(2)}) %collective-permute-start.6) | collective-permute-done | bytes 1048608 | tf_op jit(solution)/shard_map/ppermute | solution.py:53
  38.7 2.0 %collective-permute-start.8 = (bf16[64,2048]{1,0:T(8,128)(2,1)S(1)}, bf16[64,2048]{1,0:T(8,128)(2,1)S(1)}, u32[]{:S(2)}, u32[]{:S(2)}) collective-permute-start(bf16[64,2048]{1,0:T(8,128)(2,1)S(1)} %get-tuple-element.87), channel_id=1, source_target_pairs={{0,128},{1,33},{2,130},{3,35},{4,132},{5,37},{6,134},{7,39},{8,136... | collective-permute-start | bytes 786440 | tf_op jit(solution)/shard_map/ppermute | solution.py:53
  40.7 1.4 %collective-permute-start.9 = (bf16[64,2048]{1,0:T(8,128)(2,1)S(1)}, bf16[64,2048]{1,0:T(8,128)(2,1)S(1)}, u32[]{:S(2)}, u32[]{:S(2)}) collective-permute-start(bf16[64,2048]{1,0:T(8,128)(2,1)S(1)} %get-tuple-element.88), channel_id=1, source_target_pairs={{0,192},{1,49},{2,194},{3,51},{4,196},{5,53},{6,198},{7,55},{8,200... | collective-permute-start | bytes 786440 | tf_op jit(solution)/shard_map/ppermute | solution.py:53
  42.1 2.0 %back.1 = (bf16[576,1024]{1,0:T(8,128)(2,1)S(1)}, bf16[224,1024]{1,0:T(8,128)(2,1)S(1)}, bf16[80,1024]{1,0:T(8,128)(2,1)S(1)}, bf16[80,1024]{1,0:T(8,128)(2,1)S(1)}) custom-call(bf16[576,512]{1,0:T(8,128)(2,1)S(1)} %get-tuple-element.89.refs_9_.mixed, bf16[576,1536]{1,0:T(8,128)(2,1)S(1)} %get-tuple-element.90.gact, ...), custom_call_target="tpu_custom_call" | custom-call | flops 2000000000 | bytes 5000000 | tf_op jit(solution)/shard_map/back/pallas_call | solution.py:437
  44.4 2.8 %collective-permute-done.8 = bf16[64,2048]{1,0:T(8,128)(2,1)S(1)} collective-permute-done((bf16[64,2048]{1,0:T(8,128)(2,1)S(1)}, bf16[64,2048]{1,0:T(8,128)(2,1)S(1)}, u32[]{:S(2)}, u32[]{:S(2)}) %collective-permute-start.8) | collective-permute-done | bytes 262176 | tf_op jit(solution)/shard_map/ppermute | solution.py:53
  49.1 1.6 %collective-permute-start.12 = (bf16[16,2048]{1,0:T(8,128)(2,1)S(1)}, bf16[16,2048]{1,0:T(8,128)(2,1)S(1)}, u32[]{:S(2)}, u32[]{:S(2)}) collective-permute-start(bf16[16,2048]{1,0:T(8,128)(2,1)S(1)} %get-tuple-element.128), channel_id=1, source_target_pairs={{0,48},{1,193},{2,50},{3,195},{4,52},{5,197},{6,54},{7,199},{8,56}... | collective-permute-start | bytes 196616 | tf_op jit(solution)/shard_map/ppermute | solution.py:53
  51.0 5.1 %collective-permute-start.14 = (bf16[80,1024]{1,0:T(8,128)(2,1)S(1)}, bf16[80,1024]{1,0:T(8,128)(2,1)S(1)}, u32[]{:S(2)}, u32[]{:S(2)}) collective-permute-start(bf16[80,1024]{1,0:T(8,128)(2,1)S(1)} %get-tuple-element.99), channel_id=1, source_target_pairs={{0,33},{1,34},{2,35},{3,36},{4,37},{5,38},{6,39},{7,40},{8,41},{9,... | collective-permute-start | bytes 491528 | tf_op jit(solution)/shard_map/ppermute | solution.py:515
  56.1 1.7 %collective-permute-start.13 = (bf16[16,2048]{1,0:T(8,128)(2,1)S(1)}, bf16[16,2048]{1,0:T(8,128)(2,1)S(1)}, u32[]{:S(2)}, u32[]{:S(2)}) collective-permute-start(bf16[16,2048]{1,0:T(8,128)(2,1)S(1)} %add_convert_fusion.8), channel_id=1, source_target_pairs={{0,2},{1,3},{2,0},{3,1},{4,6},{5,7},{6,4},{7,5},{8,10},{9,11},{10,... | collective-permute-start | bytes 196616 | tf_op jit(solution)/shard_map/ppermute | solution.py:53
  57.9 2.5 %collective-permute-start.16 = (bf16[80,1024]{1,0:T(8,128)(2,1)S(1)}, bf16[80,1024]{1,0:T(8,128)(2,1)S(1)}, u32[]{:S(2)}, u32[]{:S(2)}) collective-permute-start(bf16[80,1024]{1,0:T(8,128)(2,1)S(1)} %get-tuple-element.101), channel_id=1, source_target_pairs={{0,1},{1,2},{2,3},{3,4},{4,5},{5,6},{6,7},{7,8},{8,9},{9,10},{10,1... | collective-permute-start | bytes 491528 | tf_op jit(solution)/shard_map/ppermute | solution.py:514
  60.4 1.4 %collective-permute-done.14.r_diag = bf16[80,1024]{1,0:T(8,128)(2,1)S(1)} collective-permute-done((bf16[80,1024]{1,0:T(8,128)(2,1)S(1)}, bf16[80,1024]{1,0:T(8,128)(2,1)S(1)}, u32[]{:S(2)}, u32[]{:S(2)}) %collective-permute-start.14) | collective-permute-done | bytes 163872 | tf_op jit(solution)/shard_map/ppermute | solution.py:515
  61.8 2.7 %collective-permute-start.15 = (bf16[16,2048]{1,0:T(8,128)(2,1)S(1)}, bf16[16,2048]{1,0:T(8,128)(2,1)S(1)}, u32[]{:S(2)}, u32[]{:S(2)}) collective-permute-start(bf16[16,2048]{1,0:T(8,128)(2,1)S(1)} %add_convert_fusion.7), channel_id=1, source_target_pairs={{0,4},{1,5},{2,6},{3,7},{4,0},{5,1},{6,2},{7,3},{8,12},{9,13},{10,... | collective-permute-start | bytes 196616 | tf_op jit(solution)/shard_map/ppermute | solution.py:53
  64.5 2.6 %collective-permute-start.18 = (bf16[224,1024]{1,0:T(8,128)(2,1)S(1)}, bf16[224,1024]{1,0:T(8,128)(2,1)S(1)}, u32[]{:S(2)}, u32[]{:S(2)}) collective-permute-start(bf16[224,1024]{1,0:T(8,128)(2,1)S(1)} %get-tuple-element.103), channel_id=1, source_target_pairs={{0,32},{1,33},{2,34},{3,35},{4,36},{5,37},{6,38},{7,39},{8,40},{9,... | collective-permute-start | bytes 1376264 | tf_op jit(solution)/shard_map/ppermute | solution.py:513
  67.1 3.2 %collective-permute-start.17 = (bf16[16,2048]{1,0:T(8,128)(2,1)S(1)}, bf16[16,2048]{1,0:T(8,128)(2,1)S(1)}, u32[]{:S(2)}, u32[]{:S(2)}) collective-permute-start(bf16[16,2048]{1,0:T(8,128)(2,1)S(1)} %add_convert_fusion.6), channel_id=1, source_target_pairs={{0,12},{1,13},{2,14},{3,15},{4,8},{5,9},{6,10},{7,11},{8,4},{9,5},... | collective-permute-start | bytes 196616 | tf_op jit(solution)/shard_map/ppermute | solution.py:53
  70.3 2.2 %collective-permute-done.17 = bf16[16,2048]{1,0:T(8,128)(2,1)S(1)} collective-permute-done((bf16[16,2048]{1,0:T(8,128)(2,1)S(1)}, bf16[16,2048]{1,0:T(8,128)(2,1)S(1)}, u32[]{:S(2)}, u32[]{:S(2)}) %collective-permute-start.17) | collective-permute-done | bytes 65568 | tf_op jit(solution)/shard_map/ppermute | solution.py:53
  72.5 5.7 %collective-permute-done.18.r_lat = bf16[224,1024]{1,0:T(8,128)(2,1)S(1)} collective-permute-done((bf16[224,1024]{1,0:T(8,128)(2,1)S(1)}, bf16[224,1024]{1,0:T(8,128)(2,1)S(1)}, u32[]{:S(2)}, u32[]{:S(2)}) %collective-permute-start.18) | collective-permute-done | bytes 458784 | tf_op jit(solution)/shard_map/ppermute | solution.py:513
  78.7 2.4 %collective-permute-start.20 = (bf16[16,2048]{1,0:T(8,128)(2,1)S(1)}, bf16[16,2048]{1,0:T(8,128)(2,1)S(1)}, u32[]{:S(2)}, u32[]{:S(2)}) collective-permute-start(bf16[16,2048]{1,0:T(8,128)(2,1)S(1)} %add_convert_fusion.5), channel_id=1, source_target_pairs={{0,32},{1,129},{2,34},{3,131},{4,36},{5,133},{6,38},{7,135},{8,40}... | collective-permute-start | bytes 196616 | tf_op jit(solution)/shard_map/ppermute | solution.py:53
  81.4 1.2 %collective-permute-done.21 = bf16[16,2048]{1,0:T(8,128)(2,1)S(1)} collective-permute-done((bf16[16,2048]{1,0:T(8,128)(2,1)S(1)}, bf16[16,2048]{1,0:T(8,128)(2,1)S(1)}, u32[]{:S(2)}, u32[]{:S(2)}) %collective-permute-start.21) | collective-permute-done | bytes 65568 | tf_op jit(solution)/shard_map/ppermute | solution.py:53
  84.3 3.2 %collective-permute-start.23 = (bf16[64,2048]{1,0:T(8,128)(2,1)S(1)}, bf16[64,2048]{1,0:T(8,128)(2,1)S(1)}, u32[]{:S(2)}, u32[]{:S(2)}) collective-permute-start(bf16[64,2048]{1,0:T(8,128)(2,1)S(1)} %pad_maximum_fusion.refs_0_), channel_id=1, source_target_pairs={{0,128},{1,33},{2,130},{3,35},{4,132},{5,37},{6,134},{7,39},{8,136... | collective-permute-start | bytes 786440 | tf_op jit(solution)/shard_map/ppermute | solution.py:53
  87.5 1.2 %collective-permute-start.22 = (bf16[64,2048]{1,0:T(8,128)(2,1)S(1)}, bf16[64,2048]{1,0:T(8,128)(2,1)S(1)}, u32[]{:S(2)}, u32[]{:S(2)}) collective-permute-start(bf16[64,2048]{1,0:T(8,128)(2,1)S(1)} %pad_maximum_fusion.refs_0_), channel_id=1, source_target_pairs={{0,192},{1,49},{2,194},{3,51},{4,196},{5,53},{6,198},{7,55},{8,200... | collective-permute-start | bytes 786440 | tf_op jit(solution)/shard_map/ppermute | solution.py:53
  88.6 2.9 %finish.1 = (bf16[576,512]{1,0:T(8,128)(2,1)}, bf16[576,512]{1,0:T(8,128)(2,1)}) custom-call(bf16[576,512]{1,0:T(8,128)(2,1)S(1)} %get-tuple-element.64.f_vm.f_loc, bf16[576,512]{1,0:T(8,128)(2,1)S(1)} %get-tuple-element.65.c_vm.c_loc, bf16[576,1024]{1,0:T(8,128)(2,1)S(1)} %get-tuple-element.105.both, bf16[224,1024]{1,0:T(8,128)(2,1)S(1)} %collective-permute-done.18.r_lat, ...), custom_call_target="tpu_custom_call" | custom-call | flops 2000000000 | bytes 8000000 | tf_op jit(solution)/shard_map/finish/pallas_call | solution.py:449
  91.5 3.5 %collective-permute-start.25 = (bf16[64,2048]{1,0:T(8,128)(2,1)S(1)}, bf16[64,2048]{1,0:T(8,128)(2,1)S(1)}, u32[]{:S(2)}, u32[]{:S(2)}) collective-permute-start(bf16[64,2048]{1,0:T(8,128)(2,1)S(1)} %pad_maximum_fusion.refs_0_), channel_id=1, source_target_pairs={{0,1},{1,0},{2,3},{3,2},{4,5},{5,4},{6,7},{7,6},{8,9},{9,8},{10,11... | collective-permute-start | bytes 786440 | tf_op jit(solution)/shard_map/ppermute | solution.py:53
  95.0 4.5 %collective-permute-start.26 = (bf16[64,2048]{1,0:T(8,128)(2,1)S(1)}, bf16[64,2048]{1,0:T(8,128)(2,1)S(1)}, u32[]{:S(2)}, u32[]{:S(2)}) collective-permute-start(bf16[64,2048]{1,0:T(8,128)(2,1)S(1)} %collective-permute-done.22.refs_1_), channel_id=1, source_target_pairs={{0,1},{1,0},{2,3},{3,2},{4,5},{5,4},{6,7},{7,6},{8,9},{9,8},{10,11... | collective-permute-start | bytes 786440 | tf_op jit(solution)/shard_map/ppermute | solution.py:53
  100.1 2.0 %weights0.1 = (f32[512,1536]{1,0:T(8,128)}, f32[512,512]{1,0:T(8,128)}, f32[1,512]{1,0:T(1,128)S(1)}) custom-call(s32[4]{0:T(128)S(1)} %pad_add_fusion.place, bf16[64,2048]{1,0:T(8,128)(2,1)S(1)} %pad_maximum_fusion.refs_0_, bf16[64,2048]{1,0:T(8,128)(2,1)S(1)} %collective-permute-done.22.refs_1_, bf16[64,2048]{1,0:T(8,128)(2,1)S(1)} %collective-permute-done.23.refs_2_, ...), custom_call_target="tpu_custom_call" | custom-call | flops 10000000 | bytes 4000000 | tf_op jit(solution)/shard_map/weights0/pallas_call | solution.py:324
  102.1 2.5 %weights1.1 = (f32[512,1536]{1,0:T(8,128)}, f32[512,512]{1,0:T(8,128)}, f32[1,512]{1,0:T(1,128)}) custom-call(s32[4]{0:T(128)S(1)} %pad_add_fusion.place, bf16[64,2048]{1,0:T(8,128)(2,1)S(1)} %collective-permute-done.25.refs_0_, bf16[64,2048]{1,0:T(8,128)(2,1)S(1)} %collective-permute-done.26.refs_1_, ...), custom_call_target="tpu_custom_call", output_to_operand_aliasing={{0}: (8, {}), {1}: (9, {})} | custom-call | flops 10000000 | bytes 4000000 | tf_op jit(solution)/shard_map/weights1/pallas_call | solution.py:324
  (43 shorter events, 8.1 us)
Async XLA Ops:
  2.8 20.6 %collective-permute-start = (bf16[224,512]{1,0:T(8,128)(2,1)S(1)}, bf16[224,512]{1,0:T(8,128)(2,1)S(1)}, u32[]{:S(2)}, u32[]{:S(2)}) collective-permute-start(bf16[224,512]{1,0:T(8,128)(2,1)S(1)} %get-tuple-element.68), channel_id=1, source_target_pairs={{0,224},{1,225},{2,226},{3,227},{4,228},{5,229},{6,230},{7,231},{8... | collective-permute-start | bytes 688136 | tf_op jit(solution)/shard_map/ppermute | solution.py:473
  8.9 18.7 %collective-permute-start.3 = (bf16[224,512]{1,0:T(8,128)(2,1)S(1)}, bf16[224,512]{1,0:T(8,128)(2,1)S(1)}, u32[]{:S(2)}, u32[]{:S(2)}) collective-permute-start(bf16[224,512]{1,0:T(8,128)(2,1)S(1)} %get-tuple-element.75), channel_id=1, source_target_pairs={{0,224},{1,225},{2,226},{3,227},{4,228},{5,229},{6,230},{7,231},{8... | collective-permute-start | bytes 688136 | tf_op jit(solution)/shard_map/ppermute | solution.py:473
  9.2 11.8 %collective-permute-start.1 = (bf16[80,512]{1,0:T(8,128)(2,1)S(1)}, bf16[80,512]{1,0:T(8,128)(2,1)S(1)}, u32[]{:S(2)}, u32[]{:S(2)}) collective-permute-start(bf16[80,512]{1,0:T(8,128)(2,1)S(1)} %get-tuple-element.69), channel_id=1, source_target_pairs={{0,31},{1,0},{2,1},{3,2},{4,3},{5,4},{6,5},{7,6},{8,7},{9,8},{10,9... | collective-permute-start | bytes 245768 | tf_op jit(solution)/shard_map/ppermute | solution.py:474
  10.4 13.0 %collective-permute-start.2 = (bf16[80,512]{1,0:T(8,128)(2,1)S(1)}, bf16[80,512]{1,0:T(8,128)(2,1)S(1)}, u32[]{:S(2)}, u32[]{:S(2)}) collective-permute-start(bf16[80,512]{1,0:T(8,128)(2,1)S(1)} %get-tuple-element.70), channel_id=1, source_target_pairs={{0,255},{1,224},{2,225},{3,226},{4,227},{5,228},{6,229},{7,230},{8... | collective-permute-start | bytes 245768 | tf_op jit(solution)/shard_map/ppermute | solution.py:475
  18.6 9.0 %collective-permute-start.4 = (bf16[80,512]{1,0:T(8,128)(2,1)S(1)}, bf16[80,512]{1,0:T(8,128)(2,1)S(1)}, u32[]{:S(2)}, u32[]{:S(2)}) collective-permute-start(bf16[80,512]{1,0:T(8,128)(2,1)S(1)} %get-tuple-element.76), channel_id=1, source_target_pairs={{0,31},{1,0},{2,1},{3,2},{4,3},{5,4},{6,5},{7,6},{8,7},{9,8},{10,9... | collective-permute-start | bytes 245768 | tf_op jit(solution)/shard_map/ppermute | solution.py:474
  21.0 6.6 %collective-permute-start.5 = (bf16[80,512]{1,0:T(8,128)(2,1)S(1)}, bf16[80,512]{1,0:T(8,128)(2,1)S(1)}, u32[]{:S(2)}, u32[]{:S(2)}) collective-permute-start(bf16[80,512]{1,0:T(8,128)(2,1)S(1)} %get-tuple-element.77), channel_id=1, source_target_pairs={{0,255},{1,224},{2,225},{3,226},{4,227},{5,228},{6,229},{7,230},{8... | collective-permute-start | bytes 245768 | tf_op jit(solution)/shard_map/ppermute | solution.py:475
  34.5 2.8 %collective-permute-start.6 = (bf16[256,2048]{1,0:T(8,128)(2,1)S(1)}, bf16[256,2048]{1,0:T(8,128)(2,1)S(1)}, u32[]{:S(2)}, u32[]{:S(2)}) collective-permute-start(bf16[256,2048]{1,0:T(8,128)(2,1)S(1)} %get-tuple-element.84), channel_id=1, source_target_pairs={{0,1},{1,0},{2,3},{3,2},{4,5},{5,4},{6,7},{7,6},{8,9},{9,8},{10,11... | collective-permute-start | bytes 3145736 | tf_op jit(solution)/shard_map/ppermute | solution.py:53
  37.6 6.8 %collective-permute-start.7 = (bf16[64,2048]{1,0:T(8,128)(2,1)S(1)}, bf16[64,2048]{1,0:T(8,128)(2,1)S(1)}, u32[]{:S(2)}, u32[]{:S(2)}) collective-permute-start(bf16[64,2048]{1,0:T(8,128)(2,1)S(1)} %get-tuple-element.86), channel_id=1, source_target_pairs={{0,64},{1,17},{2,66},{3,19},{4,68},{5,21},{6,70},{7,23},{8,72},{9,... | collective-permute-start | bytes 786440 | tf_op jit(solution)/shard_map/ppermute | solution.py:53
  38.7 8.5 %collective-permute-start.8 = (bf16[64,2048]{1,0:T(8,128)(2,1)S(1)}, bf16[64,2048]{1,0:T(8,128)(2,1)S(1)}, u32[]{:S(2)}, u32[]{:S(2)}) collective-permute-start(bf16[64,2048]{1,0:T(8,128)(2,1)S(1)} %get-tuple-element.87), channel_id=1, source_target_pairs={{0,128},{1,33},{2,130},{3,35},{4,132},{5,37},{6,134},{7,39},{8,136... | collective-permute-start | bytes 786440 | tf_op jit(solution)/shard_map/ppermute | solution.py:53
  40.7 7.2 %collective-permute-start.9 = (bf16[64,2048]{1,0:T(8,128)(2,1)S(1)}, bf16[64,2048]{1,0:T(8,128)(2,1)S(1)}, u32[]{:S(2)}, u32[]{:S(2)}) collective-permute-start(bf16[64,2048]{1,0:T(8,128)(2,1)S(1)} %get-tuple-element.88), channel_id=1, source_target_pairs={{0,192},{1,49},{2,194},{3,51},{4,196},{5,53},{6,198},{7,55},{8,200... | collective-permute-start | bytes 786440 | tf_op jit(solution)/shard_map/ppermute | solution.py:53
  48.0 8.1 %collective-permute-start.10 = (bf16[16,2048]{1,0:T(8,128)(2,1)S(1)}, bf16[16,2048]{1,0:T(8,128)(2,1)S(1)}, u32[]{:S(2)}, u32[]{:S(2)}) collective-permute-start(bf16[16,2048]{1,0:T(8,128)(2,1)S(1)} %get-tuple-element.127), channel_id=1, source_target_pairs={{0,16},{1,65},{2,18},{3,67},{4,20},{5,69},{6,22},{7,71},{8,24},{9,... | collective-permute-start | bytes 196616 | tf_op jit(solution)/shard_map/ppermute | solution.py:53
  49.1 7.0 %collective-permute-start.12 = (bf16[16,2048]{1,0:T(8,128)(2,1)S(1)}, bf16[16,2048]{1,0:T(8,128)(2,1)S(1)}, u32[]{:S(2)}, u32[]{:S(2)}) collective-permute-start(bf16[16,2048]{1,0:T(8,128)(2,1)S(1)} %get-tuple-element.128), channel_id=1, source_target_pairs={{0,48},{1,193},{2,50},{3,195},{4,52},{5,197},{6,54},{7,199},{8,56}... | collective-permute-start | bytes 196616 | tf_op jit(solution)/shard_map/ppermute | solution.py:53
  50.7 5.4 %collective-permute-start.11 = (bf16[16,2048]{1,0:T(8,128)(2,1)S(1)}, bf16[16,2048]{1,0:T(8,128)(2,1)S(1)}, u32[]{:S(2)}, u32[]{:S(2)}) collective-permute-start(bf16[16,2048]{1,0:T(8,128)(2,1)S(1)} %get-tuple-element.129), channel_id=1, source_target_pairs={{0,32},{1,129},{2,34},{3,131},{4,36},{5,133},{6,38},{7,135},{8,40}... | collective-permute-start | bytes 196616 | tf_op jit(solution)/shard_map/ppermute | solution.py:53
  51.0 10.8 %collective-permute-start.14 = (bf16[80,1024]{1,0:T(8,128)(2,1)S(1)}, bf16[80,1024]{1,0:T(8,128)(2,1)S(1)}, u32[]{:S(2)}, u32[]{:S(2)}) collective-permute-start(bf16[80,1024]{1,0:T(8,128)(2,1)S(1)} %get-tuple-element.99), channel_id=1, source_target_pairs={{0,33},{1,34},{2,35},{3,36},{4,37},{5,38},{6,39},{7,40},{8,41},{9,... | collective-permute-start | bytes 491528 | tf_op jit(solution)/shard_map/ppermute | solution.py:515
  56.1 4.2 %collective-permute-start.13 = (bf16[16,2048]{1,0:T(8,128)(2,1)S(1)}, bf16[16,2048]{1,0:T(8,128)(2,1)S(1)}, u32[]{:S(2)}, u32[]{:S(2)}) collective-permute-start(bf16[16,2048]{1,0:T(8,128)(2,1)S(1)} %add_convert_fusion.8), channel_id=1, source_target_pairs={{0,2},{1,3},{2,0},{3,1},{4,6},{5,7},{6,4},{7,5},{8,10},{9,11},{10,... | collective-permute-start | bytes 196616 | tf_op jit(solution)/shard_map/ppermute | solution.py:53
  57.9 9.2 %collective-permute-start.16 = (bf16[80,1024]{1,0:T(8,128)(2,1)S(1)}, bf16[80,1024]{1,0:T(8,128)(2,1)S(1)}, u32[]{:S(2)}, u32[]{:S(2)}) collective-permute-start(bf16[80,1024]{1,0:T(8,128)(2,1)S(1)} %get-tuple-element.101), channel_id=1, source_target_pairs={{0,1},{1,2},{2,3},{3,4},{4,5},{5,6},{6,7},{7,8},{8,9},{9,10},{10,1... | collective-permute-start | bytes 491528 | tf_op jit(solution)/shard_map/ppermute | solution.py:514
  61.8 5.3 %collective-permute-start.15 = (bf16[16,2048]{1,0:T(8,128)(2,1)S(1)}, bf16[16,2048]{1,0:T(8,128)(2,1)S(1)}, u32[]{:S(2)}, u32[]{:S(2)}) collective-permute-start(bf16[16,2048]{1,0:T(8,128)(2,1)S(1)} %add_convert_fusion.7), channel_id=1, source_target_pairs={{0,4},{1,5},{2,6},{3,7},{4,0},{5,1},{6,2},{7,3},{8,12},{9,13},{10,... | collective-permute-start | bytes 196616 | tf_op jit(solution)/shard_map/ppermute | solution.py:53
  64.5 13.7 %collective-permute-start.18 = (bf16[224,1024]{1,0:T(8,128)(2,1)S(1)}, bf16[224,1024]{1,0:T(8,128)(2,1)S(1)}, u32[]{:S(2)}, u32[]{:S(2)}) collective-permute-start(bf16[224,1024]{1,0:T(8,128)(2,1)S(1)} %get-tuple-element.103), channel_id=1, source_target_pairs={{0,32},{1,33},{2,34},{3,35},{4,36},{5,37},{6,38},{7,39},{8,40},{9,... | collective-permute-start | bytes 1376264 | tf_op jit(solution)/shard_map/ppermute | solution.py:513
  67.1 5.4 %collective-permute-start.17 = (bf16[16,2048]{1,0:T(8,128)(2,1)S(1)}, bf16[16,2048]{1,0:T(8,128)(2,1)S(1)}, u32[]{:S(2)}, u32[]{:S(2)}) collective-permute-start(bf16[16,2048]{1,0:T(8,128)(2,1)S(1)} %add_convert_fusion.6), channel_id=1, source_target_pairs={{0,12},{1,13},{2,14},{3,15},{4,8},{5,9},{6,10},{7,11},{8,4},{9,5},... | collective-permute-start | bytes 196616 | tf_op jit(solution)/shard_map/ppermute | solution.py:53
  78.2 4.4 %collective-permute-start.21 = (bf16[16,2048]{1,0:T(8,128)(2,1)S(1)}, bf16[16,2048]{1,0:T(8,128)(2,1)S(1)}, u32[]{:S(2)}, u32[]{:S(2)}) collective-permute-start(bf16[16,2048]{1,0:T(8,128)(2,1)S(1)} %add_convert_fusion.5), channel_id=1, source_target_pairs={{0,16},{1,65},{2,18},{3,67},{4,20},{5,69},{6,22},{7,71},{8,24},{9,... | collective-permute-start | bytes 196616 | tf_op jit(solution)/shard_map/ppermute | solution.py:53
  78.7 4.7 %collective-permute-start.20 = (bf16[16,2048]{1,0:T(8,128)(2,1)S(1)}, bf16[16,2048]{1,0:T(8,128)(2,1)S(1)}, u32[]{:S(2)}, u32[]{:S(2)}) collective-permute-start(bf16[16,2048]{1,0:T(8,128)(2,1)S(1)} %add_convert_fusion.5), channel_id=1, source_target_pairs={{0,32},{1,129},{2,34},{3,131},{4,36},{5,133},{6,38},{7,135},{8,40}... | collective-permute-start | bytes 196616 | tf_op jit(solution)/shard_map/ppermute | solution.py:53
  81.1 3.1 %collective-permute-start.19 = (bf16[16,2048]{1,0:T(8,128)(2,1)S(1)}, bf16[16,2048]{1,0:T(8,128)(2,1)S(1)}, u32[]{:S(2)}, u32[]{:S(2)}) collective-permute-start(bf16[16,2048]{1,0:T(8,128)(2,1)S(1)} %add_convert_fusion.5), channel_id=1, source_target_pairs={{0,48},{1,193},{2,50},{3,195},{4,52},{5,197},{6,54},{7,199},{8,56}... | collective-permute-start | bytes 196616 | tf_op jit(solution)/shard_map/ppermute | solution.py:53
  84.2 10.8 %collective-permute-start.24 = (bf16[64,2048]{1,0:T(8,128)(2,1)S(1)}, bf16[64,2048]{1,0:T(8,128)(2,1)S(1)}, u32[]{:S(2)}, u32[]{:S(2)}) collective-permute-start(bf16[64,2048]{1,0:T(8,128)(2,1)S(1)} %pad_maximum_fusion.refs_0_), channel_id=1, source_target_pairs={{0,64},{1,17},{2,66},{3,19},{4,68},{5,21},{6,70},{7,23},{8,72},{9,... | collective-permute-start | bytes 786440 | tf_op jit(solution)/shard_map/ppermute | solution.py:53
  84.3 10.7 %collective-permute-start.23 = (bf16[64,2048]{1,0:T(8,128)(2,1)S(1)}, bf16[64,2048]{1,0:T(8,128)(2,1)S(1)}, u32[]{:S(2)}, u32[]{:S(2)}) collective-permute-start(bf16[64,2048]{1,0:T(8,128)(2,1)S(1)} %pad_maximum_fusion.refs_0_), channel_id=1, source_target_pairs={{0,128},{1,33},{2,130},{3,35},{4,132},{5,37},{6,134},{7,39},{8,136... | collective-permute-start | bytes 786440 | tf_op jit(solution)/shard_map/ppermute | solution.py:53
  87.5 7.6 %collective-permute-start.22 = (bf16[64,2048]{1,0:T(8,128)(2,1)S(1)}, bf16[64,2048]{1,0:T(8,128)(2,1)S(1)}, u32[]{:S(2)}, u32[]{:S(2)}) collective-permute-start(bf16[64,2048]{1,0:T(8,128)(2,1)S(1)} %pad_maximum_fusion.refs_0_), channel_id=1, source_target_pairs={{0,192},{1,49},{2,194},{3,51},{4,196},{5,53},{6,198},{7,55},{8,200... | collective-permute-start | bytes 786440 | tf_op jit(solution)/shard_map/ppermute | solution.py:53
  91.5 10.5 %collective-permute-start.25 = (bf16[64,2048]{1,0:T(8,128)(2,1)S(1)}, bf16[64,2048]{1,0:T(8,128)(2,1)S(1)}, u32[]{:S(2)}, u32[]{:S(2)}) collective-permute-start(bf16[64,2048]{1,0:T(8,128)(2,1)S(1)} %pad_maximum_fusion.refs_0_), channel_id=1, source_target_pairs={{0,1},{1,0},{2,3},{3,2},{4,5},{5,4},{6,7},{7,6},{8,9},{9,8},{10,11... | collective-permute-start | bytes 786440 | tf_op jit(solution)/shard_map/ppermute | solution.py:53
  95.0 7.0 %collective-permute-start.26 = (bf16[64,2048]{1,0:T(8,128)(2,1)S(1)}, bf16[64,2048]{1,0:T(8,128)(2,1)S(1)}, u32[]{:S(2)}, u32[]{:S(2)}) collective-permute-start(bf16[64,2048]{1,0:T(8,128)(2,1)S(1)} %collective-permute-done.22.refs_1_), channel_id=1, source_target_pairs={{0,1},{1,0},{2,3},{3,2},{4,5},{5,4},{6,7},{7,6},{8,9},{9,8},{10,11... | collective-permute-start | bytes 786440 | tf_op jit(solution)/shard_map/ppermute | solution.py:53
  99.6 2.5 %collective-permute-start.27 = (bf16[64,2048]{1,0:T(8,128)(2,1)S(1)}, bf16[64,2048]{1,0:T(8,128)(2,1)S(1)}, u32[]{:S(2)}, u32[]{:S(2)}) collective-permute-start(bf16[64,2048]{1,0:T(8,128)(2,1)S(1)} %collective-permute-done.23.refs_2_), channel_id=1, source_target_pairs={{0,1},{1,0},{2,3},{3,2},{4,5},{5,4},{6,7},{7,6},{8,9},{9,8},{10,11... | collective-permute-start | bytes 786440 | tf_op jit(solution)/shard_map/ppermute | solution.py:53
  99.6 2.5 %collective-permute-start.28 = (bf16[64,2048]{1,0:T(8,128)(2,1)S(1)}, bf16[64,2048]{1,0:T(8,128)(2,1)S(1)}, u32[]{:S(2)}, u32[]{:S(2)}) collective-permute-start(bf16[64,2048]{1,0:T(8,128)(2,1)S(1)} %collective-permute-done.24.refs_3_), channel_id=1, source_target_pairs={{0,1},{1,0},{2,3},{3,2},{4,5},{5,4},{6,7},{7,6},{8,9},{9,8},{10,11... | collective-permute-start | bytes 786440 | tf_op jit(solution)/shard_map/ppermute | solution.py:53

commit v6 on v5

v6 whole, which is shorter than its diff:
```python
import functools
import math

import jax
import jax.numpy as jnp
import numpy as np
from jax import lax
from jax.experimental import pallas as pl
from jax.experimental.pallas import tpu as pltpu
from jax.sharding import PartitionSpec as P

HEADS = 8
LEV, ROWS, COLS = 4, 6, 24
WL, WR, WC = 2, 6, 12
D = 512
SPAN = WL * WR * WC
TOK = LEV * ROWS * COLS
BOTH = ("lat", "lon")
f32 = jnp.float32
bf16 = jnp.bfloat16
VMEM = 24 * 1024 * 1024


def index_of(y, x, z, c):
    return (y * 2 + x // 2) * 32 + (x % 2) * 16 + z * 2 + c


def place_of(i):
    return i // 64, ((i // 32) % 2) * 2 + (i // 16) % 2, (i // 2) % 8, i % 2


def route(step):
    return [(i, index_of(*step(*place_of(i)))) for i in range(256)]


def to_sibling(y, x, z, c):
    return y, x, z, 1 - c


def first_axis(k):
    return lambda y, x, z, c: ((y + k) % 4, x, z, c) if c == 0 else (y, (x + k) % 4, z, c)


def second_axis(k):
    return lambda y, x, z, c: (y, (x + k) % 4, z, c) if c == 0 else ((y + k) % 4, x, z, c)


def flip_z(k):
    return lambda y, x, z, c: (y, x, z ^ k, c)


def send(x, step):
    return lax.ppermute(x, BOTH, route(step))


def shifted(dlat, dlon):
    def pairs():
        out = []
        for i in range(256):
            a, b = i // 32, i % 32
            out.append((i, ((a + dlat) % 8) * 32 + (b + dlon) % 32))
        return out

    return pairs()


GTOK = TOK // 2
LAT, SIDE = 112, 48
HALO = LAT + 2 * SIDE
LEVELS = ((1, 2), (3, 0))


def gather_tables():
    local = np.zeros((GTOK, GTOK), np.float32)
    halo = np.zeros((GTOK, HALO), np.float32)
    for lev in range(WL):
        for rr in range(ROWS):
            for cr in range(COLS):
                t = cr // WC * SPAN + lev * WR * WC + rr * WC + cr % WC
                r, c = rr + 3, cr + 6
                if r < ROWS and c < COLS:
                    local[t, lev * ROWS * COLS + r * COLS + c] = 1
                elif c < COLS:
                    halo[t, lev * 54 + (r - ROWS) * 18 + c - 6] = 1
                elif r < ROWS:
                    halo[t, LAT + lev * 18 + (r - 3) * 6 + c - COLS] = 1
                else:
                    halo[t, LAT + SIDE + lev * 18 + (r - ROWS) * 6 + c - COLS] = 1
    return local, halo


def select_table():
    select = np.zeros((HALO, GTOK), np.float32)
    for lev in range(WL):
        for r in range(ROWS):
            for c in range(COLS):
                t = lev * ROWS * COLS + r * COLS + c
                if r < 3 and c >= 6:
                    select[lev * 54 + r * 18 + c - 6, t] = 1
                elif r >= 3 and c < 6:
                    select[LAT + lev * 18 + (r - 3) * 6 + c, t] = 1
                elif r < 3:
                    select[LAT + SIDE + lev * 18 + r * 6 + c, t] = 1
    return select


def dot(a, b, dims=((1,), (0,))):
    return lax.dot_general(a, b, (dims, ((), ())), preferred_element_type=f32)


NT = ((1,), (1,))
TN = ((0,), (0,))


def normalise(x):
    centred = x - jnp.mean(x, axis=-1, keepdims=True)
    rstd = lax.rsqrt(jnp.mean(centred * centred, axis=-1, keepdims=True) + 1e-5)
    return centred * rstd, rstd


def split(rows, lat, lon, diag):
    lat[...] = rows[:LAT].astype(bf16)
    lon[...] = rows[LAT : LAT + SIDE].astype(bf16)
    diag[...] = rows[LAT + SIDE :].astype(bf16)


def fetch(group, f_hbm, c_hbm, fc, sem):
    copies = []
    for k, level in enumerate(LEVELS[group]):
        for n, source in enumerate((f_hbm, c_hbm)):
            copies.append(
                pltpu.make_async_copy(
                    source.at[pl.ds(level * 144, 144)],
                    fc.at[pl.ds(k * 144, 144), pl.ds(n * D, D)],
                    sem.at[2 * k + n],
                )
            )
    return copies


def pack0_kernel(f_hbm, c_hbm, s_hbm, fc, select, lat, lon, diag, sem):
    copies = fetch(0, f_hbm, c_hbm, fc, sem)
    copies.append(pltpu.make_async_copy(s_hbm, select, sem.at[4]))
    for copy in copies:
        copy.start()
    for copy in copies:
        copy.wait()
    split(dot(select[...], fc[...]), lat, lon, diag)


def load_kernel(fc0, select, *refs):
    f_hbm, c_hbm, sources, targets = refs[0], refs[1], refs[2:7], refs[7:12]
    fc1, lat, lon, diag, part0, part1, fetch_sem, sem = refs[12:]
    fetches = fetch(1, f_hbm, c_hbm, fc1, fetch_sem)
    copies = [
        pltpu.make_async_copy(a, b, sem.at[i]) for i, (a, b) in enumerate(zip(sources, targets))
    ]
    for copy in fetches + copies:
        copy.start()
    for copy in fetches:
        copy.wait()
    split(dot(select[...], fc1[...]), lat, lon, diag)
    copies[0].wait()
    part0[...] = dot(targets[0][...], fc0[...]).astype(bf16)
    part1[...] = dot(targets[0][...], fc1[...]).astype(bf16)
    for copy in copies[1:]:
        copy.wait()


FACTOR = 1.0 / math.sqrt(D // HEADS)


def head_mask(heads, value):
    shape = (heads * SPAN, heads * 64)
    row = lax.broadcasted_iota(jnp.int32, shape, 0)
    first = lax.broadcasted_iota(jnp.int32, shape, 1) // 64 * SPAN
    return jnp.where((row >= first) & (row < first + SPAN), value, 0.0).astype(bf16)


def joined(r, heads, factor=1.0):
    lane = lax.broadcasted_iota(jnp.int32, (SPAN, heads * 64), 1)
    out = r[:SPAN]
    for h in range(1, heads):
        out = jnp.where(lane >= h * 64, r[h * SPAN : (h + 1) * SPAN], out)
    return (out * factor).astype(bf16)


def repeated(x, heads, pick):
    return jnp.concatenate([x] * heads, axis=0) * pick


def attend_kernel(group, place, *refs):
    part, table, lat, lon, diag, gain, w_ref, o_ref = refs[:8]
    if group == 0:
        normed, ctw, mixed, gact, qkv, gm, probs = refs[8:]
    else:
        (normed0, ctw0, mixed0, gact0, mixed, gact, own, other, normed, ctw, qkv, gm, probs, acc) = refs[8:]
    rows = jnp.concatenate([lat[...], lon[...], diag[...]], axis=0)
    tokens = part[...].astype(f32) + dot(table[...], rows)
    xhat, _ = normalise(tokens[:, :D])
    normed[...] = (xhat * gain[...]).astype(bf16)
    qkv[...] = dot(normed[...], w_ref[...]).astype(bf16)
    ctw[...] = tokens[:, D:].astype(bf16)
    gm[...] = dot(ctw[...], o_ref[...], NT).astype(bf16)

    tq = lax.rem(lax.broadcasted_iota(jnp.int32, (SPAN, 2 * SPAN), 1), SPAN)
    tk = lax.broadcasted_iota(jnp.int32, (SPAN, 2 * SPAN), 0)

    def lev_of(t):
        return (t >= SPAN // 2).astype(jnp.int32)

    def half_of(t):
        return (t - SPAN // 2 * lev_of(t) >= SPAN // 4).astype(jnp.int32)

    differ = jnp.abs(half_of(tq) - half_of(tk)) * place[0]
    if group == 1:
        differ = differ + jnp.abs(lev_of(tq) - lev_of(tk))
    same = differ == 0

    pair = head_mask(2, FACTOR)
    for w in range(2):
        at = pl.ds(w * SPAN, SPAN)
        for p in range(HEADS // 2):
            cols = pl.ds(128 * p, 128)
            q = repeated(qkv[at, cols], 2, pair)
            k = qkv[at, pl.ds(D + 128 * p, 128)]
            v = qkv[at, pl.ds(2 * D + 128 * p, 128)]
            s = jnp.where(same, dot(k, q, NT), -1000000000.0)
            e = jnp.exp(s - jnp.max(s, axis=0, keepdims=True))
            rounded = (e * (1.0 / jnp.sum(e, axis=0, keepdims=True))).astype(bf16)
            probs[pl.ds((w * 2 + p // 2) * SPAN, SPAN), pl.ds(p % 2 * 2 * SPAN, 2 * SPAN)] = rounded
            mixed[at, cols] = joined(dot(rounded, v, TN), 2)

    four = head_mask(4, 1.0)
    scaled = head_mask(4, FACTOR)
    for w in range(2):
        at = pl.ds(w * SPAN, SPAN)
        for p in range(HEADS // 4):
            cols = pl.ds(256 * p, 256)
            q = repeated(qkv[at, cols], 4, scaled)
            g = repeated(gm[at, cols], 4, four)
            k = qkv[at, pl.ds(D + 256 * p, 256)]
            v = qkv[at, pl.ds(2 * D + 256 * p, 256)]
            rounded = probs[pl.ds((w * 2 + p) * SPAN, SPAN), :]
            gact[at, pl.ds(2 * D + 256 * p, 256)] = dot(rounded, g).astype(bf16)
            dp = dot(v, g, NT)
            pr = rounded.astype(f32)
            inner = jnp.sum(dp * pr, axis=0, keepdims=True)
            ds = (pr * (dp - inner)).astype(bf16)
            gact[at, cols] = joined(dot(ds, k, TN), 4, FACTOR)
            gact[at, pl.ds(D + 256 * p, 256)] = dot(ds, q).astype(bf16)

    if group == 0:
        return

    def both(a, b):
        return jnp.concatenate([a[...], b[...]], axis=0)

    acc[:, : 3 * D] = dot(both(normed0, normed), both(gact0, gact), TN)
    acc[:, 3 * D :] = dot(both(mixed0, mixed), both(ctw0, ctw), TN)
    y, x, c = place[1], place[2], place[3]

    def fill(out, core):
        d1 = jnp.where(core == 0, y, x)
        d2 = jnp.where(core == 0, x, y)
        for s1 in range(4):
            for s2 in range(4):
                r = core * 256 + lax.rem(d1 + s1, 4) * 64 + lax.rem(d2 + s2, 4) * 16
                rows = acc[pl.ds(pl.multiple_of(r, 16), 16), :]
                out[pl.ds((s1 * 4 + s2) * 16, 16), :] = rows.astype(bf16)

    fill(own, c)
    fill(other, 1 - c)


def back_kernel(
    mixed0, mixed1, gact0, gact1, w_ref, o_ref, table,
    both0, both1, to_lat0, to_lat1, to_lon, to_diag,
):
    for g, (mixed, gact, both, to_lat) in enumerate(
        ((mixed0, gact0, both0, to_lat0), (mixed1, gact1, both1, to_lat1))
    ):
        both[:, :D] = dot(mixed[...], o_ref[...]).astype(bf16)
        both[:, D:] = dot(gact[...], w_ref[...], NT).astype(bf16)
        side = pl.ds(g * SIDE, SIDE)
        split(dot(table[...], both[...], TN), to_lat, to_lon.at[side], to_diag.at[side])


def finish_kernel(
    fc0, fc1, both0, both1, r_lat0, r_lat1, r_lon, r_diag, table, select, gain, out, grad
):
    for g, (fc, both, r_lat) in enumerate(((fc0, both0, r_lat0), (fc1, both1, r_lat1))):
        side = pl.ds(g * SIDE, SIDE)
        rows = jnp.concatenate([r_lat[...], r_lon[side, :], r_diag[side, :]], axis=0)
        grid = dot(table[...], both[...], TN) + dot(select[...], rows, TN)
        x = fc[:, :D].astype(f32)
        xhat, rstd = normalise(x)
        gs = grid[:, D:] * gain[...]
        first = jnp.mean(gs, axis=-1, keepdims=True)
        second = jnp.mean(gs * xhat, axis=-1, keepdims=True)
        result = (x + grid[:, :D]).astype(bf16)
        slope = (fc[:, D:].astype(f32) + rstd * (gs - first - xhat * second)).astype(bf16)
        for k, level in enumerate(LEVELS[g]):
            at = pl.ds(level * 144, 144)
            out[at, :] = result[k * 144 : (k + 1) * 144]
            grad[at, :] = slope[k * 144 : (k + 1) * 144]


def weights_kernel(side, place, *refs):
    pieces, refs = refs[:4], refs[4:]
    if side == 0:
        w_ref, g_qkv, g_out, g_total, buf_q, buf_o, sem = refs
    else:
        w_ref, before, gain, _, _, g_qkv, g_out, g_total, buf_q, buf_o, sem = refs
    y, x, c = place[1], place[2], place[3]
    core = c if side == 0 else 1 - c
    d1 = jnp.where(core == 0, y, x)
    d2 = jnp.where(core == 0, x, y)
    bands = [pl.multiple_of(core * 256 + lax.rem(d1 + i, 4) * 64, 64) for i in range(4)]
    copies = []
    for i in range(4):
        for s2 in range(4):
            at = pl.ds(pl.multiple_of(lax.rem(d2 + s2, 4) * 16, 16), 16)
            block = pieces[i][pl.ds(s2 * 16, 16), :].astype(f32)
            buf_q[i, at, :] = block[:, : 3 * D]
            buf_o[i, at, :] = block[:, 3 * D :]
        for k, (src, dst) in enumerate(((buf_q, g_qkv), (buf_o, g_out))):
            copy = pltpu.make_async_copy(src.at[i], dst.at[pl.ds(bands[i], 64)], sem.at[i, k])
            copy.start()
            copies.append(copy)
    total = jnp.zeros((1, D), f32) if side == 0 else before[...]
    lane = lax.broadcasted_iota(jnp.int32, (64, D), 1)
    local = lax.broadcasted_iota(jnp.int32, (64, D), 0)
    for i in range(4):
        w = w_ref[pl.ds(bands[i], 64), :].astype(f32)
        sums = jnp.sum(buf_q[i] * w, axis=1, keepdims=True)
        spread = jnp.where(lane == local + bands[i], sums, 0.0)
        total = total + jnp.sum(spread, axis=0, keepdims=True)
    g_total[...] = total if side == 0 else total / gain[...]
    for copy in copies:
        copy.wait()


def to_weights(side, place, pieces, qkv_weight, *more):
    inside = pl.BlockSpec(memory_space=pltpu.VMEM)
    anywhere = pl.BlockSpec(memory_space=pl.ANY)
    extra = [] if side == 0 else [inside, inside, anywhere, anywhere]
    return pl.pallas_call(
        functools.partial(weights_kernel, side),
        out_shape=[
            shape(D, 3 * D, dtype=f32),
            shape(D, D, dtype=f32),
            (vshape if side == 0 else shape)(1, D, dtype=f32),
        ],
        in_specs=spec(5, True) + extra,
        out_specs=[anywhere, anywhere, inside],
        scratch_shapes=[
            pltpu.VMEM((4, 64, 3 * D), f32),
            pltpu.VMEM((4, 64, D), f32),
            pltpu.SemaphoreType.DMA((4, 2)),
        ],
        input_output_aliases={} if side == 0 else {8: 0, 9: 1},
        compiler_params=params(),
        cost_estimate=cost(10**7, 4 * 10**6),
        name="weights" + str(side),
    )(place, *vms(*pieces), vm(qkv_weight), *more)


def params():
    return pltpu.CompilerParams(vmem_limit_bytes=VMEM)


def vm(x):
    return pltpu.with_memory_space_constraint(x, pltpu.VMEM)


def vms(*xs):
    return [vm(x) for x in xs]


def vshape(*dims, dtype=bf16):
    return pltpu.VMEM(dims, dtype)


def spec(count, scalar=False):
    whole = [pl.BlockSpec(memory_space=pltpu.VMEM)] * count
    return ([pl.BlockSpec(memory_space=pltpu.SMEM)] if scalar else []) + whole


def shape(*dims, dtype=bf16):
    return jax.ShapeDtypeStruct(dims, dtype)


def cost(flops, moved):
    return pl.CostEstimate(flops=flops, bytes_accessed=moved, transcendentals=0)


def hbm(*xs):
    return [pltpu.with_memory_space_constraint(x, pltpu.HBM) for x in xs]


def kernel_call(body, name, args, outs, in_hbm=0, place=None, scratch=(), price=(10**6, 10**4)):
    if in_hbm > 0:
        specs = [pl.BlockSpec(memory_space=pltpu.HBM)] * in_hbm + spec(len(args) - in_hbm)
        args = hbm(*args[:in_hbm]) + vms(*args[in_hbm:])
    else:
        specs = spec(len(args) + in_hbm) + [pl.BlockSpec(memory_space=pltpu.HBM)] * -in_hbm
        args = vms(*args[: len(args) + in_hbm]) + hbm(*args[len(args) + in_hbm :])
    if place is not None:
        specs = spec(0, True) + specs
        args = [place] + args
    return pl.pallas_call(
        body,
        out_shape=outs,
        in_specs=specs,
        out_specs=spec(len(outs)),
        scratch_shapes=list(scratch),
        compiler_params=params(),
        cost_estimate=cost(*price),
        name=name,
    )(*args)


def message_shapes():
    return [vshape(LAT, 2 * D), vshape(SIDE, 2 * D), vshape(SIDE, 2 * D)]


def to_pack0(f, c, select):
    return kernel_call(
        pack0_kernel, "pack0", (f, c, select),
        [vshape(GTOK, 2 * D), vshape(HALO, GTOK)] + message_shapes(),
        in_hbm=3, scratch=[pltpu.SemaphoreType.DMA((5,))],
    )


def to_load(fc0, select, f, c, *sources):
    return kernel_call(
        load_kernel, "load", (fc0, select, f, c, *sources),
        [vshape(*x.shape, dtype=x.dtype) for x in sources]
        + [vshape(GTOK, 2 * D)] + message_shapes() + [vshape(GTOK, 2 * D)] * 2,
        in_hbm=-2 - len(sources),
        scratch=[pltpu.SemaphoreType.DMA((4,)), pltpu.SemaphoreType.DMA((len(sources),))],
    )


def to_attend(group, place, *args):
    kept = [vshape(GTOK, D), vshape(GTOK, D)]
    results = [vshape(GTOK, D), vshape(GTOK, 3 * D)]
    inner = [
        pltpu.VMEM((GTOK, 3 * D), bf16),
        pltpu.VMEM((GTOK, D), bf16),
        pltpu.VMEM((4 * SPAN, 4 * SPAN), bf16),
    ]
    if group == 0:
        outs, scratch = kept + results, inner
    else:
        outs = results + [vshape(256, 4 * D), vshape(256, 4 * D)]
        scratch = [pltpu.VMEM((GTOK, D), bf16)] * 2 + inner + [pltpu.VMEM((D, 4 * D), f32)]
    return kernel_call(
        functools.partial(attend_kernel, group), "attend" + str(group), args, outs,
        place=place, scratch=scratch,
    )


def to_back(*args):
    return kernel_call(
        back_kernel, "back", args,
        [vshape(GTOK, 2 * D)] * 2 + [vshape(LAT, 2 * D)] * 2 + [vshape(2 * SIDE, 2 * D)] * 2,
        price=(2 * 10**9, 5 * 10**6),
    )


def to_finish(*args):
    return kernel_call(
        finish_kernel, "finish", args, [shape(TOK, D)] * 2, price=(2 * 10**9, 8 * 10**6)
    )


def add(*xs):
    total = xs[0].astype(f32)
    for x in xs[1:]:
        total = total + x.astype(f32)
    return total.astype(bf16)


def tied(x):
    return lax.optimization_barrier(x)


def halo_in(lat, lon, diag):
    return (
        lax.ppermute(lat, BOTH, shifted(-1, 0)),
        lax.ppermute(lon, BOTH, shifted(0, -1)),
        lax.ppermute(diag, BOTH, shifted(-1, -1)),
    )


def on_device(fields, cotangent, layer_norm_gain, qkv_weight, out_weight):
    a, b = lax.axis_index("lat"), lax.axis_index("lon")
    place = jnp.stack(
        [
            (a == 7).astype(jnp.int32),
            (a // 2).astype(jnp.int32),
            ((a % 2) * 2 + b // 16).astype(jnp.int32),
            (b % 2).astype(jnp.int32),
        ]
    )
    tables = [jnp.asarray(t, bf16) for t in gather_tables()]
    select = jnp.asarray(select_table(), bf16)
    f, c = fields.reshape(TOK, D), cotangent.reshape(TOK, D)
    fc0, select, *parts = to_pack0(f, c, select)
    halo0 = halo_in(*parts)
    local, table, w, o, gain, fc1, lat1, lon1, diag1, part0, part1 = to_load(
        fc0, select, f, c, *tables, qkv_weight, out_weight, layer_norm_gain.reshape(1, D)
    )
    lat1, lon1, diag1, near, far = tied((lat1, lon1, diag1, *halo0[1:]))
    halo0, halo1 = (halo0[0], near, far), halo_in(lat1, lon1, diag1)
    normed0, ctw0, mixed0, gact0 = to_attend(0, place, part0, table, *halo0, gain, w, o)
    mixed1, gact1, own, other = to_attend(
        1, place, part1, table, *halo1, gain, w, o, normed0, ctw0, mixed0, gact0
    )

    there = send(other, to_sibling)
    part = [add(own[64 * k : 64 * k + 64], there[64 * k : 64 * k + 64]) for k in range(4)]
    mixed1, part = tied((mixed1, part))
    both0, both1, to_lat0, to_lat1, to_lon, to_diag = to_back(
        mixed0, mixed1, gact0, gact1, w, o, table
    )
    recv = [send(part[k], first_axis(k)) for k in (1, 2, 3)]
    recv, to_lat0 = tied((recv, to_lat0))
    part = add(part[0], *recv)
    part, to_lat0, to_lat1, to_lon, to_diag = tied((part, to_lat0, to_lat1, to_lon, to_diag))
    part = add(part[:16], *[send(part[16 * k : 16 * k + 16], second_axis(k)) for k in (1, 2, 3)])
    r_lat0 = lax.ppermute(to_lat0, BOTH, shifted(1, 0))
    r_lat1 = lax.ppermute(to_lat1, BOTH, shifted(1, 0))
    r_lon = lax.ppermute(to_lon, BOTH, shifted(0, 1))
    r_diag = lax.ppermute(to_diag, BOTH, shifted(1, 1))
    recv = send(part, flip_z(1))
    recv, r_lat0 = tied((recv, r_lat0))
    part = add(part, recv)
    recv = send(part, flip_z(2))
    recv, r_lat1 = tied((recv, r_lat1))
    part = add(part, recv)
    recv = send(part, flip_z(6))
    recv, r_lon, r_diag = tied((recv, r_lon, r_diag))
    part = add(part, recv)

    block = jnp.concatenate([part] + [send(part, second_axis(4 - s)) for s in (1, 2, 3)], axis=0)
    mine = [send(block, first_axis(4 - s)) for s in (1, 2, 3)]
    out, grad = to_finish(
        fc0, fc1, both0, both1, r_lat0, r_lat1, r_lon, r_diag, local, select, gain
    )
    mine, out = tied((mine, out))
    mine = [block] + mine
    sibling = [send(m, to_sibling) for m in mine]
    g_qkv, g_out, total = to_weights(0, place, mine, w)
    g_qkv, g_out, g_gain = to_weights(1, place, sibling, w, vm(total), vm(gain), g_qkv, g_out)

    grid = (LEV, ROWS, COLS, D)
    return out.reshape(grid), grad.reshape(grid), g_qkv, g_out, g_gain.reshape(D)


def solution(mesh):
    return jax.shard_map(
        on_device,
        mesh=mesh,
        in_specs=(P(None, "lat", "lon", None), P(None, "lat", "lon", None), P(), P(), P()),
        out_specs=(P(None, "lat", "lon", None), P(None, "lat", "lon", None), P(), P(), P()),
        check_vma=False,
    )
```

time: 105 us -> 117 us (1.11)
  local copies, waits for them, and re-layouts: 0.02 us -> 6.22 us
  waiting for transfers between devices: 18.1 us -> 20.3 us
  Pallas kernels: 24.9 us -> 26.5 us
  starting transfers between devices: 60.2 us -> 61.8 us
    unnamed x0 -> x24, local copies, waits for them, and re-layouts: none -> 6.2 us
    ppermute x1, starting transfers between devices: 5.1 us -> 0.01 us  [on_device(): r_diag = lax.ppermute(to_diag, BOTH, shifted(1, 1))]
    ppermute x1, waiting for transfers between devices: 1.37 us -> 4.95 us  [on_device(): r_diag = lax.ppermute(to_diag, BOTH, shifted(1, 1))]
    ppermute x1 -> x2, starting transfers between devices: 2.59 us -> 6.06 us  [the longest x1 3.05 us: on_device(): r_lat1 = lax.ppermute(to_lat1, BOTH, shifted(1, 0))]
    ppermute x2, starting transfers between devices: 6.33 us -> 3.16 us  [halo_in(): lax.ppermute(lat, BOTH, shifted(-1, 0))]
    ppermute x1 -> x2, waiting for transfers between devices: 5.71 us -> 2.8 us  [the longest x1 1.53 us: on_device(): r_lat0 = lax.ppermute(to_lat0, BOTH, shifted(1, 0))]
    ppermute x1, starting transfers between devices: 2.52 us -> 5.15 us  [on_device(): r_lon = lax.ppermute(to_lon, BOTH, shifted(0, 1))]
    ppermute x2, starting transfers between devices: 1.4 us -> 3.47 us  [halo_in(): lax.ppermute(lon, BOTH, shifted(0, -1))]
  transfers between devices with their start and end apart: 29 -> 30, of which waited for: 10 -> 11; matrix products, arithmetic and copies ran while one was open for 0% -> 0% of each run, Pallas kernels for 13% -> 13%
where the time goes in v6:
time: 117 us
  starting transfers between devices  61.8 us (53%)
  Pallas kernels  26.5 us (23%)
  waiting for transfers between devices  20.3 us (17%)
  local copies, waits for them, and re-layouts  6.22 us (5%)
    ppermute x20, starting transfers between devices, send(): return lax.ppermute(x, BOTH, route(step))  32.7 us
    pallas_call x6, Pallas kernels, kernel_call(): pl.pallas_call(body, out_shape=outs, in_specs=specs, out_specs=spec(len(o...  22 us
    ppermute x20, waiting for transfers between devices, send(): return lax.ppermute(x, BOTH, route(step))  12.5 us
    ppermute x2, starting transfers between devices, halo_in(): lax.ppermute(diag, BOTH, shifted(-1, -1))  11.3 us
    unnamed x24, local copies, waits for them, and re-layouts  6.2 us
    ppermute x1, starting transfers between devices, on_device(): r_lon = lax.ppermute(to_lon, BOTH, shifted(0, 1))  5.15 us
    ppermute x1, waiting for transfers between devices, on_device(): r_diag = lax.ppermute(to_diag, BOTH, shifted(1, 1))  4.95 us
    pallas_call x2, Pallas kernels, to_weights(): pl.pallas_call(functools.partial(weights_kernel, side), out_shape=[shape(...  4.51 us
  transfers between devices with their start and end apart: 30, of which 11 were waited for; matrix products, arithmetic and copies ran while one was open for 0% of the time, Pallas kernels for 13%

profile of v6, /device:TPU:1, one launch (start us, length us, event | category | flops | bytes accessed | tf_op | source)
XLA Modules:
  0.0 116.5 jit_solution(4207479315895494473)
XLA Ops:
  0.6 2.3 %pack0.1 = (bf16[288,1024]{1,0:T(8,128)(2,1)S(1)}, bf16[208,288]{1,0:T(8,128)(2,1)S(1)}, bf16[112,1024]{1,0:T(8,128)(2,1)}, bf16[48,1024]{1,0:T(8,128)(2,1)S(1)}, bf16[48,1024]{1,0:T(8,128)(2,1)S(1)}) custom-call(bf16[576,512]{1,0:T(8,128)(2,1)} %bitcast.10, bf16[576,512]{1,0:T(8,128)(2,1)} %bitcast.12, bf16[208,288]{1,0:T(8,128)(2,1)} %constant.58.clone.s_hbm), custom_call_target="tpu_custom_call" | custom-call | flops 1000000 | bytes 10000 | tf_op jit(solution)/shard_map/pack0/pallas_call | solution.py:412
  2.9 3.3 %collective-permute-start = (bf16[48,1024]{1,0:T(8,128)(2,1)S(1)}, bf16[48,1024]{1,0:T(8,128)(2,1)S(1)}, u32[]{:S(2)}, u32[]{:S(2)}) collective-permute-start(bf16[48,1024]{1,0:T(8,128)(2,1)S(1)} %get-tuple-element.80), channel_id=1, source_target_pairs={{0,31},{1,0},{2,1},{3,2},{4,3},{5,4},{6,5},{7,6},{8,7},{9,8},{10,9... | collective-permute-start | bytes 294920 | tf_op jit(solution)/shard_map/ppermute | solution.py:493
  6.3 9.3 %collective-permute-start.1 = (bf16[48,1024]{1,0:T(8,128)(2,1)S(1)}, bf16[48,1024]{1,0:T(8,128)(2,1)S(1)}, u32[]{:S(2)}, u32[]{:S(2)}) collective-permute-start(bf16[48,1024]{1,0:T(8,128)(2,1)S(1)} %get-tuple-element.81), channel_id=1, source_target_pairs={{0,255},{1,224},{2,225},{3,226},{4,227},{5,228},{6,229},{7,230},{8... | collective-permute-start | bytes 294920 | tf_op jit(solution)/shard_map/ppermute | solution.py:494
  16.1 3.8 %load.1 = (bf16[288,288]{1,0:T(8,128)(2,1)S(1)}, bf16[288,208]{1,0:T(8,128)(2,1)S(1)}, bf16[512,1536]{1,0:T(8,128)(2,1)S(1)}, bf16[512,512]{1,0:T(8,128)(2,1)S(1...) custom-call(bf16[288,1024]{1,0:T(8,128)(2,1)S(1)} %get-tuple-element, ...), custom_call_target="tpu_custom_call" | custom-call | flops 1000000 | bytes 10000 | tf_op jit(solution)/shard_map/load/pallas_call | solution.py:412
  24.1 2.7 %collective-permute-start.2 = (bf16[112,1024]{1,0:T(8,128)(2,1)}, bf16[112,1024]{1,0:T(8,128)(2,1)}, u32[]{:S(2)}, u32[]{:S(2)}) collective-permute-start(bf16[112,1024]{1,0:T(8,128)(2,1)} %get-tuple-element.82), channel_id=1, source_target_pairs={{0,224},{1,225},{2,226},{3,227},{4,228},{5,229},{6,230},{7,231},{8... | collective-permute-start | bytes 688136 | tf_op jit(solution)/shard_map/ppermute | solution.py:492
  27.0 2.0 %collective-permute-start.4 = (bf16[48,1024]{1,0:T(8,128)(2,1)}, bf16[48,1024]{1,0:T(8,128)(2,1)S(1)}, u32[]{:S(2)}, u32[]{:S(2)}) collective-permute-start(bf16[48,1024]{1,0:T(8,128)(2,1)} %copy-done.10), channel_id=1, source_target_pairs={{0,255},{1,224},{2,225},{3,226},{4,227},{5,228},{6,229},{7,230},{8... | collective-permute-start | bytes 294920 | tf_op jit(solution)/shard_map/ppermute | solution.py:494
  31.0 4.9 %attend0.1 = (bf16[288,512]{1,0:T(8,128)(2,1)S(1)}, bf16[288,512]{1,0:T(8,128)(2,1)S(1)}, bf16[288,512]{1,0:T(8,128)(2,1)S(1)}, bf16[288,1536]{1,0:T(8,128)(2,1)S(1)}) custom-call(s32[4]{0:T(128)S(1)} %pad_add_fusion.place, bf16[288,1024]{1,0:T(8,128)(2,1)S(1)} %copy-done.1, bf16[288,208]{1,0:T(8,128)(2,1)S(1)} %get-tuple-element.76.refs_1_.table, ...), custom_call_target="tpu_custom_call" | custom-call | flops 1000000 | bytes 10000 | tf_op jit(solution)/shard_map/attend0/pallas_call | solution.py:412
  35.9 6.8 %attend1.1 = (bf16[288,512]{1,0:T(8,128)(2,1)S(1)}, bf16[288,1536]{1,0:T(8,128)(2,1)S(1)}, bf16[256,2048]{1,0:T(8,128)(2,1)S(1)}, bf16[256,2048]{1,0:T(8,128)(2,1)S(1)}) custom-call(s32[4]{0:T(128)S(1)} %pad_add_fusion.place, bf16[288,1024]{1,0:T(8,128)(2,1)S(1)} %get-tuple-element.75.refs_0_, bf16[288,208]{1,0:T(8,128)(2,1)S(1)} %get-tuple-element.76.refs_1_.table, ...), custom_call_target="tpu_custom_call" | custom-call | flops 1000000 | bytes 10000 | tf_op jit(solution)/shard_map/attend1/pallas_call | solution.py:412
  42.9 2.6 %collective-permute-done.6 = bf16[256,2048]{1,0:T(8,128)(2,1)S(1)} collective-permute-done((bf16[256,2048]{1,0:T(8,128)(2,1)S(1)}, bf16[256,2048]{1,0:T(8,128)(2,1)S(1)}, u32[]{:S(2)}, u32[]{:S(2)}) %collective-permute-start.6) | collective-permute-done | bytes 1048608 | tf_op jit(solution)/shard_map/ppermute | solution.py:53
  46.0 3.5 %collective-permute-start.8 = (bf16[64,2048]{1,0:T(8,128)(2,1)S(1)}, bf16[64,2048]{1,0:T(8,128)(2,1)S(1)}, u32[]{:S(2)}, u32[]{:S(2)}) collective-permute-start(bf16[64,2048]{1,0:T(8,128)(2,1)S(1)} %get-tuple-element.101), channel_id=1, source_target_pairs={{0,128},{1,33},{2,130},{3,35},{4,132},{5,37},{6,134},{7,39},{8,136... | collective-permute-start | bytes 786440 | tf_op jit(solution)/shard_map/ppermute | solution.py:53
  49.5 1.5 %collective-permute-start.9 = (bf16[64,2048]{1,0:T(8,128)(2,1)S(1)}, bf16[64,2048]{1,0:T(8,128)(2,1)S(1)}, u32[]{:S(2)}, u32[]{:S(2)}) collective-permute-start(bf16[64,2048]{1,0:T(8,128)(2,1)S(1)} %get-tuple-element.102), channel_id=1, source_target_pairs={{0,192},{1,49},{2,194},{3,51},{4,196},{5,53},{6,198},{7,55},{8,200... | collective-permute-start | bytes 786440 | tf_op jit(solution)/shard_map/ppermute | solution.py:53
  51.1 1.8 %back.1 = (bf16[288,1024]{1,0:T(8,128)(2,1)S(1)}, bf16[288,1024]{1,0:T(8,128)(2,1)S(1)}, bf16[112,1024]{1,0:T(8,128)(2,1)S(1)}, bf16[112,1024]{1,0:T(8,128)(2,1)...) custom-call(bf16[288,512]{1,0:T(8,128)(2,1)S(1)} %get-tuple-element.94.refs_10_.mixed0, ...), custom_call_target="tpu_custom_call" | custom-call | flops 2000000000 | bytes 5000000 | tf_op jit(solution)/shard_map/back/pallas_call | solution.py:412
  53.0 3.1 %collective-permute-done.8 = bf16[64,2048]{1,0:T(8,128)(2,1)S(1)} collective-permute-done((bf16[64,2048]{1,0:T(8,128)(2,1)S(1)}, bf16[64,2048]{1,0:T(8,128)(2,1)S(1)}, u32[]{:S(2)}, u32[]{:S(2)}) %collective-permute-start.8) | collective-permute-done | bytes 262176 | tf_op jit(solution)/shard_map/ppermute | solution.py:53
  56.3 1.1 collective-permute-start.10
  57.4 1.6 %collective-permute-start.12 = (bf16[16,2048]{1,0:T(8,128)(2,1)S(1)}, bf16[16,2048]{1,0:T(8,128)(2,1)S(1)}, u32[]{:S(2)}, u32[]{:S(2)}) collective-permute-start(bf16[16,2048]{1,0:T(8,128)(2,1)S(1)} %get-tuple-element.146), channel_id=1, source_target_pairs={{0,48},{1,193},{2,50},{3,195},{4,52},{5,197},{6,54},{7,199},{8,56}... | collective-permute-start | bytes 196616 | tf_op jit(solution)/shard_map/ppermute | solution.py:53
  59.2 3.0 %collective-permute-start.14 = (bf16[112,1024]{1,0:T(8,128)(2,1)S(1)}, bf16[112,1024]{1,0:T(8,128)(2,1)S(1)}, u32[]{:S(2)}, u32[]{:S(2)}) collective-permute-start(bf16[112,1024]{1,0:T(8,128)(2,1)S(1)} %get-tuple-element.114), channel_id=1, source_target_pairs={{0,32},{1,33},{2,34},{3,35},{4,36},{5,37},{6,38},{7,39},{8,40},{9,... | collective-permute-start | bytes 688136 | tf_op jit(solution)/shard_map/ppermute | solution.py:534
  62.3 1.4 %collective-permute-done.11 = bf16[16,2048]{1,0:T(8,128)(2,1)S(1)} collective-permute-done((bf16[16,2048]{1,0:T(8,128)(2,1)S(1)}, bf16[16,2048]{1,0:T(8,128)(2,1)S(1)}, u32[]{:S(2)}, u32[]{:S(2)}) %collective-permute-start.11) | collective-permute-done | bytes 65568 | tf_op jit(solution)/shard_map/ppermute | solution.py:53
  63.9 3.0 %collective-permute-start.16 = (bf16[112,1024]{1,0:T(8,128)(2,1)S(1)}, bf16[112,1024]{1,0:T(8,128)(2,1)S(1)}, u32[]{:S(2)}, u32[]{:S(2)}) collective-permute-start(bf16[112,1024]{1,0:T(8,128)(2,1)S(1)} %get-tuple-element.116), channel_id=1, source_target_pairs={{0,32},{1,33},{2,34},{3,35},{4,36},{5,37},{6,38},{7,39},{8,40},{9,... | collective-permute-start | bytes 688136 | tf_op jit(solution)/shard_map/ppermute | solution.py:535
  67.0 1.5 %collective-permute-done.14.r_lat0 = bf16[112,1024]{1,0:T(8,128)(2,1)S(1)} collective-permute-done((bf16[112,1024]{1,0:T(8,128)(2,1)S(1)}, bf16[112,1024]{1,0:T(8,128)(2,1)S(1)}, u32[]{:S(2)}, u32[]{:S(2)}) %collective-permute-start.14) | collective-permute-done | bytes 229408 | tf_op jit(solution)/shard_map/ppermute | solution.py:534
  68.7 5.2 %collective-permute-start.18 = (bf16[96,1024]{1,0:T(8,128)(2,1)S(1)}, bf16[96,1024]{1,0:T(8,128)(2,1)S(1)}, u32[]{:S(2)}, u32[]{:S(2)}) collective-permute-start(bf16[96,1024]{1,0:T(8,128)(2,1)S(1)} %get-tuple-element.118), channel_id=1, source_target_pairs={{0,1},{1,2},{2,3},{3,4},{4,5},{5,6},{6,7},{7,8},{8,9},{9,10},{10,1... | collective-permute-start | bytes 589832 | tf_op jit(solution)/shard_map/ppermute | solution.py:536
  73.8 1.3 %collective-permute-done.16.r_lat1 = bf16[112,1024]{1,0:T(8,128)(2,1)S(1)} collective-permute-done((bf16[112,1024]{1,0:T(8,128)(2,1)S(1)}, bf16[112,1024]{1,0:T(8,128)(2,1)S(1)}, u32[]{:S(2)}, u32[]{:S(2)}) %collective-permute-start.16) | collective-permute-done | bytes 229408 | tf_op jit(solution)/shard_map/ppermute | solution.py:535
  75.1 2.4 %collective-permute-start.17 = (bf16[16,2048]{1,0:T(8,128)(2,1)S(1)}, bf16[16,2048]{1,0:T(8,128)(2,1)S(1)}, u32[]{:S(2)}, u32[]{:S(2)}) collective-permute-start(bf16[16,2048]{1,0:T(8,128)(2,1)S(1)} %add_convert_fusion.6), channel_id=1, source_target_pairs={{0,12},{1,13},{2,14},{3,15},{4,8},{5,9},{6,10},{7,11},{8,4},{9,5},... | collective-permute-start | bytes 196616 | tf_op jit(solution)/shard_map/ppermute | solution.py:53
  77.6 5.0 %collective-permute-done.19.r_diag = bf16[96,1024]{1,0:T(8,128)(2,1)S(1)} collective-permute-done((bf16[96,1024]{1,0:T(8,128)(2,1)S(1)}, bf16[96,1024]{1,0:T(8,128)(2,1)S(1)}, u32[]{:S(2)}, u32[]{:S(2)}) %collective-permute-start.19) | collective-permute-done | bytes 196640 | tf_op jit(solution)/shard_map/ppermute | solution.py:537
  82.5 1.8 %collective-permute-done.17 = bf16[16,2048]{1,0:T(8,128)(2,1)S(1)} collective-permute-done((bf16[16,2048]{1,0:T(8,128)(2,1)S(1)}, bf16[16,2048]{1,0:T(8,128)(2,1)S(1)}, u32[]{:S(2)}, u32[]{:S(2)}) %collective-permute-start.17) | collective-permute-done | bytes 65568 | tf_op jit(solution)/shard_map/ppermute | solution.py:53
  84.5 3.9 %collective-permute-start.21 = (bf16[16,2048]{1,0:T(8,128)(2,1)S(1)}, bf16[16,2048]{1,0:T(8,128)(2,1)S(1)}, u32[]{:S(2)}, u32[]{:S(2)}) collective-permute-start(bf16[16,2048]{1,0:T(8,128)(2,1)S(1)} %add_convert_fusion.5), channel_id=1, source_target_pairs={{0,32},{1,129},{2,34},{3,131},{4,36},{5,133},{6,38},{7,135},{8,40}... | collective-permute-start | bytes 196616 | tf_op jit(solution)/shard_map/ppermute | solution.py:53
  88.9 1.9 %collective-permute-done.21 = bf16[16,2048]{1,0:T(8,128)(2,1)S(1)} collective-permute-done((bf16[16,2048]{1,0:T(8,128)(2,1)S(1)}, bf16[16,2048]{1,0:T(8,128)(2,1)S(1)}, u32[]{:S(2)}, u32[]{:S(2)}) %collective-permute-start.21) | collective-permute-done | bytes 65568 | tf_op jit(solution)/shard_map/ppermute | solution.py:53
  92.4 4.1 %collective-permute-start.24 = (bf16[64,2048]{1,0:T(8,128)(2,1)S(1)}, bf16[64,2048]{1,0:T(8,128)(2,1)S(1)}, u32[]{:S(2)}, u32[]{:S(2)}) collective-permute-start(bf16[64,2048]{1,0:T(8,128)(2,1)S(1)} %pad_maximum_fusion.refs_0_), channel_id=1, source_target_pairs={{0,128},{1,33},{2,130},{3,35},{4,132},{5,37},{6,134},{7,39},{8,136... | collective-permute-start | bytes 786440 | tf_op jit(solution)/shard_map/ppermute | solution.py:53
  96.5 2.3 %finish.1 = (bf16[576,512]{1,0:T(8,128)(2,1)}, bf16[576,512]{1,0:T(8,128)(2,1)}) custom-call(bf16[288,1024]{1,0:T(8,128)(2,1)S(1)} %get-tuple-element.73.fc0, bf16[288,1024]{1,0:T(8,128)(2,1)S(1)} %copy-done.7, bf16[288,1024]{1,0:T(8,128)(2,1)S(1)} %get-tuple-element.122.both0, bf16[288,1024]{1,0:T(8,128)(2,1)S(1)} %get-tuple-element.123.both1, ...), custom_call_target="tpu_custom_call" | custom-call | flops 2000000000 | bytes 8000000 | tf_op jit(solution)/shard_map/finish/pallas_call | solution.py:412
  98.8 6.7 %collective-permute-start.26 = (bf16[64,2048]{1,0:T(8,128)(2,1)S(1)}, bf16[64,2048]{1,0:T(8,128)(2,1)S(1)}, u32[]{:S(2)}, u32[]{:S(2)}) collective-permute-start(bf16[64,2048]{1,0:T(8,128)(2,1)S(1)} %pad_maximum_fusion.refs_0_), channel_id=1, source_target_pairs={{0,1},{1,0},{2,3},{3,2},{4,5},{5,4},{6,7},{7,6},{8,9},{9,8},{10,11... | collective-permute-start | bytes 786440 | tf_op jit(solution)/shard_map/ppermute | solution.py:53
  105.5 5.7 %collective-permute-start.27 = (bf16[64,2048]{1,0:T(8,128)(2,1)S(1)}, bf16[64,2048]{1,0:T(8,128)(2,1)S(1)}, u32[]{:S(2)}, u32[]{:S(2)}) collective-permute-start(bf16[64,2048]{1,0:T(8,128)(2,1)S(1)} %collective-permute-done.23.refs_1_), channel_id=1, source_target_pairs={{0,1},{1,0},{2,3},{3,2},{4,5},{5,4},{6,7},{7,6},{8,9},{9,8},{10,11... | collective-permute-start | bytes 786440 | tf_op jit(solution)/shard_map/ppermute | solution.py:53
  111.8 2.0 %weights0.1 = (f32[512,1536]{1,0:T(8,128)}, f32[512,512]{1,0:T(8,128)}, f32[1,512]{1,0:T(1,128)S(1)}) custom-call(s32[4]{0:T(128)S(1)} %pad_add_fusion.place, bf16[64,2048]{1,0:T(8,128)(2,1)S(1)} %pad_maximum_fusion.refs_0_, bf16[64,2048]{1,0:T(8,128)(2,1)S(1)} %collective-permute-done.23.refs_1_, bf16[64,2048]{1,0:T(8,128)(2,1)S(1)} %collective-permute-done.24.refs_2_, ...), custom_call_target="tpu_custom_call" | custom-call | flops 10000000 | bytes 4000000 | tf_op jit(solution)/shard_map/weights0/pallas_call | solution.py:348
  113.8 2.5 %weights1.1 = (f32[512,1536]{1,0:T(8,128)}, f32[512,512]{1,0:T(8,128)}, f32[1,512]{1,0:T(1,128)}) custom-call(s32[4]{0:T(128)S(1)} %pad_add_fusion.place, bf16[64,2048]{1,0:T(8,128)(2,1)S(1)} %collective-permute-done.26.refs_0_, bf16[64,2048]{1,0:T(8,128)(2,1)S(1)} %collective-permute-done.27.refs_1_, ...), custom_call_target="tpu_custom_call", output_to_operand_aliasing={{0}: (8, {}), {1}: (9, {})} | custom-call | flops 10000000 | bytes 4000000 | tf_op jit(solution)/shard_map/weights1/pallas_call | solution.py:348
  (69 shorter events, 11.2 us)
Async XLA Ops:
  2.9 20.6 %collective-permute-start = (bf16[48,1024]{1,0:T(8,128)(2,1)S(1)}, bf16[48,1024]{1,0:T(8,128)(2,1)S(1)}, u32[]{:S(2)}, u32[]{:S(2)}) collective-permute-start(bf16[48,1024]{1,0:T(8,128)(2,1)S(1)} %get-tuple-element.80), channel_id=1, source_target_pairs={{0,31},{1,0},{2,1},{3,2},{4,3},{5,4},{6,5},{7,6},{8,7},{9,8},{10,9... | collective-permute-start | bytes 294920 | tf_op jit(solution)/shard_map/ppermute | solution.py:493
  6.3 17.2 %collective-permute-start.1 = (bf16[48,1024]{1,0:T(8,128)(2,1)S(1)}, bf16[48,1024]{1,0:T(8,128)(2,1)S(1)}, u32[]{:S(2)}, u32[]{:S(2)}) collective-permute-start(bf16[48,1024]{1,0:T(8,128)(2,1)S(1)} %get-tuple-element.81), channel_id=1, source_target_pairs={{0,255},{1,224},{2,225},{3,226},{4,227},{5,228},{6,229},{7,230},{8... | collective-permute-start | bytes 294920 | tf_op jit(solution)/shard_map/ppermute | solution.py:494
  15.5 13.5 %collective-permute-start.5 = (bf16[112,1024]{1,0:T(8,128)(2,1)}, bf16[112,1024]{1,0:T(8,128)(2,1)}, u32[]{:S(2)}, u32[]{:S(2)}) collective-permute-start(bf16[112,1024]{1,0:T(8,128)(2,1)} %get-tuple-element.89), channel_id=1, source_target_pairs={{0,224},{1,225},{2,226},{3,227},{4,228},{5,229},{6,230},{7,231},{8... | collective-permute-start | bytes 688136 | tf_op jit(solution)/shard_map/ppermute | solution.py:492
  24.1 11.8 %collective-permute-start.2 = (bf16[112,1024]{1,0:T(8,128)(2,1)}, bf16[112,1024]{1,0:T(8,128)(2,1)}, u32[]{:S(2)}, u32[]{:S(2)}) collective-permute-start(bf16[112,1024]{1,0:T(8,128)(2,1)} %get-tuple-element.82), channel_id=1, source_target_pairs={{0,224},{1,225},{2,226},{3,227},{4,228},{5,229},{6,230},{7,231},{8... | collective-permute-start | bytes 688136 | tf_op jit(solution)/shard_map/ppermute | solution.py:492
  26.8 9.1 %collective-permute-start.3 = (bf16[48,1024]{1,0:T(8,128)(2,1)}, bf16[48,1024]{1,0:T(8,128)(2,1)S(1)}, u32[]{:S(2)}, u32[]{:S(2)}) collective-permute-start(bf16[48,1024]{1,0:T(8,128)(2,1)} %copy-done.11), channel_id=1, source_target_pairs={{0,31},{1,0},{2,1},{3,2},{4,3},{5,4},{6,5},{7,6},{8,7},{9,8},{10,9... | collective-permute-start | bytes 294920 | tf_op jit(solution)/shard_map/ppermute | solution.py:493
  27.0 9.0 %collective-permute-start.4 = (bf16[48,1024]{1,0:T(8,128)(2,1)}, bf16[48,1024]{1,0:T(8,128)(2,1)S(1)}, u32[]{:S(2)}, u32[]{:S(2)}) collective-permute-start(bf16[48,1024]{1,0:T(8,128)(2,1)} %copy-done.10), channel_id=1, source_target_pairs={{0,255},{1,224},{2,225},{3,226},{4,227},{5,228},{6,229},{7,230},{8... | collective-permute-start | bytes 294920 | tf_op jit(solution)/shard_map/ppermute | solution.py:494
  42.8 2.7 %collective-permute-start.6 = (bf16[256,2048]{1,0:T(8,128)(2,1)S(1)}, bf16[256,2048]{1,0:T(8,128)(2,1)S(1)}, u32[]{:S(2)}, u32[]{:S(2)}) collective-permute-start(bf16[256,2048]{1,0:T(8,128)(2,1)S(1)} %get-tuple-element.98), channel_id=1, source_target_pairs={{0,1},{1,0},{2,3},{3,2},{4,5},{5,4},{6,7},{7,6},{8,9},{9,8},{10,11... | collective-permute-start | bytes 3145736 | tf_op jit(solution)/shard_map/ppermute | solution.py:53
  45.9 7.1 %collective-permute-start.7 = (bf16[64,2048]{1,0:T(8,128)(2,1)S(1)}, bf16[64,2048]{1,0:T(8,128)(2,1)S(1)}, u32[]{:S(2)}, u32[]{:S(2)}) collective-permute-start(bf16[64,2048]{1,0:T(8,128)(2,1)S(1)} %get-tuple-element.100), channel_id=1, source_target_pairs={{0,64},{1,17},{2,66},{3,19},{4,68},{5,21},{6,70},{7,23},{8,72},{9,... | collective-permute-start | bytes 786440 | tf_op jit(solution)/shard_map/ppermute | solution.py:53
  46.0 10.1 %collective-permute-start.8 = (bf16[64,2048]{1,0:T(8,128)(2,1)S(1)}, bf16[64,2048]{1,0:T(8,128)(2,1)S(1)}, u32[]{:S(2)}, u32[]{:S(2)}) collective-permute-start(bf16[64,2048]{1,0:T(8,128)(2,1)S(1)} %get-tuple-element.101), channel_id=1, source_target_pairs={{0,128},{1,33},{2,130},{3,35},{4,132},{5,37},{6,134},{7,39},{8,136... | collective-permute-start | bytes 786440 | tf_op jit(solution)/shard_map/ppermute | solution.py:53
  49.5 6.6 %collective-permute-start.9 = (bf16[64,2048]{1,0:T(8,128)(2,1)S(1)}, bf16[64,2048]{1,0:T(8,128)(2,1)S(1)}, u32[]{:S(2)}, u32[]{:S(2)}) collective-permute-start(bf16[64,2048]{1,0:T(8,128)(2,1)S(1)} %get-tuple-element.102), channel_id=1, source_target_pairs={{0,192},{1,49},{2,194},{3,51},{4,196},{5,53},{6,198},{7,55},{8,200... | collective-permute-start | bytes 786440 | tf_op jit(solution)/shard_map/ppermute | solution.py:53
  52.9 43.6 %copy-start.3 = (bf16[208,288]{1,0:T(8,128)(2,1)S(1)}, bf16[208,288]{1,0:T(8,128)(2,1)}, u32[]{:S(2)}) copy-start(bf16[208,288]{1,0:T(8,128)(2,1)} %copy-done.2) | copy-start | bytes 359428
  52.9 43.6 %copy-start.7 = (bf16[288,1024]{1,0:T(8,128)(2,1)S(1)}, bf16[288,1024]{1,0:T(8,128)(2,1)}, u32[]{:S(2)}) copy-start(bf16[288,1024]{1,0:T(8,128)(2,1)} %copy-done.6) | copy-start | bytes 1769476
  56.3 6.0 %collective-permute-start.10 = (bf16[16,2048]{1,0:T(8,128)(2,1)S(1)}, bf16[16,2048]{1,0:T(8,128)(2,1)S(1)}, u32[]{:S(2)}, u32[]{:S(2)}) collective-permute-start(bf16[16,2048]{1,0:T(8,128)(2,1)S(1)} %get-tuple-element.145), channel_id=1, source_target_pairs={{0,16},{1,65},{2,18},{3,67},{4,20},{5,69},{6,22},{7,71},{8,24},{9,... | collective-permute-start | bytes 196616 | tf_op jit(solution)/shard_map/ppermute | solution.py:53
  57.4 4.9 %collective-permute-start.12 = (bf16[16,2048]{1,0:T(8,128)(2,1)S(1)}, bf16[16,2048]{1,0:T(8,128)(2,1)S(1)}, u32[]{:S(2)}, u32[]{:S(2)}) collective-permute-start(bf16[16,2048]{1,0:T(8,128)(2,1)S(1)} %get-tuple-element.146), channel_id=1, source_target_pairs={{0,48},{1,193},{2,50},{3,195},{4,52},{5,197},{6,54},{7,199},{8,56}... | collective-permute-start | bytes 196616 | tf_op jit(solution)/shard_map/ppermute | solution.py:53
  59.0 4.6 %collective-permute-start.11 = (bf16[16,2048]{1,0:T(8,128)(2,1)S(1)}, bf16[16,2048]{1,0:T(8,128)(2,1)S(1)}, u32[]{:S(2)}, u32[]{:S(2)}) collective-permute-start(bf16[16,2048]{1,0:T(8,128)(2,1)S(1)} %get-tuple-element.147), channel_id=1, source_target_pairs={{0,32},{1,129},{2,34},{3,131},{4,36},{5,133},{6,38},{7,135},{8,40}... | collective-permute-start | bytes 196616 | tf_op jit(solution)/shard_map/ppermute | solution.py:53
  59.2 9.3 %collective-permute-start.14 = (bf16[112,1024]{1,0:T(8,128)(2,1)S(1)}, bf16[112,1024]{1,0:T(8,128)(2,1)S(1)}, u32[]{:S(2)}, u32[]{:S(2)}) collective-permute-start(bf16[112,1024]{1,0:T(8,128)(2,1)S(1)} %get-tuple-element.114), channel_id=1, source_target_pairs={{0,32},{1,33},{2,34},{3,35},{4,36},{5,37},{6,38},{7,39},{8,40},{9,... | collective-permute-start | bytes 688136 | tf_op jit(solution)/shard_map/ppermute | solution.py:534
  63.7 3.3 %collective-permute-start.13 = (bf16[16,2048]{1,0:T(8,128)(2,1)S(1)}, bf16[16,2048]{1,0:T(8,128)(2,1)S(1)}, u32[]{:S(2)}, u32[]{:S(2)}) collective-permute-start(bf16[16,2048]{1,0:T(8,128)(2,1)S(1)} %add_convert_fusion.8), channel_id=1, source_target_pairs={{0,2},{1,3},{2,0},{3,1},{4,6},{5,7},{6,4},{7,5},{8,10},{9,11},{10,... | collective-permute-start | bytes 196616 | tf_op jit(solution)/shard_map/ppermute | solution.py:53
  63.9 11.2 %collective-permute-start.16 = (bf16[112,1024]{1,0:T(8,128)(2,1)S(1)}, bf16[112,1024]{1,0:T(8,128)(2,1)S(1)}, u32[]{:S(2)}, u32[]{:S(2)}) collective-permute-start(bf16[112,1024]{1,0:T(8,128)(2,1)S(1)} %get-tuple-element.116), channel_id=1, source_target_pairs={{0,32},{1,33},{2,34},{3,35},{4,36},{5,37},{6,38},{7,39},{8,40},{9,... | collective-permute-start | bytes 688136 | tf_op jit(solution)/shard_map/ppermute | solution.py:535
  68.6 6.5 %collective-permute-start.15 = (bf16[16,2048]{1,0:T(8,128)(2,1)S(1)}, bf16[16,2048]{1,0:T(8,128)(2,1)S(1)}, u32[]{:S(2)}, u32[]{:S(2)}) collective-permute-start(bf16[16,2048]{1,0:T(8,128)(2,1)S(1)} %add_convert_fusion.7), channel_id=1, source_target_pairs={{0,4},{1,5},{2,6},{3,7},{4,0},{5,1},{6,2},{7,3},{8,12},{9,13},{10,... | collective-permute-start | bytes 196616 | tf_op jit(solution)/shard_map/ppermute | solution.py:53
  68.7 8.9 %collective-permute-start.18 = (bf16[96,1024]{1,0:T(8,128)(2,1)S(1)}, bf16[96,1024]{1,0:T(8,128)(2,1)S(1)}, u32[]{:S(2)}, u32[]{:S(2)}) collective-permute-start(bf16[96,1024]{1,0:T(8,128)(2,1)S(1)} %get-tuple-element.118), channel_id=1, source_target_pairs={{0,1},{1,2},{2,3},{3,4},{4,5},{5,6},{6,7},{7,8},{8,9},{9,10},{10,1... | collective-permute-start | bytes 589832 | tf_op jit(solution)/shard_map/ppermute | solution.py:536
  73.8 8.7 %collective-permute-start.19 = (bf16[96,1024]{1,0:T(8,128)(2,1)S(1)}, bf16[96,1024]{1,0:T(8,128)(2,1)S(1)}, u32[]{:S(2)}, u32[]{:S(2)}) collective-permute-start(bf16[96,1024]{1,0:T(8,128)(2,1)S(1)} %get-tuple-element.119), channel_id=1, source_target_pairs={{0,33},{1,34},{2,35},{3,36},{4,37},{5,38},{6,39},{7,40},{8,41},{9,... | collective-permute-start | bytes 589832 | tf_op jit(solution)/shard_map/ppermute | solution.py:537
  75.1 9.2 %collective-permute-start.17 = (bf16[16,2048]{1,0:T(8,128)(2,1)S(1)}, bf16[16,2048]{1,0:T(8,128)(2,1)S(1)}, u32[]{:S(2)}, u32[]{:S(2)}) collective-permute-start(bf16[16,2048]{1,0:T(8,128)(2,1)S(1)} %add_convert_fusion.6), channel_id=1, source_target_pairs={{0,12},{1,13},{2,14},{3,15},{4,8},{5,9},{6,10},{7,11},{8,4},{9,5},... | collective-permute-start | bytes 196616 | tf_op jit(solution)/shard_map/ppermute | solution.py:53
  84.4 4.5 %collective-permute-start.22 = (bf16[16,2048]{1,0:T(8,128)(2,1)S(1)}, bf16[16,2048]{1,0:T(8,128)(2,1)S(1)}, u32[]{:S(2)}, u32[]{:S(2)}) collective-permute-start(bf16[16,2048]{1,0:T(8,128)(2,1)S(1)} %add_convert_fusion.5), channel_id=1, source_target_pairs={{0,16},{1,65},{2,18},{3,67},{4,20},{5,69},{6,22},{7,71},{8,24},{9,... | collective-permute-start | bytes 196616 | tf_op jit(solution)/shard_map/ppermute | solution.py:53
  84.5 6.3 %collective-permute-start.21 = (bf16[16,2048]{1,0:T(8,128)(2,1)S(1)}, bf16[16,2048]{1,0:T(8,128)(2,1)S(1)}, u32[]{:S(2)}, u32[]{:S(2)}) collective-permute-start(bf16[16,2048]{1,0:T(8,128)(2,1)S(1)} %add_convert_fusion.5), channel_id=1, source_target_pairs={{0,32},{1,129},{2,34},{3,131},{4,36},{5,133},{6,38},{7,135},{8,40}... | collective-permute-start | bytes 196616 | tf_op jit(solution)/shard_map/ppermute | solution.py:53
  88.4 3.4 %collective-permute-start.20 = (bf16[16,2048]{1,0:T(8,128)(2,1)S(1)}, bf16[16,2048]{1,0:T(8,128)(2,1)S(1)}, u32[]{:S(2)}, u32[]{:S(2)}) collective-permute-start(bf16[16,2048]{1,0:T(8,128)(2,1)S(1)} %add_convert_fusion.5), channel_id=1, source_target_pairs={{0,48},{1,193},{2,50},{3,195},{4,52},{5,197},{6,54},{7,199},{8,56}... | collective-permute-start | bytes 196616 | tf_op jit(solution)/shard_map/ppermute | solution.py:53
  91.8 13.7 %collective-permute-start.25 = (bf16[64,2048]{1,0:T(8,128)(2,1)S(1)}, bf16[64,2048]{1,0:T(8,128)(2,1)S(1)}, u32[]{:S(2)}, u32[]{:S(2)}) collective-permute-start(bf16[64,2048]{1,0:T(8,128)(2,1)S(1)} %pad_maximum_fusion.refs_0_), channel_id=1, source_target_pairs={{0,64},{1,17},{2,66},{3,19},{4,68},{5,21},{6,70},{7,23},{8,72},{9,... | collective-permute-start | bytes 786440 | tf_op jit(solution)/shard_map/ppermute | solution.py:53
  92.4 13.1 %collective-permute-start.24 = (bf16[64,2048]{1,0:T(8,128)(2,1)S(1)}, bf16[64,2048]{1,0:T(8,128)(2,1)S(1)}, u32[]{:S(2)}, u32[]{:S(2)}) collective-permute-start(bf16[64,2048]{1,0:T(8,128)(2,1)S(1)} %pad_maximum_fusion.refs_0_), channel_id=1, source_target_pairs={{0,128},{1,33},{2,130},{3,35},{4,132},{5,37},{6,134},{7,39},{8,136... | collective-permute-start | bytes 786440 | tf_op jit(solution)/shard_map/ppermute | solution.py:53
  96.5 9.0 %collective-permute-start.23 = (bf16[64,2048]{1,0:T(8,128)(2,1)S(1)}, bf16[64,2048]{1,0:T(8,128)(2,1)S(1)}, u32[]{:S(2)}, u32[]{:S(2)}) collective-permute-start(bf16[64,2048]{1,0:T(8,128)(2,1)S(1)} %pad_maximum_fusion.refs_0_), channel_id=1, source_target_pairs={{0,192},{1,49},{2,194},{3,51},{4,196},{5,53},{6,198},{7,55},{8,200... | collective-permute-start | bytes 786440 | tf_op jit(solution)/shard_map/ppermute | solution.py:53
  98.8 14.9 %collective-permute-start.26 = (bf16[64,2048]{1,0:T(8,128)(2,1)S(1)}, bf16[64,2048]{1,0:T(8,128)(2,1)S(1)}, u32[]{:S(2)}, u32[]{:S(2)}) collective-permute-start(bf16[64,2048]{1,0:T(8,128)(2,1)S(1)} %pad_maximum_fusion.refs_0_), channel_id=1, source_target_pairs={{0,1},{1,0},{2,3},{3,2},{4,5},{5,4},{6,7},{7,6},{8,9},{9,8},{10,11... | collective-permute-start | bytes 786440 | tf_op jit(solution)/shard_map/ppermute | solution.py:53
  105.5 8.2 %collective-permute-start.27 = (bf16[64,2048]{1,0:T(8,128)(2,1)S(1)}, bf16[64,2048]{1,0:T(8,128)(2,1)S(1)}, u32[]{:S(2)}, u32[]{:S(2)}) collective-permute-start(bf16[64,2048]{1,0:T(8,128)(2,1)S(1)} %collective-permute-done.23.refs_1_), channel_id=1, source_target_pairs={{0,1},{1,0},{2,3},{3,2},{4,5},{5,4},{6,7},{7,6},{8,9},{9,8},{10,11... | collective-permute-start | bytes 786440 | tf_op jit(solution)/shard_map/ppermute | solution.py:53
  111.3 2.5 %collective-permute-start.28 = (bf16[64,2048]{1,0:T(8,128)(2,1)S(1)}, bf16[64,2048]{1,0:T(8,128)(2,1)S(1)}, u32[]{:S(2)}, u32[]{:S(2)}) collective-permute-start(bf16[64,2048]{1,0:T(8,128)(2,1)S(1)} %collective-permute-done.24.refs_2_), channel_id=1, source_target_pairs={{0,1},{1,0},{2,3},{3,2},{4,5},{5,4},{6,7},{7,6},{8,9},{9,8},{10,11... | collective-permute-start | bytes 786440 | tf_op jit(solution)/shard_map/ppermute | solution.py:53
  111.3 2.5 %collective-permute-start.29 = (bf16[64,2048]{1,0:T(8,128)(2,1)S(1)}, bf16[64,2048]{1,0:T(8,128)(2,1)S(1)}, u32[]{:S(2)}, u32[]{:S(2)}) collective-permute-start(bf16[64,2048]{1,0:T(8,128)(2,1)S(1)} %collective-permute-done.25.refs_3_), channel_id=1, source_target_pairs={{0,1},{1,0},{2,3},{3,2},{4,5},{5,4},{6,7},{7,6},{8,9},{9,8},{10,11... | collective-permute-start | bytes 786440 | tf_op jit(solution)/shard_map/ppermute | solution.py:53
  (10 other events, 66.7 us)

commit v7 on v6

--- a/solution.py
+++ b/solution.py
@@ -148,18 +148,22 @@
     split(dot(select[...], fc[...]), lat, lon, diag)
 
 
-def load_kernel(fc0, select, *refs):
-    f_hbm, c_hbm, sources, targets = refs[0], refs[1], refs[2:7], refs[7:12]
-    fc1, lat, lon, diag, part0, part1, fetch_sem, sem = refs[12:]
-    fetches = fetch(1, f_hbm, c_hbm, fc1, fetch_sem)
+def pack1_kernel(f_hbm, c_hbm, select, fc, lat, lon, diag, sem):
+    copies = fetch(1, f_hbm, c_hbm, fc, sem)
+    for copy in copies:
+        copy.start()
+    for copy in copies:
+        copy.wait()
+    split(dot(select[...], fc[...]), lat, lon, diag)
+
+
+def load_kernel(fc0, fc1, *refs):
+    sources, targets, (part0, part1, sem) = refs[:5], refs[5:10], refs[10:]
     copies = [
         pltpu.make_async_copy(a, b, sem.at[i]) for i, (a, b) in enumerate(zip(sources, targets))
     ]
-    for copy in fetches + copies:
+    for copy in copies:
         copy.start()
-    for copy in fetches:
-        copy.wait()
-    split(dot(select[...], fc1[...]), lat, lon, diag)
     copies[0].wait()
     part0[...] = dot(targets[0][...], fc0[...]).astype(bf16)
     part1[...] = dot(targets[0][...], fc1[...]).astype(bf16)
@@ -287,8 +291,16 @@
 
 
 def finish_kernel(
-    fc0, fc1, both0, both1, r_lat0, r_lat1, r_lon, r_diag, table, select, gain, out, grad
+    both0, both1, r_lat0, r_lat1, r_lon, r_diag, gain, f_hbm, c_hbm, t_hbm, s_hbm,
+    out, grad, fc0, fc1, table, select, sem,
 ):
+    copies = fetch(0, f_hbm, c_hbm, fc0, sem.at[0]) + fetch(1, f_hbm, c_hbm, fc1, sem.at[1])
+    copies.append(pltpu.make_async_copy(t_hbm, table, sem.at[2, 0]))
+    copies.append(pltpu.make_async_copy(s_hbm, select, sem.at[2, 1]))
+    for copy in copies:
+        copy.start()
+    for copy in copies:
+        copy.wait()
     for g, (fc, both, r_lat) in enumerate(((fc0, both0, r_lat0), (fc1, both1, r_lat1))):
         side = pl.ds(g * SIDE, SIDE)
         rows = jnp.concatenate([r_lat[...], r_lon[side, :], r_diag[side, :]], axis=0)
@@ -399,13 +411,17 @@
     return [pltpu.with_memory_space_constraint(x, pltpu.HBM) for x in xs]
 
 
-def kernel_call(body, name, args, outs, in_hbm=0, place=None, scratch=(), price=(10**6, 10**4)):
+def kernel_call(
+    body, name, args, outs, in_hbm=0, place=None, scratch=(), price=(10**6, 10**4), loose=()
+):
     if in_hbm > 0:
         specs = [pl.BlockSpec(memory_space=pltpu.HBM)] * in_hbm + spec(len(args) - in_hbm)
         args = hbm(*args[:in_hbm]) + vms(*args[in_hbm:])
     else:
         specs = spec(len(args) + in_hbm) + [pl.BlockSpec(memory_space=pltpu.HBM)] * -in_hbm
-        args = vms(*args[: len(args) + in_hbm]) + hbm(*args[len(args) + in_hbm :])
+        inside = args[: len(args) + in_hbm]
+        inside = [x if i in loose else vm(x) for i, x in enumerate(inside)]
+        args = inside + hbm(*args[len(args) + in_hbm :])
     if place is not None:
         specs = spec(0, True) + specs
         args = [place] + args
@@ -422,7 +438,7 @@
 
 
 def message_shapes():
-    return [vshape(LAT, 2 * D), vshape(SIDE, 2 * D), vshape(SIDE, 2 * D)]
+    return [shape(LAT, 2 * D), shape(SIDE, 2 * D), shape(SIDE, 2 * D)]
 
 
 def to_pack0(f, c, select):
@@ -433,13 +449,19 @@
     )
 
 
-def to_load(fc0, select, f, c, *sources):
+def to_pack1(f, c, select):
     return kernel_call(
-        load_kernel, "load", (fc0, select, f, c, *sources),
-        [vshape(*x.shape, dtype=x.dtype) for x in sources]
-        + [vshape(GTOK, 2 * D)] + message_shapes() + [vshape(GTOK, 2 * D)] * 2,
-        in_hbm=-2 - len(sources),
-        scratch=[pltpu.SemaphoreType.DMA((4,)), pltpu.SemaphoreType.DMA((len(sources),))],
+        pack1_kernel, "pack1", (f, c, select),
+        [vshape(GTOK, 2 * D)] + [pltpu.HBM(x.shape, x.dtype) for x in message_shapes()],
+        in_hbm=2, scratch=[pltpu.SemaphoreType.DMA((4,))],
+    )
+
+
+def to_load(fc0, fc1, *sources):
+    return kernel_call(
+        load_kernel, "load", (fc0, fc1, *sources),
+        [vshape(*x.shape, dtype=x.dtype) for x in sources] + [vshape(GTOK, 2 * D)] * 2,
+        in_hbm=-len(sources), scratch=[pltpu.SemaphoreType.DMA((len(sources),))],
     )
 
 
@@ -458,7 +480,7 @@
         scratch = [pltpu.VMEM((GTOK, D), bf16)] * 2 + inner + [pltpu.VMEM((D, 4 * D), f32)]
     return kernel_call(
         functools.partial(attend_kernel, group), "attend" + str(group), args, outs,
-        place=place, scratch=scratch,
+        place=place, scratch=scratch, loose=(2, 3, 4),
     )
 
 
@@ -472,7 +494,15 @@
 
 def to_finish(*args):
     return kernel_call(
-        finish_kernel, "finish", args, [shape(TOK, D)] * 2, price=(2 * 10**9, 8 * 10**6)
+        finish_kernel, "finish", args, [shape(TOK, D)] * 2, in_hbm=-4,
+        scratch=[
+            pltpu.VMEM((GTOK, 2 * D), bf16),
+            pltpu.VMEM((GTOK, 2 * D), bf16),
+            pltpu.VMEM((GTOK, GTOK), bf16),
+            pltpu.VMEM((HALO, GTOK), bf16),
+            pltpu.SemaphoreType.DMA((3, 4)),
+        ],
+        price=(2 * 10**9, 8 * 10**6),
     )
 
 
@@ -506,15 +536,16 @@
         ]
     )
     tables = [jnp.asarray(t, bf16) for t in gather_tables()]
-    select = jnp.asarray(select_table(), bf16)
+    select_all = jnp.asarray(select_table(), bf16)
     f, c = fields.reshape(TOK, D), cotangent.reshape(TOK, D)
-    fc0, select, *parts = to_pack0(f, c, select)
+    fc0, select, *parts = to_pack0(f, c, select_all)
     halo0 = halo_in(*parts)
-    local, table, w, o, gain, fc1, lat1, lon1, diag1, part0, part1 = to_load(
-        fc0, select, f, c, *tables, qkv_weight, out_weight, layer_norm_gain.reshape(1, D)
-    )
-    lat1, lon1, diag1, near, far = tied((lat1, lon1, diag1, *halo0[1:]))
-    halo0, halo1 = (halo0[0], near, far), halo_in(lat1, lon1, diag1)
+    fc1, *parts = to_pack1(f, c, select)
+    local, table, w, o, gain, part0, part1 = to_load(
+        fc0, fc1, *tables, qkv_weight, out_weight, layer_norm_gain.reshape(1, D)
+    )
+    gain, near, far, *parts = tied((gain, *halo0[1:], *parts))
+    halo0, halo1 = (halo0[0], near, far), halo_in(*parts)
     normed0, ctw0, mixed0, gact0 = to_attend(0, place, part0, table, *halo0, gain, w, o)
     mixed1, gact1, own, other = to_attend(
         1, place, part1, table, *halo1, gain, w, o, normed0, ctw0, mixed0, gact0
@@ -548,7 +579,7 @@
     block = jnp.concatenate([part] + [send(part, second_axis(4 - s)) for s in (1, 2, 3)], axis=0)
     mine = [send(block, first_axis(4 - s)) for s in (1, 2, 3)]
     out, grad = to_finish(
-        fc0, fc1, both0, both1, r_lat0, r_lat1, r_lon, r_diag, local, select, gain
+        both0, both1, r_lat0, r_lat1, r_lon, r_diag, gain, f, c, tables[0], select_all
     )
     mine, out = tied((mine, out))
     mine = [block] + mine

time: 117 us -> 110 us (0.940)
  starting transfers between devices: 61.8 us -> 56.7 us
  local copies, waits for them, and re-layouts: 6.22 us -> 1.55 us
  Pallas kernels: 26.5 us -> 28.9 us
    ppermute x20, starting transfers between devices: 32.7 us -> 26.8 us  [send(): return lax.ppermute(x, BOTH, route(step))]
    unnamed x24 -> x4, local copies, waits for them, and re-layouts: 6.2 us -> 1.53 us
    pallas_call x6 -> x7, Pallas kernels: 22 us -> 24.4 us  [kernel_call(): pl.pallas_call(body, out_shape=outs, in_specs=specs, out_specs=spec(len(o...]
  transfers between devices with their start and end apart: 30 -> 30, of which waited for: 11 -> 11; matrix products, arithmetic and copies ran while one was open for 0% -> 0% of each run, Pallas kernels for 13% -> 16%
where the time goes in v7:
time: 110 us
  starting transfers between devices  56.7 us (52%)
  Pallas kernels  28.9 us (26%)
  waiting for transfers between devices  20.9 us (19%)
  local copies, waits for them, and re-layouts  1.55 us (1%)
    ppermute x20, starting transfers between devices, send(): return lax.ppermute(x, BOTH, route(step))  26.8 us
    pallas_call x7, Pallas kernels, kernel_call(): pl.pallas_call(body, out_shape=outs, in_specs=specs, out_specs=spec(len(o...  24.4 us
    ppermute x20, waiting for transfers between devices, send(): return lax.ppermute(x, BOTH, route(step))  13 us
    ppermute x2, starting transfers between devices, halo_in(): lax.ppermute(diag, BOTH, shifted(-1, -1))  12.1 us
    ppermute x1, starting transfers between devices, on_device(): r_lon = lax.ppermute(to_lon, BOTH, shifted(0, 1))  4.72 us
    ppermute x1, waiting for transfers between devices, on_device(): r_diag = lax.ppermute(to_diag, BOTH, shifted(1, 1))  4.64 us
    pallas_call x2, Pallas kernels, to_weights(): pl.pallas_call(functools.partial(weights_kernel, side), out_shape=[shape(...  4.51 us
    ppermute x2, starting transfers between devices, halo_in(): lax.ppermute(lon, BOTH, shifted(0, -1))  3.68 us
  transfers between devices with their start and end apart: 30, of which 11 were waited for; matrix products, arithmetic and copies ran while one was open for 0% of the time, Pallas kernels for 16%

profile of v7, /device:TPU:1, one launch (start us, length us, event | category | flops | bytes accessed | tf_op | source)
XLA Modules:
  0.0 109.8 jit_solution(1552501674245073627)
XLA Ops:
  0.6 2.3 %pack0.1 = (bf16[288,1024]{1,0:T(8,128)(2,1)S(1)}, bf16[208,288]{1,0:T(8,128)(2,1)S(1)}, bf16[112,1024]{1,0:T(8,128)(2,1)}, bf16[48,1024]{1,0:T(8,128)(2,1)S(1)}, bf16[48,1024]{1,0:T(8,128)(2,1)S(1)}) custom-call(bf16[576,512]{1,0:T(8,128)(2,1)} %bitcast.10, bf16[576,512]{1,0:T(8,128)(2,1)} %bitcast.13, bf16[208,288]{1,0:T(8,128)(2,1)} %constant.58.clone.s_hbm), custom_call_target="tpu_custom_call" | custom-call | flops 1000000 | bytes 10000 | tf_op jit(solution)/shard_map/pack0/pallas_call | solution.py:428
  2.9 3.3 %collective-permute-start = (bf16[48,1024]{1,0:T(8,128)(2,1)S(1)}, bf16[48,1024]{1,0:T(8,128)(2,1)S(1)}, u32[]{:S(2)}, u32[]{:S(2)}) collective-permute-start(bf16[48,1024]{1,0:T(8,128)(2,1)S(1)} %get-tuple-element.79), channel_id=1, source_target_pairs={{0,31},{1,0},{2,1},{3,2},{4,3},{5,4},{6,5},{7,6},{8,7},{9,8},{10,9... | collective-permute-start | bytes 294920 | tf_op jit(solution)/shard_map/ppermute | solution.py:523
  6.3 9.3 %collective-permute-start.1 = (bf16[48,1024]{1,0:T(8,128)(2,1)S(1)}, bf16[48,1024]{1,0:T(8,128)(2,1)S(1)}, u32[]{:S(2)}, u32[]{:S(2)}) collective-permute-start(bf16[48,1024]{1,0:T(8,128)(2,1)S(1)} %get-tuple-element.80), channel_id=1, source_target_pairs={{0,255},{1,224},{2,225},{3,226},{4,227},{5,228},{6,229},{7,230},{8... | collective-permute-start | bytes 294920 | tf_op jit(solution)/shard_map/ppermute | solution.py:524
  16.1 2.3 %pack1.1 = (bf16[288,1024]{1,0:T(8,128)(2,1)S(1)}, bf16[112,1024]{1,0:T(8,128)(2,1)}, bf16[48,1024]{1,0:T(8,128)(2,1)}, bf16[48,1024]{1,0:T(8,128)(2,1)}) custom-call(bf16[576,512]{1,0:T(8,128)(2,1)} %bitcast.11, bf16[576,512]{1,0:T(8,128)(2,1)} %bitcast.14, bf16[208,288]{1,0:T(8,128)(2,1)S(1)} %get-tuple-element.74.select), custom_call_target="tpu_custom_call" | custom-call | flops 1000000 | bytes 10000 | tf_op jit(solution)/shard_map/pack1/pallas_call | solution.py:428
  18.3 2.5 %load.1 = (bf16[288,288]{1,0:T(8,128)(2,1)}, bf16[288,208]{1,0:T(8,128)(2,1)S(1)}, bf16[512,1536]{1,0:T(8,128)(2,1)S(1)}, bf16[512,512]{1,0:T(8,128)(2,1)S(1)}, ...) custom-call(bf16[288,1024]{1,0:T(8,128)(2,1)S(1)} %get-tuple-element.73.fc0, ...), custom_call_target="tpu_custom_call" | custom-call | flops 1000000 | bytes 10000 | tf_op jit(solution)/shard_map/load/pallas_call | solution.py:428
  21.5 2.6 %collective-permute-start.2 = (bf16[112,1024]{1,0:T(8,128)(2,1)}, bf16[112,1024]{1,0:T(8,128)(2,1)}, u32[]{:S(2)}, u32[]{:S(2)}) collective-permute-start(bf16[112,1024]{1,0:T(8,128)(2,1)} %get-tuple-element.84), channel_id=1, source_target_pairs={{0,224},{1,225},{2,226},{3,227},{4,228},{5,229},{6,230},{7,231},{8... | collective-permute-start | bytes 688136 | tf_op jit(solution)/shard_map/ppermute | solution.py:522
  24.5 2.9 %collective-permute-start.4 = (bf16[48,1024]{1,0:T(8,128)(2,1)}, bf16[48,1024]{1,0:T(8,128)(2,1)S(1)}, u32[]{:S(2)}, u32[]{:S(2)}) collective-permute-start(bf16[48,1024]{1,0:T(8,128)(2,1)} %get-tuple-element.86), channel_id=1, source_target_pairs={{0,255},{1,224},{2,225},{3,226},{4,227},{5,228},{6,229},{7,230},{8... | collective-permute-start | bytes 294920 | tf_op jit(solution)/shard_map/ppermute | solution.py:524
  28.3 4.9 %attend0.1 = (bf16[288,512]{1,0:T(8,128)(2,1)S(1)}, bf16[288,512]{1,0:T(8,128)(2,1)S(1)}, bf16[288,512]{1,0:T(8,128)(2,1)S(1)}, bf16[288,1536]{1,0:T(8,128)(2,1)S(1)}) custom-call(s32[4]{0:T(128)S(1)} %pad_add_fusion.place, bf16[288,1024]{1,0:T(8,128)(2,1)S(1)} %get-tuple-element.90.refs_0_, bf16[288,208]{1,0:T(8,128)(2,1)S(1)} %get-tuple-element.77.refs_1_.table, ...), custom_call_target="tpu_custom_call" | custom-call | flops 1000000 | bytes 10000 | tf_op jit(solution)/shard_map/attend0/pallas_call | solution.py:428
  33.3 6.8 %attend1.1 = (bf16[288,512]{1,0:T(8,128)(2,1)S(1)}, bf16[288,1536]{1,0:T(8,128)(2,1)S(1)}, bf16[256,2048]{1,0:T(8,128)(2,1)S(1)}, bf16[256,2048]{1,0:T(8,128)(2,1)S(1)}) custom-call(s32[4]{0:T(128)S(1)} %pad_add_fusion.place, bf16[288,1024]{1,0:T(8,128)(2,1)S(1)} %get-tuple-element.76.refs_0_, bf16[288,208]{1,0:T(8,128)(2,1)S(1)} %get-tuple-element.77.refs_1_.table, ...), custom_call_target="tpu_custom_call" | custom-call | flops 1000000 | bytes 10000 | tf_op jit(solution)/shard_map/attend1/pallas_call | solution.py:428
  40.2 2.6 %collective-permute-done.6 = bf16[256,2048]{1,0:T(8,128)(2,1)S(1)} collective-permute-done((bf16[256,2048]{1,0:T(8,128)(2,1)S(1)}, bf16[256,2048]{1,0:T(8,128)(2,1)S(1)}, u32[]{:S(2)}, u32[]{:S(2)}) %collective-permute-start.6) | collective-permute-done | bytes 1048608 | tf_op jit(solution)/shard_map/ppermute | solution.py:53
  43.3 3.5 %collective-permute-start.8 = (bf16[64,2048]{1,0:T(8,128)(2,1)S(1)}, bf16[64,2048]{1,0:T(8,128)(2,1)S(1)}, u32[]{:S(2)}, u32[]{:S(2)}) collective-permute-start(bf16[64,2048]{1,0:T(8,128)(2,1)S(1)} %get-tuple-element.103), channel_id=1, source_target_pairs={{0,128},{1,33},{2,130},{3,35},{4,132},{5,37},{6,134},{7,39},{8,136... | collective-permute-start | bytes 786440 | tf_op jit(solution)/shard_map/ppermute | solution.py:53
  46.8 1.5 %collective-permute-start.9 = (bf16[64,2048]{1,0:T(8,128)(2,1)S(1)}, bf16[64,2048]{1,0:T(8,128)(2,1)S(1)}, u32[]{:S(2)}, u32[]{:S(2)}) collective-permute-start(bf16[64,2048]{1,0:T(8,128)(2,1)S(1)} %get-tuple-element.104), channel_id=1, source_target_pairs={{0,192},{1,49},{2,194},{3,51},{4,196},{5,53},{6,198},{7,55},{8,200... | collective-permute-start | bytes 786440 | tf_op jit(solution)/shard_map/ppermute | solution.py:53
  48.4 1.8 %back.1 = (bf16[288,1024]{1,0:T(8,128)(2,1)S(1)}, bf16[288,1024]{1,0:T(8,128)(2,1)S(1)}, bf16[112,1024]{1,0:T(8,128)(2,1)S(1)}, bf16[112,1024]{1,0:T(8,128)(2,1)...) custom-call(bf16[288,512]{1,0:T(8,128)(2,1)S(1)} %get-tuple-element.96.refs_10_.mixed0, ...), custom_call_target="tpu_custom_call" | custom-call | flops 2000000000 | bytes 5000000 | tf_op jit(solution)/shard_map/back/pallas_call | solution.py:428
  50.2 3.2 %collective-permute-done.8 = bf16[64,2048]{1,0:T(8,128)(2,1)S(1)} collective-permute-done((bf16[64,2048]{1,0:T(8,128)(2,1)S(1)}, bf16[64,2048]{1,0:T(8,128)(2,1)S(1)}, u32[]{:S(2)}, u32[]{:S(2)}) %collective-permute-start.8) | collective-permute-done | bytes 262176 | tf_op jit(solution)/shard_map/ppermute | solution.py:53
  53.7 2.7 %collective-permute-start.12 = (bf16[16,2048]{1,0:T(8,128)(2,1)S(1)}, bf16[16,2048]{1,0:T(8,128)(2,1)S(1)}, u32[]{:S(2)}, u32[]{:S(2)}) collective-permute-start(bf16[16,2048]{1,0:T(8,128)(2,1)S(1)} %get-tuple-element.146), channel_id=1, source_target_pairs={{0,48},{1,193},{2,50},{3,195},{4,52},{5,197},{6,54},{7,199},{8,56}... | collective-permute-start | bytes 196616 | tf_op jit(solution)/shard_map/ppermute | solution.py:53
  56.5 3.0 %collective-permute-start.14 = (bf16[112,1024]{1,0:T(8,128)(2,1)S(1)}, bf16[112,1024]{1,0:T(8,128)(2,1)S(1)}, u32[]{:S(2)}, u32[]{:S(2)}) collective-permute-start(bf16[112,1024]{1,0:T(8,128)(2,1)S(1)} %get-tuple-element.116), channel_id=1, source_target_pairs={{0,32},{1,33},{2,34},{3,35},{4,36},{5,37},{6,38},{7,39},{8,40},{9,... | collective-permute-start | bytes 688136 | tf_op jit(solution)/shard_map/ppermute | solution.py:565
  59.6 1.4 %collective-permute-done.11 = bf16[16,2048]{1,0:T(8,128)(2,1)S(1)} collective-permute-done((bf16[16,2048]{1,0:T(8,128)(2,1)S(1)}, bf16[16,2048]{1,0:T(8,128)(2,1)S(1)}, u32[]{:S(2)}, u32[]{:S(2)}) %collective-permute-start.11) | collective-permute-done | bytes 65568 | tf_op jit(solution)/shard_map/ppermute | solution.py:53
  61.1 3.1 %collective-permute-start.16 = (bf16[112,1024]{1,0:T(8,128)(2,1)S(1)}, bf16[112,1024]{1,0:T(8,128)(2,1)S(1)}, u32[]{:S(2)}, u32[]{:S(2)}) collective-permute-start(bf16[112,1024]{1,0:T(8,128)(2,1)S(1)} %get-tuple-element.118), channel_id=1, source_target_pairs={{0,32},{1,33},{2,34},{3,35},{4,36},{5,37},{6,38},{7,39},{8,40},{9,... | collective-permute-start | bytes 688136 | tf_op jit(solution)/shard_map/ppermute | solution.py:566
  64.4 1.6 %collective-permute-done.14.r_lat0 = bf16[112,1024]{1,0:T(8,128)(2,1)S(1)} collective-permute-done((bf16[112,1024]{1,0:T(8,128)(2,1)S(1)}, bf16[112,1024]{1,0:T(8,128)(2,1)S(1)}, u32[]{:S(2)}, u32[]{:S(2)}) %collective-permute-start.14) | collective-permute-done | bytes 229408 | tf_op jit(solution)/shard_map/ppermute | solution.py:565
  66.1 4.7 %collective-permute-start.18 = (bf16[96,1024]{1,0:T(8,128)(2,1)S(1)}, bf16[96,1024]{1,0:T(8,128)(2,1)S(1)}, u32[]{:S(2)}, u32[]{:S(2)}) collective-permute-start(bf16[96,1024]{1,0:T(8,128)(2,1)S(1)} %get-tuple-element.120), channel_id=1, source_target_pairs={{0,1},{1,2},{2,3},{3,4},{4,5},{5,6},{6,7},{7,8},{8,9},{9,10},{10,1... | collective-permute-start | bytes 589832 | tf_op jit(solution)/shard_map/ppermute | solution.py:567
  70.8 1.6 %collective-permute-done.16.r_lat1 = bf16[112,1024]{1,0:T(8,128)(2,1)S(1)} collective-permute-done((bf16[112,1024]{1,0:T(8,128)(2,1)S(1)}, bf16[112,1024]{1,0:T(8,128)(2,1)S(1)}, u32[]{:S(2)}, u32[]{:S(2)}) %collective-permute-start.16) | collective-permute-done | bytes 229408 | tf_op jit(solution)/shard_map/ppermute | solution.py:566
  72.5 2.4 %collective-permute-start.17 = (bf16[16,2048]{1,0:T(8,128)(2,1)S(1)}, bf16[16,2048]{1,0:T(8,128)(2,1)S(1)}, u32[]{:S(2)}, u32[]{:S(2)}) collective-permute-start(bf16[16,2048]{1,0:T(8,128)(2,1)S(1)} %add_convert_fusion.6), channel_id=1, source_target_pairs={{0,12},{1,13},{2,14},{3,15},{4,8},{5,9},{6,10},{7,11},{8,4},{9,5},... | collective-permute-start | bytes 196616 | tf_op jit(solution)/shard_map/ppermute | solution.py:53
  74.9 4.6 %collective-permute-done.19.r_diag = bf16[96,1024]{1,0:T(8,128)(2,1)S(1)} collective-permute-done((bf16[96,1024]{1,0:T(8,128)(2,1)S(1)}, bf16[96,1024]{1,0:T(8,128)(2,1)S(1)}, u32[]{:S(2)}, u32[]{:S(2)}) %collective-permute-start.19) | collective-permute-done | bytes 196640 | tf_op jit(solution)/shard_map/ppermute | solution.py:568
  79.5 2.1 %collective-permute-done.17 = bf16[16,2048]{1,0:T(8,128)(2,1)S(1)} collective-permute-done((bf16[16,2048]{1,0:T(8,128)(2,1)S(1)}, bf16[16,2048]{1,0:T(8,128)(2,1)S(1)}, u32[]{:S(2)}, u32[]{:S(2)}) %collective-permute-start.17) | collective-permute-done | bytes 65568 | tf_op jit(solution)/shard_map/ppermute | solution.py:53
  82.0 3.3 %collective-permute-start.21 = (bf16[16,2048]{1,0:T(8,128)(2,1)S(1)}, bf16[16,2048]{1,0:T(8,128)(2,1)S(1)}, u32[]{:S(2)}, u32[]{:S(2)}) collective-permute-start(bf16[16,2048]{1,0:T(8,128)(2,1)S(1)} %add_convert_fusion.5), channel_id=1, source_target_pairs={{0,32},{1,129},{2,34},{3,131},{4,36},{5,133},{6,38},{7,135},{8,40}... | collective-permute-start | bytes 196616 | tf_op jit(solution)/shard_map/ppermute | solution.py:53
  86.0 1.6 %collective-permute-done.21 = bf16[16,2048]{1,0:T(8,128)(2,1)S(1)} collective-permute-done((bf16[16,2048]{1,0:T(8,128)(2,1)S(1)}, bf16[16,2048]{1,0:T(8,128)(2,1)S(1)}, u32[]{:S(2)}, u32[]{:S(2)}) %collective-permute-start.21) | collective-permute-done | bytes 65568 | tf_op jit(solution)/shard_map/ppermute | solution.py:53
  90.1 3.4 %collective-permute-start.24 = (bf16[64,2048]{1,0:T(8,128)(2,1)S(1)}, bf16[64,2048]{1,0:T(8,128)(2,1)S(1)}, u32[]{:S(2)}, u32[]{:S(2)}) collective-permute-start(bf16[64,2048]{1,0:T(8,128)(2,1)S(1)} %pad_maximum_fusion.refs_0_), channel_id=1, source_target_pairs={{0,128},{1,33},{2,130},{3,35},{4,132},{5,37},{6,134},{7,39},{8,136... | collective-permute-start | bytes 786440 | tf_op jit(solution)/shard_map/ppermute | solution.py:53
  93.5 3.8 %finish.1 = (bf16[576,512]{1,0:T(8,128)(2,1)}, bf16[576,512]{1,0:T(8,128)(2,1)}) custom-call(bf16[288,1024]{1,0:T(8,128)(2,1)S(1)} %get-tuple-element.123.both0, bf16[288,1024]{1,0:T(8,128)(2,1)S(1)} %get-tuple-element.124.both1, bf16[112,1024]{1,0:T(8,128)(2,1)S(1)} %collective-permute-done.14.r_lat0, bf16[112,1024]{1,0:T(8,128)(2,1)S(1)} %collective-permute-done.16.r_lat1, ...), custom_call_target="tpu_custom_call" | custom-call | flops 2000000000 | bytes 8000000 | tf_op jit(solution)/shard_map/finish/pallas_call | solution.py:428
  97.4 3.9 %collective-permute-start.26 = (bf16[64,2048]{1,0:T(8,128)(2,1)S(1)}, bf16[64,2048]{1,0:T(8,128)(2,1)S(1)}, u32[]{:S(2)}, u32[]{:S(2)}) collective-permute-start(bf16[64,2048]{1,0:T(8,128)(2,1)S(1)} %pad_maximum_fusion.refs_0_), channel_id=1, source_target_pairs={{0,1},{1,0},{2,3},{3,2},{4,5},{5,4},{6,7},{7,6},{8,9},{9,8},{10,11... | collective-permute-start | bytes 786440 | tf_op jit(solution)/shard_map/ppermute | solution.py:53
  101.3 3.2 %collective-permute-start.27 = (bf16[64,2048]{1,0:T(8,128)(2,1)S(1)}, bf16[64,2048]{1,0:T(8,128)(2,1)S(1)}, u32[]{:S(2)}, u32[]{:S(2)}) collective-permute-start(bf16[64,2048]{1,0:T(8,128)(2,1)S(1)} %collective-permute-done.23.refs_1_), channel_id=1, source_target_pairs={{0,1},{1,0},{2,3},{3,2},{4,5},{5,4},{6,7},{7,6},{8,9},{9,8},{10,11... | collective-permute-start | bytes 786440 | tf_op jit(solution)/shard_map/ppermute | solution.py:53
  105.0 2.0 %weights0.1 = (f32[512,1536]{1,0:T(8,128)}, f32[512,512]{1,0:T(8,128)}, f32[1,512]{1,0:T(1,128)S(1)}) custom-call(s32[4]{0:T(128)S(1)} %pad_add_fusion.place, bf16[64,2048]{1,0:T(8,128)(2,1)S(1)} %pad_maximum_fusion.refs_0_, bf16[64,2048]{1,0:T(8,128)(2,1)S(1)} %collective-permute-done.23.refs_1_, bf16[64,2048]{1,0:T(8,128)(2,1)S(1)} %collective-permute-done.24.refs_2_, ...), custom_call_target="tpu_custom_call" | custom-call | flops 10000000 | bytes 4000000 | tf_op jit(solution)/shard_map/weights0/pallas_call | solution.py:360
  107.0 2.5 %weights1.1 = (f32[512,1536]{1,0:T(8,128)}, f32[512,512]{1,0:T(8,128)}, f32[1,512]{1,0:T(1,128)}) custom-call(s32[4]{0:T(128)S(1)} %pad_add_fusion.place, bf16[64,2048]{1,0:T(8,128)(2,1)S(1)} %collective-permute-done.26.refs_0_, bf16[64,2048]{1,0:T(8,128)(2,1)S(1)} %collective-permute-done.27.refs_1_, ...), custom_call_target="tpu_custom_call", output_to_operand_aliasing={{0}: (8, {}), {1}: (9, {})} | custom-call | flops 10000000 | bytes 4000000 | tf_op jit(solution)/shard_map/weights1/pallas_call | solution.py:360
  (50 shorter events, 8.0 us)
Async XLA Ops:
  2.9 17.9 %collective-permute-start = (bf16[48,1024]{1,0:T(8,128)(2,1)S(1)}, bf16[48,1024]{1,0:T(8,128)(2,1)S(1)}, u32[]{:S(2)}, u32[]{:S(2)}) collective-permute-start(bf16[48,1024]{1,0:T(8,128)(2,1)S(1)} %get-tuple-element.79), channel_id=1, source_target_pairs={{0,31},{1,0},{2,1},{3,2},{4,3},{5,4},{6,5},{7,6},{8,7},{9,8},{10,9... | collective-permute-start | bytes 294920 | tf_op jit(solution)/shard_map/ppermute | solution.py:523
  6.3 14.6 %collective-permute-start.1 = (bf16[48,1024]{1,0:T(8,128)(2,1)S(1)}, bf16[48,1024]{1,0:T(8,128)(2,1)S(1)}, u32[]{:S(2)}, u32[]{:S(2)}) collective-permute-start(bf16[48,1024]{1,0:T(8,128)(2,1)S(1)} %get-tuple-element.80), channel_id=1, source_target_pairs={{0,255},{1,224},{2,225},{3,226},{4,227},{5,228},{6,229},{7,230},{8... | collective-permute-start | bytes 294920 | tf_op jit(solution)/shard_map/ppermute | solution.py:524
  15.5 11.9 %collective-permute-start.5 = (bf16[112,1024]{1,0:T(8,128)(2,1)}, bf16[112,1024]{1,0:T(8,128)(2,1)}, u32[]{:S(2)}, u32[]{:S(2)}) collective-permute-start(bf16[112,1024]{1,0:T(8,128)(2,1)} %get-tuple-element.91), channel_id=1, source_target_pairs={{0,224},{1,225},{2,226},{3,227},{4,228},{5,229},{6,230},{7,231},{8... | collective-permute-start | bytes 688136 | tf_op jit(solution)/shard_map/ppermute | solution.py:522
  20.8 0.6 copy-start
  21.5 11.8 %collective-permute-start.2 = (bf16[112,1024]{1,0:T(8,128)(2,1)}, bf16[112,1024]{1,0:T(8,128)(2,1)}, u32[]{:S(2)}, u32[]{:S(2)}) collective-permute-start(bf16[112,1024]{1,0:T(8,128)(2,1)} %get-tuple-element.84), channel_id=1, source_target_pairs={{0,224},{1,225},{2,226},{3,227},{4,228},{5,229},{6,230},{7,231},{8... | collective-permute-start | bytes 688136 | tf_op jit(solution)/shard_map/ppermute | solution.py:522
  24.1 9.2 %collective-permute-start.3 = (bf16[48,1024]{1,0:T(8,128)(2,1)}, bf16[48,1024]{1,0:T(8,128)(2,1)S(1)}, u32[]{:S(2)}, u32[]{:S(2)}) collective-permute-start(bf16[48,1024]{1,0:T(8,128)(2,1)} %get-tuple-element.85), channel_id=1, source_target_pairs={{0,31},{1,0},{2,1},{3,2},{4,3},{5,4},{6,5},{7,6},{8,7},{9,8},{10,9... | collective-permute-start | bytes 294920 | tf_op jit(solution)/shard_map/ppermute | solution.py:523
  24.5 8.8 %collective-permute-start.4 = (bf16[48,1024]{1,0:T(8,128)(2,1)}, bf16[48,1024]{1,0:T(8,128)(2,1)S(1)}, u32[]{:S(2)}, u32[]{:S(2)}) collective-permute-start(bf16[48,1024]{1,0:T(8,128)(2,1)} %get-tuple-element.86), channel_id=1, source_target_pairs={{0,255},{1,224},{2,225},{3,226},{4,227},{5,228},{6,229},{7,230},{8... | collective-permute-start | bytes 294920 | tf_op jit(solution)/shard_map/ppermute | solution.py:524
  27.4 0.9 copy-start.1
  40.1 2.7 %collective-permute-start.6 = (bf16[256,2048]{1,0:T(8,128)(2,1)S(1)}, bf16[256,2048]{1,0:T(8,128)(2,1)S(1)}, u32[]{:S(2)}, u32[]{:S(2)}) collective-permute-start(bf16[256,2048]{1,0:T(8,128)(2,1)S(1)} %get-tuple-element.100), channel_id=1, source_target_pairs={{0,1},{1,0},{2,3},{3,2},{4,5},{5,4},{6,7},{7,6},{8,9},{9,8},{10,11... | collective-permute-start | bytes 3145736 | tf_op jit(solution)/shard_map/ppermute | solution.py:53
  43.3 6.9 %collective-permute-start.7 = (bf16[64,2048]{1,0:T(8,128)(2,1)S(1)}, bf16[64,2048]{1,0:T(8,128)(2,1)S(1)}, u32[]{:S(2)}, u32[]{:S(2)}) collective-permute-start(bf16[64,2048]{1,0:T(8,128)(2,1)S(1)} %get-tuple-element.102), channel_id=1, source_target_pairs={{0,64},{1,17},{2,66},{3,19},{4,68},{5,21},{6,70},{7,23},{8,72},{9,... | collective-permute-start | bytes 786440 | tf_op jit(solution)/shard_map/ppermute | solution.py:53
  43.3 10.1 %collective-permute-start.8 = (bf16[64,2048]{1,0:T(8,128)(2,1)S(1)}, bf16[64,2048]{1,0:T(8,128)(2,1)S(1)}, u32[]{:S(2)}, u32[]{:S(2)}) collective-permute-start(bf16[64,2048]{1,0:T(8,128)(2,1)S(1)} %get-tuple-element.103), channel_id=1, source_target_pairs={{0,128},{1,33},{2,130},{3,35},{4,132},{5,37},{6,134},{7,39},{8,136... | collective-permute-start | bytes 786440 | tf_op jit(solution)/shard_map/ppermute | solution.py:53
  46.8 6.6 %collective-permute-start.9 = (bf16[64,2048]{1,0:T(8,128)(2,1)S(1)}, bf16[64,2048]{1,0:T(8,128)(2,1)S(1)}, u32[]{:S(2)}, u32[]{:S(2)}) collective-permute-start(bf16[64,2048]{1,0:T(8,128)(2,1)S(1)} %get-tuple-element.104), channel_id=1, source_target_pairs={{0,192},{1,49},{2,194},{3,51},{4,196},{5,53},{6,198},{7,55},{8,200... | collective-permute-start | bytes 786440 | tf_op jit(solution)/shard_map/ppermute | solution.py:53
  53.6 6.0 %collective-permute-start.10 = (bf16[16,2048]{1,0:T(8,128)(2,1)S(1)}, bf16[16,2048]{1,0:T(8,128)(2,1)S(1)}, u32[]{:S(2)}, u32[]{:S(2)}) collective-permute-start(bf16[16,2048]{1,0:T(8,128)(2,1)S(1)} %get-tuple-element.145), channel_id=1, source_target_pairs={{0,16},{1,65},{2,18},{3,67},{4,20},{5,69},{6,22},{7,71},{8,24},{9,... | collective-permute-start | bytes 196616 | tf_op jit(solution)/shard_map/ppermute | solution.py:53
  53.7 5.9 %collective-permute-start.12 = (bf16[16,2048]{1,0:T(8,128)(2,1)S(1)}, bf16[16,2048]{1,0:T(8,128)(2,1)S(1)}, u32[]{:S(2)}, u32[]{:S(2)}) collective-permute-start(bf16[16,2048]{1,0:T(8,128)(2,1)S(1)} %get-tuple-element.146), channel_id=1, source_target_pairs={{0,48},{1,193},{2,50},{3,195},{4,52},{5,197},{6,54},{7,199},{8,56}... | collective-permute-start | bytes 196616 | tf_op jit(solution)/shard_map/ppermute | solution.py:53
  56.4 4.6 %collective-permute-start.11 = (bf16[16,2048]{1,0:T(8,128)(2,1)S(1)}, bf16[16,2048]{1,0:T(8,128)(2,1)S(1)}, u32[]{:S(2)}, u32[]{:S(2)}) collective-permute-start(bf16[16,2048]{1,0:T(8,128)(2,1)S(1)} %get-tuple-element.147), channel_id=1, source_target_pairs={{0,32},{1,129},{2,34},{3,131},{4,36},{5,133},{6,38},{7,135},{8,40}... | collective-permute-start | bytes 196616 | tf_op jit(solution)/shard_map/ppermute | solution.py:53
  56.5 9.5 %collective-permute-start.14 = (bf16[112,1024]{1,0:T(8,128)(2,1)S(1)}, bf16[112,1024]{1,0:T(8,128)(2,1)S(1)}, u32[]{:S(2)}, u32[]{:S(2)}) collective-permute-start(bf16[112,1024]{1,0:T(8,128)(2,1)S(1)} %get-tuple-element.116), channel_id=1, source_target_pairs={{0,32},{1,33},{2,34},{3,35},{4,36},{5,37},{6,38},{7,39},{8,40},{9,... | collective-permute-start | bytes 688136 | tf_op jit(solution)/shard_map/ppermute | solution.py:565
  61.0 3.4 %collective-permute-start.13 = (bf16[16,2048]{1,0:T(8,128)(2,1)S(1)}, bf16[16,2048]{1,0:T(8,128)(2,1)S(1)}, u32[]{:S(2)}, u32[]{:S(2)}) collective-permute-start(bf16[16,2048]{1,0:T(8,128)(2,1)S(1)} %add_convert_fusion.8), channel_id=1, source_target_pairs={{0,2},{1,3},{2,0},{3,1},{4,6},{5,7},{6,4},{7,5},{8,10},{9,11},{10,... | collective-permute-start | bytes 196616 | tf_op jit(solution)/shard_map/ppermute | solution.py:53
  61.1 11.3 %collective-permute-start.16 = (bf16[112,1024]{1,0:T(8,128)(2,1)S(1)}, bf16[112,1024]{1,0:T(8,128)(2,1)S(1)}, u32[]{:S(2)}, u32[]{:S(2)}) collective-permute-start(bf16[112,1024]{1,0:T(8,128)(2,1)S(1)} %get-tuple-element.118), channel_id=1, source_target_pairs={{0,32},{1,33},{2,34},{3,35},{4,36},{5,37},{6,38},{7,39},{8,40},{9,... | collective-permute-start | bytes 688136 | tf_op jit(solution)/shard_map/ppermute | solution.py:566
  66.0 6.4 %collective-permute-start.15 = (bf16[16,2048]{1,0:T(8,128)(2,1)S(1)}, bf16[16,2048]{1,0:T(8,128)(2,1)S(1)}, u32[]{:S(2)}, u32[]{:S(2)}) collective-permute-start(bf16[16,2048]{1,0:T(8,128)(2,1)S(1)} %add_convert_fusion.7), channel_id=1, source_target_pairs={{0,4},{1,5},{2,6},{3,7},{4,0},{5,1},{6,2},{7,3},{8,12},{9,13},{10,... | collective-permute-start | bytes 196616 | tf_op jit(solution)/shard_map/ppermute | solution.py:53
  66.1 8.8 %collective-permute-start.18 = (bf16[96,1024]{1,0:T(8,128)(2,1)S(1)}, bf16[96,1024]{1,0:T(8,128)(2,1)S(1)}, u32[]{:S(2)}, u32[]{:S(2)}) collective-permute-start(bf16[96,1024]{1,0:T(8,128)(2,1)S(1)} %get-tuple-element.120), channel_id=1, source_target_pairs={{0,1},{1,2},{2,3},{3,4},{4,5},{5,6},{6,7},{7,8},{8,9},{9,10},{10,1... | collective-permute-start | bytes 589832 | tf_op jit(solution)/shard_map/ppermute | solution.py:567
  70.8 8.7 %collective-permute-start.19 = (bf16[96,1024]{1,0:T(8,128)(2,1)S(1)}, bf16[96,1024]{1,0:T(8,128)(2,1)S(1)}, u32[]{:S(2)}, u32[]{:S(2)}) collective-permute-start(bf16[96,1024]{1,0:T(8,128)(2,1)S(1)} %get-tuple-element.121), channel_id=1, source_target_pairs={{0,33},{1,34},{2,35},{3,36},{4,37},{5,38},{6,39},{7,40},{8,41},{9,... | collective-permute-start | bytes 589832 | tf_op jit(solution)/shard_map/ppermute | solution.py:568
  72.5 9.2 %collective-permute-start.17 = (bf16[16,2048]{1,0:T(8,128)(2,1)S(1)}, bf16[16,2048]{1,0:T(8,128)(2,1)S(1)}, u32[]{:S(2)}, u32[]{:S(2)}) collective-permute-start(bf16[16,2048]{1,0:T(8,128)(2,1)S(1)} %add_convert_fusion.6), channel_id=1, source_target_pairs={{0,12},{1,13},{2,14},{3,15},{4,8},{5,9},{6,10},{7,11},{8,4},{9,5},... | collective-permute-start | bytes 196616 | tf_op jit(solution)/shard_map/ppermute | solution.py:53
  81.6 4.4 %collective-permute-start.22 = (bf16[16,2048]{1,0:T(8,128)(2,1)S(1)}, bf16[16,2048]{1,0:T(8,128)(2,1)S(1)}, u32[]{:S(2)}, u32[]{:S(2)}) collective-permute-start(bf16[16,2048]{1,0:T(8,128)(2,1)S(1)} %add_convert_fusion.5), channel_id=1, source_target_pairs={{0,16},{1,65},{2,18},{3,67},{4,20},{5,69},{6,22},{7,71},{8,24},{9,... | collective-permute-start | bytes 196616 | tf_op jit(solution)/shard_map/ppermute | solution.py:53
  82.0 5.7 %collective-permute-start.21 = (bf16[16,2048]{1,0:T(8,128)(2,1)S(1)}, bf16[16,2048]{1,0:T(8,128)(2,1)S(1)}, u32[]{:S(2)}, u32[]{:S(2)}) collective-permute-start(bf16[16,2048]{1,0:T(8,128)(2,1)S(1)} %add_convert_fusion.5), channel_id=1, source_target_pairs={{0,32},{1,129},{2,34},{3,131},{4,36},{5,133},{6,38},{7,135},{8,40}... | collective-permute-start | bytes 196616 | tf_op jit(solution)/shard_map/ppermute | solution.py:53
  85.3 3.4 %collective-permute-start.20 = (bf16[16,2048]{1,0:T(8,128)(2,1)S(1)}, bf16[16,2048]{1,0:T(8,128)(2,1)S(1)}, u32[]{:S(2)}, u32[]{:S(2)}) collective-permute-start(bf16[16,2048]{1,0:T(8,128)(2,1)S(1)} %add_convert_fusion.5), channel_id=1, source_target_pairs={{0,48},{1,193},{2,50},{3,195},{4,52},{5,197},{6,54},{7,199},{8,56}... | collective-permute-start | bytes 196616 | tf_op jit(solution)/shard_map/ppermute | solution.py:53
  88.8 12.5 %collective-permute-start.25 = (bf16[64,2048]{1,0:T(8,128)(2,1)S(1)}, bf16[64,2048]{1,0:T(8,128)(2,1)S(1)}, u32[]{:S(2)}, u32[]{:S(2)}) collective-permute-start(bf16[64,2048]{1,0:T(8,128)(2,1)S(1)} %pad_maximum_fusion.refs_0_), channel_id=1, source_target_pairs={{0,64},{1,17},{2,66},{3,19},{4,68},{5,21},{6,70},{7,23},{8,72},{9,... | collective-permute-start | bytes 786440 | tf_op jit(solution)/shard_map/ppermute | solution.py:53
  90.1 11.2 %collective-permute-start.24 = (bf16[64,2048]{1,0:T(8,128)(2,1)S(1)}, bf16[64,2048]{1,0:T(8,128)(2,1)S(1)}, u32[]{:S(2)}, u32[]{:S(2)}) collective-permute-start(bf16[64,2048]{1,0:T(8,128)(2,1)S(1)} %pad_maximum_fusion.refs_0_), channel_id=1, source_target_pairs={{0,128},{1,33},{2,130},{3,35},{4,132},{5,37},{6,134},{7,39},{8,136... | collective-permute-start | bytes 786440 | tf_op jit(solution)/shard_map/ppermute | solution.py:53
  93.5 7.8 %collective-permute-start.23 = (bf16[64,2048]{1,0:T(8,128)(2,1)S(1)}, bf16[64,2048]{1,0:T(8,128)(2,1)S(1)}, u32[]{:S(2)}, u32[]{:S(2)}) collective-permute-start(bf16[64,2048]{1,0:T(8,128)(2,1)S(1)} %pad_maximum_fusion.refs_0_), channel_id=1, source_target_pairs={{0,192},{1,49},{2,194},{3,51},{4,196},{5,53},{6,198},{7,55},{8,200... | collective-permute-start | bytes 786440 | tf_op jit(solution)/shard_map/ppermute | solution.py:53
  97.4 9.6 %collective-permute-start.26 = (bf16[64,2048]{1,0:T(8,128)(2,1)S(1)}, bf16[64,2048]{1,0:T(8,128)(2,1)S(1)}, u32[]{:S(2)}, u32[]{:S(2)}) collective-permute-start(bf16[64,2048]{1,0:T(8,128)(2,1)S(1)} %pad_maximum_fusion.refs_0_), channel_id=1, source_target_pairs={{0,1},{1,0},{2,3},{3,2},{4,5},{5,4},{6,7},{7,6},{8,9},{9,8},{10,11... | collective-permute-start | bytes 786440 | tf_op jit(solution)/shard_map/ppermute | solution.py:53
  101.3 5.7 %collective-permute-start.27 = (bf16[64,2048]{1,0:T(8,128)(2,1)S(1)}, bf16[64,2048]{1,0:T(8,128)(2,1)S(1)}, u32[]{:S(2)}, u32[]{:S(2)}) collective-permute-start(bf16[64,2048]{1,0:T(8,128)(2,1)S(1)} %collective-permute-done.23.refs_1_), channel_id=1, source_target_pairs={{0,1},{1,0},{2,3},{3,2},{4,5},{5,4},{6,7},{7,6},{8,9},{9,8},{10,11... | collective-permute-start | bytes 786440 | tf_op jit(solution)/shard_map/ppermute | solution.py:53
  104.5 2.5 %collective-permute-start.28 = (bf16[64,2048]{1,0:T(8,128)(2,1)S(1)}, bf16[64,2048]{1,0:T(8,128)(2,1)S(1)}, u32[]{:S(2)}, u32[]{:S(2)}) collective-permute-start(bf16[64,2048]{1,0:T(8,128)(2,1)S(1)} %collective-permute-done.24.refs_2_), channel_id=1, source_target_pairs={{0,1},{1,0},{2,3},{3,2},{4,5},{5,4},{6,7},{7,6},{8,9},{9,8},{10,11... | collective-permute-start | bytes 786440 | tf_op jit(solution)/shard_map/ppermute | solution.py:53
  104.5 2.5 %collective-permute-start.29 = (bf16[64,2048]{1,0:T(8,128)(2,1)S(1)}, bf16[64,2048]{1,0:T(8,128)(2,1)S(1)}, u32[]{:S(2)}, u32[]{:S(2)}) collective-permute-start(bf16[64,2048]{1,0:T(8,128)(2,1)S(1)} %collective-permute-done.25.refs_3_), channel_id=1, source_target_pairs={{0,1},{1,0},{2,3},{3,2},{4,5},{5,4},{6,7},{7,6},{8,9},{9,8},{10,11... | collective-permute-start | bytes 786440 | tf_op jit(solution)/shard_map/ppermute | solution.py:53

commit v8 on v5

--- a/solution.py
+++ b/solution.py
@@ -264,14 +264,23 @@
     fill(other, 1 - c)
 
 
-def back_kernel(mixed, gact, w_ref, o_ref, p_halo, both, to_lat, to_lon, to_diag):
+def back_kernel(
+    mixed, gact, w_ref, o_ref, p_halo, both, to_lat_p, to_lat_g, to_lon, to_diag
+):
     both[:, :D] = dot(mixed[...], o_ref[...]).astype(bf16)
     both[:, D:] = dot(gact[...], w_ref[...], NT).astype(bf16)
-    split(dot(p_halo[...], both[...], TN), to_lat, to_lon, to_diag)
-
-
-def finish_kernel(f_loc, c_loc, both, r_lat, r_lon, r_diag, p_loc, select, gain, out, grad):
-    rows = jnp.concatenate([r_lat[...], r_lon[...], r_diag[...]], axis=0)
+    rows = dot(p_halo[...], both[...], TN)
+    to_lat_p[...] = rows[:LAT, :D].astype(bf16)
+    to_lat_g[...] = rows[:LAT, D:].astype(bf16)
+    to_lon[...] = rows[LAT : LAT + LON].astype(bf16)
+    to_diag[...] = rows[LAT + LON :].astype(bf16)
+
+
+def finish_kernel(
+    f_loc, c_loc, both, r_lat_p, r_lat_g, r_lon, r_diag, p_loc, select, gain, out, grad
+):
+    r_lat = jnp.concatenate([r_lat_p[...], r_lat_g[...]], axis=1)
+    rows = jnp.concatenate([r_lat, r_lon[...], r_diag[...]], axis=0)
     grid = dot(p_loc[...], both[...], TN) + dot(select[...], rows, TN)
     x = f_loc[...].astype(f32)
     out[...] = (x + grid[:, :D]).astype(bf16)
@@ -436,9 +445,9 @@
 def to_back(*args):
     return pl.pallas_call(
         back_kernel,
-        out_shape=[vshape(TOK, 2 * D)] + halo_shapes(2 * D),
+        out_shape=[vshape(TOK, 2 * D), vshape(LAT, D), vshape(LAT, D)] + halo_shapes(2 * D)[1:],
         in_specs=spec(5),
-        out_specs=spec(4),
+        out_specs=spec(5),
         compiler_params=params(),
         cost_estimate=cost(2 * 10**9, 5 * 10**6),
         name="back",
@@ -449,7 +458,7 @@
     return pl.pallas_call(
         finish_kernel,
         out_shape=[shape(TOK, D), shape(TOK, D)],
-        in_specs=spec(9),
+        in_specs=spec(10),
         out_specs=spec(2),
         compiler_params=params(),
         cost_estimate=cost(2 * 10**9, 8 * 10**6),
@@ -492,10 +501,11 @@
         fields.reshape(TOK, D), cotangent.reshape(TOK, D), select
     )
     f_halo = halo_in(*parts[:3])
-    c_halo = halo_in(*parts[3:])
     p_loc, p_halo, w, o, gain, fw, cw = to_load(
         f_vm, c_vm, *tables, qkv_weight, out_weight, layer_norm_gain.reshape(1, D)
     )
+    near, far, *parts = tied((*f_halo[1:], *parts[3:]))
+    f_halo, c_halo = (f_halo[0], near, far), halo_in(*parts)
     normed, qkv, probs, mixed = to_forward(place, fw, p_halo, *f_halo, gain, w)
     gact, own, other = to_backward(
         place, cw, p_halo, *c_halo, o, normed, qkv, probs, mixed
@@ -504,28 +514,28 @@
     there = send(other, to_sibling)
     part = [add(own[64 * k : 64 * k + 64], there[64 * k : 64 * k + 64]) for k in range(4)]
     mixed, gact, part = tied((mixed, gact, part))
-    both, to_lat, to_lon, to_diag = to_back(mixed, gact, w, o, p_halo)
+    both, to_lat_p, to_lat_g, to_lon, to_diag = to_back(mixed, gact, w, o, p_halo)
     recv = [send(part[k], first_axis(k)) for k in (1, 2, 3)]
-    recv, to_lat = tied((recv, to_lat))
+    recv, to_lon = tied((recv, to_lon))
     part = add(part[0], *recv)
-    part, to_lat, to_lon, to_diag = tied((part, to_lat, to_lon, to_diag))
+    part, to_lat_p, to_lat_g, to_lon, to_diag = tied((part, to_lat_p, to_lat_g, to_lon, to_diag))
     part = add(part[:16], *[send(part[16 * k : 16 * k + 16], second_axis(k)) for k in (1, 2, 3)])
-    r_lat = lax.ppermute(to_lat, BOTH, shifted(1, 0))
+    r_lat_p = lax.ppermute(to_lat_p, BOTH, shifted(1, 0))
+    r_lat_g = lax.ppermute(to_lat_g, BOTH, shifted(1, 0))
     r_lon = lax.ppermute(to_lon, BOTH, shifted(0, 1))
     r_diag = lax.ppermute(to_diag, BOTH, shifted(1, 1))
-    recv = send(part, flip_z(1))
-    recv, r_diag = tied((recv, r_diag))
-    part = add(part, recv)
-    recv = send(part, flip_z(2))
-    recv, r_lon = tied((recv, r_lon))
-    part = add(part, recv)
+    recv = [send(part, flip_z(k)) for k in (1, 2, 3)]
+    recv, r_lat_p, r_diag = tied((recv, r_lat_p, r_diag))
+    part = add(part, *recv)
     recv = send(part, flip_z(6))
-    recv, r_lat = tied((recv, r_lat))
+    recv, r_lat_g, r_lon = tied((recv, r_lat_g, r_lon))
     part = add(part, recv)
 
     block = jnp.concatenate([part] + [send(part, second_axis(4 - s)) for s in (1, 2, 3)], axis=0)
     mine = [send(block, first_axis(4 - s)) for s in (1, 2, 3)]
-    out, grad = to_finish(f_vm, c_vm, both, r_lat, r_lon, r_diag, p_loc, select, gain)
+    out, grad = to_finish(
+        f_vm, c_vm, both, r_lat_p, r_lat_g, r_lon, r_diag, p_loc, select, gain
+    )
     mine, out = tied((mine, out))
     mine = [block] + mine
     sibling = [send(m, to_sibling) for m in mine]

time: 105 us -> 113 us (1.076); the launches traced: 105 us -> 111 us
  starting transfers between devices: 60.2 us -> 65 us
  waiting for transfers between devices: 18.1 us -> 19.6 us
    ppermute x2, starting transfers between devices: 1.4 us -> 8.43 us  [halo_in(): lax.ppermute(lon, BOTH, shifted(0, -1))]
    ppermute x1, starting transfers between devices: 2.52 us -> 7.36 us  [on_device(): r_lon = lax.ppermute(to_lon, BOTH, shifted(0, 1))]
    ppermute x2, starting transfers between devices: 6.33 us -> 1.97 us  [halo_in(): lax.ppermute(lat, BOTH, shifted(-1, 0))]
    ppermute x1, starting transfers between devices: 5.1 us -> 2.67 us  [on_device(): r_diag = lax.ppermute(to_diag, BOTH, shifted(1, 1))]
    ppermute x1, waiting for transfers between devices: 0.01 us -> 1.81 us  [on_device(): r_lon = lax.ppermute(to_lon, BOTH, shifted(0, 1))]
    ppermute x2, starting transfers between devices: 10.5 us -> 11.9 us  [halo_in(): lax.ppermute(diag, BOTH, shifted(-1, -1))]
    ppermute x1, waiting for transfers between devices: 1.37 us -> 0.01 us  [on_device(): r_diag = lax.ppermute(to_diag, BOTH, shifted(1, 1))]
    ppermute x2, waiting for transfers between devices: 0.01 us -> 1.19 us  [halo_in(): lax.ppermute(diag, BOTH, shifted(-1, -1))]
  transfers between devices with their start and end apart: 29 -> 31, of which waited for: 10 -> 10; matrix products, arithmetic and copies ran while one was open for 0% -> 0% of each run, Pallas kernels for 13% -> 12%
where the time goes in v8:
time: 113 us; the launch traced here: 111 us
  starting transfers between devices  65 us (58%)
  Pallas kernels  24.8 us (22%)
  waiting for transfers between devices  19.6 us (17%)
    ppermute x21, starting transfers between devices, send(): return lax.ppermute(x, BOTH, route(step))  31.2 us
    ppermute x2, starting transfers between devices, halo_in(): lax.ppermute(diag, BOTH, shifted(-1, -1))  11.9 us
    ppermute x21, waiting for transfers between devices, send(): return lax.ppermute(x, BOTH, route(step))  11.1 us
    ppermute x2, starting transfers between devices, halo_in(): lax.ppermute(lon, BOTH, shifted(0, -1))  8.43 us
    ppermute x1, starting transfers between devices, on_device(): r_lon = lax.ppermute(to_lon, BOTH, shifted(0, 1))  7.36 us
    pallas_call x1, Pallas kernels, to_backward(): pl.pallas_call(backward_kernel, out_shape=[vshape(TOK, 3 * D), vshape(256...  6.84 us
    ppermute x1, waiting for transfers between devices, on_device(): r_lat_g = lax.ppermute(to_lat_g, BOTH, shifted(1, 0))  5.44 us
    pallas_call x2, Pallas kernels, to_weights(): pl.pallas_call(functools.partial(weights_kernel, side), out_shape=[shape(...  4.51 us
  transfers between devices with their start and end apart: 31, of which 10 were waited for; matrix products, arithmetic and copies ran while one was open for 0% of the time, Pallas kernels for 12%

profile of v8, /device:TPU:1, one launch (start us, length us, event | category | flops | bytes accessed | tf_op | source)
XLA Modules:
  0.0 111.1 jit_solution(608329071422895279)
XLA Ops:
  0.6 2.2 %pack.1 = (bf16[576,512]{1,0:T(8,128)(2,1)S(1)}, bf16[576,512]{1,0:T(8,128)(2,1)S(1)}, bf16[384,576]{1,0:T(8,128)(2,1)S(1)}, bf16[224,512]{1,0:T(8,128)(2,1)S(1)...) custom-call(bf16[576,512]{1,0:T(8,128)(2,1)} %bitcast.10, ...), custom_call_target="tpu_custom_call" | custom-call | flops 400000000 | bytes 2000000 | tf_op jit(solution)/shard_map/pack/pallas_call | solution.py:388
  2.8 3.3 %collective-permute-start.1 = (bf16[80,512]{1,0:T(8,128)(2,1)S(1)}, bf16[80,512]{1,0:T(8,128)(2,1)S(1)}, u32[]{:S(2)}, u32[]{:S(2)}) collective-permute-start(bf16[80,512]{1,0:T(8,128)(2,1)S(1)} %get-tuple-element.78), channel_id=1, source_target_pairs={{0,31},{1,0},{2,1},{3,2},{4,3},{5,4},{6,5},{7,6},{8,7},{9,8},{10,9... | collective-permute-start | bytes 245768 | tf_op jit(solution)/shard_map/ppermute | solution.py:483
  6.1 9.3 %collective-permute-start.2 = (bf16[80,512]{1,0:T(8,128)(2,1)S(1)}, bf16[80,512]{1,0:T(8,128)(2,1)S(1)}, u32[]{:S(2)}, u32[]{:S(2)}) collective-permute-start(bf16[80,512]{1,0:T(8,128)(2,1)S(1)} %get-tuple-element.79), channel_id=1, source_target_pairs={{0,255},{1,224},{2,225},{3,226},{4,227},{5,228},{6,229},{7,230},{8... | collective-permute-start | bytes 245768 | tf_op jit(solution)/shard_map/ppermute | solution.py:484
  17.1 1.4 %collective-permute-start.3 = (bf16[224,512]{1,0:T(8,128)(2,1)S(1)}, bf16[224,512]{1,0:T(8,128)(2,1)S(1)}, u32[]{:S(2)}, u32[]{:S(2)}) collective-permute-start(bf16[224,512]{1,0:T(8,128)(2,1)S(1)} %get-tuple-element.89), channel_id=1, source_target_pairs={{0,224},{1,225},{2,226},{3,227},{4,228},{5,229},{6,230},{7,231},{8... | collective-permute-start | bytes 688136 | tf_op jit(solution)/shard_map/ppermute | solution.py:482
  18.6 2.3 %load.1 = (bf16[576,576]{1,0:T(8,128)(2,1)S(1)}, bf16[576,384]{1,0:T(8,128)(2,1)S(1)}, bf16[512,1536]{1,0:T(8,128)(2,1)S(1)}, bf16[512,512]{1,0:T(8,128)(2,1)S(1...) custom-call(bf16[576,512]{1,0:T(8,128)(2,1)S(1)} %get-tuple-element.73.f_vm.f_loc, ...), custom_call_target="tpu_custom_call" | custom-call | flops 1000000 | bytes 10000 | tf_op jit(solution)/shard_map/load/pallas_call | solution.py:401
  20.8 5.1 %collective-permute-start.4 = (bf16[80,512]{1,0:T(8,128)(2,1)S(1)}, bf16[80,512]{1,0:T(8,128)(2,1)S(1)}, u32[]{:S(2)}, u32[]{:S(2)}) collective-permute-start(bf16[80,512]{1,0:T(8,128)(2,1)S(1)} %get-tuple-element.90), channel_id=1, source_target_pairs={{0,31},{1,0},{2,1},{3,2},{4,3},{5,4},{6,5},{7,6},{8,7},{9,8},{10,9... | collective-permute-start | bytes 245768 | tf_op jit(solution)/shard_map/ppermute | solution.py:483
  26.0 2.6 %collective-permute-start.5 = (bf16[80,512]{1,0:T(8,128)(2,1)S(1)}, bf16[80,512]{1,0:T(8,128)(2,1)S(1)}, u32[]{:S(2)}, u32[]{:S(2)}) collective-permute-start(bf16[80,512]{1,0:T(8,128)(2,1)S(1)} %get-tuple-element.91), channel_id=1, source_target_pairs={{0,255},{1,224},{2,225},{3,226},{4,227},{5,228},{6,229},{7,230},{8... | collective-permute-start | bytes 245768 | tf_op jit(solution)/shard_map/ppermute | solution.py:484
  28.7 4.2 %forward.1 = (bf16[576,512]{1,0:T(8,128)(2,1)S(1)}, bf16[576,1536]{1,0:T(8,128)(2,1)S(1)}, bf16[1152,576]{1,0:T(8,128)(2,1)S(1)}, bf16[576,512]{1,0:T(8,128)(2,1)S(1)}) custom-call(s32[4]{0:T(128)S(1)} %pad_add_fusion.place, bf16[576,512]{1,0:T(8,128)(2,1)S(1)} %get-tuple-element.75.refs_0_, bf16[576,384]{1,0:T(8,128)(2,1)S(1)} %get-tuple-element.76.refs_1_.p_halo, ...), custom_call_target="tpu_custom_call" | custom-call | flops 1000000 | bytes 10000 | tf_op jit(solution)/shard_map/forward/pallas_call | solution.py:415
  32.9 6.8 %backward.1 = (bf16[576,1536]{1,0:T(8,128)(2,1)S(1)}, bf16[256,2048]{1,0:T(8,128)(2,1)S(1)}, bf16[256,2048]{1,0:T(8,128)(2,1)S(1)}) custom-call(s32[4]{0:T(128)S(1)} %pad_add_fusion.place, bf16[576,512]{1,0:T(8,128)(2,1)S(1)} %get-tuple-element.88.refs_0_, bf16[576,384]{1,0:T(8,128)(2,1)S(1)} %get-tuple-element.76.refs_1_.p_halo, ...), custom_call_target="tpu_custom_call" | custom-call | flops 5000000000 | bytes 10000000 | tf_op jit(solution)/shard_map/backward/pallas_call | solution.py:429
  40.7 2.3 %collective-permute-done.6 = bf16[256,2048]{1,0:T(8,128)(2,1)S(1)} collective-permute-done((bf16[256,2048]{1,0:T(8,128)(2,1)S(1)}, bf16[256,2048]{1,0:T(8,128)(2,1)S(1)}, u32[]{:S(2)}, u32[]{:S(2)}) %collective-permute-start.6) | collective-permute-done | bytes 1048608 | tf_op jit(solution)/shard_map/ppermute | solution.py:53
  43.5 2.4 %collective-permute-start.8 = (bf16[64,2048]{1,0:T(8,128)(2,1)S(1)}, bf16[64,2048]{1,0:T(8,128)(2,1)S(1)}, u32[]{:S(2)}, u32[]{:S(2)}) collective-permute-start(bf16[64,2048]{1,0:T(8,128)(2,1)S(1)} %get-tuple-element.101), channel_id=1, source_target_pairs={{0,128},{1,33},{2,130},{3,35},{4,132},{5,37},{6,134},{7,39},{8,136... | collective-permute-start | bytes 786440 | tf_op jit(solution)/shard_map/ppermute | solution.py:53
  45.8 1.5 %collective-permute-start.9 = (bf16[64,2048]{1,0:T(8,128)(2,1)S(1)}, bf16[64,2048]{1,0:T(8,128)(2,1)S(1)}, u32[]{:S(2)}, u32[]{:S(2)}) collective-permute-start(bf16[64,2048]{1,0:T(8,128)(2,1)S(1)} %get-tuple-element.102), channel_id=1, source_target_pairs={{0,192},{1,49},{2,194},{3,51},{4,196},{5,53},{6,198},{7,55},{8,200... | collective-permute-start | bytes 786440 | tf_op jit(solution)/shard_map/ppermute | solution.py:53
  47.3 2.0 %back.1 = (bf16[576,1024]{1,0:T(8,128)(2,1)S(1)}, bf16[224,512]{1,0:T(8,128)(2,1)S(1)}, bf16[224,512]{1,0:T(8,128)(2,1)S(1)}, bf16[80,1024]{1,0:T(8,128)(2,1)S(1)}, bf16[80,1024]{1,0:T(8,128)(2,1)S(1)}) custom-call(bf16[576,512]{1,0:T(8,128)(2,1)S(1)} %get-tuple-element.103.refs_9_.mixed, bf16[576,1536]{1,0:T(8,128)(2,1)S(1)} %get-tuple-element.104.gact, ...), custom_call_target="tpu_custom_call" | custom-call | flops 2000000000 | bytes 5000000 | tf_op jit(solution)/shard_map/back/pallas_call | solution.py:446
  49.4 3.6 %collective-permute-done.7 = bf16[64,2048]{1,0:T(8,128)(2,1)S(1)} collective-permute-done((bf16[64,2048]{1,0:T(8,128)(2,1)S(1)}, bf16[64,2048]{1,0:T(8,128)(2,1)S(1)}, u32[]{:S(2)}, u32[]{:S(2)}) %collective-permute-start.7) | collective-permute-done | bytes 262176 | tf_op jit(solution)/shard_map/ppermute | solution.py:53
  53.8 2.7 %collective-permute-start.12 = (bf16[16,2048]{1,0:T(8,128)(2,1)S(1)}, bf16[16,2048]{1,0:T(8,128)(2,1)S(1)}, u32[]{:S(2)}, u32[]{:S(2)}) collective-permute-start(bf16[16,2048]{1,0:T(8,128)(2,1)S(1)} %get-tuple-element.146), channel_id=1, source_target_pairs={{0,48},{1,193},{2,50},{3,195},{4,52},{5,197},{6,54},{7,199},{8,56}... | collective-permute-start | bytes 196616 | tf_op jit(solution)/shard_map/ppermute | solution.py:53
  56.5 2.7 %collective-permute-start.17 = (bf16[80,1024]{1,0:T(8,128)(2,1)S(1)}, bf16[80,1024]{1,0:T(8,128)(2,1)S(1)}, u32[]{:S(2)}, u32[]{:S(2)}) collective-permute-start(bf16[80,1024]{1,0:T(8,128)(2,1)S(1)} %get-tuple-element.115), channel_id=1, source_target_pairs={{0,33},{1,34},{2,35},{3,36},{4,37},{5,38},{6,39},{7,40},{8,41},{9,... | collective-permute-start | bytes 491528 | tf_op jit(solution)/shard_map/ppermute | solution.py:526
  59.2 1.4 %collective-permute-start.16 = (bf16[224,512]{1,0:T(8,128)(2,1)S(1)}, bf16[224,512]{1,0:T(8,128)(2,1)S(1)}, u32[]{:S(2)}, u32[]{:S(2)}) collective-permute-start(bf16[224,512]{1,0:T(8,128)(2,1)S(1)} %get-tuple-element.114), channel_id=1, source_target_pairs={{0,32},{1,33},{2,34},{3,35},{4,36},{5,37},{6,38},{7,39},{8,40},{9,... | collective-permute-start | bytes 688136 | tf_op jit(solution)/shard_map/ppermute | solution.py:523
  61.2 1.9 %collective-permute-start.15 = (bf16[16,2048]{1,0:T(8,128)(2,1)S(1)}, bf16[16,2048]{1,0:T(8,128)(2,1)S(1)}, u32[]{:S(2)}, u32[]{:S(2)}) collective-permute-start(bf16[16,2048]{1,0:T(8,128)(2,1)S(1)} %add_convert_fusion.7), channel_id=1, source_target_pairs={{0,6},{1,7},{2,4},{3,5},{4,2},{5,3},{6,0},{7,1},{8,14},{9,15},{10,... | collective-permute-start | bytes 196616 | tf_op jit(solution)/shard_map/ppermute | solution.py:53
  63.1 1.7 %collective-permute-start.13 = (bf16[16,2048]{1,0:T(8,128)(2,1)S(1)}, bf16[16,2048]{1,0:T(8,128)(2,1)S(1)}, u32[]{:S(2)}, u32[]{:S(2)}) collective-permute-start(bf16[16,2048]{1,0:T(8,128)(2,1)S(1)} %add_convert_fusion.7), channel_id=1, source_target_pairs={{0,2},{1,3},{2,0},{3,1},{4,6},{5,7},{6,4},{7,5},{8,10},{9,11},{10,... | collective-permute-start | bytes 196616 | tf_op jit(solution)/shard_map/ppermute | solution.py:53
  64.8 1.5 %collective-permute-done.15 = bf16[16,2048]{1,0:T(8,128)(2,1)S(1)} collective-permute-done((bf16[16,2048]{1,0:T(8,128)(2,1)S(1)}, bf16[16,2048]{1,0:T(8,128)(2,1)S(1)}, u32[]{:S(2)}, u32[]{:S(2)}) %collective-permute-start.15) | collective-permute-done | bytes 65568 | tf_op jit(solution)/shard_map/ppermute | solution.py:53
  66.3 7.4 %collective-permute-start.20 = (bf16[80,1024]{1,0:T(8,128)(2,1)S(1)}, bf16[80,1024]{1,0:T(8,128)(2,1)S(1)}, u32[]{:S(2)}, u32[]{:S(2)}) collective-permute-start(bf16[80,1024]{1,0:T(8,128)(2,1)S(1)} %get-tuple-element.120), channel_id=1, source_target_pairs={{0,1},{1,2},{2,3},{3,4},{4,5},{5,6},{6,7},{7,8},{8,9},{9,10},{10,1... | collective-permute-start | bytes 491528 | tf_op jit(solution)/shard_map/ppermute | solution.py:525
  74.9 1.8 %collective-permute-done.20.r_lon = bf16[80,1024]{1,0:T(8,128)(2,1)S(1)} collective-permute-done((bf16[80,1024]{1,0:T(8,128)(2,1)S(1)}, bf16[80,1024]{1,0:T(8,128)(2,1)S(1)}, u32[]{:S(2)}, u32[]{:S(2)}) %collective-permute-start.20) | collective-permute-done | bytes 163872 | tf_op jit(solution)/shard_map/ppermute | solution.py:525
  76.7 5.4 %collective-permute-done.19.r_lat_g = bf16[224,512]{1,0:T(8,128)(2,1)S(1)} collective-permute-done((bf16[224,512]{1,0:T(8,128)(2,1)S(1)}, bf16[224,512]{1,0:T(8,128)(2,1)S(1)}, u32[]{:S(2)}, u32[]{:S(2)}) %collective-permute-start.19) | collective-permute-done | bytes 229408 | tf_op jit(solution)/shard_map/ppermute | solution.py:524
  82.3 2.0 %collective-permute-start.22 = (bf16[16,2048]{1,0:T(8,128)(2,1)S(1)}, bf16[16,2048]{1,0:T(8,128)(2,1)S(1)}, u32[]{:S(2)}, u32[]{:S(2)}) collective-permute-start(bf16[16,2048]{1,0:T(8,128)(2,1)S(1)} %add_convert_fusion.5), channel_id=1, source_target_pairs={{0,32},{1,129},{2,34},{3,131},{4,36},{5,133},{6,38},{7,135},{8,40}... | collective-permute-start | bytes 196616 | tf_op jit(solution)/shard_map/ppermute | solution.py:53
  85.3 2.2 %collective-permute-done.23 = bf16[16,2048]{1,0:T(8,128)(2,1)S(1)} collective-permute-done((bf16[16,2048]{1,0:T(8,128)(2,1)S(1)}, bf16[16,2048]{1,0:T(8,128)(2,1)S(1)}, u32[]{:S(2)}, u32[]{:S(2)}) %collective-permute-start.23) | collective-permute-done | bytes 65568 | tf_op jit(solution)/shard_map/ppermute | solution.py:53
  87.9 1.8 %collective-permute-start.26 = (bf16[64,2048]{1,0:T(8,128)(2,1)S(1)}, bf16[64,2048]{1,0:T(8,128)(2,1)S(1)}, u32[]{:S(2)}, u32[]{:S(2)}) collective-permute-start(bf16[64,2048]{1,0:T(8,128)(2,1)S(1)} %pad_maximum_fusion.refs_0_), channel_id=1, source_target_pairs={{0,64},{1,17},{2,66},{3,19},{4,68},{5,21},{6,70},{7,23},{8,72},{9,... | collective-permute-start | bytes 786440 | tf_op jit(solution)/shard_map/ppermute | solution.py:53
  89.7 4.2 %collective-permute-start.25 = (bf16[64,2048]{1,0:T(8,128)(2,1)S(1)}, bf16[64,2048]{1,0:T(8,128)(2,1)S(1)}, u32[]{:S(2)}, u32[]{:S(2)}) collective-permute-start(bf16[64,2048]{1,0:T(8,128)(2,1)S(1)} %pad_maximum_fusion.refs_0_), channel_id=1, source_target_pairs={{0,128},{1,33},{2,130},{3,35},{4,132},{5,37},{6,134},{7,39},{8,136... | collective-permute-start | bytes 786440 | tf_op jit(solution)/shard_map/ppermute | solution.py:53
  93.9 2.9 %finish.1 = (bf16[576,512]{1,0:T(8,128)(2,1)}, bf16[576,512]{1,0:T(8,128)(2,1)}) custom-call(bf16[576,512]{1,0:T(8,128)(2,1)S(1)} %get-tuple-element.73.f_vm.f_loc, bf16[576,512]{1,0:T(8,128)(2,1)S(1)} %get-tuple-element.74.c_vm.c_loc, bf16[576,1024]{1,0:T(8,128)(2,1)S(1)} %get-tuple-element.122.both, bf16[224,512]{1,0:T(8,128)(2,1)S(1)} %collective-permute-done.16.r_lat_p, ...), custom_call_target="tpu_custom_call" | custom-call | flops 2000000000 | bytes 8000000 | tf_op jit(solution)/shard_map/finish/pallas_call | solution.py:458
  96.8 4.5 %collective-permute-start.27 = (bf16[64,2048]{1,0:T(8,128)(2,1)S(1)}, bf16[64,2048]{1,0:T(8,128)(2,1)S(1)}, u32[]{:S(2)}, u32[]{:S(2)}) collective-permute-start(bf16[64,2048]{1,0:T(8,128)(2,1)S(1)} %pad_maximum_fusion.refs_0_), channel_id=1, source_target_pairs={{0,1},{1,0},{2,3},{3,2},{4,5},{5,4},{6,7},{7,6},{8,9},{9,8},{10,11... | collective-permute-start | bytes 786440 | tf_op jit(solution)/shard_map/ppermute | solution.py:53
  101.3 4.6 %collective-permute-start.28 = (bf16[64,2048]{1,0:T(8,128)(2,1)S(1)}, bf16[64,2048]{1,0:T(8,128)(2,1)S(1)}, u32[]{:S(2)}, u32[]{:S(2)}) collective-permute-start(bf16[64,2048]{1,0:T(8,128)(2,1)S(1)} %collective-permute-done.24.refs_1_), channel_id=1, source_target_pairs={{0,1},{1,0},{2,3},{3,2},{4,5},{5,4},{6,7},{7,6},{8,9},{9,8},{10,11... | collective-permute-start | bytes 786440 | tf_op jit(solution)/shard_map/ppermute | solution.py:53
  106.4 2.0 %weights0.1 = (f32[512,1536]{1,0:T(8,128)}, f32[512,512]{1,0:T(8,128)}, f32[1,512]{1,0:T(1,128)S(1)}) custom-call(s32[4]{0:T(128)S(1)} %pad_add_fusion.place, bf16[64,2048]{1,0:T(8,128)(2,1)S(1)} %pad_maximum_fusion.refs_0_, bf16[64,2048]{1,0:T(8,128)(2,1)S(1)} %collective-permute-done.24.refs_1_, bf16[64,2048]{1,0:T(8,128)(2,1)S(1)} %collective-permute-done.25.refs_2_, ...), custom_call_target="tpu_custom_call" | custom-call | flops 10000000 | bytes 4000000 | tf_op jit(solution)/shard_map/weights0/pallas_call | solution.py:333
  108.4 2.5 %weights1.1 = (f32[512,1536]{1,0:T(8,128)}, f32[512,512]{1,0:T(8,128)}, f32[1,512]{1,0:T(1,128)}) custom-call(s32[4]{0:T(128)S(1)} %pad_add_fusion.place, bf16[64,2048]{1,0:T(8,128)(2,1)S(1)} %collective-permute-done.27.refs_0_, bf16[64,2048]{1,0:T(8,128)(2,1)S(1)} %collective-permute-done.28.refs_1_, ...), custom_call_target="tpu_custom_call", output_to_operand_aliasing={{0}: (8, {}), {1}: (9, {})} | custom-call | flops 10000000 | bytes 4000000 | tf_op jit(solution)/shard_map/weights1/pallas_call | solution.py:333
  (46 shorter events, 7.8 us)
Async XLA Ops:
  2.8 13.1 %collective-permute-start.1 = (bf16[80,512]{1,0:T(8,128)(2,1)S(1)}, bf16[80,512]{1,0:T(8,128)(2,1)S(1)}, u32[]{:S(2)}, u32[]{:S(2)}) collective-permute-start(bf16[80,512]{1,0:T(8,128)(2,1)S(1)} %get-tuple-element.78), channel_id=1, source_target_pairs={{0,31},{1,0},{2,1},{3,2},{4,3},{5,4},{6,5},{7,6},{8,7},{9,8},{10,9... | collective-permute-start | bytes 245768 | tf_op jit(solution)/shard_map/ppermute | solution.py:483
  6.1 11.0 %collective-permute-start.2 = (bf16[80,512]{1,0:T(8,128)(2,1)S(1)}, bf16[80,512]{1,0:T(8,128)(2,1)S(1)}, u32[]{:S(2)}, u32[]{:S(2)}) collective-permute-start(bf16[80,512]{1,0:T(8,128)(2,1)S(1)} %get-tuple-element.79), channel_id=1, source_target_pairs={{0,255},{1,224},{2,225},{3,226},{4,227},{5,228},{6,229},{7,230},{8... | collective-permute-start | bytes 245768 | tf_op jit(solution)/shard_map/ppermute | solution.py:484
  15.4 13.3 %collective-permute-start = (bf16[224,512]{1,0:T(8,128)(2,1)S(1)}, bf16[224,512]{1,0:T(8,128)(2,1)S(1)}, u32[]{:S(2)}, u32[]{:S(2)}) collective-permute-start(bf16[224,512]{1,0:T(8,128)(2,1)S(1)} %get-tuple-element.77), channel_id=1, source_target_pairs={{0,224},{1,225},{2,226},{3,227},{4,228},{5,229},{6,230},{7,231},{8... | collective-permute-start | bytes 688136 | tf_op jit(solution)/shard_map/ppermute | solution.py:482
  17.1 15.8 %collective-permute-start.3 = (bf16[224,512]{1,0:T(8,128)(2,1)S(1)}, bf16[224,512]{1,0:T(8,128)(2,1)S(1)}, u32[]{:S(2)}, u32[]{:S(2)}) collective-permute-start(bf16[224,512]{1,0:T(8,128)(2,1)S(1)} %get-tuple-element.89), channel_id=1, source_target_pairs={{0,224},{1,225},{2,226},{3,227},{4,228},{5,229},{6,230},{7,231},{8... | collective-permute-start | bytes 688136 | tf_op jit(solution)/shard_map/ppermute | solution.py:482
  20.8 12.0 %collective-permute-start.4 = (bf16[80,512]{1,0:T(8,128)(2,1)S(1)}, bf16[80,512]{1,0:T(8,128)(2,1)S(1)}, u32[]{:S(2)}, u32[]{:S(2)}) collective-permute-start(bf16[80,512]{1,0:T(8,128)(2,1)S(1)} %get-tuple-element.90), channel_id=1, source_target_pairs={{0,31},{1,0},{2,1},{3,2},{4,3},{5,4},{6,5},{7,6},{8,7},{9,8},{10,9... | collective-permute-start | bytes 245768 | tf_op jit(solution)/shard_map/ppermute | solution.py:483
  26.0 6.9 %collective-permute-start.5 = (bf16[80,512]{1,0:T(8,128)(2,1)S(1)}, bf16[80,512]{1,0:T(8,128)(2,1)S(1)}, u32[]{:S(2)}, u32[]{:S(2)}) collective-permute-start(bf16[80,512]{1,0:T(8,128)(2,1)S(1)} %get-tuple-element.91), channel_id=1, source_target_pairs={{0,255},{1,224},{2,225},{3,226},{4,227},{5,228},{6,229},{7,230},{8... | collective-permute-start | bytes 245768 | tf_op jit(solution)/shard_map/ppermute | solution.py:484
  39.7 3.3 %collective-permute-start.6 = (bf16[256,2048]{1,0:T(8,128)(2,1)S(1)}, bf16[256,2048]{1,0:T(8,128)(2,1)S(1)}, u32[]{:S(2)}, u32[]{:S(2)}) collective-permute-start(bf16[256,2048]{1,0:T(8,128)(2,1)S(1)} %get-tuple-element.98), channel_id=1, source_target_pairs={{0,1},{1,0},{2,3},{3,2},{4,5},{5,4},{6,7},{7,6},{8,9},{9,8},{10,11... | collective-permute-start | bytes 3145736 | tf_op jit(solution)/shard_map/ppermute | solution.py:53
  43.4 9.6 %collective-permute-start.7 = (bf16[64,2048]{1,0:T(8,128)(2,1)S(1)}, bf16[64,2048]{1,0:T(8,128)(2,1)S(1)}, u32[]{:S(2)}, u32[]{:S(2)}) collective-permute-start(bf16[64,2048]{1,0:T(8,128)(2,1)S(1)} %get-tuple-element.100), channel_id=1, source_target_pairs={{0,64},{1,17},{2,66},{3,19},{4,68},{5,21},{6,70},{7,23},{8,72},{9,... | collective-permute-start | bytes 786440 | tf_op jit(solution)/shard_map/ppermute | solution.py:53
  43.5 9.5 %collective-permute-start.8 = (bf16[64,2048]{1,0:T(8,128)(2,1)S(1)}, bf16[64,2048]{1,0:T(8,128)(2,1)S(1)}, u32[]{:S(2)}, u32[]{:S(2)}) collective-permute-start(bf16[64,2048]{1,0:T(8,128)(2,1)S(1)} %get-tuple-element.101), channel_id=1, source_target_pairs={{0,128},{1,33},{2,130},{3,35},{4,132},{5,37},{6,134},{7,39},{8,136... | collective-permute-start | bytes 786440 | tf_op jit(solution)/shard_map/ppermute | solution.py:53
  45.8 7.8 %collective-permute-start.9 = (bf16[64,2048]{1,0:T(8,128)(2,1)S(1)}, bf16[64,2048]{1,0:T(8,128)(2,1)S(1)}, u32[]{:S(2)}, u32[]{:S(2)}) collective-permute-start(bf16[64,2048]{1,0:T(8,128)(2,1)S(1)} %get-tuple-element.102), channel_id=1, source_target_pairs={{0,192},{1,49},{2,194},{3,51},{4,196},{5,53},{6,198},{7,55},{8,200... | collective-permute-start | bytes 786440 | tf_op jit(solution)/shard_map/ppermute | solution.py:53
  53.8 6.9 %collective-permute-start.10 = (bf16[16,2048]{1,0:T(8,128)(2,1)S(1)}, bf16[16,2048]{1,0:T(8,128)(2,1)S(1)}, u32[]{:S(2)}, u32[]{:S(2)}) collective-permute-start(bf16[16,2048]{1,0:T(8,128)(2,1)S(1)} %get-tuple-element.145), channel_id=1, source_target_pairs={{0,16},{1,65},{2,18},{3,67},{4,20},{5,69},{6,22},{7,71},{8,24},{9,... | collective-permute-start | bytes 196616 | tf_op jit(solution)/shard_map/ppermute | solution.py:53
  53.8 6.8 %collective-permute-start.12 = (bf16[16,2048]{1,0:T(8,128)(2,1)S(1)}, bf16[16,2048]{1,0:T(8,128)(2,1)S(1)}, u32[]{:S(2)}, u32[]{:S(2)}) collective-permute-start(bf16[16,2048]{1,0:T(8,128)(2,1)S(1)} %get-tuple-element.146), channel_id=1, source_target_pairs={{0,48},{1,193},{2,50},{3,195},{4,52},{5,197},{6,54},{7,199},{8,56}... | collective-permute-start | bytes 196616 | tf_op jit(solution)/shard_map/ppermute | solution.py:53
  56.5 4.6 %collective-permute-start.11 = (bf16[16,2048]{1,0:T(8,128)(2,1)S(1)}, bf16[16,2048]{1,0:T(8,128)(2,1)S(1)}, u32[]{:S(2)}, u32[]{:S(2)}) collective-permute-start(bf16[16,2048]{1,0:T(8,128)(2,1)S(1)} %get-tuple-element.147), channel_id=1, source_target_pairs={{0,32},{1,129},{2,34},{3,131},{4,36},{5,133},{6,38},{7,135},{8,40}... | collective-permute-start | bytes 196616 | tf_op jit(solution)/shard_map/ppermute | solution.py:53
  56.5 17.2 %collective-permute-start.17 = (bf16[80,1024]{1,0:T(8,128)(2,1)S(1)}, bf16[80,1024]{1,0:T(8,128)(2,1)S(1)}, u32[]{:S(2)}, u32[]{:S(2)}) collective-permute-start(bf16[80,1024]{1,0:T(8,128)(2,1)S(1)} %get-tuple-element.115), channel_id=1, source_target_pairs={{0,33},{1,34},{2,35},{3,36},{4,37},{5,38},{6,39},{7,40},{8,41},{9,... | collective-permute-start | bytes 491528 | tf_op jit(solution)/shard_map/ppermute | solution.py:526
  59.2 14.5 %collective-permute-start.16 = (bf16[224,512]{1,0:T(8,128)(2,1)S(1)}, bf16[224,512]{1,0:T(8,128)(2,1)S(1)}, u32[]{:S(2)}, u32[]{:S(2)}) collective-permute-start(bf16[224,512]{1,0:T(8,128)(2,1)S(1)} %get-tuple-element.114), channel_id=1, source_target_pairs={{0,32},{1,33},{2,34},{3,35},{4,36},{5,37},{6,38},{7,39},{8,40},{9,... | collective-permute-start | bytes 688136 | tf_op jit(solution)/shard_map/ppermute | solution.py:523
  61.2 5.2 %collective-permute-start.15 = (bf16[16,2048]{1,0:T(8,128)(2,1)S(1)}, bf16[16,2048]{1,0:T(8,128)(2,1)S(1)}, u32[]{:S(2)}, u32[]{:S(2)}) collective-permute-start(bf16[16,2048]{1,0:T(8,128)(2,1)S(1)} %add_convert_fusion.7), channel_id=1, source_target_pairs={{0,6},{1,7},{2,4},{3,5},{4,2},{5,3},{6,0},{7,1},{8,14},{9,15},{10,... | collective-permute-start | bytes 196616 | tf_op jit(solution)/shard_map/ppermute | solution.py:53
  63.1 10.6 %collective-permute-start.14 = (bf16[16,2048]{1,0:T(8,128)(2,1)S(1)}, bf16[16,2048]{1,0:T(8,128)(2,1)S(1)}, u32[]{:S(2)}, u32[]{:S(2)}) collective-permute-start(bf16[16,2048]{1,0:T(8,128)(2,1)S(1)} %add_convert_fusion.7), channel_id=1, source_target_pairs={{0,4},{1,5},{2,6},{3,7},{4,0},{5,1},{6,2},{7,3},{8,12},{9,13},{10,... | collective-permute-start | bytes 196616 | tf_op jit(solution)/shard_map/ppermute | solution.py:53
  63.1 10.6 %collective-permute-start.13 = (bf16[16,2048]{1,0:T(8,128)(2,1)S(1)}, bf16[16,2048]{1,0:T(8,128)(2,1)S(1)}, u32[]{:S(2)}, u32[]{:S(2)}) collective-permute-start(bf16[16,2048]{1,0:T(8,128)(2,1)S(1)} %add_convert_fusion.7), channel_id=1, source_target_pairs={{0,2},{1,3},{2,0},{3,1},{4,6},{5,7},{6,4},{7,5},{8,10},{9,11},{10,... | collective-permute-start | bytes 196616 | tf_op jit(solution)/shard_map/ppermute | solution.py:53
  66.3 10.4 %collective-permute-start.20 = (bf16[80,1024]{1,0:T(8,128)(2,1)S(1)}, bf16[80,1024]{1,0:T(8,128)(2,1)S(1)}, u32[]{:S(2)}, u32[]{:S(2)}) collective-permute-start(bf16[80,1024]{1,0:T(8,128)(2,1)S(1)} %get-tuple-element.120), channel_id=1, source_target_pairs={{0,1},{1,2},{2,3},{3,4},{4,5},{5,6},{6,7},{7,8},{8,9},{9,10},{10,1... | collective-permute-start | bytes 491528 | tf_op jit(solution)/shard_map/ppermute | solution.py:525
  73.7 8.5 %collective-permute-start.19 = (bf16[224,512]{1,0:T(8,128)(2,1)S(1)}, bf16[224,512]{1,0:T(8,128)(2,1)S(1)}, u32[]{:S(2)}, u32[]{:S(2)}) collective-permute-start(bf16[224,512]{1,0:T(8,128)(2,1)S(1)} %get-tuple-element.119), channel_id=1, source_target_pairs={{0,32},{1,33},{2,34},{3,35},{4,36},{5,37},{6,38},{7,39},{8,40},{9,... | collective-permute-start | bytes 688136 | tf_op jit(solution)/shard_map/ppermute | solution.py:524
  73.8 8.4 %collective-permute-start.18 = (bf16[16,2048]{1,0:T(8,128)(2,1)S(1)}, bf16[16,2048]{1,0:T(8,128)(2,1)S(1)}, u32[]{:S(2)}, u32[]{:S(2)}) collective-permute-start(bf16[16,2048]{1,0:T(8,128)(2,1)S(1)} %add_convert_fusion.6), channel_id=1, source_target_pairs={{0,12},{1,13},{2,14},{3,15},{4,8},{5,9},{6,10},{7,11},{8,4},{9,5},... | collective-permute-start | bytes 196616 | tf_op jit(solution)/shard_map/ppermute | solution.py:53
  82.2 5.4 %collective-permute-start.23 = (bf16[16,2048]{1,0:T(8,128)(2,1)S(1)}, bf16[16,2048]{1,0:T(8,128)(2,1)S(1)}, u32[]{:S(2)}, u32[]{:S(2)}) collective-permute-start(bf16[16,2048]{1,0:T(8,128)(2,1)S(1)} %add_convert_fusion.5), channel_id=1, source_target_pairs={{0,16},{1,65},{2,18},{3,67},{4,20},{5,69},{6,22},{7,71},{8,24},{9,... | collective-permute-start | bytes 196616 | tf_op jit(solution)/shard_map/ppermute | solution.py:53
  82.3 5.3 %collective-permute-start.22 = (bf16[16,2048]{1,0:T(8,128)(2,1)S(1)}, bf16[16,2048]{1,0:T(8,128)(2,1)S(1)}, u32[]{:S(2)}, u32[]{:S(2)}) collective-permute-start(bf16[16,2048]{1,0:T(8,128)(2,1)S(1)} %add_convert_fusion.5), channel_id=1, source_target_pairs={{0,32},{1,129},{2,34},{3,131},{4,36},{5,133},{6,38},{7,135},{8,40}... | collective-permute-start | bytes 196616 | tf_op jit(solution)/shard_map/ppermute | solution.py:53
  84.3 3.6 %collective-permute-start.21 = (bf16[16,2048]{1,0:T(8,128)(2,1)S(1)}, bf16[16,2048]{1,0:T(8,128)(2,1)S(1)}, u32[]{:S(2)}, u32[]{:S(2)}) collective-permute-start(bf16[16,2048]{1,0:T(8,128)(2,1)S(1)} %add_convert_fusion.5), channel_id=1, source_target_pairs={{0,48},{1,193},{2,50},{3,195},{4,52},{5,197},{6,54},{7,199},{8,56}... | collective-permute-start | bytes 196616 | tf_op jit(solution)/shard_map/ppermute | solution.py:53
  87.9 13.3 %collective-permute-start.26 = (bf16[64,2048]{1,0:T(8,128)(2,1)S(1)}, bf16[64,2048]{1,0:T(8,128)(2,1)S(1)}, u32[]{:S(2)}, u32[]{:S(2)}) collective-permute-start(bf16[64,2048]{1,0:T(8,128)(2,1)S(1)} %pad_maximum_fusion.refs_0_), channel_id=1, source_target_pairs={{0,64},{1,17},{2,66},{3,19},{4,68},{5,21},{6,70},{7,23},{8,72},{9,... | collective-permute-start | bytes 786440 | tf_op jit(solution)/shard_map/ppermute | solution.py:53
  89.7 11.6 %collective-permute-start.25 = (bf16[64,2048]{1,0:T(8,128)(2,1)S(1)}, bf16[64,2048]{1,0:T(8,128)(2,1)S(1)}, u32[]{:S(2)}, u32[]{:S(2)}) collective-permute-start(bf16[64,2048]{1,0:T(8,128)(2,1)S(1)} %pad_maximum_fusion.refs_0_), channel_id=1, source_target_pairs={{0,128},{1,33},{2,130},{3,35},{4,132},{5,37},{6,134},{7,39},{8,136... | collective-permute-start | bytes 786440 | tf_op jit(solution)/shard_map/ppermute | solution.py:53
  93.9 7.4 %collective-permute-start.24 = (bf16[64,2048]{1,0:T(8,128)(2,1)S(1)}, bf16[64,2048]{1,0:T(8,128)(2,1)S(1)}, u32[]{:S(2)}, u32[]{:S(2)}) collective-permute-start(bf16[64,2048]{1,0:T(8,128)(2,1)S(1)} %pad_maximum_fusion.refs_0_), channel_id=1, source_target_pairs={{0,192},{1,49},{2,194},{3,51},{4,196},{5,53},{6,198},{7,55},{8,200... | collective-permute-start | bytes 786440 | tf_op jit(solution)/shard_map/ppermute | solution.py:53
  96.8 11.6 %collective-permute-start.27 = (bf16[64,2048]{1,0:T(8,128)(2,1)S(1)}, bf16[64,2048]{1,0:T(8,128)(2,1)S(1)}, u32[]{:S(2)}, u32[]{:S(2)}) collective-permute-start(bf16[64,2048]{1,0:T(8,128)(2,1)S(1)} %pad_maximum_fusion.refs_0_), channel_id=1, source_target_pairs={{0,1},{1,0},{2,3},{3,2},{4,5},{5,4},{6,7},{7,6},{8,9},{9,8},{10,11... | collective-permute-start | bytes 786440 | tf_op jit(solution)/shard_map/ppermute | solution.py:53
  101.3 7.1 %collective-permute-start.28 = (bf16[64,2048]{1,0:T(8,128)(2,1)S(1)}, bf16[64,2048]{1,0:T(8,128)(2,1)S(1)}, u32[]{:S(2)}, u32[]{:S(2)}) collective-permute-start(bf16[64,2048]{1,0:T(8,128)(2,1)S(1)} %collective-permute-done.24.refs_1_), channel_id=1, source_target_pairs={{0,1},{1,0},{2,3},{3,2},{4,5},{5,4},{6,7},{7,6},{8,9},{9,8},{10,11... | collective-permute-start | bytes 786440 | tf_op jit(solution)/shard_map/ppermute | solution.py:53
  105.9 2.5 %collective-permute-start.29 = (bf16[64,2048]{1,0:T(8,128)(2,1)S(1)}, bf16[64,2048]{1,0:T(8,128)(2,1)S(1)}, u32[]{:S(2)}, u32[]{:S(2)}) collective-permute-start(bf16[64,2048]{1,0:T(8,128)(2,1)S(1)} %collective-permute-done.25.refs_2_), channel_id=1, source_target_pairs={{0,1},{1,0},{2,3},{3,2},{4,5},{5,4},{6,7},{7,6},{8,9},{9,8},{10,11... | collective-permute-start | bytes 786440 | tf_op jit(solution)/shard_map/ppermute | solution.py:53
  105.9 2.5 %collective-permute-start.30 = (bf16[64,2048]{1,0:T(8,128)(2,1)S(1)}, bf16[64,2048]{1,0:T(8,128)(2,1)S(1)}, u32[]{:S(2)}, u32[]{:S(2)}) collective-permute-start(bf16[64,2048]{1,0:T(8,128)(2,1)S(1)} %collective-permute-done.26.refs_3_), channel_id=1, source_target_pairs={{0,1},{1,0},{2,3},{3,2},{4,5},{5,4},{6,7},{7,6},{8,9},{9,8},{10,11... | collective-permute-start | bytes 786440 | tf_op jit(solution)/shard_map/ppermute | solution.py:53

commit v9 on v5

--- a/solution.py
+++ b/solution.py
@@ -287,7 +287,7 @@
     if side == 0:
         w_ref, g_qkv, g_out, g_total, buf_q, buf_o, sem = refs
     else:
-        w_ref, before, gain, _, _, g_qkv, g_out, g_total, buf_q, buf_o, sem = refs
+        w_ref, before, gain, _, _, g_qkv, g_out, g_gain, buf_q, buf_o, sem, g_total = refs
     y, x, c = place[1], place[2], place[3]
     core = c if side == 0 else 1 - c
     d1 = jnp.where(core == 0, y, x)
@@ -313,6 +313,9 @@
         spread = jnp.where(lane == local + bands[i], sums, 0.0)
         total = total + jnp.sum(spread, axis=0, keepdims=True)
     g_total[...] = total if side == 0 else total / gain[...]
+    if side == 1:
+        copies.append(pltpu.make_async_copy(g_total, g_gain, sem.at[4, 0]))
+        copies[-1].start()
     for copy in copies:
         copy.wait()
 
@@ -329,12 +332,13 @@
             (vshape if side == 0 else shape)(1, D, dtype=f32),
         ],
         in_specs=spec(5, True) + extra,
-        out_specs=[anywhere, anywhere, inside],
+        out_specs=[anywhere, anywhere, inside if side == 0 else anywhere],
         scratch_shapes=[
             pltpu.VMEM((4, 64, 3 * D), f32),
             pltpu.VMEM((4, 64, D), f32),
-            pltpu.SemaphoreType.DMA((4, 2)),
-        ],
+            pltpu.SemaphoreType.DMA((5, 2)),
+        ]
+        + ([] if side == 0 else [pltpu.VMEM((1, D), f32)]),
         input_output_aliases={} if side == 0 else {8: 0, 9: 1},
         compiler_params=params(),
         cost_estimate=cost(10**7, 4 * 10**6),

time: 105 us -> 105 us (level)
  no operation moved by 1% of the time
where the time goes in v9:
time: 105 us; the launch traced here: 104 us
  starting transfers between devices  60.2 us (57%)
  Pallas kernels  24.3 us (23%)
  waiting for transfers between devices  18.1 us (17%)
    ppermute x20, starting transfers between devices, send(): return lax.ppermute(x, BOTH, route(step))  31.8 us
    ppermute x20, waiting for transfers between devices, send(): return lax.ppermute(x, BOTH, route(step))  11 us
    ppermute x2, starting transfers between devices, halo_in(): lax.ppermute(diag, BOTH, shifted(-1, -1))  10.5 us
    pallas_call x1, Pallas kernels, to_backward(): pl.pallas_call(backward_kernel, out_shape=[vshape(TOK, 3 * D), vshape(256...  6.84 us
    ppermute x2, starting transfers between devices, halo_in(): lax.ppermute(lat, BOTH, shifted(-1, 0))  6.33 us
    ppermute x1, waiting for transfers between devices, on_device(): r_lat = lax.ppermute(to_lat, BOTH, shifted(1, 0))  5.71 us
    ppermute x1, starting transfers between devices, on_device(): r_diag = lax.ppermute(to_diag, BOTH, shifted(1, 1))  5.1 us
    pallas_call x1, Pallas kernels, to_forward(): pl.pallas_call(forward_kernel, out_shape=[vshape(TOK, D), vshape(TOK, 3 *...  4.17 us
  transfers between devices with their start and end apart: 29, of which 10 were waited for; matrix products, arithmetic and copies ran while one was open for 0% of the time, Pallas kernels for 13%

profile of v9, /device:TPU:1, one launch (start us, length us, event | category | flops | bytes accessed | tf_op | source)
XLA Modules:
  0.0 104.3 jit_solution(10382391495518726423)
XLA Ops:
  0.6 2.2 %pack.1 = (bf16[576,512]{1,0:T(8,128)(2,1)S(1)}, bf16[576,512]{1,0:T(8,128)(2,1)S(1)}, bf16[384,576]{1,0:T(8,128)(2,1)S(1)}, bf16[224,512]{1,0:T(8,128)(2,1)S(1)...) custom-call(bf16[576,512]{1,0:T(8,128)(2,1)} %bitcast.10, ...), custom_call_target="tpu_custom_call" | custom-call | flops 400000000 | bytes 2000000 | tf_op jit(solution)/shard_map/pack/pallas_call | solution.py:383
  2.8 6.1 %collective-permute-start = (bf16[224,512]{1,0:T(8,128)(2,1)S(1)}, bf16[224,512]{1,0:T(8,128)(2,1)S(1)}, u32[]{:S(2)}, u32[]{:S(2)}) collective-permute-start(bf16[224,512]{1,0:T(8,128)(2,1)S(1)} %get-tuple-element.68), channel_id=1, source_target_pairs={{0,224},{1,225},{2,226},{3,227},{4,228},{5,229},{6,230},{7,231},{8... | collective-permute-start | bytes 688136 | tf_op jit(solution)/shard_map/ppermute | solution.py:477
  9.2 1.2 %collective-permute-start.1 = (bf16[80,512]{1,0:T(8,128)(2,1)S(1)}, bf16[80,512]{1,0:T(8,128)(2,1)S(1)}, u32[]{:S(2)}, u32[]{:S(2)}) collective-permute-start(bf16[80,512]{1,0:T(8,128)(2,1)S(1)} %get-tuple-element.69), channel_id=1, source_target_pairs={{0,31},{1,0},{2,1},{3,2},{4,3},{5,4},{6,5},{7,6},{8,7},{9,8},{10,9... | collective-permute-start | bytes 245768 | tf_op jit(solution)/shard_map/ppermute | solution.py:478
  10.4 8.2 %collective-permute-start.2 = (bf16[80,512]{1,0:T(8,128)(2,1)S(1)}, bf16[80,512]{1,0:T(8,128)(2,1)S(1)}, u32[]{:S(2)}, u32[]{:S(2)}) collective-permute-start(bf16[80,512]{1,0:T(8,128)(2,1)S(1)} %get-tuple-element.70), channel_id=1, source_target_pairs={{0,255},{1,224},{2,225},{3,226},{4,227},{5,228},{6,229},{7,230},{8... | collective-permute-start | bytes 245768 | tf_op jit(solution)/shard_map/ppermute | solution.py:479
  18.7 2.3 %load.1 = (bf16[576,576]{1,0:T(8,128)(2,1)S(1)}, bf16[576,384]{1,0:T(8,128)(2,1)S(1)}, bf16[512,1536]{1,0:T(8,128)(2,1)S(1)}, bf16[512,512]{1,0:T(8,128)(2,1)S(1...) custom-call(bf16[576,512]{1,0:T(8,128)(2,1)S(1)} %get-tuple-element.64.f_vm.f_loc, ...), custom_call_target="tpu_custom_call" | custom-call | flops 1000000 | bytes 10000 | tf_op jit(solution)/shard_map/load/pallas_call | solution.py:396
  21.0 2.3 %collective-permute-start.5 = (bf16[80,512]{1,0:T(8,128)(2,1)S(1)}, bf16[80,512]{1,0:T(8,128)(2,1)S(1)}, u32[]{:S(2)}, u32[]{:S(2)}) collective-permute-start(bf16[80,512]{1,0:T(8,128)(2,1)S(1)} %get-tuple-element.77), channel_id=1, source_target_pairs={{0,255},{1,224},{2,225},{3,226},{4,227},{5,228},{6,229},{7,230},{8... | collective-permute-start | bytes 245768 | tf_op jit(solution)/shard_map/ppermute | solution.py:479
  23.4 4.2 %forward.1 = (bf16[576,512]{1,0:T(8,128)(2,1)S(1)}, bf16[576,1536]{1,0:T(8,128)(2,1)S(1)}, bf16[1152,576]{1,0:T(8,128)(2,1)S(1)}, bf16[576,512]{1,0:T(8,128)(2,1)S(1)}) custom-call(s32[4]{0:T(128)S(1)} %pad_add_fusion.place, bf16[576,512]{1,0:T(8,128)(2,1)S(1)} %get-tuple-element.66.refs_0_, bf16[576,384]{1,0:T(8,128)(2,1)S(1)} %get-tuple-element.67.refs_1_.p_halo, ...), custom_call_target="tpu_custom_call" | custom-call | flops 1000000 | bytes 10000 | tf_op jit(solution)/shard_map/forward/pallas_call | solution.py:410
  27.6 6.8 %backward.1 = (bf16[576,1536]{1,0:T(8,128)(2,1)S(1)}, bf16[256,2048]{1,0:T(8,128)(2,1)S(1)}, bf16[256,2048]{1,0:T(8,128)(2,1)S(1)}) custom-call(s32[4]{0:T(128)S(1)} %pad_add_fusion.place, bf16[576,512]{1,0:T(8,128)(2,1)S(1)} %get-tuple-element.74.refs_0_, bf16[576,384]{1,0:T(8,128)(2,1)S(1)} %get-tuple-element.67.refs_1_.p_halo, ...), custom_call_target="tpu_custom_call" | custom-call | flops 5000000000 | bytes 10000000 | tf_op jit(solution)/shard_map/backward/pallas_call | solution.py:424
  35.0 2.3 %collective-permute-done.6 = bf16[256,2048]{1,0:T(8,128)(2,1)S(1)} collective-permute-done((bf16[256,2048]{1,0:T(8,128)(2,1)S(1)}, bf16[256,2048]{1,0:T(8,128)(2,1)S(1)}, u32[]{:S(2)}, u32[]{:S(2)}) %collective-permute-start.6) | collective-permute-done | bytes 1048608 | tf_op jit(solution)/shard_map/ppermute | solution.py:53
  38.7 2.0 %collective-permute-start.8 = (bf16[64,2048]{1,0:T(8,128)(2,1)S(1)}, bf16[64,2048]{1,0:T(8,128)(2,1)S(1)}, u32[]{:S(2)}, u32[]{:S(2)}) collective-permute-start(bf16[64,2048]{1,0:T(8,128)(2,1)S(1)} %get-tuple-element.87), channel_id=1, source_target_pairs={{0,128},{1,33},{2,130},{3,35},{4,132},{5,37},{6,134},{7,39},{8,136... | collective-permute-start | bytes 786440 | tf_op jit(solution)/shard_map/ppermute | solution.py:53
  40.7 1.4 %collective-permute-start.9 = (bf16[64,2048]{1,0:T(8,128)(2,1)S(1)}, bf16[64,2048]{1,0:T(8,128)(2,1)S(1)}, u32[]{:S(2)}, u32[]{:S(2)}) collective-permute-start(bf16[64,2048]{1,0:T(8,128)(2,1)S(1)} %get-tuple-element.88), channel_id=1, source_target_pairs={{0,192},{1,49},{2,194},{3,51},{4,196},{5,53},{6,198},{7,55},{8,200... | collective-permute-start | bytes 786440 | tf_op jit(solution)/shard_map/ppermute | solution.py:53
  42.1 2.0 %back.1 = (bf16[576,1024]{1,0:T(8,128)(2,1)S(1)}, bf16[224,1024]{1,0:T(8,128)(2,1)S(1)}, bf16[80,1024]{1,0:T(8,128)(2,1)S(1)}, bf16[80,1024]{1,0:T(8,128)(2,1)S(1)}) custom-call(bf16[576,512]{1,0:T(8,128)(2,1)S(1)} %get-tuple-element.89.refs_9_.mixed, bf16[576,1536]{1,0:T(8,128)(2,1)S(1)} %get-tuple-element.90.gact, ...), custom_call_target="tpu_custom_call" | custom-call | flops 2000000000 | bytes 5000000 | tf_op jit(solution)/shard_map/back/pallas_call | solution.py:441
  44.4 2.8 %collective-permute-done.8 = bf16[64,2048]{1,0:T(8,128)(2,1)S(1)} collective-permute-done((bf16[64,2048]{1,0:T(8,128)(2,1)S(1)}, bf16[64,2048]{1,0:T(8,128)(2,1)S(1)}, u32[]{:S(2)}, u32[]{:S(2)}) %collective-permute-start.8) | collective-permute-done | bytes 262176 | tf_op jit(solution)/shard_map/ppermute | solution.py:53
  49.1 1.6 %collective-permute-start.12 = (bf16[16,2048]{1,0:T(8,128)(2,1)S(1)}, bf16[16,2048]{1,0:T(8,128)(2,1)S(1)}, u32[]{:S(2)}, u32[]{:S(2)}) collective-permute-start(bf16[16,2048]{1,0:T(8,128)(2,1)S(1)} %get-tuple-element.128), channel_id=1, source_target_pairs={{0,48},{1,193},{2,50},{3,195},{4,52},{5,197},{6,54},{7,199},{8,56}... | collective-permute-start | bytes 196616 | tf_op jit(solution)/shard_map/ppermute | solution.py:53
  51.0 5.1 %collective-permute-start.14 = (bf16[80,1024]{1,0:T(8,128)(2,1)S(1)}, bf16[80,1024]{1,0:T(8,128)(2,1)S(1)}, u32[]{:S(2)}, u32[]{:S(2)}) collective-permute-start(bf16[80,1024]{1,0:T(8,128)(2,1)S(1)} %get-tuple-element.99), channel_id=1, source_target_pairs={{0,33},{1,34},{2,35},{3,36},{4,37},{5,38},{6,39},{7,40},{8,41},{9,... | collective-permute-start | bytes 491528 | tf_op jit(solution)/shard_map/ppermute | solution.py:519
  56.1 1.7 %collective-permute-start.13 = (bf16[16,2048]{1,0:T(8,128)(2,1)S(1)}, bf16[16,2048]{1,0:T(8,128)(2,1)S(1)}, u32[]{:S(2)}, u32[]{:S(2)}) collective-permute-start(bf16[16,2048]{1,0:T(8,128)(2,1)S(1)} %add_convert_fusion.8), channel_id=1, source_target_pairs={{0,2},{1,3},{2,0},{3,1},{4,6},{5,7},{6,4},{7,5},{8,10},{9,11},{10,... | collective-permute-start | bytes 196616 | tf_op jit(solution)/shard_map/ppermute | solution.py:53
  57.9 2.5 %collective-permute-start.16 = (bf16[80,1024]{1,0:T(8,128)(2,1)S(1)}, bf16[80,1024]{1,0:T(8,128)(2,1)S(1)}, u32[]{:S(2)}, u32[]{:S(2)}) collective-permute-start(bf16[80,1024]{1,0:T(8,128)(2,1)S(1)} %get-tuple-element.101), channel_id=1, source_target_pairs={{0,1},{1,2},{2,3},{3,4},{4,5},{5,6},{6,7},{7,8},{8,9},{9,10},{10,1... | collective-permute-start | bytes 491528 | tf_op jit(solution)/shard_map/ppermute | solution.py:518
  60.4 1.4 %collective-permute-done.14.r_diag = bf16[80,1024]{1,0:T(8,128)(2,1)S(1)} collective-permute-done((bf16[80,1024]{1,0:T(8,128)(2,1)S(1)}, bf16[80,1024]{1,0:T(8,128)(2,1)S(1)}, u32[]{:S(2)}, u32[]{:S(2)}) %collective-permute-start.14) | collective-permute-done | bytes 163872 | tf_op jit(solution)/shard_map/ppermute | solution.py:519
  61.8 2.7 %collective-permute-start.15 = (bf16[16,2048]{1,0:T(8,128)(2,1)S(1)}, bf16[16,2048]{1,0:T(8,128)(2,1)S(1)}, u32[]{:S(2)}, u32[]{:S(2)}) collective-permute-start(bf16[16,2048]{1,0:T(8,128)(2,1)S(1)} %add_convert_fusion.7), channel_id=1, source_target_pairs={{0,4},{1,5},{2,6},{3,7},{4,0},{5,1},{6,2},{7,3},{8,12},{9,13},{10,... | collective-permute-start | bytes 196616 | tf_op jit(solution)/shard_map/ppermute | solution.py:53
  64.5 2.6 %collective-permute-start.18 = (bf16[224,1024]{1,0:T(8,128)(2,1)S(1)}, bf16[224,1024]{1,0:T(8,128)(2,1)S(1)}, u32[]{:S(2)}, u32[]{:S(2)}) collective-permute-start(bf16[224,1024]{1,0:T(8,128)(2,1)S(1)} %get-tuple-element.103), channel_id=1, source_target_pairs={{0,32},{1,33},{2,34},{3,35},{4,36},{5,37},{6,38},{7,39},{8,40},{9,... | collective-permute-start | bytes 1376264 | tf_op jit(solution)/shard_map/ppermute | solution.py:517
  67.1 3.2 %collective-permute-start.17 = (bf16[16,2048]{1,0:T(8,128)(2,1)S(1)}, bf16[16,2048]{1,0:T(8,128)(2,1)S(1)}, u32[]{:S(2)}, u32[]{:S(2)}) collective-permute-start(bf16[16,2048]{1,0:T(8,128)(2,1)S(1)} %add_convert_fusion.6), channel_id=1, source_target_pairs={{0,12},{1,13},{2,14},{3,15},{4,8},{5,9},{6,10},{7,11},{8,4},{9,5},... | collective-permute-start | bytes 196616 | tf_op jit(solution)/shard_map/ppermute | solution.py:53
  70.3 2.2 %collective-permute-done.17 = bf16[16,2048]{1,0:T(8,128)(2,1)S(1)} collective-permute-done((bf16[16,2048]{1,0:T(8,128)(2,1)S(1)}, bf16[16,2048]{1,0:T(8,128)(2,1)S(1)}, u32[]{:S(2)}, u32[]{:S(2)}) %collective-permute-start.17) | collective-permute-done | bytes 65568 | tf_op jit(solution)/shard_map/ppermute | solution.py:53
  72.5 5.7 %collective-permute-done.18.r_lat = bf16[224,1024]{1,0:T(8,128)(2,1)S(1)} collective-permute-done((bf16[224,1024]{1,0:T(8,128)(2,1)S(1)}, bf16[224,1024]{1,0:T(8,128)(2,1)S(1)}, u32[]{:S(2)}, u32[]{:S(2)}) %collective-permute-start.18) | collective-permute-done | bytes 458784 | tf_op jit(solution)/shard_map/ppermute | solution.py:517
  78.7 2.4 %collective-permute-start.20 = (bf16[16,2048]{1,0:T(8,128)(2,1)S(1)}, bf16[16,2048]{1,0:T(8,128)(2,1)S(1)}, u32[]{:S(2)}, u32[]{:S(2)}) collective-permute-start(bf16[16,2048]{1,0:T(8,128)(2,1)S(1)} %add_convert_fusion.5), channel_id=1, source_target_pairs={{0,32},{1,129},{2,34},{3,131},{4,36},{5,133},{6,38},{7,135},{8,40}... | collective-permute-start | bytes 196616 | tf_op jit(solution)/shard_map/ppermute | solution.py:53
  81.4 1.2 %collective-permute-done.21 = bf16[16,2048]{1,0:T(8,128)(2,1)S(1)} collective-permute-done((bf16[16,2048]{1,0:T(8,128)(2,1)S(1)}, bf16[16,2048]{1,0:T(8,128)(2,1)S(1)}, u32[]{:S(2)}, u32[]{:S(2)}) %collective-permute-start.21) | collective-permute-done | bytes 65568 | tf_op jit(solution)/shard_map/ppermute | solution.py:53
  84.3 3.2 %collective-permute-start.23 = (bf16[64,2048]{1,0:T(8,128)(2,1)S(1)}, bf16[64,2048]{1,0:T(8,128)(2,1)S(1)}, u32[]{:S(2)}, u32[]{:S(2)}) collective-permute-start(bf16[64,2048]{1,0:T(8,128)(2,1)S(1)} %pad_maximum_fusion.refs_0_), channel_id=1, source_target_pairs={{0,128},{1,33},{2,130},{3,35},{4,132},{5,37},{6,134},{7,39},{8,136... | collective-permute-start | bytes 786440 | tf_op jit(solution)/shard_map/ppermute | solution.py:53
  87.5 1.2 %collective-permute-start.22 = (bf16[64,2048]{1,0:T(8,128)(2,1)S(1)}, bf16[64,2048]{1,0:T(8,128)(2,1)S(1)}, u32[]{:S(2)}, u32[]{:S(2)}) collective-permute-start(bf16[64,2048]{1,0:T(8,128)(2,1)S(1)} %pad_maximum_fusion.refs_0_), channel_id=1, source_target_pairs={{0,192},{1,49},{2,194},{3,51},{4,196},{5,53},{6,198},{7,55},{8,200... | collective-permute-start | bytes 786440 | tf_op jit(solution)/shard_map/ppermute | solution.py:53
  88.6 2.9 %finish.1 = (bf16[576,512]{1,0:T(8,128)(2,1)}, bf16[576,512]{1,0:T(8,128)(2,1)}) custom-call(bf16[576,512]{1,0:T(8,128)(2,1)S(1)} %get-tuple-element.64.f_vm.f_loc, bf16[576,512]{1,0:T(8,128)(2,1)S(1)} %get-tuple-element.65.c_vm.c_loc, bf16[576,1024]{1,0:T(8,128)(2,1)S(1)} %get-tuple-element.105.both, bf16[224,1024]{1,0:T(8,128)(2,1)S(1)} %collective-permute-done.18.r_lat, ...), custom_call_target="tpu_custom_call" | custom-call | flops 2000000000 | bytes 8000000 | tf_op jit(solution)/shard_map/finish/pallas_call | solution.py:453
  91.5 3.5 %collective-permute-start.25 = (bf16[64,2048]{1,0:T(8,128)(2,1)S(1)}, bf16[64,2048]{1,0:T(8,128)(2,1)S(1)}, u32[]{:S(2)}, u32[]{:S(2)}) collective-permute-start(bf16[64,2048]{1,0:T(8,128)(2,1)S(1)} %pad_maximum_fusion.refs_0_), channel_id=1, source_target_pairs={{0,1},{1,0},{2,3},{3,2},{4,5},{5,4},{6,7},{7,6},{8,9},{9,8},{10,11... | collective-permute-start | bytes 786440 | tf_op jit(solution)/shard_map/ppermute | solution.py:53
  95.0 4.5 %collective-permute-start.26 = (bf16[64,2048]{1,0:T(8,128)(2,1)S(1)}, bf16[64,2048]{1,0:T(8,128)(2,1)S(1)}, u32[]{:S(2)}, u32[]{:S(2)}) collective-permute-start(bf16[64,2048]{1,0:T(8,128)(2,1)S(1)} %collective-permute-done.22.refs_1_), channel_id=1, source_target_pairs={{0,1},{1,0},{2,3},{3,2},{4,5},{5,4},{6,7},{7,6},{8,9},{9,8},{10,11... | collective-permute-start | bytes 786440 | tf_op jit(solution)/shard_map/ppermute | solution.py:53
  100.1 2.0 %weights0.1 = (f32[512,1536]{1,0:T(8,128)}, f32[512,512]{1,0:T(8,128)}, f32[1,512]{1,0:T(1,128)S(1)}) custom-call(s32[4]{0:T(128)S(1)} %pad_add_fusion.place, bf16[64,2048]{1,0:T(8,128)(2,1)S(1)} %pad_maximum_fusion.refs_0_, bf16[64,2048]{1,0:T(8,128)(2,1)S(1)} %collective-permute-done.22.refs_1_, bf16[64,2048]{1,0:T(8,128)(2,1)S(1)} %collective-permute-done.23.refs_2_, ...), custom_call_target="tpu_custom_call" | custom-call | flops 10000000 | bytes 4000000 | tf_op jit(solution)/shard_map/weights0/pallas_call | solution.py:327
  102.1 2.0 %weights1.1 = (f32[512,1536]{1,0:T(8,128)}, f32[512,512]{1,0:T(8,128)}, f32[1,512]{1,0:T(1,128)}) custom-call(s32[4]{0:T(128)S(1)} %pad_add_fusion.place, bf16[64,2048]{1,0:T(8,128)(2,1)S(1)} %collective-permute-done.25.refs_0_, bf16[64,2048]{1,0:T(8,128)(2,1)S(1)} %collective-permute-done.26.refs_1_, ...), custom_call_target="tpu_custom_call", output_to_operand_aliasing={{0}: (8, {}), {1}: (9, {})} | custom-call | flops 10000000 | bytes 4000000 | tf_op jit(solution)/shard_map/weights1/pallas_call | solution.py:327
  (43 shorter events, 8.1 us)
Async XLA Ops:
  2.8 20.6 %collective-permute-start = (bf16[224,512]{1,0:T(8,128)(2,1)S(1)}, bf16[224,512]{1,0:T(8,128)(2,1)S(1)}, u32[]{:S(2)}, u32[]{:S(2)}) collective-permute-start(bf16[224,512]{1,0:T(8,128)(2,1)S(1)} %get-tuple-element.68), channel_id=1, source_target_pairs={{0,224},{1,225},{2,226},{3,227},{4,228},{5,229},{6,230},{7,231},{8... | collective-permute-start | bytes 688136 | tf_op jit(solution)/shard_map/ppermute | solution.py:477
  8.9 18.7 %collective-permute-start.3 = (bf16[224,512]{1,0:T(8,128)(2,1)S(1)}, bf16[224,512]{1,0:T(8,128)(2,1)S(1)}, u32[]{:S(2)}, u32[]{:S(2)}) collective-permute-start(bf16[224,512]{1,0:T(8,128)(2,1)S(1)} %get-tuple-element.75), channel_id=1, source_target_pairs={{0,224},{1,225},{2,226},{3,227},{4,228},{5,229},{6,230},{7,231},{8... | collective-permute-start | bytes 688136 | tf_op jit(solution)/shard_map/ppermute | solution.py:477
  9.2 11.8 %collective-permute-start.1 = (bf16[80,512]{1,0:T(8,128)(2,1)S(1)}, bf16[80,512]{1,0:T(8,128)(2,1)S(1)}, u32[]{:S(2)}, u32[]{:S(2)}) collective-permute-start(bf16[80,512]{1,0:T(8,128)(2,1)S(1)} %get-tuple-element.69), channel_id=1, source_target_pairs={{0,31},{1,0},{2,1},{3,2},{4,3},{5,4},{6,5},{7,6},{8,7},{9,8},{10,9... | collective-permute-start | bytes 245768 | tf_op jit(solution)/shard_map/ppermute | solution.py:478
  10.4 13.0 %collective-permute-start.2 = (bf16[80,512]{1,0:T(8,128)(2,1)S(1)}, bf16[80,512]{1,0:T(8,128)(2,1)S(1)}, u32[]{:S(2)}, u32[]{:S(2)}) collective-permute-start(bf16[80,512]{1,0:T(8,128)(2,1)S(1)} %get-tuple-element.70), channel_id=1, source_target_pairs={{0,255},{1,224},{2,225},{3,226},{4,227},{5,228},{6,229},{7,230},{8... | collective-permute-start | bytes 245768 | tf_op jit(solution)/shard_map/ppermute | solution.py:479
  18.6 9.0 %collective-permute-start.4 = (bf16[80,512]{1,0:T(8,128)(2,1)S(1)}, bf16[80,512]{1,0:T(8,128)(2,1)S(1)}, u32[]{:S(2)}, u32[]{:S(2)}) collective-permute-start(bf16[80,512]{1,0:T(8,128)(2,1)S(1)} %get-tuple-element.76), channel_id=1, source_target_pairs={{0,31},{1,0},{2,1},{3,2},{4,3},{5,4},{6,5},{7,6},{8,7},{9,8},{10,9... | collective-permute-start | bytes 245768 | tf_op jit(solution)/shard_map/ppermute | solution.py:478
  21.0 6.6 %collective-permute-start.5 = (bf16[80,512]{1,0:T(8,128)(2,1)S(1)}, bf16[80,512]{1,0:T(8,128)(2,1)S(1)}, u32[]{:S(2)}, u32[]{:S(2)}) collective-permute-start(bf16[80,512]{1,0:T(8,128)(2,1)S(1)} %get-tuple-element.77), channel_id=1, source_target_pairs={{0,255},{1,224},{2,225},{3,226},{4,227},{5,228},{6,229},{7,230},{8... | collective-permute-start | bytes 245768 | tf_op jit(solution)/shard_map/ppermute | solution.py:479
  34.5 2.8 %collective-permute-start.6 = (bf16[256,2048]{1,0:T(8,128)(2,1)S(1)}, bf16[256,2048]{1,0:T(8,128)(2,1)S(1)}, u32[]{:S(2)}, u32[]{:S(2)}) collective-permute-start(bf16[256,2048]{1,0:T(8,128)(2,1)S(1)} %get-tuple-element.84), channel_id=1, source_target_pairs={{0,1},{1,0},{2,3},{3,2},{4,5},{5,4},{6,7},{7,6},{8,9},{9,8},{10,11... | collective-permute-start | bytes 3145736 | tf_op jit(solution)/shard_map/ppermute | solution.py:53
  37.6 6.8 %collective-permute-start.7 = (bf16[64,2048]{1,0:T(8,128)(2,1)S(1)}, bf16[64,2048]{1,0:T(8,128)(2,1)S(1)}, u32[]{:S(2)}, u32[]{:S(2)}) collective-permute-start(bf16[64,2048]{1,0:T(8,128)(2,1)S(1)} %get-tuple-element.86), channel_id=1, source_target_pairs={{0,64},{1,17},{2,66},{3,19},{4,68},{5,21},{6,70},{7,23},{8,72},{9,... | collective-permute-start | bytes 786440 | tf_op jit(solution)/shard_map/ppermute | solution.py:53
  38.7 8.5 %collective-permute-start.8 = (bf16[64,2048]{1,0:T(8,128)(2,1)S(1)}, bf16[64,2048]{1,0:T(8,128)(2,1)S(1)}, u32[]{:S(2)}, u32[]{:S(2)}) collective-permute-start(bf16[64,2048]{1,0:T(8,128)(2,1)S(1)} %get-tuple-element.87), channel_id=1, source_target_pairs={{0,128},{1,33},{2,130},{3,35},{4,132},{5,37},{6,134},{7,39},{8,136... | collective-permute-start | bytes 786440 | tf_op jit(solution)/shard_map/ppermute | solution.py:53
  40.7 7.2 %collective-permute-start.9 = (bf16[64,2048]{1,0:T(8,128)(2,1)S(1)}, bf16[64,2048]{1,0:T(8,128)(2,1)S(1)}, u32[]{:S(2)}, u32[]{:S(2)}) collective-permute-start(bf16[64,2048]{1,0:T(8,128)(2,1)S(1)} %get-tuple-element.88), channel_id=1, source_target_pairs={{0,192},{1,49},{2,194},{3,51},{4,196},{5,53},{6,198},{7,55},{8,200... | collective-permute-start | bytes 786440 | tf_op jit(solution)/shard_map/ppermute | solution.py:53
  48.0 8.1 %collective-permute-start.10 = (bf16[16,2048]{1,0:T(8,128)(2,1)S(1)}, bf16[16,2048]{1,0:T(8,128)(2,1)S(1)}, u32[]{:S(2)}, u32[]{:S(2)}) collective-permute-start(bf16[16,2048]{1,0:T(8,128)(2,1)S(1)} %get-tuple-element.127), channel_id=1, source_target_pairs={{0,16},{1,65},{2,18},{3,67},{4,20},{5,69},{6,22},{7,71},{8,24},{9,... | collective-permute-start | bytes 196616 | tf_op jit(solution)/shard_map/ppermute | solution.py:53
  49.1 7.0 %collective-permute-start.12 = (bf16[16,2048]{1,0:T(8,128)(2,1)S(1)}, bf16[16,2048]{1,0:T(8,128)(2,1)S(1)}, u32[]{:S(2)}, u32[]{:S(2)}) collective-permute-start(bf16[16,2048]{1,0:T(8,128)(2,1)S(1)} %get-tuple-element.128), channel_id=1, source_target_pairs={{0,48},{1,193},{2,50},{3,195},{4,52},{5,197},{6,54},{7,199},{8,56}... | collective-permute-start | bytes 196616 | tf_op jit(solution)/shard_map/ppermute | solution.py:53
  50.7 5.4 %collective-permute-start.11 = (bf16[16,2048]{1,0:T(8,128)(2,1)S(1)}, bf16[16,2048]{1,0:T(8,128)(2,1)S(1)}, u32[]{:S(2)}, u32[]{:S(2)}) collective-permute-start(bf16[16,2048]{1,0:T(8,128)(2,1)S(1)} %get-tuple-element.129), channel_id=1, source_target_pairs={{0,32},{1,129},{2,34},{3,131},{4,36},{5,133},{6,38},{7,135},{8,40}... | collective-permute-start | bytes 196616 | tf_op jit(solution)/shard_map/ppermute | solution.py:53
  51.0 10.8 %collective-permute-start.14 = (bf16[80,1024]{1,0:T(8,128)(2,1)S(1)}, bf16[80,1024]{1,0:T(8,128)(2,1)S(1)}, u32[]{:S(2)}, u32[]{:S(2)}) collective-permute-start(bf16[80,1024]{1,0:T(8,128)(2,1)S(1)} %get-tuple-element.99), channel_id=1, source_target_pairs={{0,33},{1,34},{2,35},{3,36},{4,37},{5,38},{6,39},{7,40},{8,41},{9,... | collective-permute-start | bytes 491528 | tf_op jit(solution)/shard_map/ppermute | solution.py:519
  56.1 4.2 %collective-permute-start.13 = (bf16[16,2048]{1,0:T(8,128)(2,1)S(1)}, bf16[16,2048]{1,0:T(8,128)(2,1)S(1)}, u32[]{:S(2)}, u32[]{:S(2)}) collective-permute-start(bf16[16,2048]{1,0:T(8,128)(2,1)S(1)} %add_convert_fusion.8), channel_id=1, source_target_pairs={{0,2},{1,3},{2,0},{3,1},{4,6},{5,7},{6,4},{7,5},{8,10},{9,11},{10,... | collective-permute-start | bytes 196616 | tf_op jit(solution)/shard_map/ppermute | solution.py:53
  57.9 9.2 %collective-permute-start.16 = (bf16[80,1024]{1,0:T(8,128)(2,1)S(1)}, bf16[80,1024]{1,0:T(8,128)(2,1)S(1)}, u32[]{:S(2)}, u32[]{:S(2)}) collective-permute-start(bf16[80,1024]{1,0:T(8,128)(2,1)S(1)} %get-tuple-element.101), channel_id=1, source_target_pairs={{0,1},{1,2},{2,3},{3,4},{4,5},{5,6},{6,7},{7,8},{8,9},{9,10},{10,1... | collective-permute-start | bytes 491528 | tf_op jit(solution)/shard_map/ppermute | solution.py:518
  61.8 5.3 %collective-permute-start.15 = (bf16[16,2048]{1,0:T(8,128)(2,1)S(1)}, bf16[16,2048]{1,0:T(8,128)(2,1)S(1)}, u32[]{:S(2)}, u32[]{:S(2)}) collective-permute-start(bf16[16,2048]{1,0:T(8,128)(2,1)S(1)} %add_convert_fusion.7), channel_id=1, source_target_pairs={{0,4},{1,5},{2,6},{3,7},{4,0},{5,1},{6,2},{7,3},{8,12},{9,13},{10,... | collective-permute-start | bytes 196616 | tf_op jit(solution)/shard_map/ppermute | solution.py:53
  64.5 13.7 %collective-permute-start.18 = (bf16[224,1024]{1,0:T(8,128)(2,1)S(1)}, bf16[224,1024]{1,0:T(8,128)(2,1)S(1)}, u32[]{:S(2)}, u32[]{:S(2)}) collective-permute-start(bf16[224,1024]{1,0:T(8,128)(2,1)S(1)} %get-tuple-element.103), channel_id=1, source_target_pairs={{0,32},{1,33},{2,34},{3,35},{4,36},{5,37},{6,38},{7,39},{8,40},{9,... | collective-permute-start | bytes 1376264 | tf_op jit(solution)/shard_map/ppermute | solution.py:517
  67.1 5.4 %collective-permute-start.17 = (bf16[16,2048]{1,0:T(8,128)(2,1)S(1)}, bf16[16,2048]{1,0:T(8,128)(2,1)S(1)}, u32[]{:S(2)}, u32[]{:S(2)}) collective-permute-start(bf16[16,2048]{1,0:T(8,128)(2,1)S(1)} %add_convert_fusion.6), channel_id=1, source_target_pairs={{0,12},{1,13},{2,14},{3,15},{4,8},{5,9},{6,10},{7,11},{8,4},{9,5},... | collective-permute-start | bytes 196616 | tf_op jit(solution)/shard_map/ppermute | solution.py:53
  78.2 4.4 %collective-permute-start.21 = (bf16[16,2048]{1,0:T(8,128)(2,1)S(1)}, bf16[16,2048]{1,0:T(8,128)(2,1)S(1)}, u32[]{:S(2)}, u32[]{:S(2)}) collective-permute-start(bf16[16,2048]{1,0:T(8,128)(2,1)S(1)} %add_convert_fusion.5), channel_id=1, source_target_pairs={{0,16},{1,65},{2,18},{3,67},{4,20},{5,69},{6,22},{7,71},{8,24},{9,... | collective-permute-start | bytes 196616 | tf_op jit(solution)/shard_map/ppermute | solution.py:53
  78.7 4.7 %collective-permute-start.20 = (bf16[16,2048]{1,0:T(8,128)(2,1)S(1)}, bf16[16,2048]{1,0:T(8,128)(2,1)S(1)}, u32[]{:S(2)}, u32[]{:S(2)}) collective-permute-start(bf16[16,2048]{1,0:T(8,128)(2,1)S(1)} %add_convert_fusion.5), channel_id=1, source_target_pairs={{0,32},{1,129},{2,34},{3,131},{4,36},{5,133},{6,38},{7,135},{8,40}... | collective-permute-start | bytes 196616 | tf_op jit(solution)/shard_map/ppermute | solution.py:53
  81.1 3.1 %collective-permute-start.19 = (bf16[16,2048]{1,0:T(8,128)(2,1)S(1)}, bf16[16,2048]{1,0:T(8,128)(2,1)S(1)}, u32[]{:S(2)}, u32[]{:S(2)}) collective-permute-start(bf16[16,2048]{1,0:T(8,128)(2,1)S(1)} %add_convert_fusion.5), channel_id=1, source_target_pairs={{0,48},{1,193},{2,50},{3,195},{4,52},{5,197},{6,54},{7,199},{8,56}... | collective-permute-start | bytes 196616 | tf_op jit(solution)/shard_map/ppermute | solution.py:53
  84.2 10.8 %collective-permute-start.24 = (bf16[64,2048]{1,0:T(8,128)(2,1)S(1)}, bf16[64,2048]{1,0:T(8,128)(2,1)S(1)}, u32[]{:S(2)}, u32[]{:S(2)}) collective-permute-start(bf16[64,2048]{1,0:T(8,128)(2,1)S(1)} %pad_maximum_fusion.refs_0_), channel_id=1, source_target_pairs={{0,64},{1,17},{2,66},{3,19},{4,68},{5,21},{6,70},{7,23},{8,72},{9,... | collective-permute-start | bytes 786440 | tf_op jit(solution)/shard_map/ppermute | solution.py:53
  84.3 10.7 %collective-permute-start.23 = (bf16[64,2048]{1,0:T(8,128)(2,1)S(1)}, bf16[64,2048]{1,0:T(8,128)(2,1)S(1)}, u32[]{:S(2)}, u32[]{:S(2)}) collective-permute-start(bf16[64,2048]{1,0:T(8,128)(2,1)S(1)} %pad_maximum_fusion.refs_0_), channel_id=1, source_target_pairs={{0,128},{1,33},{2,130},{3,35},{4,132},{5,37},{6,134},{7,39},{8,136... | collective-permute-start | bytes 786440 | tf_op jit(solution)/shard_map/ppermute | solution.py:53
  87.5 7.6 %collective-permute-start.22 = (bf16[64,2048]{1,0:T(8,128)(2,1)S(1)}, bf16[64,2048]{1,0:T(8,128)(2,1)S(1)}, u32[]{:S(2)}, u32[]{:S(2)}) collective-permute-start(bf16[64,2048]{1,0:T(8,128)(2,1)S(1)} %pad_maximum_fusion.refs_0_), channel_id=1, source_target_pairs={{0,192},{1,49},{2,194},{3,51},{4,196},{5,53},{6,198},{7,55},{8,200... | collective-permute-start | bytes 786440 | tf_op jit(solution)/shard_map/ppermute | solution.py:53
  91.5 10.5 %collective-permute-start.25 = (bf16[64,2048]{1,0:T(8,128)(2,1)S(1)}, bf16[64,2048]{1,0:T(8,128)(2,1)S(1)}, u32[]{:S(2)}, u32[]{:S(2)}) collective-permute-start(bf16[64,2048]{1,0:T(8,128)(2,1)S(1)} %pad_maximum_fusion.refs_0_), channel_id=1, source_target_pairs={{0,1},{1,0},{2,3},{3,2},{4,5},{5,4},{6,7},{7,6},{8,9},{9,8},{10,11... | collective-permute-start | bytes 786440 | tf_op jit(solution)/shard_map/ppermute | solution.py:53
  95.0 7.0 %collective-permute-start.26 = (bf16[64,2048]{1,0:T(8,128)(2,1)S(1)}, bf16[64,2048]{1,0:T(8,128)(2,1)S(1)}, u32[]{:S(2)}, u32[]{:S(2)}) collective-permute-start(bf16[64,2048]{1,0:T(8,128)(2,1)S(1)} %collective-permute-done.22.refs_1_), channel_id=1, source_target_pairs={{0,1},{1,0},{2,3},{3,2},{4,5},{5,4},{6,7},{7,6},{8,9},{9,8},{10,11... | collective-permute-start | bytes 786440 | tf_op jit(solution)/shard_map/ppermute | solution.py:53
  99.6 2.5 %collective-permute-start.27 = (bf16[64,2048]{1,0:T(8,128)(2,1)S(1)}, bf16[64,2048]{1,0:T(8,128)(2,1)S(1)}, u32[]{:S(2)}, u32[]{:S(2)}) collective-permute-start(bf16[64,2048]{1,0:T(8,128)(2,1)S(1)} %collective-permute-done.23.refs_2_), channel_id=1, source_target_pairs={{0,1},{1,0},{2,3},{3,2},{4,5},{5,4},{6,7},{7,6},{8,9},{9,8},{10,11... | collective-permute-start | bytes 786440 | tf_op jit(solution)/shard_map/ppermute | solution.py:53
  99.6 2.5 %collective-permute-start.28 = (bf16[64,2048]{1,0:T(8,128)(2,1)S(1)}, bf16[64,2048]{1,0:T(8,128)(2,1)S(1)}, u32[]{:S(2)}, u32[]{:S(2)}) collective-permute-start(bf16[64,2048]{1,0:T(8,128)(2,1)S(1)} %collective-permute-done.24.refs_3_), channel_id=1, source_target_pairs={{0,1},{1,0},{2,3},{3,2},{4,5},{5,4},{6,7},{7,6},{8,9},{9,8},{10,11... | collective-permute-start | bytes 786440 | tf_op jit(solution)/shard_map/ppermute | solution.py:53

commit v10 on v9

--- a/solution.py
+++ b/solution.py
@@ -518,10 +518,10 @@
     r_lon = lax.ppermute(to_lon, BOTH, shifted(0, 1))
     r_diag = lax.ppermute(to_diag, BOTH, shifted(1, 1))
     recv = send(part, flip_z(1))
-    recv, r_diag = tied((recv, r_diag))
+    recv, r_lon = tied((recv, r_lon))
     part = add(part, recv)
     recv = send(part, flip_z(2))
-    recv, r_lon = tied((recv, r_lon))
+    recv, r_diag = tied((recv, r_diag))
     part = add(part, recv)
     recv = send(part, flip_z(6))
     recv, r_lat = tied((recv, r_lat))

time: 105 us -> 104 us (level)
  waiting for transfers between devices: 18.1 us -> 13.8 us
  starting transfers between devices: 60.2 us -> 63.9 us
    ppermute x20, starting transfers between devices: 31.8 us -> 35.8 us  [send(): return lax.ppermute(x, BOTH, route(step))]
    ppermute x1, waiting for transfers between devices: 5.71 us -> 1.94 us  [on_device(): r_lat = lax.ppermute(to_lat, BOTH, shifted(1, 0))]
    ppermute x1, starting transfers between devices: 2.52 us -> 4.33 us  [on_device(): r_lon = lax.ppermute(to_lon, BOTH, shifted(0, 1))]
    ppermute x1, starting transfers between devices: 2.59 us -> 1.47 us  [on_device(): r_lat = lax.ppermute(to_lat, BOTH, shifted(1, 0))]
where the time goes in v10:
time: 104 us
  starting transfers between devices  63.9 us (61%)
  Pallas kernels  24.3 us (23%)
  waiting for transfers between devices  13.8 us (13%)
    ppermute x20, starting transfers between devices, send(): return lax.ppermute(x, BOTH, route(step))  35.8 us
    ppermute x20, waiting for transfers between devices, send(): return lax.ppermute(x, BOTH, route(step))  11.3 us
    ppermute x2, starting transfers between devices, halo_in(): lax.ppermute(diag, BOTH, shifted(-1, -1))  10.5 us
    pallas_call x1, Pallas kernels, to_backward(): pl.pallas_call(backward_kernel, out_shape=[vshape(TOK, 3 * D), vshape(256...  6.84 us
    ppermute x2, starting transfers between devices, halo_in(): lax.ppermute(lat, BOTH, shifted(-1, 0))  6.33 us
    ppermute x1, starting transfers between devices, on_device(): r_lon = lax.ppermute(to_lon, BOTH, shifted(0, 1))  4.33 us
    pallas_call x1, Pallas kernels, to_forward(): pl.pallas_call(forward_kernel, out_shape=[vshape(TOK, D), vshape(TOK, 3 *...  4.17 us
    ppermute x1, starting transfers between devices, on_device(): r_diag = lax.ppermute(to_diag, BOTH, shifted(1, 1))  4.07 us
  transfers between devices with their start and end apart: 29, of which 10 were waited for; matrix products, arithmetic and copies ran while one was open for 0% of the time, Pallas kernels for 13%

profile of v10, /device:TPU:1, one launch (start us, length us, event | category | flops | bytes accessed | tf_op | source)
XLA Modules:
  0.0 103.7 jit_solution(3525289083512107039)
XLA Ops:
  0.6 2.2 %pack.1 = (bf16[576,512]{1,0:T(8,128)(2,1)S(1)}, bf16[576,512]{1,0:T(8,128)(2,1)S(1)}, bf16[384,576]{1,0:T(8,128)(2,1)S(1)}, bf16[224,512]{1,0:T(8,128)(2,1)S(1)...) custom-call(bf16[576,512]{1,0:T(8,128)(2,1)} %bitcast.10, ...), custom_call_target="tpu_custom_call" | custom-call | flops 400000000 | bytes 2000000 | tf_op jit(solution)/shard_map/pack/pallas_call | solution.py:383
  2.8 6.1 %collective-permute-start = (bf16[224,512]{1,0:T(8,128)(2,1)S(1)}, bf16[224,512]{1,0:T(8,128)(2,1)S(1)}, u32[]{:S(2)}, u32[]{:S(2)}) collective-permute-start(bf16[224,512]{1,0:T(8,128)(2,1)S(1)} %get-tuple-element.68), channel_id=1, source_target_pairs={{0,224},{1,225},{2,226},{3,227},{4,228},{5,229},{6,230},{7,231},{8... | collective-permute-start | bytes 688136 | tf_op jit(solution)/shard_map/ppermute | solution.py:477
  9.2 1.2 %collective-permute-start.1 = (bf16[80,512]{1,0:T(8,128)(2,1)S(1)}, bf16[80,512]{1,0:T(8,128)(2,1)S(1)}, u32[]{:S(2)}, u32[]{:S(2)}) collective-permute-start(bf16[80,512]{1,0:T(8,128)(2,1)S(1)} %get-tuple-element.69), channel_id=1, source_target_pairs={{0,31},{1,0},{2,1},{3,2},{4,3},{5,4},{6,5},{7,6},{8,7},{9,8},{10,9... | collective-permute-start | bytes 245768 | tf_op jit(solution)/shard_map/ppermute | solution.py:478
  10.4 8.2 %collective-permute-start.2 = (bf16[80,512]{1,0:T(8,128)(2,1)S(1)}, bf16[80,512]{1,0:T(8,128)(2,1)S(1)}, u32[]{:S(2)}, u32[]{:S(2)}) collective-permute-start(bf16[80,512]{1,0:T(8,128)(2,1)S(1)} %get-tuple-element.70), channel_id=1, source_target_pairs={{0,255},{1,224},{2,225},{3,226},{4,227},{5,228},{6,229},{7,230},{8... | collective-permute-start | bytes 245768 | tf_op jit(solution)/shard_map/ppermute | solution.py:479
  18.7 2.3 %load.1 = (bf16[576,576]{1,0:T(8,128)(2,1)S(1)}, bf16[576,384]{1,0:T(8,128)(2,1)S(1)}, bf16[512,1536]{1,0:T(8,128)(2,1)S(1)}, bf16[512,512]{1,0:T(8,128)(2,1)S(1...) custom-call(bf16[576,512]{1,0:T(8,128)(2,1)S(1)} %get-tuple-element.64.f_vm.f_loc, ...), custom_call_target="tpu_custom_call" | custom-call | flops 1000000 | bytes 10000 | tf_op jit(solution)/shard_map/load/pallas_call | solution.py:396
  21.0 2.3 %collective-permute-start.5 = (bf16[80,512]{1,0:T(8,128)(2,1)S(1)}, bf16[80,512]{1,0:T(8,128)(2,1)S(1)}, u32[]{:S(2)}, u32[]{:S(2)}) collective-permute-start(bf16[80,512]{1,0:T(8,128)(2,1)S(1)} %get-tuple-element.77), channel_id=1, source_target_pairs={{0,255},{1,224},{2,225},{3,226},{4,227},{5,228},{6,229},{7,230},{8... | collective-permute-start | bytes 245768 | tf_op jit(solution)/shard_map/ppermute | solution.py:479
  23.4 4.2 %forward.1 = (bf16[576,512]{1,0:T(8,128)(2,1)S(1)}, bf16[576,1536]{1,0:T(8,128)(2,1)S(1)}, bf16[1152,576]{1,0:T(8,128)(2,1)S(1)}, bf16[576,512]{1,0:T(8,128)(2,1)S(1)}) custom-call(s32[4]{0:T(128)S(1)} %pad_add_fusion.place, bf16[576,512]{1,0:T(8,128)(2,1)S(1)} %get-tuple-element.66.refs_0_, bf16[576,384]{1,0:T(8,128)(2,1)S(1)} %get-tuple-element.67.refs_1_.p_halo, ...), custom_call_target="tpu_custom_call" | custom-call | flops 1000000 | bytes 10000 | tf_op jit(solution)/shard_map/forward/pallas_call | solution.py:410
  27.6 6.8 %backward.1 = (bf16[576,1536]{1,0:T(8,128)(2,1)S(1)}, bf16[256,2048]{1,0:T(8,128)(2,1)S(1)}, bf16[256,2048]{1,0:T(8,128)(2,1)S(1)}) custom-call(s32[4]{0:T(128)S(1)} %pad_add_fusion.place, bf16[576,512]{1,0:T(8,128)(2,1)S(1)} %get-tuple-element.74.refs_0_, bf16[576,384]{1,0:T(8,128)(2,1)S(1)} %get-tuple-element.67.refs_1_.p_halo, ...), custom_call_target="tpu_custom_call" | custom-call | flops 5000000000 | bytes 10000000 | tf_op jit(solution)/shard_map/backward/pallas_call | solution.py:424
  35.0 2.3 %collective-permute-done.6 = bf16[256,2048]{1,0:T(8,128)(2,1)S(1)} collective-permute-done((bf16[256,2048]{1,0:T(8,128)(2,1)S(1)}, bf16[256,2048]{1,0:T(8,128)(2,1)S(1)}, u32[]{:S(2)}, u32[]{:S(2)}) %collective-permute-start.6) | collective-permute-done | bytes 1048608 | tf_op jit(solution)/shard_map/ppermute | solution.py:53
  37.6 1.1 %collective-permute-start.7 = (bf16[64,2048]{1,0:T(8,128)(2,1)S(1)}, bf16[64,2048]{1,0:T(8,128)(2,1)S(1)}, u32[]{:S(2)}, u32[]{:S(2)}) collective-permute-start(bf16[64,2048]{1,0:T(8,128)(2,1)S(1)} %get-tuple-element.86), channel_id=1, source_target_pairs={{0,64},{1,17},{2,66},{3,19},{4,68},{5,21},{6,70},{7,23},{8,72},{9,... | collective-permute-start | bytes 786440 | tf_op jit(solution)/shard_map/ppermute | solution.py:53
  38.7 2.0 %collective-permute-start.8 = (bf16[64,2048]{1,0:T(8,128)(2,1)S(1)}, bf16[64,2048]{1,0:T(8,128)(2,1)S(1)}, u32[]{:S(2)}, u32[]{:S(2)}) collective-permute-start(bf16[64,2048]{1,0:T(8,128)(2,1)S(1)} %get-tuple-element.87), channel_id=1, source_target_pairs={{0,128},{1,33},{2,130},{3,35},{4,132},{5,37},{6,134},{7,39},{8,136... | collective-permute-start | bytes 786440 | tf_op jit(solution)/shard_map/ppermute | solution.py:53
  40.7 1.4 %collective-permute-start.9 = (bf16[64,2048]{1,0:T(8,128)(2,1)S(1)}, bf16[64,2048]{1,0:T(8,128)(2,1)S(1)}, u32[]{:S(2)}, u32[]{:S(2)}) collective-permute-start(bf16[64,2048]{1,0:T(8,128)(2,1)S(1)} %get-tuple-element.88), channel_id=1, source_target_pairs={{0,192},{1,49},{2,194},{3,51},{4,196},{5,53},{6,198},{7,55},{8,200... | collective-permute-start | bytes 786440 | tf_op jit(solution)/shard_map/ppermute | solution.py:53
  42.1 2.0 %back.1 = (bf16[576,1024]{1,0:T(8,128)(2,1)S(1)}, bf16[224,1024]{1,0:T(8,128)(2,1)S(1)}, bf16[80,1024]{1,0:T(8,128)(2,1)S(1)}, bf16[80,1024]{1,0:T(8,128)(2,1)S(1)}) custom-call(bf16[576,512]{1,0:T(8,128)(2,1)S(1)} %get-tuple-element.89.refs_9_.mixed, bf16[576,1536]{1,0:T(8,128)(2,1)S(1)} %get-tuple-element.90.gact, ...), custom_call_target="tpu_custom_call" | custom-call | flops 2000000000 | bytes 5000000 | tf_op jit(solution)/shard_map/back/pallas_call | solution.py:441
  44.4 2.8 %collective-permute-done.8 = bf16[64,2048]{1,0:T(8,128)(2,1)S(1)} collective-permute-done((bf16[64,2048]{1,0:T(8,128)(2,1)S(1)}, bf16[64,2048]{1,0:T(8,128)(2,1)S(1)}, u32[]{:S(2)}, u32[]{:S(2)}) %collective-permute-start.8) | collective-permute-done | bytes 262176 | tf_op jit(solution)/shard_map/ppermute | solution.py:53
  48.0 1.1 %collective-permute-start.10 = (bf16[16,2048]{1,0:T(8,128)(2,1)S(1)}, bf16[16,2048]{1,0:T(8,128)(2,1)S(1)}, u32[]{:S(2)}, u32[]{:S(2)}) collective-permute-start(bf16[16,2048]{1,0:T(8,128)(2,1)S(1)} %get-tuple-element.127), channel_id=1, source_target_pairs={{0,16},{1,65},{2,18},{3,67},{4,20},{5,69},{6,22},{7,71},{8,24},{9,... | collective-permute-start | bytes 196616 | tf_op jit(solution)/shard_map/ppermute | solution.py:53
  49.1 1.6 %collective-permute-start.12 = (bf16[16,2048]{1,0:T(8,128)(2,1)S(1)}, bf16[16,2048]{1,0:T(8,128)(2,1)S(1)}, u32[]{:S(2)}, u32[]{:S(2)}) collective-permute-start(bf16[16,2048]{1,0:T(8,128)(2,1)S(1)} %get-tuple-element.128), channel_id=1, source_target_pairs={{0,48},{1,193},{2,50},{3,195},{4,52},{5,197},{6,54},{7,199},{8,56}... | collective-permute-start | bytes 196616 | tf_op jit(solution)/shard_map/ppermute | solution.py:53
  51.0 4.3 %collective-permute-start.14 = (bf16[80,1024]{1,0:T(8,128)(2,1)S(1)}, bf16[80,1024]{1,0:T(8,128)(2,1)S(1)}, u32[]{:S(2)}, u32[]{:S(2)}) collective-permute-start(bf16[80,1024]{1,0:T(8,128)(2,1)S(1)} %get-tuple-element.99), channel_id=1, source_target_pairs={{0,1},{1,2},{2,3},{3,4},{4,5},{5,6},{6,7},{7,8},{8,9},{9,10},{10,1... | collective-permute-start | bytes 491528 | tf_op jit(solution)/shard_map/ppermute | solution.py:518
  55.4 1.7 %collective-permute-start.13 = (bf16[16,2048]{1,0:T(8,128)(2,1)S(1)}, bf16[16,2048]{1,0:T(8,128)(2,1)S(1)}, u32[]{:S(2)}, u32[]{:S(2)}) collective-permute-start(bf16[16,2048]{1,0:T(8,128)(2,1)S(1)} %add_convert_fusion.8), channel_id=1, source_target_pairs={{0,2},{1,3},{2,0},{3,1},{4,6},{5,7},{6,4},{7,5},{8,10},{9,11},{10,... | collective-permute-start | bytes 196616 | tf_op jit(solution)/shard_map/ppermute | solution.py:53
  57.1 4.1 %collective-permute-start.16 = (bf16[80,1024]{1,0:T(8,128)(2,1)S(1)}, bf16[80,1024]{1,0:T(8,128)(2,1)S(1)}, u32[]{:S(2)}, u32[]{:S(2)}) collective-permute-start(bf16[80,1024]{1,0:T(8,128)(2,1)S(1)} %get-tuple-element.101), channel_id=1, source_target_pairs={{0,33},{1,34},{2,35},{3,36},{4,37},{5,38},{6,39},{7,40},{8,41},{9,... | collective-permute-start | bytes 491528 | tf_op jit(solution)/shard_map/ppermute | solution.py:519
  61.2 2.7 %collective-permute-start.15 = (bf16[16,2048]{1,0:T(8,128)(2,1)S(1)}, bf16[16,2048]{1,0:T(8,128)(2,1)S(1)}, u32[]{:S(2)}, u32[]{:S(2)}) collective-permute-start(bf16[16,2048]{1,0:T(8,128)(2,1)S(1)} %add_convert_fusion.7), channel_id=1, source_target_pairs={{0,4},{1,5},{2,6},{3,7},{4,0},{5,1},{6,2},{7,3},{8,12},{9,13},{10,... | collective-permute-start | bytes 196616 | tf_op jit(solution)/shard_map/ppermute | solution.py:53
  63.9 1.5 %collective-permute-start.18 = (bf16[224,1024]{1,0:T(8,128)(2,1)S(1)}, bf16[224,1024]{1,0:T(8,128)(2,1)S(1)}, u32[]{:S(2)}, u32[]{:S(2)}) collective-permute-start(bf16[224,1024]{1,0:T(8,128)(2,1)S(1)} %get-tuple-element.103), channel_id=1, source_target_pairs={{0,32},{1,33},{2,34},{3,35},{4,36},{5,37},{6,38},{7,39},{8,40},{9,... | collective-permute-start | bytes 1376264 | tf_op jit(solution)/shard_map/ppermute | solution.py:517
  65.8 8.5 %collective-permute-start.17 = (bf16[16,2048]{1,0:T(8,128)(2,1)S(1)}, bf16[16,2048]{1,0:T(8,128)(2,1)S(1)}, u32[]{:S(2)}, u32[]{:S(2)}) collective-permute-start(bf16[16,2048]{1,0:T(8,128)(2,1)S(1)} %add_convert_fusion.6), channel_id=1, source_target_pairs={{0,12},{1,13},{2,14},{3,15},{4,8},{5,9},{6,10},{7,11},{8,4},{9,5},... | collective-permute-start | bytes 196616 | tf_op jit(solution)/shard_map/ppermute | solution.py:53
  74.3 2.0 %collective-permute-done.17 = bf16[16,2048]{1,0:T(8,128)(2,1)S(1)} collective-permute-done((bf16[16,2048]{1,0:T(8,128)(2,1)S(1)}, bf16[16,2048]{1,0:T(8,128)(2,1)S(1)}, u32[]{:S(2)}, u32[]{:S(2)}) %collective-permute-start.17) | collective-permute-done | bytes 65568 | tf_op jit(solution)/shard_map/ppermute | solution.py:53
  76.3 1.9 %collective-permute-done.18.r_lat = bf16[224,1024]{1,0:T(8,128)(2,1)S(1)} collective-permute-done((bf16[224,1024]{1,0:T(8,128)(2,1)S(1)}, bf16[224,1024]{1,0:T(8,128)(2,1)S(1)}, u32[]{:S(2)}, u32[]{:S(2)}) %collective-permute-start.18) | collective-permute-done | bytes 458784 | tf_op jit(solution)/shard_map/ppermute | solution.py:517
  78.3 1.8 %collective-permute-start.20 = (bf16[16,2048]{1,0:T(8,128)(2,1)S(1)}, bf16[16,2048]{1,0:T(8,128)(2,1)S(1)}, u32[]{:S(2)}, u32[]{:S(2)}) collective-permute-start(bf16[16,2048]{1,0:T(8,128)(2,1)S(1)} %add_convert_fusion.5), channel_id=1, source_target_pairs={{0,32},{1,129},{2,34},{3,131},{4,36},{5,133},{6,38},{7,135},{8,40}... | collective-permute-start | bytes 196616 | tf_op jit(solution)/shard_map/ppermute | solution.py:53
  81.0 2.3 %collective-permute-done.21 = bf16[16,2048]{1,0:T(8,128)(2,1)S(1)} collective-permute-done((bf16[16,2048]{1,0:T(8,128)(2,1)S(1)}, bf16[16,2048]{1,0:T(8,128)(2,1)S(1)}, u32[]{:S(2)}, u32[]{:S(2)}) %collective-permute-start.21) | collective-permute-done | bytes 65568 | tf_op jit(solution)/shard_map/ppermute | solution.py:53
  84.8 2.5 %collective-permute-start.22 = (bf16[64,2048]{1,0:T(8,128)(2,1)S(1)}, bf16[64,2048]{1,0:T(8,128)(2,1)S(1)}, u32[]{:S(2)}, u32[]{:S(2)}) collective-permute-start(bf16[64,2048]{1,0:T(8,128)(2,1)S(1)} %pad_maximum_fusion.refs_0_), channel_id=1, source_target_pairs={{0,192},{1,49},{2,194},{3,51},{4,196},{5,53},{6,198},{7,55},{8,200... | collective-permute-start | bytes 786440 | tf_op jit(solution)/shard_map/ppermute | solution.py:53
  87.3 2.9 %finish.1 = (bf16[576,512]{1,0:T(8,128)(2,1)}, bf16[576,512]{1,0:T(8,128)(2,1)}) custom-call(bf16[576,512]{1,0:T(8,128)(2,1)S(1)} %get-tuple-element.64.f_vm.f_loc, bf16[576,512]{1,0:T(8,128)(2,1)S(1)} %get-tuple-element.65.c_vm.c_loc, bf16[576,1024]{1,0:T(8,128)(2,1)S(1)} %get-tuple-element.105.both, bf16[224,1024]{1,0:T(8,128)(2,1)S(1)} %collective-permute-done.18.r_lat, ...), custom_call_target="tpu_custom_call" | custom-call | flops 2000000000 | bytes 8000000 | tf_op jit(solution)/shard_map/finish/pallas_call | solution.py:453
  90.2 3.6 %collective-permute-start.25 = (bf16[64,2048]{1,0:T(8,128)(2,1)S(1)}, bf16[64,2048]{1,0:T(8,128)(2,1)S(1)}, u32[]{:S(2)}, u32[]{:S(2)}) collective-permute-start(bf16[64,2048]{1,0:T(8,128)(2,1)S(1)} %pad_maximum_fusion.refs_0_), channel_id=1, source_target_pairs={{0,1},{1,0},{2,3},{3,2},{4,5},{5,4},{6,7},{7,6},{8,9},{9,8},{10,11... | collective-permute-start | bytes 786440 | tf_op jit(solution)/shard_map/ppermute | solution.py:53
  94.2 4.8 %collective-permute-start.26 = (bf16[64,2048]{1,0:T(8,128)(2,1)S(1)}, bf16[64,2048]{1,0:T(8,128)(2,1)S(1)}, u32[]{:S(2)}, u32[]{:S(2)}) collective-permute-start(bf16[64,2048]{1,0:T(8,128)(2,1)S(1)} %collective-permute-done.22.refs_1_), channel_id=1, source_target_pairs={{0,1},{1,0},{2,3},{3,2},{4,5},{5,4},{6,7},{7,6},{8,9},{9,8},{10,11... | collective-permute-start | bytes 786440 | tf_op jit(solution)/shard_map/ppermute | solution.py:53
  99.5 2.0 %weights0.1 = (f32[512,1536]{1,0:T(8,128)}, f32[512,512]{1,0:T(8,128)}, f32[1,512]{1,0:T(1,128)S(1)}) custom-call(s32[4]{0:T(128)S(1)} %pad_add_fusion.place, bf16[64,2048]{1,0:T(8,128)(2,1)S(1)} %pad_maximum_fusion.refs_0_, bf16[64,2048]{1,0:T(8,128)(2,1)S(1)} %collective-permute-done.22.refs_1_, bf16[64,2048]{1,0:T(8,128)(2,1)S(1)} %collective-permute-done.23.refs_2_, ...), custom_call_target="tpu_custom_call" | custom-call | flops 10000000 | bytes 4000000 | tf_op jit(solution)/shard_map/weights0/pallas_call | solution.py:327
  101.5 2.0 %weights1.1 = (f32[512,1536]{1,0:T(8,128)}, f32[512,512]{1,0:T(8,128)}, f32[1,512]{1,0:T(1,128)}) custom-call(s32[4]{0:T(128)S(1)} %pad_add_fusion.place, bf16[64,2048]{1,0:T(8,128)(2,1)S(1)} %collective-permute-done.25.refs_0_, bf16[64,2048]{1,0:T(8,128)(2,1)S(1)} %collective-permute-done.26.refs_1_, ...), custom_call_target="tpu_custom_call", output_to_operand_aliasing={{0}: (8, {}), {1}: (9, {})} | custom-call | flops 10000000 | bytes 4000000 | tf_op jit(solution)/shard_map/weights1/pallas_call | solution.py:327
  (43 shorter events, 6.6 us)
Async XLA Ops:
  2.8 20.6 %collective-permute-start = (bf16[224,512]{1,0:T(8,128)(2,1)S(1)}, bf16[224,512]{1,0:T(8,128)(2,1)S(1)}, u32[]{:S(2)}, u32[]{:S(2)}) collective-permute-start(bf16[224,512]{1,0:T(8,128)(2,1)S(1)} %get-tuple-element.68), channel_id=1, source_target_pairs={{0,224},{1,225},{2,226},{3,227},{4,228},{5,229},{6,230},{7,231},{8... | collective-permute-start | bytes 688136 | tf_op jit(solution)/shard_map/ppermute | solution.py:477
  8.9 18.7 %collective-permute-start.3 = (bf16[224,512]{1,0:T(8,128)(2,1)S(1)}, bf16[224,512]{1,0:T(8,128)(2,1)S(1)}, u32[]{:S(2)}, u32[]{:S(2)}) collective-permute-start(bf16[224,512]{1,0:T(8,128)(2,1)S(1)} %get-tuple-element.75), channel_id=1, source_target_pairs={{0,224},{1,225},{2,226},{3,227},{4,228},{5,229},{6,230},{7,231},{8... | collective-permute-start | bytes 688136 | tf_op jit(solution)/shard_map/ppermute | solution.py:477
  9.2 11.8 %collective-permute-start.1 = (bf16[80,512]{1,0:T(8,128)(2,1)S(1)}, bf16[80,512]{1,0:T(8,128)(2,1)S(1)}, u32[]{:S(2)}, u32[]{:S(2)}) collective-permute-start(bf16[80,512]{1,0:T(8,128)(2,1)S(1)} %get-tuple-element.69), channel_id=1, source_target_pairs={{0,31},{1,0},{2,1},{3,2},{4,3},{5,4},{6,5},{7,6},{8,7},{9,8},{10,9... | collective-permute-start | bytes 245768 | tf_op jit(solution)/shard_map/ppermute | solution.py:478
  10.4 13.0 %collective-permute-start.2 = (bf16[80,512]{1,0:T(8,128)(2,1)S(1)}, bf16[80,512]{1,0:T(8,128)(2,1)S(1)}, u32[]{:S(2)}, u32[]{:S(2)}) collective-permute-start(bf16[80,512]{1,0:T(8,128)(2,1)S(1)} %get-tuple-element.70), channel_id=1, source_target_pairs={{0,255},{1,224},{2,225},{3,226},{4,227},{5,228},{6,229},{7,230},{8... | collective-permute-start | bytes 245768 | tf_op jit(solution)/shard_map/ppermute | solution.py:479
  18.6 9.0 %collective-permute-start.4 = (bf16[80,512]{1,0:T(8,128)(2,1)S(1)}, bf16[80,512]{1,0:T(8,128)(2,1)S(1)}, u32[]{:S(2)}, u32[]{:S(2)}) collective-permute-start(bf16[80,512]{1,0:T(8,128)(2,1)S(1)} %get-tuple-element.76), channel_id=1, source_target_pairs={{0,31},{1,0},{2,1},{3,2},{4,3},{5,4},{6,5},{7,6},{8,7},{9,8},{10,9... | collective-permute-start | bytes 245768 | tf_op jit(solution)/shard_map/ppermute | solution.py:478
  21.0 6.6 %collective-permute-start.5 = (bf16[80,512]{1,0:T(8,128)(2,1)S(1)}, bf16[80,512]{1,0:T(8,128)(2,1)S(1)}, u32[]{:S(2)}, u32[]{:S(2)}) collective-permute-start(bf16[80,512]{1,0:T(8,128)(2,1)S(1)} %get-tuple-element.77), channel_id=1, source_target_pairs={{0,255},{1,224},{2,225},{3,226},{4,227},{5,228},{6,229},{7,230},{8... | collective-permute-start | bytes 245768 | tf_op jit(solution)/shard_map/ppermute | solution.py:479
  34.5 2.8 %collective-permute-start.6 = (bf16[256,2048]{1,0:T(8,128)(2,1)S(1)}, bf16[256,2048]{1,0:T(8,128)(2,1)S(1)}, u32[]{:S(2)}, u32[]{:S(2)}) collective-permute-start(bf16[256,2048]{1,0:T(8,128)(2,1)S(1)} %get-tuple-element.84), channel_id=1, source_target_pairs={{0,1},{1,0},{2,3},{3,2},{4,5},{5,4},{6,7},{7,6},{8,9},{9,8},{10,11... | collective-permute-start | bytes 3145736 | tf_op jit(solution)/shard_map/ppermute | solution.py:53
  37.6 6.8 %collective-permute-start.7 = (bf16[64,2048]{1,0:T(8,128)(2,1)S(1)}, bf16[64,2048]{1,0:T(8,128)(2,1)S(1)}, u32[]{:S(2)}, u32[]{:S(2)}) collective-permute-start(bf16[64,2048]{1,0:T(8,128)(2,1)S(1)} %get-tuple-element.86), channel_id=1, source_target_pairs={{0,64},{1,17},{2,66},{3,19},{4,68},{5,21},{6,70},{7,23},{8,72},{9,... | collective-permute-start | bytes 786440 | tf_op jit(solution)/shard_map/ppermute | solution.py:53
  38.7 8.5 %collective-permute-start.8 = (bf16[64,2048]{1,0:T(8,128)(2,1)S(1)}, bf16[64,2048]{1,0:T(8,128)(2,1)S(1)}, u32[]{:S(2)}, u32[]{:S(2)}) collective-permute-start(bf16[64,2048]{1,0:T(8,128)(2,1)S(1)} %get-tuple-element.87), channel_id=1, source_target_pairs={{0,128},{1,33},{2,130},{3,35},{4,132},{5,37},{6,134},{7,39},{8,136... | collective-permute-start | bytes 786440 | tf_op jit(solution)/shard_map/ppermute | solution.py:53
  40.7 7.2 %collective-permute-start.9 = (bf16[64,2048]{1,0:T(8,128)(2,1)S(1)}, bf16[64,2048]{1,0:T(8,128)(2,1)S(1)}, u32[]{:S(2)}, u32[]{:S(2)}) collective-permute-start(bf16[64,2048]{1,0:T(8,128)(2,1)S(1)} %get-tuple-element.88), channel_id=1, source_target_pairs={{0,192},{1,49},{2,194},{3,51},{4,196},{5,53},{6,198},{7,55},{8,200... | collective-permute-start | bytes 786440 | tf_op jit(solution)/shard_map/ppermute | solution.py:53
  48.0 7.3 %collective-permute-start.10 = (bf16[16,2048]{1,0:T(8,128)(2,1)S(1)}, bf16[16,2048]{1,0:T(8,128)(2,1)S(1)}, u32[]{:S(2)}, u32[]{:S(2)}) collective-permute-start(bf16[16,2048]{1,0:T(8,128)(2,1)S(1)} %get-tuple-element.127), channel_id=1, source_target_pairs={{0,16},{1,65},{2,18},{3,67},{4,20},{5,69},{6,22},{7,71},{8,24},{9,... | collective-permute-start | bytes 196616 | tf_op jit(solution)/shard_map/ppermute | solution.py:53
  49.1 6.2 %collective-permute-start.12 = (bf16[16,2048]{1,0:T(8,128)(2,1)S(1)}, bf16[16,2048]{1,0:T(8,128)(2,1)S(1)}, u32[]{:S(2)}, u32[]{:S(2)}) collective-permute-start(bf16[16,2048]{1,0:T(8,128)(2,1)S(1)} %get-tuple-element.128), channel_id=1, source_target_pairs={{0,48},{1,193},{2,50},{3,195},{4,52},{5,197},{6,54},{7,199},{8,56}... | collective-permute-start | bytes 196616 | tf_op jit(solution)/shard_map/ppermute | solution.py:53
  50.7 4.6 %collective-permute-start.11 = (bf16[16,2048]{1,0:T(8,128)(2,1)S(1)}, bf16[16,2048]{1,0:T(8,128)(2,1)S(1)}, u32[]{:S(2)}, u32[]{:S(2)}) collective-permute-start(bf16[16,2048]{1,0:T(8,128)(2,1)S(1)} %get-tuple-element.129), channel_id=1, source_target_pairs={{0,32},{1,129},{2,34},{3,131},{4,36},{5,133},{6,38},{7,135},{8,40}... | collective-permute-start | bytes 196616 | tf_op jit(solution)/shard_map/ppermute | solution.py:53
  51.0 10.2 %collective-permute-start.14 = (bf16[80,1024]{1,0:T(8,128)(2,1)S(1)}, bf16[80,1024]{1,0:T(8,128)(2,1)S(1)}, u32[]{:S(2)}, u32[]{:S(2)}) collective-permute-start(bf16[80,1024]{1,0:T(8,128)(2,1)S(1)} %get-tuple-element.99), channel_id=1, source_target_pairs={{0,1},{1,2},{2,3},{3,4},{4,5},{5,6},{6,7},{7,8},{8,9},{9,10},{10,1... | collective-permute-start | bytes 491528 | tf_op jit(solution)/shard_map/ppermute | solution.py:518
  55.4 5.8 %collective-permute-start.13 = (bf16[16,2048]{1,0:T(8,128)(2,1)S(1)}, bf16[16,2048]{1,0:T(8,128)(2,1)S(1)}, u32[]{:S(2)}, u32[]{:S(2)}) collective-permute-start(bf16[16,2048]{1,0:T(8,128)(2,1)S(1)} %add_convert_fusion.8), channel_id=1, source_target_pairs={{0,2},{1,3},{2,0},{3,1},{4,6},{5,7},{6,4},{7,5},{8,10},{9,11},{10,... | collective-permute-start | bytes 196616 | tf_op jit(solution)/shard_map/ppermute | solution.py:53
  57.1 8.7 %collective-permute-start.16 = (bf16[80,1024]{1,0:T(8,128)(2,1)S(1)}, bf16[80,1024]{1,0:T(8,128)(2,1)S(1)}, u32[]{:S(2)}, u32[]{:S(2)}) collective-permute-start(bf16[80,1024]{1,0:T(8,128)(2,1)S(1)} %get-tuple-element.101), channel_id=1, source_target_pairs={{0,33},{1,34},{2,35},{3,36},{4,37},{5,38},{6,39},{7,40},{8,41},{9,... | collective-permute-start | bytes 491528 | tf_op jit(solution)/shard_map/ppermute | solution.py:519
  61.2 4.6 %collective-permute-start.15 = (bf16[16,2048]{1,0:T(8,128)(2,1)S(1)}, bf16[16,2048]{1,0:T(8,128)(2,1)S(1)}, u32[]{:S(2)}, u32[]{:S(2)}) collective-permute-start(bf16[16,2048]{1,0:T(8,128)(2,1)S(1)} %add_convert_fusion.7), channel_id=1, source_target_pairs={{0,4},{1,5},{2,6},{3,7},{4,0},{5,1},{6,2},{7,3},{8,12},{9,13},{10,... | collective-permute-start | bytes 196616 | tf_op jit(solution)/shard_map/ppermute | solution.py:53
  63.9 14.4 %collective-permute-start.18 = (bf16[224,1024]{1,0:T(8,128)(2,1)S(1)}, bf16[224,1024]{1,0:T(8,128)(2,1)S(1)}, u32[]{:S(2)}, u32[]{:S(2)}) collective-permute-start(bf16[224,1024]{1,0:T(8,128)(2,1)S(1)} %get-tuple-element.103), channel_id=1, source_target_pairs={{0,32},{1,33},{2,34},{3,35},{4,36},{5,37},{6,38},{7,39},{8,40},{9,... | collective-permute-start | bytes 1376264 | tf_op jit(solution)/shard_map/ppermute | solution.py:517
  65.8 10.4 %collective-permute-start.17 = (bf16[16,2048]{1,0:T(8,128)(2,1)S(1)}, bf16[16,2048]{1,0:T(8,128)(2,1)S(1)}, u32[]{:S(2)}, u32[]{:S(2)}) collective-permute-start(bf16[16,2048]{1,0:T(8,128)(2,1)S(1)} %add_convert_fusion.6), channel_id=1, source_target_pairs={{0,12},{1,13},{2,14},{3,15},{4,8},{5,9},{6,10},{7,11},{8,4},{9,5},... | collective-permute-start | bytes 196616 | tf_op jit(solution)/shard_map/ppermute | solution.py:53
  78.2 5.1 %collective-permute-start.21 = (bf16[16,2048]{1,0:T(8,128)(2,1)S(1)}, bf16[16,2048]{1,0:T(8,128)(2,1)S(1)}, u32[]{:S(2)}, u32[]{:S(2)}) collective-permute-start(bf16[16,2048]{1,0:T(8,128)(2,1)S(1)} %add_convert_fusion.5), channel_id=1, source_target_pairs={{0,16},{1,65},{2,18},{3,67},{4,20},{5,69},{6,22},{7,71},{8,24},{9,... | collective-permute-start | bytes 196616 | tf_op jit(solution)/shard_map/ppermute | solution.py:53
  78.3 5.0 %collective-permute-start.20 = (bf16[16,2048]{1,0:T(8,128)(2,1)S(1)}, bf16[16,2048]{1,0:T(8,128)(2,1)S(1)}, u32[]{:S(2)}, u32[]{:S(2)}) collective-permute-start(bf16[16,2048]{1,0:T(8,128)(2,1)S(1)} %add_convert_fusion.5), channel_id=1, source_target_pairs={{0,32},{1,129},{2,34},{3,131},{4,36},{5,133},{6,38},{7,135},{8,40}... | collective-permute-start | bytes 196616 | tf_op jit(solution)/shard_map/ppermute | solution.py:53
  80.2 3.8 %collective-permute-start.19 = (bf16[16,2048]{1,0:T(8,128)(2,1)S(1)}, bf16[16,2048]{1,0:T(8,128)(2,1)S(1)}, u32[]{:S(2)}, u32[]{:S(2)}) collective-permute-start(bf16[16,2048]{1,0:T(8,128)(2,1)S(1)} %add_convert_fusion.5), channel_id=1, source_target_pairs={{0,48},{1,193},{2,50},{3,195},{4,52},{5,197},{6,54},{7,199},{8,56}... | collective-permute-start | bytes 196616 | tf_op jit(solution)/shard_map/ppermute | solution.py:53
  83.9 9.9 %collective-permute-start.24 = (bf16[64,2048]{1,0:T(8,128)(2,1)S(1)}, bf16[64,2048]{1,0:T(8,128)(2,1)S(1)}, u32[]{:S(2)}, u32[]{:S(2)}) collective-permute-start(bf16[64,2048]{1,0:T(8,128)(2,1)S(1)} %pad_maximum_fusion.refs_0_), channel_id=1, source_target_pairs={{0,64},{1,17},{2,66},{3,19},{4,68},{5,21},{6,70},{7,23},{8,72},{9,... | collective-permute-start | bytes 786440 | tf_op jit(solution)/shard_map/ppermute | solution.py:53
  84.8 9.0 %collective-permute-start.23 = (bf16[64,2048]{1,0:T(8,128)(2,1)S(1)}, bf16[64,2048]{1,0:T(8,128)(2,1)S(1)}, u32[]{:S(2)}, u32[]{:S(2)}) collective-permute-start(bf16[64,2048]{1,0:T(8,128)(2,1)S(1)} %pad_maximum_fusion.refs_0_), channel_id=1, source_target_pairs={{0,128},{1,33},{2,130},{3,35},{4,132},{5,37},{6,134},{7,39},{8,136... | collective-permute-start | bytes 786440 | tf_op jit(solution)/shard_map/ppermute | solution.py:53
  84.8 9.4 %collective-permute-start.22 = (bf16[64,2048]{1,0:T(8,128)(2,1)S(1)}, bf16[64,2048]{1,0:T(8,128)(2,1)S(1)}, u32[]{:S(2)}, u32[]{:S(2)}) collective-permute-start(bf16[64,2048]{1,0:T(8,128)(2,1)S(1)} %pad_maximum_fusion.refs_0_), channel_id=1, source_target_pairs={{0,192},{1,49},{2,194},{3,51},{4,196},{5,53},{6,198},{7,55},{8,200... | collective-permute-start | bytes 786440 | tf_op jit(solution)/shard_map/ppermute | solution.py:53
  90.2 11.3 %collective-permute-start.25 = (bf16[64,2048]{1,0:T(8,128)(2,1)S(1)}, bf16[64,2048]{1,0:T(8,128)(2,1)S(1)}, u32[]{:S(2)}, u32[]{:S(2)}) collective-permute-start(bf16[64,2048]{1,0:T(8,128)(2,1)S(1)} %pad_maximum_fusion.refs_0_), channel_id=1, source_target_pairs={{0,1},{1,0},{2,3},{3,2},{4,5},{5,4},{6,7},{7,6},{8,9},{9,8},{10,11... | collective-permute-start | bytes 786440 | tf_op jit(solution)/shard_map/ppermute | solution.py:53
  94.2 7.3 %collective-permute-start.26 = (bf16[64,2048]{1,0:T(8,128)(2,1)S(1)}, bf16[64,2048]{1,0:T(8,128)(2,1)S(1)}, u32[]{:S(2)}, u32[]{:S(2)}) collective-permute-start(bf16[64,2048]{1,0:T(8,128)(2,1)S(1)} %collective-permute-done.22.refs_1_), channel_id=1, source_target_pairs={{0,1},{1,0},{2,3},{3,2},{4,5},{5,4},{6,7},{7,6},{8,9},{9,8},{10,11... | collective-permute-start | bytes 786440 | tf_op jit(solution)/shard_map/ppermute | solution.py:53
  99.0 2.5 %collective-permute-start.27 = (bf16[64,2048]{1,0:T(8,128)(2,1)S(1)}, bf16[64,2048]{1,0:T(8,128)(2,1)S(1)}, u32[]{:S(2)}, u32[]{:S(2)}) collective-permute-start(bf16[64,2048]{1,0:T(8,128)(2,1)S(1)} %collective-permute-done.23.refs_2_), channel_id=1, source_target_pairs={{0,1},{1,0},{2,3},{3,2},{4,5},{5,4},{6,7},{7,6},{8,9},{9,8},{10,11... | collective-permute-start | bytes 786440 | tf_op jit(solution)/shard_map/ppermute | solution.py:53
  99.0 2.5 %collective-permute-start.28 = (bf16[64,2048]{1,0:T(8,128)(2,1)S(1)}, bf16[64,2048]{1,0:T(8,128)(2,1)S(1)}, u32[]{:S(2)}, u32[]{:S(2)}) collective-permute-start(bf16[64,2048]{1,0:T(8,128)(2,1)S(1)} %collective-permute-done.24.refs_3_), channel_id=1, source_target_pairs={{0,1},{1,0},{2,3},{3,2},{4,5},{5,4},{6,7},{7,6},{8,9},{9,8},{10,11... | collective-permute-start | bytes 786440 | tf_op jit(solution)/shard_map/ppermute | solution.py:53

commit v11 on v10

--- a/solution.py
+++ b/solution.py
@@ -521,10 +521,9 @@
     recv, r_lon = tied((recv, r_lon))
     part = add(part, recv)
     recv = send(part, flip_z(2))
-    recv, r_diag = tied((recv, r_diag))
     part = add(part, recv)
     recv = send(part, flip_z(6))
-    recv, r_lat = tied((recv, r_lat))
+    recv, r_lat, r_diag = tied((recv, r_lat, r_diag))
     part = add(part, recv)
 
     block = jnp.concatenate([part] + [send(part, second_axis(4 - s)) for s in (1, 2, 3)], axis=0)

time: 104 us -> 107 us (1.029); the launches traced: 104 us -> 106 us
  waiting for transfers between devices: 13.8 us -> 23.4 us
  starting transfers between devices: 63.9 us -> 56.2 us
    ppermute x20, starting transfers between devices: 35.8 us -> 27.5 us  [send(): return lax.ppermute(x, BOTH, route(step))]
    ppermute x20, waiting for transfers between devices: 11.3 us -> 16.4 us  [send(): return lax.ppermute(x, BOTH, route(step))]
    ppermute x1, waiting for transfers between devices: 1.94 us -> 6.93 us  [on_device(): r_lat = lax.ppermute(to_lat, BOTH, shifted(1, 0))]
  transfers between devices with their start and end apart: 29 -> 29, of which waited for: 10 -> 11; matrix products, arithmetic and copies ran while one was open for 0% -> 0% of each run, Pallas kernels for 13% -> 13%
where the time goes in v11:
time: 107 us; the launch traced here: 106 us
  starting transfers between devices  56.2 us (53%)
  Pallas kernels  24.3 us (23%)
  waiting for transfers between devices  23.4 us (22%)
    ppermute x20, starting transfers between devices, send(): return lax.ppermute(x, BOTH, route(step))  27.5 us
    ppermute x20, waiting for transfers between devices, send(): return lax.ppermute(x, BOTH, route(step))  16.4 us
    ppermute x2, starting transfers between devices, halo_in(): lax.ppermute(diag, BOTH, shifted(-1, -1))  10.5 us
    ppermute x1, waiting for transfers between devices, on_device(): r_lat = lax.ppermute(to_lat, BOTH, shifted(1, 0))  6.93 us
    pallas_call x1, Pallas kernels, to_backward(): pl.pallas_call(backward_kernel, out_shape=[vshape(TOK, 3 * D), vshape(256...  6.84 us
    ppermute x2, starting transfers between devices, halo_in(): lax.ppermute(lat, BOTH, shifted(-1, 0))  6.33 us
    ppermute x1, starting transfers between devices, on_device(): r_diag = lax.ppermute(to_diag, BOTH, shifted(1, 1))  4.34 us
    ppermute x1, starting transfers between devices, on_device(): r_lon = lax.ppermute(to_lon, BOTH, shifted(0, 1))  4.33 us
  transfers between devices with their start and end apart: 29, of which 11 were waited for; matrix products, arithmetic and copies ran while one was open for 0% of the time, Pallas kernels for 13%

profile of v11, /device:TPU:1, one launch (start us, length us, event | category | flops | bytes accessed | tf_op | source)
XLA Modules:
  0.0 105.6 jit_solution(17398130943051765182)
XLA Ops:
  0.6 2.2 %pack.1 = (bf16[576,512]{1,0:T(8,128)(2,1)S(1)}, bf16[576,512]{1,0:T(8,128)(2,1)S(1)}, bf16[384,576]{1,0:T(8,128)(2,1)S(1)}, bf16[224,512]{1,0:T(8,128)(2,1)S(1)...) custom-call(bf16[576,512]{1,0:T(8,128)(2,1)} %bitcast.10, ...), custom_call_target="tpu_custom_call" | custom-call | flops 400000000 | bytes 2000000 | tf_op jit(solution)/shard_map/pack/pallas_call | solution.py:383
  2.8 6.1 %collective-permute-start = (bf16[224,512]{1,0:T(8,128)(2,1)S(1)}, bf16[224,512]{1,0:T(8,128)(2,1)S(1)}, u32[]{:S(2)}, u32[]{:S(2)}) collective-permute-start(bf16[224,512]{1,0:T(8,128)(2,1)S(1)} %get-tuple-element.67), channel_id=1, source_target_pairs={{0,224},{1,225},{2,226},{3,227},{4,228},{5,229},{6,230},{7,231},{8... | collective-permute-start | bytes 688136 | tf_op jit(solution)/shard_map/ppermute | solution.py:477
  9.2 1.2 %collective-permute-start.1 = (bf16[80,512]{1,0:T(8,128)(2,1)S(1)}, bf16[80,512]{1,0:T(8,128)(2,1)S(1)}, u32[]{:S(2)}, u32[]{:S(2)}) collective-permute-start(bf16[80,512]{1,0:T(8,128)(2,1)S(1)} %get-tuple-element.68), channel_id=1, source_target_pairs={{0,31},{1,0},{2,1},{3,2},{4,3},{5,4},{6,5},{7,6},{8,7},{9,8},{10,9... | collective-permute-start | bytes 245768 | tf_op jit(solution)/shard_map/ppermute | solution.py:478
  10.4 8.2 %collective-permute-start.2 = (bf16[80,512]{1,0:T(8,128)(2,1)S(1)}, bf16[80,512]{1,0:T(8,128)(2,1)S(1)}, u32[]{:S(2)}, u32[]{:S(2)}) collective-permute-start(bf16[80,512]{1,0:T(8,128)(2,1)S(1)} %get-tuple-element.69), channel_id=1, source_target_pairs={{0,255},{1,224},{2,225},{3,226},{4,227},{5,228},{6,229},{7,230},{8... | collective-permute-start | bytes 245768 | tf_op jit(solution)/shard_map/ppermute | solution.py:479
  18.7 2.3 %load.1 = (bf16[576,576]{1,0:T(8,128)(2,1)S(1)}, bf16[576,384]{1,0:T(8,128)(2,1)S(1)}, bf16[512,1536]{1,0:T(8,128)(2,1)S(1)}, bf16[512,512]{1,0:T(8,128)(2,1)S(1...) custom-call(bf16[576,512]{1,0:T(8,128)(2,1)S(1)} %get-tuple-element.63.f_vm.f_loc, ...), custom_call_target="tpu_custom_call" | custom-call | flops 1000000 | bytes 10000 | tf_op jit(solution)/shard_map/load/pallas_call | solution.py:396
  21.0 2.3 %collective-permute-start.5 = (bf16[80,512]{1,0:T(8,128)(2,1)S(1)}, bf16[80,512]{1,0:T(8,128)(2,1)S(1)}, u32[]{:S(2)}, u32[]{:S(2)}) collective-permute-start(bf16[80,512]{1,0:T(8,128)(2,1)S(1)} %get-tuple-element.76), channel_id=1, source_target_pairs={{0,255},{1,224},{2,225},{3,226},{4,227},{5,228},{6,229},{7,230},{8... | collective-permute-start | bytes 245768 | tf_op jit(solution)/shard_map/ppermute | solution.py:479
  23.4 4.2 %forward.1 = (bf16[576,512]{1,0:T(8,128)(2,1)S(1)}, bf16[576,1536]{1,0:T(8,128)(2,1)S(1)}, bf16[1152,576]{1,0:T(8,128)(2,1)S(1)}, bf16[576,512]{1,0:T(8,128)(2,1)S(1)}) custom-call(s32[4]{0:T(128)S(1)} %pad_add_fusion.place, bf16[576,512]{1,0:T(8,128)(2,1)S(1)} %get-tuple-element.65.refs_0_, bf16[576,384]{1,0:T(8,128)(2,1)S(1)} %get-tuple-element.66.refs_1_.p_halo, ...), custom_call_target="tpu_custom_call" | custom-call | flops 1000000 | bytes 10000 | tf_op jit(solution)/shard_map/forward/pallas_call | solution.py:410
  27.6 6.8 %backward.1 = (bf16[576,1536]{1,0:T(8,128)(2,1)S(1)}, bf16[256,2048]{1,0:T(8,128)(2,1)S(1)}, bf16[256,2048]{1,0:T(8,128)(2,1)S(1)}) custom-call(s32[4]{0:T(128)S(1)} %pad_add_fusion.place, bf16[576,512]{1,0:T(8,128)(2,1)S(1)} %get-tuple-element.73.refs_0_, bf16[576,384]{1,0:T(8,128)(2,1)S(1)} %get-tuple-element.66.refs_1_.p_halo, ...), custom_call_target="tpu_custom_call" | custom-call | flops 5000000000 | bytes 10000000 | tf_op jit(solution)/shard_map/backward/pallas_call | solution.py:424
  35.0 2.3 %collective-permute-done.6 = bf16[256,2048]{1,0:T(8,128)(2,1)S(1)} collective-permute-done((bf16[256,2048]{1,0:T(8,128)(2,1)S(1)}, bf16[256,2048]{1,0:T(8,128)(2,1)S(1)}, u32[]{:S(2)}, u32[]{:S(2)}) %collective-permute-start.6) | collective-permute-done | bytes 1048608 | tf_op jit(solution)/shard_map/ppermute | solution.py:53
  38.7 2.0 %collective-permute-start.8 = (bf16[64,2048]{1,0:T(8,128)(2,1)S(1)}, bf16[64,2048]{1,0:T(8,128)(2,1)S(1)}, u32[]{:S(2)}, u32[]{:S(2)}) collective-permute-start(bf16[64,2048]{1,0:T(8,128)(2,1)S(1)} %get-tuple-element.86), channel_id=1, source_target_pairs={{0,128},{1,33},{2,130},{3,35},{4,132},{5,37},{6,134},{7,39},{8,136... | collective-permute-start | bytes 786440 | tf_op jit(solution)/shard_map/ppermute | solution.py:53
  40.7 1.4 %collective-permute-start.9 = (bf16[64,2048]{1,0:T(8,128)(2,1)S(1)}, bf16[64,2048]{1,0:T(8,128)(2,1)S(1)}, u32[]{:S(2)}, u32[]{:S(2)}) collective-permute-start(bf16[64,2048]{1,0:T(8,128)(2,1)S(1)} %get-tuple-element.87), channel_id=1, source_target_pairs={{0,192},{1,49},{2,194},{3,51},{4,196},{5,53},{6,198},{7,55},{8,200... | collective-permute-start | bytes 786440 | tf_op jit(solution)/shard_map/ppermute | solution.py:53
  42.1 2.0 %back.1 = (bf16[576,1024]{1,0:T(8,128)(2,1)S(1)}, bf16[224,1024]{1,0:T(8,128)(2,1)S(1)}, bf16[80,1024]{1,0:T(8,128)(2,1)S(1)}, bf16[80,1024]{1,0:T(8,128)(2,1)S(1)}) custom-call(bf16[576,512]{1,0:T(8,128)(2,1)S(1)} %get-tuple-element.88.refs_9_.mixed, bf16[576,1536]{1,0:T(8,128)(2,1)S(1)} %get-tuple-element.89.gact, ...), custom_call_target="tpu_custom_call" | custom-call | flops 2000000000 | bytes 5000000 | tf_op jit(solution)/shard_map/back/pallas_call | solution.py:441
  44.4 2.8 %collective-permute-done.8 = bf16[64,2048]{1,0:T(8,128)(2,1)S(1)} collective-permute-done((bf16[64,2048]{1,0:T(8,128)(2,1)S(1)}, bf16[64,2048]{1,0:T(8,128)(2,1)S(1)}, u32[]{:S(2)}, u32[]{:S(2)}) %collective-permute-start.8) | collective-permute-done | bytes 262176 | tf_op jit(solution)/shard_map/ppermute | solution.py:53
  49.1 1.6 %collective-permute-start.12 = (bf16[16,2048]{1,0:T(8,128)(2,1)S(1)}, bf16[16,2048]{1,0:T(8,128)(2,1)S(1)}, u32[]{:S(2)}, u32[]{:S(2)}) collective-permute-start(bf16[16,2048]{1,0:T(8,128)(2,1)S(1)} %get-tuple-element.126), channel_id=1, source_target_pairs={{0,48},{1,193},{2,50},{3,195},{4,52},{5,197},{6,54},{7,199},{8,56}... | collective-permute-start | bytes 196616 | tf_op jit(solution)/shard_map/ppermute | solution.py:53
  51.0 4.3 %collective-permute-start.14 = (bf16[80,1024]{1,0:T(8,128)(2,1)S(1)}, bf16[80,1024]{1,0:T(8,128)(2,1)S(1)}, u32[]{:S(2)}, u32[]{:S(2)}) collective-permute-start(bf16[80,1024]{1,0:T(8,128)(2,1)S(1)} %get-tuple-element.98), channel_id=1, source_target_pairs={{0,1},{1,2},{2,3},{3,4},{4,5},{5,6},{6,7},{7,8},{8,9},{9,10},{10,1... | collective-permute-start | bytes 491528 | tf_op jit(solution)/shard_map/ppermute | solution.py:518
  55.4 1.7 %collective-permute-start.13 = (bf16[16,2048]{1,0:T(8,128)(2,1)S(1)}, bf16[16,2048]{1,0:T(8,128)(2,1)S(1)}, u32[]{:S(2)}, u32[]{:S(2)}) collective-permute-start(bf16[16,2048]{1,0:T(8,128)(2,1)S(1)} %add_convert_fusion.8), channel_id=1, source_target_pairs={{0,2},{1,3},{2,0},{3,1},{4,6},{5,7},{6,4},{7,5},{8,10},{9,11},{10,... | collective-permute-start | bytes 196616 | tf_op jit(solution)/shard_map/ppermute | solution.py:53
  57.1 1.7 %collective-permute-done.13 = bf16[16,2048]{1,0:T(8,128)(2,1)S(1)} collective-permute-done((bf16[16,2048]{1,0:T(8,128)(2,1)S(1)}, bf16[16,2048]{1,0:T(8,128)(2,1)S(1)}, u32[]{:S(2)}, u32[]{:S(2)}) %collective-permute-start.13) | collective-permute-done | bytes 65568 | tf_op jit(solution)/shard_map/ppermute | solution.py:53
  58.8 4.3 %collective-permute-start.15 = (bf16[16,2048]{1,0:T(8,128)(2,1)S(1)}, bf16[16,2048]{1,0:T(8,128)(2,1)S(1)}, u32[]{:S(2)}, u32[]{:S(2)}) collective-permute-start(bf16[16,2048]{1,0:T(8,128)(2,1)S(1)} %add_convert_fusion.7), channel_id=1, source_target_pairs={{0,4},{1,5},{2,6},{3,7},{4,0},{5,1},{6,2},{7,3},{8,12},{9,13},{10,... | collective-permute-start | bytes 196616 | tf_op jit(solution)/shard_map/ppermute | solution.py:53
  63.1 4.3 %collective-permute-start.18 = (bf16[80,1024]{1,0:T(8,128)(2,1)S(1)}, bf16[80,1024]{1,0:T(8,128)(2,1)S(1)}, u32[]{:S(2)}, u32[]{:S(2)}) collective-permute-start(bf16[80,1024]{1,0:T(8,128)(2,1)S(1)} %get-tuple-element.101), channel_id=1, source_target_pairs={{0,33},{1,34},{2,35},{3,36},{4,37},{5,38},{6,39},{7,40},{8,41},{9,... | collective-permute-start | bytes 491528 | tf_op jit(solution)/shard_map/ppermute | solution.py:519
  67.4 1.8 %collective-permute-start.17 = (bf16[224,1024]{1,0:T(8,128)(2,1)S(1)}, bf16[224,1024]{1,0:T(8,128)(2,1)S(1)}, u32[]{:S(2)}, u32[]{:S(2)}) collective-permute-start(bf16[224,1024]{1,0:T(8,128)(2,1)S(1)} %get-tuple-element.100), channel_id=1, source_target_pairs={{0,32},{1,33},{2,34},{3,35},{4,36},{5,37},{6,38},{7,39},{8,40},{9,... | collective-permute-start | bytes 1376264 | tf_op jit(solution)/shard_map/ppermute | solution.py:517
  69.2 4.0 %collective-permute-start.16 = (bf16[16,2048]{1,0:T(8,128)(2,1)S(1)}, bf16[16,2048]{1,0:T(8,128)(2,1)S(1)}, u32[]{:S(2)}, u32[]{:S(2)}) collective-permute-start(bf16[16,2048]{1,0:T(8,128)(2,1)S(1)} %add_convert_fusion.6), channel_id=1, source_target_pairs={{0,12},{1,13},{2,14},{3,15},{4,8},{5,9},{6,10},{7,11},{8,4},{9,5},... | collective-permute-start | bytes 196616 | tf_op jit(solution)/shard_map/ppermute | solution.py:53
  73.2 3.1 %collective-permute-done.16 = bf16[16,2048]{1,0:T(8,128)(2,1)S(1)} collective-permute-done((bf16[16,2048]{1,0:T(8,128)(2,1)S(1)}, bf16[16,2048]{1,0:T(8,128)(2,1)S(1)}, u32[]{:S(2)}, u32[]{:S(2)}) %collective-permute-start.16) | collective-permute-done | bytes 65568 | tf_op jit(solution)/shard_map/ppermute | solution.py:53
  76.3 6.9 %collective-permute-done.17.r_lat = bf16[224,1024]{1,0:T(8,128)(2,1)S(1)} collective-permute-done((bf16[224,1024]{1,0:T(8,128)(2,1)S(1)}, bf16[224,1024]{1,0:T(8,128)(2,1)S(1)}, u32[]{:S(2)}, u32[]{:S(2)}) %collective-permute-start.17) | collective-permute-done | bytes 458784 | tf_op jit(solution)/shard_map/ppermute | solution.py:517
  83.3 1.8 %collective-permute-start.20 = (bf16[16,2048]{1,0:T(8,128)(2,1)S(1)}, bf16[16,2048]{1,0:T(8,128)(2,1)S(1)}, u32[]{:S(2)}, u32[]{:S(2)}) collective-permute-start(bf16[16,2048]{1,0:T(8,128)(2,1)S(1)} %add_convert_fusion.5), channel_id=1, source_target_pairs={{0,32},{1,129},{2,34},{3,131},{4,36},{5,133},{6,38},{7,135},{8,40}... | collective-permute-start | bytes 196616 | tf_op jit(solution)/shard_map/ppermute | solution.py:53
  86.0 2.6 %collective-permute-done.21 = bf16[16,2048]{1,0:T(8,128)(2,1)S(1)} collective-permute-done((bf16[16,2048]{1,0:T(8,128)(2,1)S(1)}, bf16[16,2048]{1,0:T(8,128)(2,1)S(1)}, u32[]{:S(2)}, u32[]{:S(2)}) %collective-permute-start.21) | collective-permute-done | bytes 65568 | tf_op jit(solution)/shard_map/ppermute | solution.py:53
  90.9 1.4 %collective-permute-start.22 = (bf16[64,2048]{1,0:T(8,128)(2,1)S(1)}, bf16[64,2048]{1,0:T(8,128)(2,1)S(1)}, u32[]{:S(2)}, u32[]{:S(2)}) collective-permute-start(bf16[64,2048]{1,0:T(8,128)(2,1)S(1)} %pad_maximum_fusion.refs_0_), channel_id=1, source_target_pairs={{0,192},{1,49},{2,194},{3,51},{4,196},{5,53},{6,198},{7,55},{8,200... | collective-permute-start | bytes 786440 | tf_op jit(solution)/shard_map/ppermute | solution.py:53
  92.3 2.9 %finish.1 = (bf16[576,512]{1,0:T(8,128)(2,1)}, bf16[576,512]{1,0:T(8,128)(2,1)}) custom-call(bf16[576,512]{1,0:T(8,128)(2,1)S(1)} %get-tuple-element.63.f_vm.f_loc, bf16[576,512]{1,0:T(8,128)(2,1)S(1)} %get-tuple-element.64.c_vm.c_loc, bf16[576,1024]{1,0:T(8,128)(2,1)S(1)} %get-tuple-element.103.both, bf16[224,1024]{1,0:T(8,128)(2,1)S(1)} %collective-permute-done.17.r_lat, ...), custom_call_target="tpu_custom_call" | custom-call | flops 2000000000 | bytes 8000000 | tf_op jit(solution)/shard_map/finish/pallas_call | solution.py:453
  95.2 1.6 %collective-permute-start.25 = (bf16[64,2048]{1,0:T(8,128)(2,1)S(1)}, bf16[64,2048]{1,0:T(8,128)(2,1)S(1)}, u32[]{:S(2)}, u32[]{:S(2)}) collective-permute-start(bf16[64,2048]{1,0:T(8,128)(2,1)S(1)} %pad_maximum_fusion.refs_0_), channel_id=1, source_target_pairs={{0,1},{1,0},{2,3},{3,2},{4,5},{5,4},{6,7},{7,6},{8,9},{9,8},{10,11... | collective-permute-start | bytes 786440 | tf_op jit(solution)/shard_map/ppermute | solution.py:53
  96.8 1.9 %collective-permute-done.24.refs_3_ = bf16[64,2048]{1,0:T(8,128)(2,1)S(1)} collective-permute-done((bf16[64,2048]{1,0:T(8,128)(2,1)S(1)}, bf16[64,2048]{1,0:T(8,128)(2,1)S(1)}, u32[]{:S(2)}, u32[]{:S(2)}) %collective-permute-start.24) | collective-permute-done | bytes 262176 | tf_op jit(solution)/shard_map/ppermute | solution.py:53
  99.3 1.5 %collective-permute-start.26 = (bf16[64,2048]{1,0:T(8,128)(2,1)S(1)}, bf16[64,2048]{1,0:T(8,128)(2,1)S(1)}, u32[]{:S(2)}, u32[]{:S(2)}) collective-permute-start(bf16[64,2048]{1,0:T(8,128)(2,1)S(1)} %collective-permute-done.22.refs_1_), channel_id=1, source_target_pairs={{0,1},{1,0},{2,3},{3,2},{4,5},{5,4},{6,7},{7,6},{8,9},{9,8},{10,11... | collective-permute-start | bytes 786440 | tf_op jit(solution)/shard_map/ppermute | solution.py:53
  101.4 2.0 %weights0.1 = (f32[512,1536]{1,0:T(8,128)}, f32[512,512]{1,0:T(8,128)}, f32[1,512]{1,0:T(1,128)S(1)}) custom-call(s32[4]{0:T(128)S(1)} %pad_add_fusion.place, bf16[64,2048]{1,0:T(8,128)(2,1)S(1)} %pad_maximum_fusion.refs_0_, bf16[64,2048]{1,0:T(8,128)(2,1)S(1)} %collective-permute-done.22.refs_1_, bf16[64,2048]{1,0:T(8,128)(2,1)S(1)} %collective-permute-done.23.refs_2_, ...), custom_call_target="tpu_custom_call" | custom-call | flops 10000000 | bytes 4000000 | tf_op jit(solution)/shard_map/weights0/pallas_call | solution.py:327
  103.4 2.0 %weights1.1 = (f32[512,1536]{1,0:T(8,128)}, f32[512,512]{1,0:T(8,128)}, f32[1,512]{1,0:T(1,128)}) custom-call(s32[4]{0:T(128)S(1)} %pad_add_fusion.place, bf16[64,2048]{1,0:T(8,128)(2,1)S(1)} %collective-permute-done.25.refs_0_, bf16[64,2048]{1,0:T(8,128)(2,1)S(1)} %collective-permute-done.26.refs_1_, ...), custom_call_target="tpu_custom_call", output_to_operand_aliasing={{0}: (8, {}), {1}: (9, {})} | custom-call | flops 10000000 | bytes 4000000 | tf_op jit(solution)/shard_map/weights1/pallas_call | solution.py:327
  (43 shorter events, 9.3 us)
Async XLA Ops:
  2.8 20.6 %collective-permute-start = (bf16[224,512]{1,0:T(8,128)(2,1)S(1)}, bf16[224,512]{1,0:T(8,128)(2,1)S(1)}, u32[]{:S(2)}, u32[]{:S(2)}) collective-permute-start(bf16[224,512]{1,0:T(8,128)(2,1)S(1)} %get-tuple-element.67), channel_id=1, source_target_pairs={{0,224},{1,225},{2,226},{3,227},{4,228},{5,229},{6,230},{7,231},{8... | collective-permute-start | bytes 688136 | tf_op jit(solution)/shard_map/ppermute | solution.py:477
  8.9 18.7 %collective-permute-start.3 = (bf16[224,512]{1,0:T(8,128)(2,1)S(1)}, bf16[224,512]{1,0:T(8,128)(2,1)S(1)}, u32[]{:S(2)}, u32[]{:S(2)}) collective-permute-start(bf16[224,512]{1,0:T(8,128)(2,1)S(1)} %get-tuple-element.74), channel_id=1, source_target_pairs={{0,224},{1,225},{2,226},{3,227},{4,228},{5,229},{6,230},{7,231},{8... | collective-permute-start | bytes 688136 | tf_op jit(solution)/shard_map/ppermute | solution.py:477
  9.2 11.8 %collective-permute-start.1 = (bf16[80,512]{1,0:T(8,128)(2,1)S(1)}, bf16[80,512]{1,0:T(8,128)(2,1)S(1)}, u32[]{:S(2)}, u32[]{:S(2)}) collective-permute-start(bf16[80,512]{1,0:T(8,128)(2,1)S(1)} %get-tuple-element.68), channel_id=1, source_target_pairs={{0,31},{1,0},{2,1},{3,2},{4,3},{5,4},{6,5},{7,6},{8,7},{9,8},{10,9... | collective-permute-start | bytes 245768 | tf_op jit(solution)/shard_map/ppermute | solution.py:478
  10.4 13.0 %collective-permute-start.2 = (bf16[80,512]{1,0:T(8,128)(2,1)S(1)}, bf16[80,512]{1,0:T(8,128)(2,1)S(1)}, u32[]{:S(2)}, u32[]{:S(2)}) collective-permute-start(bf16[80,512]{1,0:T(8,128)(2,1)S(1)} %get-tuple-element.69), channel_id=1, source_target_pairs={{0,255},{1,224},{2,225},{3,226},{4,227},{5,228},{6,229},{7,230},{8... | collective-permute-start | bytes 245768 | tf_op jit(solution)/shard_map/ppermute | solution.py:479
  18.6 9.0 %collective-permute-start.4 = (bf16[80,512]{1,0:T(8,128)(2,1)S(1)}, bf16[80,512]{1,0:T(8,128)(2,1)S(1)}, u32[]{:S(2)}, u32[]{:S(2)}) collective-permute-start(bf16[80,512]{1,0:T(8,128)(2,1)S(1)} %get-tuple-element.75), channel_id=1, source_target_pairs={{0,31},{1,0},{2,1},{3,2},{4,3},{5,4},{6,5},{7,6},{8,7},{9,8},{10,9... | collective-permute-start | bytes 245768 | tf_op jit(solution)/shard_map/ppermute | solution.py:478
  21.0 6.6 %collective-permute-start.5 = (bf16[80,512]{1,0:T(8,128)(2,1)S(1)}, bf16[80,512]{1,0:T(8,128)(2,1)S(1)}, u32[]{:S(2)}, u32[]{:S(2)}) collective-permute-start(bf16[80,512]{1,0:T(8,128)(2,1)S(1)} %get-tuple-element.76), channel_id=1, source_target_pairs={{0,255},{1,224},{2,225},{3,226},{4,227},{5,228},{6,229},{7,230},{8... | collective-permute-start | bytes 245768 | tf_op jit(solution)/shard_map/ppermute | solution.py:479
  34.5 2.8 %collective-permute-start.6 = (bf16[256,2048]{1,0:T(8,128)(2,1)S(1)}, bf16[256,2048]{1,0:T(8,128)(2,1)S(1)}, u32[]{:S(2)}, u32[]{:S(2)}) collective-permute-start(bf16[256,2048]{1,0:T(8,128)(2,1)S(1)} %get-tuple-element.83), channel_id=1, source_target_pairs={{0,1},{1,0},{2,3},{3,2},{4,5},{5,4},{6,7},{7,6},{8,9},{9,8},{10,11... | collective-permute-start | bytes 3145736 | tf_op jit(solution)/shard_map/ppermute | solution.py:53
  37.6 6.8 %collective-permute-start.7 = (bf16[64,2048]{1,0:T(8,128)(2,1)S(1)}, bf16[64,2048]{1,0:T(8,128)(2,1)S(1)}, u32[]{:S(2)}, u32[]{:S(2)}) collective-permute-start(bf16[64,2048]{1,0:T(8,128)(2,1)S(1)} %get-tuple-element.85), channel_id=1, source_target_pairs={{0,64},{1,17},{2,66},{3,19},{4,68},{5,21},{6,70},{7,23},{8,72},{9,... | collective-permute-start | bytes 786440 | tf_op jit(solution)/shard_map/ppermute | solution.py:53
  38.7 8.5 %collective-permute-start.8 = (bf16[64,2048]{1,0:T(8,128)(2,1)S(1)}, bf16[64,2048]{1,0:T(8,128)(2,1)S(1)}, u32[]{:S(2)}, u32[]{:S(2)}) collective-permute-start(bf16[64,2048]{1,0:T(8,128)(2,1)S(1)} %get-tuple-element.86), channel_id=1, source_target_pairs={{0,128},{1,33},{2,130},{3,35},{4,132},{5,37},{6,134},{7,39},{8,136... | collective-permute-start | bytes 786440 | tf_op jit(solution)/shard_map/ppermute | solution.py:53
  40.7 7.2 %collective-permute-start.9 = (bf16[64,2048]{1,0:T(8,128)(2,1)S(1)}, bf16[64,2048]{1,0:T(8,128)(2,1)S(1)}, u32[]{:S(2)}, u32[]{:S(2)}) collective-permute-start(bf16[64,2048]{1,0:T(8,128)(2,1)S(1)} %get-tuple-element.87), channel_id=1, source_target_pairs={{0,192},{1,49},{2,194},{3,51},{4,196},{5,53},{6,198},{7,55},{8,200... | collective-permute-start | bytes 786440 | tf_op jit(solution)/shard_map/ppermute | solution.py:53
  48.0 7.3 %collective-permute-start.10 = (bf16[16,2048]{1,0:T(8,128)(2,1)S(1)}, bf16[16,2048]{1,0:T(8,128)(2,1)S(1)}, u32[]{:S(2)}, u32[]{:S(2)}) collective-permute-start(bf16[16,2048]{1,0:T(8,128)(2,1)S(1)} %get-tuple-element.125), channel_id=1, source_target_pairs={{0,16},{1,65},{2,18},{3,67},{4,20},{5,69},{6,22},{7,71},{8,24},{9,... | collective-permute-start | bytes 196616 | tf_op jit(solution)/shard_map/ppermute | solution.py:53
  49.1 6.2 %collective-permute-start.12 = (bf16[16,2048]{1,0:T(8,128)(2,1)S(1)}, bf16[16,2048]{1,0:T(8,128)(2,1)S(1)}, u32[]{:S(2)}, u32[]{:S(2)}) collective-permute-start(bf16[16,2048]{1,0:T(8,128)(2,1)S(1)} %get-tuple-element.126), channel_id=1, source_target_pairs={{0,48},{1,193},{2,50},{3,195},{4,52},{5,197},{6,54},{7,199},{8,56}... | collective-permute-start | bytes 196616 | tf_op jit(solution)/shard_map/ppermute | solution.py:53
  50.7 4.6 %collective-permute-start.11 = (bf16[16,2048]{1,0:T(8,128)(2,1)S(1)}, bf16[16,2048]{1,0:T(8,128)(2,1)S(1)}, u32[]{:S(2)}, u32[]{:S(2)}) collective-permute-start(bf16[16,2048]{1,0:T(8,128)(2,1)S(1)} %get-tuple-element.127), channel_id=1, source_target_pairs={{0,32},{1,129},{2,34},{3,131},{4,36},{5,133},{6,38},{7,135},{8,40}... | collective-permute-start | bytes 196616 | tf_op jit(solution)/shard_map/ppermute | solution.py:53
  51.0 7.8 %collective-permute-start.14 = (bf16[80,1024]{1,0:T(8,128)(2,1)S(1)}, bf16[80,1024]{1,0:T(8,128)(2,1)S(1)}, u32[]{:S(2)}, u32[]{:S(2)}) collective-permute-start(bf16[80,1024]{1,0:T(8,128)(2,1)S(1)} %get-tuple-element.98), channel_id=1, source_target_pairs={{0,1},{1,2},{2,3},{3,4},{4,5},{5,6},{6,7},{7,8},{8,9},{9,10},{10,1... | collective-permute-start | bytes 491528 | tf_op jit(solution)/shard_map/ppermute | solution.py:518
  55.4 3.4 %collective-permute-start.13 = (bf16[16,2048]{1,0:T(8,128)(2,1)S(1)}, bf16[16,2048]{1,0:T(8,128)(2,1)S(1)}, u32[]{:S(2)}, u32[]{:S(2)}) collective-permute-start(bf16[16,2048]{1,0:T(8,128)(2,1)S(1)} %add_convert_fusion.8), channel_id=1, source_target_pairs={{0,2},{1,3},{2,0},{3,1},{4,6},{5,7},{6,4},{7,5},{8,10},{9,11},{10,... | collective-permute-start | bytes 196616 | tf_op jit(solution)/shard_map/ppermute | solution.py:53
  58.8 10.4 %collective-permute-start.15 = (bf16[16,2048]{1,0:T(8,128)(2,1)S(1)}, bf16[16,2048]{1,0:T(8,128)(2,1)S(1)}, u32[]{:S(2)}, u32[]{:S(2)}) collective-permute-start(bf16[16,2048]{1,0:T(8,128)(2,1)S(1)} %add_convert_fusion.7), channel_id=1, source_target_pairs={{0,4},{1,5},{2,6},{3,7},{4,0},{5,1},{6,2},{7,3},{8,12},{9,13},{10,... | collective-permute-start | bytes 196616 | tf_op jit(solution)/shard_map/ppermute | solution.py:53
  63.1 10.1 %collective-permute-start.18 = (bf16[80,1024]{1,0:T(8,128)(2,1)S(1)}, bf16[80,1024]{1,0:T(8,128)(2,1)S(1)}, u32[]{:S(2)}, u32[]{:S(2)}) collective-permute-start(bf16[80,1024]{1,0:T(8,128)(2,1)S(1)} %get-tuple-element.101), channel_id=1, source_target_pairs={{0,33},{1,34},{2,35},{3,36},{4,37},{5,38},{6,39},{7,40},{8,41},{9,... | collective-permute-start | bytes 491528 | tf_op jit(solution)/shard_map/ppermute | solution.py:519
  67.4 15.8 %collective-permute-start.17 = (bf16[224,1024]{1,0:T(8,128)(2,1)S(1)}, bf16[224,1024]{1,0:T(8,128)(2,1)S(1)}, u32[]{:S(2)}, u32[]{:S(2)}) collective-permute-start(bf16[224,1024]{1,0:T(8,128)(2,1)S(1)} %get-tuple-element.100), channel_id=1, source_target_pairs={{0,32},{1,33},{2,34},{3,35},{4,36},{5,37},{6,38},{7,39},{8,40},{9,... | collective-permute-start | bytes 1376264 | tf_op jit(solution)/shard_map/ppermute | solution.py:517
  69.2 7.1 %collective-permute-start.16 = (bf16[16,2048]{1,0:T(8,128)(2,1)S(1)}, bf16[16,2048]{1,0:T(8,128)(2,1)S(1)}, u32[]{:S(2)}, u32[]{:S(2)}) collective-permute-start(bf16[16,2048]{1,0:T(8,128)(2,1)S(1)} %add_convert_fusion.6), channel_id=1, source_target_pairs={{0,12},{1,13},{2,14},{3,15},{4,8},{5,9},{6,10},{7,11},{8,4},{9,5},... | collective-permute-start | bytes 196616 | tf_op jit(solution)/shard_map/ppermute | solution.py:53
  83.2 5.4 %collective-permute-start.21 = (bf16[16,2048]{1,0:T(8,128)(2,1)S(1)}, bf16[16,2048]{1,0:T(8,128)(2,1)S(1)}, u32[]{:S(2)}, u32[]{:S(2)}) collective-permute-start(bf16[16,2048]{1,0:T(8,128)(2,1)S(1)} %add_convert_fusion.5), channel_id=1, source_target_pairs={{0,16},{1,65},{2,18},{3,67},{4,20},{5,69},{6,22},{7,71},{8,24},{9,... | collective-permute-start | bytes 196616 | tf_op jit(solution)/shard_map/ppermute | solution.py:53
  83.3 5.3 %collective-permute-start.20 = (bf16[16,2048]{1,0:T(8,128)(2,1)S(1)}, bf16[16,2048]{1,0:T(8,128)(2,1)S(1)}, u32[]{:S(2)}, u32[]{:S(2)}) collective-permute-start(bf16[16,2048]{1,0:T(8,128)(2,1)S(1)} %add_convert_fusion.5), channel_id=1, source_target_pairs={{0,32},{1,129},{2,34},{3,131},{4,36},{5,133},{6,38},{7,135},{8,40}... | collective-permute-start | bytes 196616 | tf_op jit(solution)/shard_map/ppermute | solution.py:53
  85.2 3.9 %collective-permute-start.19 = (bf16[16,2048]{1,0:T(8,128)(2,1)S(1)}, bf16[16,2048]{1,0:T(8,128)(2,1)S(1)}, u32[]{:S(2)}, u32[]{:S(2)}) collective-permute-start(bf16[16,2048]{1,0:T(8,128)(2,1)S(1)} %add_convert_fusion.5), channel_id=1, source_target_pairs={{0,48},{1,193},{2,50},{3,195},{4,52},{5,197},{6,54},{7,199},{8,56}... | collective-permute-start | bytes 196616 | tf_op jit(solution)/shard_map/ppermute | solution.py:53
  89.1 9.6 %collective-permute-start.24 = (bf16[64,2048]{1,0:T(8,128)(2,1)S(1)}, bf16[64,2048]{1,0:T(8,128)(2,1)S(1)}, u32[]{:S(2)}, u32[]{:S(2)}) collective-permute-start(bf16[64,2048]{1,0:T(8,128)(2,1)S(1)} %pad_maximum_fusion.refs_0_), channel_id=1, source_target_pairs={{0,64},{1,17},{2,66},{3,19},{4,68},{5,21},{6,70},{7,23},{8,72},{9,... | collective-permute-start | bytes 786440 | tf_op jit(solution)/shard_map/ppermute | solution.py:53
  89.8 8.9 %collective-permute-start.23 = (bf16[64,2048]{1,0:T(8,128)(2,1)S(1)}, bf16[64,2048]{1,0:T(8,128)(2,1)S(1)}, u32[]{:S(2)}, u32[]{:S(2)}) collective-permute-start(bf16[64,2048]{1,0:T(8,128)(2,1)S(1)} %pad_maximum_fusion.refs_0_), channel_id=1, source_target_pairs={{0,128},{1,33},{2,130},{3,35},{4,132},{5,37},{6,134},{7,39},{8,136... | collective-permute-start | bytes 786440 | tf_op jit(solution)/shard_map/ppermute | solution.py:53
  90.9 8.4 %collective-permute-start.22 = (bf16[64,2048]{1,0:T(8,128)(2,1)S(1)}, bf16[64,2048]{1,0:T(8,128)(2,1)S(1)}, u32[]{:S(2)}, u32[]{:S(2)}) collective-permute-start(bf16[64,2048]{1,0:T(8,128)(2,1)S(1)} %pad_maximum_fusion.refs_0_), channel_id=1, source_target_pairs={{0,192},{1,49},{2,194},{3,51},{4,196},{5,53},{6,198},{7,55},{8,200... | collective-permute-start | bytes 786440 | tf_op jit(solution)/shard_map/ppermute | solution.py:53
  95.2 8.1 %collective-permute-start.25 = (bf16[64,2048]{1,0:T(8,128)(2,1)S(1)}, bf16[64,2048]{1,0:T(8,128)(2,1)S(1)}, u32[]{:S(2)}, u32[]{:S(2)}) collective-permute-start(bf16[64,2048]{1,0:T(8,128)(2,1)S(1)} %pad_maximum_fusion.refs_0_), channel_id=1, source_target_pairs={{0,1},{1,0},{2,3},{3,2},{4,5},{5,4},{6,7},{7,6},{8,9},{9,8},{10,11... | collective-permute-start | bytes 786440 | tf_op jit(solution)/shard_map/ppermute | solution.py:53
  99.3 4.0 %collective-permute-start.26 = (bf16[64,2048]{1,0:T(8,128)(2,1)S(1)}, bf16[64,2048]{1,0:T(8,128)(2,1)S(1)}, u32[]{:S(2)}, u32[]{:S(2)}) collective-permute-start(bf16[64,2048]{1,0:T(8,128)(2,1)S(1)} %collective-permute-done.22.refs_1_), channel_id=1, source_target_pairs={{0,1},{1,0},{2,3},{3,2},{4,5},{5,4},{6,7},{7,6},{8,9},{9,8},{10,11... | collective-permute-start | bytes 786440 | tf_op jit(solution)/shard_map/ppermute | solution.py:53
  100.9 2.5 %collective-permute-start.27 = (bf16[64,2048]{1,0:T(8,128)(2,1)S(1)}, bf16[64,2048]{1,0:T(8,128)(2,1)S(1)}, u32[]{:S(2)}, u32[]{:S(2)}) collective-permute-start(bf16[64,2048]{1,0:T(8,128)(2,1)S(1)} %collective-permute-done.23.refs_2_), channel_id=1, source_target_pairs={{0,1},{1,0},{2,3},{3,2},{4,5},{5,4},{6,7},{7,6},{8,9},{9,8},{10,11... | collective-permute-start | bytes 786440 | tf_op jit(solution)/shard_map/ppermute | solution.py:53
  100.9 2.5 %collective-permute-start.28 = (bf16[64,2048]{1,0:T(8,128)(2,1)S(1)}, bf16[64,2048]{1,0:T(8,128)(2,1)S(1)}, u32[]{:S(2)}, u32[]{:S(2)}) collective-permute-start(bf16[64,2048]{1,0:T(8,128)(2,1)S(1)} %collective-permute-done.24.refs_3_), channel_id=1, source_target_pairs={{0,1},{1,0},{2,3},{3,2},{4,5},{5,4},{6,7},{7,6},{8,9},{9,8},{10,11... | collective-permute-start | bytes 786440 | tf_op jit(solution)/shard_map/ppermute | solution.py:53
